TPU v7x, 32 devices: a whole 2x2x4 slice. The times are simulated.
32 devices in a mesh: ctx: 8 (over z, y), head: 4 (over x, core).
Axes of the slice: x: 2, y: 2, z: 4, core: 2. Of those that a mesh axis runs over, the one named last changes fastest.
Arguments:
- queries: bfloat16 [8192, 12288], P('ctx', 'head'), may hold values from -24 to 24
- key_rows: bfloat16 [8192, 768], P('ctx'), may hold values from -6 to 6
- value_rows: bfloat16 [8192, 512], P('ctx'), may hold values from -6 to 6
- comp_key_weight: float32 [32, 768], replicated, may hold values from 0.35355338 to 0.70710677
- comp_value_weight: float32 [32, 512], replicated, may hold values from 0.17677669 to 0.53033006
- block_picks: int32 [32, 4, 16], P('ctx'), may hold values from 0 to 124, as said below
- gate_logits: float32 [8192, 3, 64], P('ctx', None, 'head'), may hold values from -6 to 6
- out_weight: bfloat16 [8192, 2560], P('head'), may hold values from -0.25 to 0.25
Outputs:
- layer_out: bfloat16 [8192, 2560], P(('ctx', 'head'))
Inputs may be any that keep to these rules, and one draw needn't show every extreme that they name: `block_picks`: for each group, the lists of the 256-position query blocks held by one ctx shard name exactly 1024 / 256 distinct blocks of each earlier shard and of their own shard, and none of later shards; the own-shard blocks named are the first blocks of those query blocks. Every list names the first block of its own query block. Names may repeat within a list.
All inputs are finite; a program needn't handle non-finite values.
Results may differ from a plain program's by a relative error of at most 0.03.
Values may be sent and summed in bfloat16 or wider, within the bound.
No kernel may reach another device: no remote copies, remote signals or barrier semaphores. Data moves between devices by JAX's collectives and lax.ppermute only.
A program may use at most 192 MiB of HBM per device.

v0:
```python
import functools

import jax
import jax.numpy as jnp
from jax import lax
from jax.experimental import pallas as pl
from jax.experimental.pallas import tpu as pltpu
from jax.sharding import PartitionSpec as P

HEADS = 64
GROUPS = 4
QK = 192
DV = 128
CBLK = 32
KBLK = 64
PICKS = 16
WINDOW = 512
QBLK = 256
PAIR = 2 * QK
BROWS = KBLK + KBLK // 2 + KBLK
VMEM_LIMIT = 50 * 1024 * 1024
NEG = -1e30
SCALE = QK ** (-0.5) * 1.4426950408889634
NT = (((1,), (1,)), ((), ()))
F32 = jnp.float32
BF16 = jnp.bfloat16


def half_lanes(rows):
    return lax.broadcasted_iota(jnp.int32, (rows, 128), 1) < 64


def swap_halves(x):
    return pltpu.roll(x, 64, 1)


def shift_matrix():
    return jnp.where(iota(256, 256, 1) == iota(256, 256, 0) + 64, 1.0, 0.0).astype(BF16)


def shifted_keys(even):
    return jnp.dot(even, shift_matrix(), preferred_element_type=F32).astype(BF16)


def with_ones(values):
    return jnp.concatenate([values, jnp.ones_like(values)], axis=1)


def prep_kernel(group_ref, keys_ref, values_ref, kw_ref, vw_ref, packed_ref, even_ref, odd_ref, val_ref):
    group = group_ref[0]
    odd = lax.rem(group, 2) == 1
    first = pl.multiple_of(lax.div(group, 2) * PAIR, 128)
    vfirst = pl.multiple_of(group * DV, 128)

    def own_columns(ref):
        t0 = ref[:, pl.ds(first, 128)].astype(F32)
        t1 = ref[:, pl.ds(first + 128, 128)].astype(F32)
        t2 = ref[:, pl.ds(first + 256, 128)].astype(F32)
        r1, r2 = swap_halves(t1), swap_halves(t2)
        left = half_lanes(t0.shape[0])
        low = jnp.where(odd, jnp.where(left, r1, r2), t0)
        high = jnp.where(left, jnp.where(odd, r2, t1), 0.0)
        return low, high

    low, high = own_columns(keys_ref)
    values = values_ref[:, pl.ds(vfirst, DV)]
    rows = low.shape[0]
    count = rows // KBLK
    high3 = high.reshape(count, KBLK, 128)
    packed_high = high3[:, : KBLK // 2] + swap_halves(
        high3[:, KBLK // 2 :].reshape(count * KBLK // 2, 128)
    ).reshape(count, KBLK // 2, 128)
    even = jnp.concatenate([low.astype(BF16), high.astype(BF16)], axis=1)
    even_ref[...] = even
    odd_ref[...] = shifted_keys(even)
    val_ref[...] = with_ones(values)
    for block in range(count):
        at = block * BROWS
        token = slice(block * KBLK, block * KBLK + KBLK)
        packed_ref[at : at + KBLK] = low[token].astype(BF16)
        packed_ref[at + KBLK : at + KBLK + KBLK // 2] = packed_high[block].astype(BF16)
        packed_ref[at + KBLK + KBLK // 2 : at + BROWS] = values[token]

    wlow, whigh = own_columns(kw_ref)
    wval = vw_ref[:, pl.ds(vfirst, DV)]
    folds = rows // CBLK

    def fold(x, w):
        return jnp.sum(x.reshape(folds, CBLK, 128) * w[None], axis=1).astype(BF16)

    at = count * BROWS
    packed_ref[at : at + folds] = fold(low, wlow)
    packed_ref[at + folds : at + 2 * folds] = fold(high, whigh)
    packed_ref[at + 2 * folds :] = fold(values.astype(F32), wval)


def pack_kernel(groups, lists, per_owner, me_ref, *refs):
    picks, (own_ref, other_ref), outs = refs[:groups], refs[groups : groups + 2], refs[groups + 2 :]
    me = me_ref[0]
    parity = lax.rem(me, 2)
    base = me - parity
    data = per_owner * BROWS
    folded = own_ref.shape[0] - data
    for distance in range(groups):
        out = outs[distance]

        @pl.when(base + 2 * distance < 2 * groups)
        def _():
            named = [jnp.int32(0), jnp.int32(0)]
            for row in range(lists):
                for col in range(PICKS):
                    entry = picks[distance][row, col]
                    for side in range(2):
                        block = entry - (base + side) * per_owner
                        here = (block >= 0) & (block < per_owner)
                        bit = jnp.int32(1) << jnp.where(here, block, 0)
                        named[side] = named[side] | jnp.where(here, bit, 0)
            for mine, ref in ((True, own_ref), (False, other_ref)):
                side = parity if mine else 1 - parity
                bits = jnp.where(side == 0, named[0], named[1])
                rank = jnp.int32(0)
                for block in range(per_owner):
                    bit = (bits >> block) & 1

                    @pl.when((bit == 1) & (rank < lists))
                    def _():
                        at = pl.multiple_of(
                            (side * lists + jnp.minimum(rank, lists - 1)) * BROWS, 16
                        )
                        out[pl.ds(at, BROWS)] = ref[block * BROWS : (block + 1) * BROWS]

                    rank = rank + bit
                at = pl.multiple_of(2 * lists * BROWS + side * folded, 16)
                out[pl.ds(at, folded)] = ref[data:]


def unpack(ref, at, count):
    lows, packed, values = [], [], []
    for block in range(count):
        first = at + block * BROWS
        lows.append(ref[first : first + KBLK])
        packed.append(ref[first + KBLK : first + KBLK + KBLK // 2])
        values.append(ref[first + KBLK + KBLK // 2 : first + BROWS])
    packed = jnp.concatenate(packed, axis=0)
    row, col = iota(128, 256, 0), iota(128, 256, 1)
    take = (row == jnp.where(col < 128, col, col - 64)) & (lax.rem(col, 128) < 64)
    both = jnp.dot(packed, take.astype(BF16), preferred_element_type=F32).astype(BF16)
    half = KBLK // 2
    highs = []
    for block in range(count):
        rows = slice(block * half, block * half + half)
        highs += [both[rows, :128], both[rows, 128:]]
    even = jnp.concatenate(
        [jnp.concatenate(lows, axis=0), jnp.concatenate(highs, axis=0)], axis=1
    )
    return even, jnp.concatenate(values, axis=0)


def rim_kernel(rim_at, shard_ref, near_ref, far_ref, even_in, odd_in, val_in, even_ref, odd_ref, val_ref):
    shard = shard_ref[0]
    rim_blocks = WINDOW // KBLK
    even_ref[WINDOW:] = even_in[:WINDOW]
    odd_ref[WINDOW:] = odd_in[:WINDOW]
    val_ref[WINDOW:] = val_in[:WINDOW]

    def fill(ref, at):
        even, values = unpack(ref, at, rim_blocks)
        even_ref[:WINDOW] = even
        odd_ref[:WINDOW] = shifted_keys(even)
        val_ref[:WINDOW] = with_ones(values)

    @pl.when(lax.rem(shard, 2) == 1)
    def _():
        fill(near_ref, rim_at)

    @pl.when((lax.rem(shard, 2) == 0) & (shard > 0))
    def _():
        fill(far_ref, 0)

    @pl.when(shard == 0)
    def _():
        even_ref[:WINDOW] = jnp.broadcast_to(even_in[:1], (WINDOW, 256))
        odd_ref[:WINDOW] = jnp.broadcast_to(odd_in[:1], (WINDOW, 256))
        val_ref[:WINDOW] = jnp.zeros((WINDOW, 256), BF16)


def pool_kernel(groups, lists, shard_ref, *refs):
    ins, (even_ref, odd_ref, val_ref, ceven_ref, codd_ref, cval_ref) = refs[:groups], refs[groups:]
    shard = shard_ref[0]
    base = shard - lax.rem(shard, 2)
    blocks = 2 * lists
    rows = blocks * KBLK
    folds = (ins[0].shape[0] - blocks * BROWS) // 6
    ceven_ref[...] = jnp.zeros_like(ceven_ref)
    codd_ref[...] = jnp.zeros_like(codd_ref)
    cval_ref[...] = jnp.zeros_like(cval_ref)
    for distance in range(groups):
        ref = ins[distance]

        @pl.when(base >= 2 * distance)
        def _():
            even, values = unpack(ref, 0, blocks)
            at = slice(distance * rows, distance * rows + rows)
            even_ref[at] = even
            odd_ref[at] = shifted_keys(even)
            val_ref[at] = with_ones(values)
            for side in range(2):
                first = blocks * BROWS + side * 3 * folds
                low = ref[first : first + folds]
                high = ref[first + folds : first + 2 * folds]
                folded = jnp.concatenate([low, high], axis=1)
                place = pl.ds(pl.multiple_of((base - 2 * distance + side) * folds, 32), folds)
                ceven_ref[place] = folded
                codd_ref[place] = shifted_keys(folded)
                cval_ref[place] = with_ones(ref[first + 2 * folds : first + 3 * folds])


def iota(rows, cols, axis):
    return lax.broadcasted_iota(jnp.int32, (rows, cols), axis)


def attend(q, keys, values, mask, floor=None):
    scores = lax.dot_general(q, keys, NT, preferred_element_type=F32)
    scores = mask(scores)
    top = jnp.max(scores, axis=1, keepdims=True)
    if floor is not None:
        top = jnp.maximum(top, floor)
    weights = jnp.exp2(scores * SCALE - top * SCALE).astype(BF16)
    out = jnp.dot(weights, values, preferred_element_type=F32)
    return out[:, :DV], out[:, DV:]


def stacked(x, times):
    return jnp.concatenate([x] * times, axis=0) if times > 1 else x


def stacked_queries(q_ref, side):
    pairs = q_ref.shape[1] // PAIR
    return jnp.concatenate(
        [q_ref[:, p * PAIR + side * 128 : p * PAIR + side * 128 + 256] for p in range(pairs)],
        axis=0,
    )


def gate_columns(gate_ref, first, branch, heads, side, count):
    turned = pltpu.roll(gate_ref[...], lax.rem(128 - first, 128), 1)
    at = branch * heads + side
    rows = turned.shape[0]
    return jnp.concatenate(
        [
            jnp.broadcast_to(turned[:, at + 2 * p : at + 2 * p + 1], (rows, DV))
            for p in range(count)
        ],
        axis=0,
    )


def near_kernel(heads, q_ref, gate_ref, even_ref, odd_ref, val_ref, *refs):
    out_ref = refs[-1]
    rows = pl.ds(pl.multiple_of(pl.program_id(0) * QBLK, QBLK), WINDOW + QBLK)
    pairs = q_ref.shape[1] // PAIR
    first = pl.program_id(1) * 2 * pairs

    def mask(scores):
        row, col = iota(QBLK, QBLK, 0), iota(QBLK, QBLK, 1)
        old = jnp.where(stacked(col >= row, pairs), scores[:, :QBLK], NEG)
        new = jnp.where(stacked(col <= row, pairs), scores[:, WINDOW:], NEG)
        return jnp.concatenate([old, scores[:, QBLK:WINDOW], new], axis=1)

    for side in range(2):
        keys = (even_ref, odd_ref)[side][rows]
        num, den = attend(stacked_queries(q_ref, side), keys, val_ref[rows], mask)
        total = gate_columns(gate_ref, first, 2, heads, side, pairs) * (num / den)
        for p in range(pairs):
            at = (2 * p + side) * DV
            out_ref[:, at : at + DV] = total[p * QBLK : (p + 1) * QBLK]


def near_branch(first_block, block_count, queries, gates, even, odd, val, prior):
    tokens, width = queries.shape
    heads = width // QK
    steps = heads // 4
    row_block = lambda i, p: (i + first_block, p)
    whole = lambda x: pl.BlockSpec(x.shape, lambda i, p: (0,) * x.ndim)
    operands = [queries, gates, even, odd, val]
    specs = [
        pl.BlockSpec((QBLK, 2 * PAIR), row_block),
        pl.BlockSpec((QBLK, 128), lambda i, p: (i + first_block, 0)),
        whole(even),
        whole(odd),
        whole(val),
    ]
    alias = {}
    if prior is not None:
        alias = {len(operands): 0}
        operands.append(prior)
        specs.append(pl.BlockSpec(memory_space=pl.ANY))
    rows = block_count * QBLK * heads
    return pl.pallas_call(
        functools.partial(near_kernel, heads),
        grid=(block_count, steps),
        in_specs=specs,
        out_specs=pl.BlockSpec((QBLK, 4 * DV), row_block),
        out_shape=jax.ShapeDtypeStruct((tokens, heads * DV), F32),
        input_output_aliases=alias,
        compiler_params=pltpu.CompilerParams(vmem_limit_bytes=VMEM_LIMIT),
        cost_estimate=pl.CostEstimate(
            flops=rows * (WINDOW + QBLK) * 1024,
            bytes_accessed=rows * (2 * QK + 4 * DV),
            transcendentals=0,
        ),
        name="near_branch",
    )(*operands)


def chosen_kernel(heads, *refs):
    meta_ref, slots_ref, dead_ref, q_ref, gate_ref, near_ref = refs[:6]
    pools, cfold, (weight_ref, out_ref) = refs[6:9], refs[9:12], refs[12:14]
    keys, (attended, weight, weight_sem) = refs[14:17], refs[17:]
    step = pl.program_id(0)
    last = pl.num_programs(0) - 1
    rows = q_ref.shape[0]
    pairs = q_ref.shape[1] // PAIR
    first = step * 2 * pairs
    list_at = meta_ref[1] * PICKS
    first_row = meta_ref[2]
    position = meta_ref[3]
    copy = pltpu.make_async_copy(weight_ref, weight, weight_sem)

    @pl.when(step == 0)
    def _():
        for slot in range(PICKS):
            source = pl.multiple_of(slots_ref[list_at + slot] * KBLK, KBLK)
            for pool, key in zip(pools, keys):
                key[slot * KBLK : (slot + 1) * KBLK] = pool[pl.ds(source, KBLK)]
        for slot in range(1, PICKS):

            @pl.when(dead_ref[list_at + slot] == 1)
            def _():
                at = slice(slot * KBLK, (slot + 1) * KBLK)
                for key in keys[:2]:
                    key[at] = jnp.broadcast_to(key[:1], (KBLK, 256))
                keys[2][at] = jnp.zeros((KBLK, 256), BF16)

        copy.start()

    def own_mask(scores):
        row, col = iota(rows, 128, 0) + first_row, iota(rows, 128, 1)
        keep = stacked((col >= KBLK) | (col <= row), pairs)
        own = jnp.where(keep, scores[:, :128], NEG)
        return jnp.concatenate([own, scores[:, 128:]], axis=1)

    def comp_mask(scores):
        cols = scores.shape[1]
        ends = (iota(rows, cols, 1) + 1) * CBLK - 1
        return jnp.where(stacked(ends <= position + iota(rows, cols, 0), pairs), scores, NEG)

    for side in range(2):
        q = stacked_queries(q_ref, side)
        num, den = attend(q, keys[side][...], keys[2][...], own_mask)
        total = gate_columns(gate_ref, first, 1, heads, side, pairs) * (num / den)
        num, den = attend(q, cfold[side][...], cfold[2][...], comp_mask, -1e29)
        gate = gate_columns(gate_ref, first, 0, heads, side, pairs)
        total = total + gate * (num / jnp.maximum(den, 1.0))
        for p in range(pairs):
            at = (2 * p + side) * DV
            mixed = near_ref[:, at : at + DV] + total[p * rows : (p + 1) * rows]
            attended[step, :, at : at + DV] = mixed.astype(BF16)

    @pl.when(step == last)
    def _():
        copy.wait()
        rows_in = jnp.concatenate([attended[s] for s in range(heads // 4)], axis=1)
        for at in range(0, out_ref.shape[1], 256):
            out_ref[:, at : at + 256] = jnp.dot(
                rows_in, weight[:, at : at + 256], preferred_element_type=F32
            ).astype(out_ref.dtype)


def chosen_and_project(chunk, rows, shard, slots, dead, queries, gates, near, pools, out_weight):
    tokens, width = queries.shape
    heads = width // QK
    steps = heads // 4
    model = out_weight.shape[1]
    start = chunk * rows
    meta = jnp.stack([chunk, start // QBLK, lax.rem(start, QBLK), shard * tokens + start])
    whole = lambda x: pl.BlockSpec(x.shape, lambda p, *_: (0,) * x.ndim)
    return pl.pallas_call(
        functools.partial(chosen_kernel, heads),
        grid_spec=pltpu.PrefetchScalarGridSpec(
            num_scalar_prefetch=3,
            grid=(steps,),
            in_specs=[
                pl.BlockSpec((rows, 2 * PAIR), lambda p, m, *_: (m[0], p)),
                pl.BlockSpec((rows, 128), lambda p, m, *_: (m[0], 0)),
                pl.BlockSpec((rows, 4 * DV), lambda p, m, *_: (m[0], p)),
            ]
            + [whole(x) for x in pools]
            + [pl.BlockSpec(memory_space=pl.ANY)],
            out_specs=pl.BlockSpec((rows, model), lambda p, *_: (0, 0)),
            scratch_shapes=[pltpu.VMEM((PICKS * KBLK, 256), BF16)] * 3
            + [
                pltpu.VMEM((steps, rows, 4 * DV), BF16),
                pltpu.VMEM(out_weight.shape, BF16),
                pltpu.SemaphoreType.DMA,
            ],
        ),
        out_shape=jax.ShapeDtypeStruct((rows, model), BF16),
        compiler_params=pltpu.CompilerParams(vmem_limit_bytes=VMEM_LIMIT),
        cost_estimate=pl.CostEstimate(
            flops=rows * heads * (PICKS * KBLK * 1280 + 2 * DV * model),
            bytes_accessed=out_weight.size * 2 + rows * width * 2,
            transcendentals=0,
        ),
        name="chosen_and_project",
    )(meta.astype(jnp.int32), slots, dead, queries, gates, near, *pools, out_weight)


def plan_picks(my_picks, shard, per_owner, n_ctx):
    lists = my_picks.shape[0]
    first = shard * per_owner + jnp.arange(lists, dtype=jnp.int32) * (QBLK // KBLK)
    place = jnp.arange(PICKS, dtype=jnp.int32)[None, :]
    found = jnp.min(jnp.where(my_picks == first[:, None], place, PICKS), axis=1, keepdims=True)
    ordered = jnp.where(place == found, my_picks[:, :1], my_picks)
    ordered = jnp.where(place == 0, first[:, None], ordered)
    repeated = jnp.any(
        (ordered[:, :, None] == ordered[:, None, :]) & (place[0][None, :] < place[0][:, None]),
        axis=-1,
    )
    dead = repeated | (ordered > first[:, None])
    named = jnp.any(
        my_picks.reshape(-1)[None, :] == jnp.arange(n_ctx * per_owner, dtype=jnp.int32)[:, None],
        axis=1,
    ).astype(jnp.int32)
    owner_start = (ordered // per_owner) * per_owner
    block = jnp.arange(n_ctx * per_owner, dtype=jnp.int32)
    before = (block >= owner_start[..., None]) & (block < ordered[..., None])
    rank = jnp.sum(jnp.where(before, named, 0), axis=-1)
    owner = ordered // per_owner
    slot = (shard // 2 - owner // 2) * 2 * lists + lax.rem(owner, 2) * lists
    slot = slot + jnp.minimum(rank, lists - 1)
    slot = jnp.clip(slot, 0, n_ctx * lists - 1)
    return slot.reshape(-1).astype(jnp.int32), dead.reshape(-1).astype(jnp.int32)


def local(
    queries,
    key_rows,
    value_rows,
    comp_key_weight,
    comp_value_weight,
    block_picks,
    gate_logits,
    out_weight,
):
    tokens = queries.shape[0]
    heads = queries.shape[1] // QK
    n_ctx, n_head = lax.axis_size("ctx"), lax.axis_size("head")
    shard, head_at = lax.axis_index("ctx"), lax.axis_index("head")
    group = head_at * heads // (HEADS // GROUPS)
    per_owner = tokens // KBLK
    lists = tokens // QBLK
    folds = tokens // CBLK
    groups = n_ctx // 2
    rim_blocks = WINDOW // KBLK
    packed_rows = per_owner * BROWS
    params = pltpu.CompilerParams(vmem_limit_bytes=VMEM_LIMIT)
    smem = pl.BlockSpec(memory_space=pltpu.SMEM)
    vmem = pl.BlockSpec(memory_space=pltpu.VMEM)
    bf16 = lambda *shape: jax.ShapeDtypeStruct(shape, BF16)

    my_picks = lax.dynamic_index_in_dim(block_picks, group, 1, keepdims=False)
    picks = [my_picks] + [
        lax.ppermute(my_picks, "ctx", [(i, i - 2 * d) for i in range(2 * d, n_ctx)])
        for d in range(1, groups)
    ]
    packed, even, odd, val = pl.pallas_call(
        prep_kernel,
        in_specs=[smem] + [vmem] * 4,
        out_specs=[vmem] * 4,
        out_shape=[bf16(packed_rows + 3 * folds, 128)] + [bf16(tokens, 256)] * 3,
        compiler_params=params,
        name="prep",
    )(group.reshape(1), key_rows, value_rows, comp_key_weight, comp_value_weight)
    other = lax.ppermute(packed, "ctx", [(i, i ^ 1) for i in range(n_ctx)])
    rim_at = (per_owner - rim_blocks) * BROWS
    far_rim = lax.ppermute(
        packed[rim_at:packed_rows], "ctx", [(i, i + 1) for i in range(1, n_ctx - 1, 2)]
    )

    gates = jax.nn.sigmoid(gate_logits).reshape(tokens, 3 * heads)
    gates = jnp.pad(gates, ((0, 0), (0, 128 - 3 * heads)))
    reach = WINDOW // QBLK
    mixed = near_branch(reach, lists - reach, queries, gates, even, odd, val, None)

    sent_rows = 2 * lists * BROWS + 6 * folds
    sends = pl.pallas_call(
        functools.partial(pack_kernel, groups, lists, per_owner),
        in_specs=[smem] * (1 + groups) + [vmem] * 2,
        out_specs=[vmem] * groups,
        out_shape=[bf16(sent_rows, 128)] * groups,
        compiler_params=params,
        name="pack",
    )(shard.reshape(1), *picks, packed, other)
    received = [sends[0]] + [
        lax.ppermute(sends[d], "ctx", [(i, i + 2 * d) for i in range(n_ctx - 2 * d)])
        for d in range(1, groups)
    ]

    ext = pl.pallas_call(
        functools.partial(rim_kernel, rim_at),
        in_specs=[smem] + [vmem] * 5,
        out_specs=[vmem] * 3,
        out_shape=[bf16(2 * WINDOW, 256)] * 3,
        compiler_params=params,
        name="rim",
    )(shard.reshape(1), other, far_rim, even, odd, val)
    mixed = near_branch(0, reach, queries, gates, *ext, mixed)

    slots, dead = plan_picks(my_picks, shard, per_owner, n_ctx)
    pools = pl.pallas_call(
        functools.partial(pool_kernel, groups, lists),
        in_specs=[smem] + [vmem] * groups,
        out_specs=[vmem] * 6,
        out_shape=[bf16(n_ctx * lists * KBLK, 256)] * 3 + [bf16(n_ctx * folds, 256)] * 3,
        compiler_params=params,
        name="pool",
    )(shard.reshape(1), *received)
    rows = tokens // n_head
    project = lambda chunk: chosen_and_project(
        chunk, rows, shard, slots, dead, queries, gates, mixed, pools, out_weight
    )
    chips = n_head // 2
    chip, core = head_at // 2, lax.rem(head_at, 2)
    across = [(i, i ^ 1) for i in range(n_head)]
    arrived = []
    for step in range(1, chips):
        target = lax.rem(chip + step, chips) * 2
        other = lax.ppermute(project(target + 1 - core), "head", across)
        mine = project(target + core)
        summed = (mine.astype(F32) + other.astype(F32)).astype(BF16)
        route = [(i, (i + 2 * step) % n_head) for i in range(n_head)]
        arrived.append(lax.ppermute(summed, "head", route))
    arrived.append(lax.ppermute(project(chip * 2 + 1 - core), "head", across))
    total = project(head_at).astype(F32)
    for part in arrived:
        total = total + part.astype(F32)
    return total.astype(BF16)


def solution(mesh):
    placed = (
        P("ctx", "head"),
        P("ctx", None),
        P("ctx", None),
        P(),
        P(),
        P("ctx", None, None),
        P("ctx", None, "head"),
        P("head", None),
    )
    return jax.shard_map(
        local, mesh=mesh, in_specs=placed, out_specs=P(("ctx", "head"), None), check_vma=False
    )
```

profile of v0, /device:TPU:30, one launch (start us, length us, event | category | flops | bytes accessed | tf_op | source)
XLA Modules:
  0.0 163.6 jit_solution(12554150076907453072)
XLA Ops:
  0.5 1.4 fusion.5
  1.9 2.3 %collective-permute-start.2 = (s32[4,16]{1,0:T(4,128)S(1)}, s32[4,16]{1,0:T(4,128)S(1)}, u32[]{:S(2)}, u32[]{:S(2)}) collective-permute-start(s32[4,16]{1,0:T(4,128)S(1)} %bitcast.21), channel_id=1, source_target_pairs={{8,0},{12,4},{16,8},{20,12},{24,16},{28,20},{9,1},{13,5},{17,9},{2... | collective-permute-start | bytes 776 | tf_op jit(solution)/shard_map/ppermute | solution.py:474
  4.2 2.2 %collective-permute-start.3 = (s32[4,16]{1,0:T(4,128)S(1)}, s32[4,16]{1,0:T(4,128)S(1)}, u32[]{:S(2)}, u32[]{:S(2)}) collective-permute-start(s32[4,16]{1,0:T(4,128)S(1)} %bitcast.22), channel_id=1, source_target_pairs={{16,0},{20,4},{24,8},{28,12},{17,1},{21,5},{25,9},{29,13},{18,2},{... | collective-permute-start | bytes 776 | tf_op jit(solution)/shard_map/ppermute | solution.py:474
  6.5 1.3 collective-permute-start.4
  7.8 1.2 copy-done.3
  9.0 0.9 copy-done.4
  9.9 0.8 copy-done.5
  10.7 2.2 %prep.1 = (bf16[2656,128]{1,0:T(8,128)(2,1)S(1)}, bf16[1024,256]{1,0:T(8,128)(2,1)S(1)}, bf16[1024,256]{1,0:T(8,128)(2,1)S(1)}, bf16[1024,256]{1,0:T(8,128)(2,1)S(1)}) custom-call(s32[1]{0:T(128)} %bitcast.8.group_ref, bf16[1024,768]{1,0:T(8,128)(2,1)} %keys_ref.1, bf16[1024,512]{1,0:T(8,128)(2,1)S(1)} %copy-done.3, f32[32,768]{1,0:T(8,128)S(1)} %copy-done.4, ...), custom_call_target="tpu_custom_call" | custom-call | tf_op jit(solution)/shard_map/prep/pallas_call | solution.py:477
  12.9 0.6 collective-permute-start
  13.5 0.8 slice.7
  14.3 1.4 collective-permute-start.1
  16.8 1.0 copy.12
  18.0 1.1 pad.4.gate_ref.refs_4_
  19.1 14.8 %near_branch.2.refs_0_ = f32[1024,2048]{1,0:T(8,128)} custom-call(bf16[1024,3072]{1,0:T(8,128)(2,1)} %refs_3_.7, f32[1024,128]{1,0:T(8,128)S(1)} %pad.4.gate_ref.refs_4_, bf16[1024,256]{1,0:T(8,128)(2,1)S(1)} %get-tuple-element.23.even_in.even_ref, bf16[1024,256]{1,0:T(8,128)(2,1)S(1)} %get-tuple-element.24.odd_in.odd_ref, ...), custom_call_target="tpu_custom_call" | custom-call | flops 6442450944 | bytes 7340032 | tf_op jit(solution)/shard_map/near_branch/pallas_call | solution.py:299
  34.8 1.2 pack.1
  36.0 1.3 collective-permute-start.5
  37.3 1.3 collective-permute-start.6
  38.6 1.3 collective-permute-start.7
  40.0 1.6 rim.1
  41.6 15.1 %near_branch.3.refs_5_ = f32[1024,2048]{1,0:T(8,128)} custom-call(bf16[1024,3072]{1,0:T(8,128)(2,1)} %refs_3_.7, f32[1024,128]{1,0:T(8,128)S(1)} %pad.4.gate_ref.refs_4_, bf16[1024,256]{1,0:T(8,128)(2,1)S(1)} %get-tuple-element.26.even_ref, bf16[1024,256]{1,0:T(8,128)(2,1)S(1)} %get-tuple-element.27.odd_ref, ...), custom_call_target="tpu_custom_call", output_to_operand_aliasing={{}: (5, {})} | custom-call | flops 6442450944 | bytes 7340032 | tf_op jit(solution)/shard_map/near_branch/pallas_call | solution.py:299
  56.7 19.1 %collective-permute-done.6.refs_2_ = bf16[1472,128]{1,0:T(8,128)(2,1)S(1)} collective-permute-done((bf16[1472,128]{1,0:T(8,128)(2,1)S(1)}, bf16[1472,128]{1,0:T(8,128)(2,1)S(1)}, u32[]{:S(2)}, u32[]{:S(2)}) %collective-permute-start.6) | collective-permute-done | bytes 376864 | tf_op jit(solution)/shard_map/ppermute | solution.py:506
  75.8 2.7 %pool.1 = (bf16[2048,256]{1,0:T(8,128)(2,1)S(1)}, bf16[2048,256]{1,0:T(8,128)(2,1)S(1)}, bf16[2048,256]{1,0:T(8,128)(2,1)}, bf16[256,256]{1,0:T(8,128)(2,1)S(1)}...) custom-call(s32[1]{0:T(128)} %bitcast.7.shard_ref.me_ref, bf16[1472,128]{1,0:T(8,128)(2,1)S(1)} %get-tuple-element.29.refs_0_, ...), custom_call_target="tpu_custom_call" | custom-call | tf_op jit(solution)/shard_map/pool/pallas_call | solution.py:521
  78.5 1.2 copy-done
  79.7 15.2 %chosen_and_project.6 = bf16[256,2560]{1,0:T(8,128)(2,1)} custom-call(s32[4]{0:T(128)S(1)} %pad_add_fusion.2.refs_0_, s32[64]{0:T(128)S(1)} %add_clamp_fusion.refs_1_, s32[64]{0:T(128)S(1)} %get-tuple-element.39.refs_2_, bf16[1024,3072]{1,0:T(8,128)(2,1)} %refs_3_.7, f32[1024,128]{1,0:T(8,128)S(1)} %pad.4.gate_ref.refs_4_, f32[1024,2048]{1,0:T(8,128)} %near_branch.3.refs_5_, ...), custom_call_target="tpu_custom_call" | custom-call | flops 8053063680 | bytes 12058624 | tf_op jit(solution)/shard_map/chosen_and_project/pallas_call | solution.py:388
  95.0 15.2 %chosen_and_project.7 = bf16[256,2560]{1,0:T(8,128)(2,1)} custom-call(s32[4]{0:T(128)S(1)} %pad_add_fusion.3.refs_0_, s32[64]{0:T(128)S(1)} %add_clamp_fusion.refs_1_, s32[64]{0:T(128)S(1)} %get-tuple-element.39.refs_2_, bf16[1024,3072]{1,0:T(8,128)(2,1)} %refs_3_.7, f32[1024,128]{1,0:T(8,128)S(1)} %pad.4.gate_ref.refs_4_, f32[1024,2048]{1,0:T(8,128)} %near_branch.3.refs_5_, ...), custom_call_target="tpu_custom_call" | custom-call | flops 8053063680 | bytes 12058624 | tf_op jit(solution)/shard_map/chosen_and_project/pallas_call | solution.py:388
  110.1 0.6 collective-permute-start.10
  110.7 15.4 %chosen_and_project.5 = bf16[256,2560]{1,0:T(8,128)(2,1)} custom-call(s32[4]{0:T(128)S(1)} %pad_add_fusion.1.refs_0_, s32[64]{0:T(128)S(1)} %add_clamp_fusion.refs_1_, s32[64]{0:T(128)S(1)} %get-tuple-element.39.refs_2_, bf16[1024,3072]{1,0:T(8,128)(2,1)} %refs_3_.7, f32[1024,128]{1,0:T(8,128)S(1)} %pad.4.gate_ref.refs_4_, f32[1024,2048]{1,0:T(8,128)} %near_branch.3.refs_5_, ...), custom_call_target="tpu_custom_call" | custom-call | flops 8053063680 | bytes 12058624 | tf_op jit(solution)/shard_map/chosen_and_project/pallas_call | solution.py:388
  126.1 2.8 %add_convert_fusion.1 = bf16[256,2560]{1,0:T(8,128)(2,1)} fusion(bf16[256,2560]{1,0:T(8,128)(2,1)S(1)} %collective-permute-done.8, bf16[256,2560]{1,0:T(8,128)(2,1)} %chosen_and_project.5), kind=kLoop, calls=%fused_computation.1 | loop fusion | flops 2621440 | bytes 3932160 | tf_op jit(solution)/shard_map/convert_element_type | solution.py:541
  129.5 1.2 copy-done.1
  130.8 15.1 %chosen_and_project.4 = bf16[256,2560]{1,0:T(8,128)(2,1)} custom-call(s32[4]{0:T(128)S(1)} %pad_add_fusion.refs_0_, s32[64]{0:T(128)S(1)} %add_clamp_fusion.refs_1_, s32[64]{0:T(128)S(1)} %get-tuple-element.39.refs_2_, bf16[1024,3072]{1,0:T(8,128)(2,1)} %refs_3_.7, f32[1024,128]{1,0:T(8,128)S(1)} %pad.4.gate_ref.refs_4_, f32[1024,2048]{1,0:T(8,128)} %near_branch.3.refs_5_, ...), custom_call_target="tpu_custom_call" | custom-call | flops 8053063680 | bytes 12058624 | tf_op jit(solution)/shard_map/chosen_and_project/pallas_call | solution.py:388
  145.9 14.1 %collective-permute-done.9 = bf16[256,2560]{1,0:T(8,128)(2,1)} collective-permute-done((bf16[256,2560]{1,0:T(8,128)(2,1)}, bf16[256,2560]{1,0:T(8,128)(2,1)}, u32[]{:S(2)}, u32[]{:S(2)}) %collective-permute-start.9) | collective-permute-done | bytes 1310752 | tf_op jit(solution)/shard_map/ppermute | solution.py:543
  160.0 3.6 %add_convert_fusion = bf16[256,2560]{1,0:T(8,128)(2,1)} fusion(bf16[256,2560]{1,0:T(8,128)(2,1)} %collective-permute-done.10, bf16[256,2560]{1,0:T(8,128)(2,1)} %collective-permute-done.9, bf16[256,2560]{1,0:T(8,128)(2,1)} %chosen_and_project.4), kind=kLoop, calls=%fused_computation | loop fusion | flops 3932160 | bytes 5242880 | tf_op jit(solution)/shard_map/convert_element_type | solution.py:548
  (51 shorter events, 3.4 us)
Async XLA Ops:
  1.9 32.9 %collective-permute-start.2 = (s32[4,16]{1,0:T(4,128)S(1)}, s32[4,16]{1,0:T(4,128)S(1)}, u32[]{:S(2)}, u32[]{:S(2)}) collective-permute-start(s32[4,16]{1,0:T(4,128)S(1)} %bitcast.21), channel_id=1, source_target_pairs={{8,0},{12,4},{16,8},{20,12},{24,16},{28,20},{9,1},{13,5},{17,9},{2... | collective-permute-start | bytes 776 | tf_op jit(solution)/shard_map/ppermute | solution.py:474
  4.2 30.5 %collective-permute-start.3 = (s32[4,16]{1,0:T(4,128)S(1)}, s32[4,16]{1,0:T(4,128)S(1)}, u32[]{:S(2)}, u32[]{:S(2)}) collective-permute-start(s32[4,16]{1,0:T(4,128)S(1)} %bitcast.22), channel_id=1, source_target_pairs={{16,0},{20,4},{24,8},{28,12},{17,1},{21,5},{25,9},{29,13},{18,2},{... | collective-permute-start | bytes 776 | tf_op jit(solution)/shard_map/ppermute | solution.py:474
  6.5 28.3 %collective-permute-start.4 = (s32[4,16]{1,0:T(4,128)S(1)}, s32[4,16]{1,0:T(4,128)S(1)}, u32[]{:S(2)}, u32[]{:S(2)}) collective-permute-start(s32[4,16]{1,0:T(4,128)S(1)} %bitcast.23), channel_id=1, source_target_pairs={{24,0},{28,4},{25,1},{29,5},{26,2},{30,6},{27,3},{31,7}} | collective-permute-start | bytes 776 | tf_op jit(solution)/shard_map/ppermute | solution.py:474
  7.8 1.2 copy-start.3
  9.0 0.9 copy-start.4
  9.9 0.8 copy-start.5
  10.7 5.9 %copy-start.6 = (f32[1024,3,16]{0,2,1:T(8,128)S(1)}, f32[1024,3,16]{0,2,1:T(8,128)}, u32[]{:S(2)}) copy-start(f32[1024,3,16]{0,2,1:T(8,128)} %param.14) | copy-start | bytes 589828
  12.9 21.9 %collective-permute-start = (bf16[2656,128]{1,0:T(8,128)(2,1)S(1)}, bf16[2656,128]{1,0:T(8,128)(2,1)S(1)}, u32[]{:S(2)}, u32[]{:S(2)}) collective-permute-start(bf16[2656,128]{1,0:T(8,128)(2,1)S(1)} %get-tuple-element.22.refs_4_), channel_id=1, source_target_pairs={{0,4},{4,0},{8,12},{12,8},{16,20},{20,16},{24,28},{28,24},{1,5},{5... | collective-permute-start | bytes 2039816 | tf_op jit(solution)/shard_map/ppermute | solution.py:485
  14.3 25.7 %collective-permute-start.1 = (bf16[1280,128]{1,0:T(8,128)(2,1)}, bf16[1280,128]{1,0:T(8,128)(2,1)}, u32[]{:S(2)}, u32[]{:S(2)}) collective-permute-start(bf16[1280,128]{1,0:T(8,128)(2,1)} %slice.7), channel_id=1, source_target_pairs={{4,8},{12,16},{20,24},{5,9},{13,17},{21,25},{6,10},{14,18},{22,26}... | collective-permute-start | bytes 983048 | tf_op jit(solution)/shard_map/ppermute | solution.py:487
  34.8 5.2 %copy-start.2 = (bf16[2656,128]{1,0:T(8,128)(2,1)}, bf16[2656,128]{1,0:T(8,128)(2,1)S(1)}, u32[]{:S(2)}) copy-start(bf16[2656,128]{1,0:T(8,128)(2,1)S(1)} %collective-permute-done.near_ref.refs_5_) | copy-start | bytes 2039812
  36.0 20.6 %collective-permute-start.5 = (bf16[1472,128]{1,0:T(8,128)(2,1)S(1)}, bf16[1472,128]{1,0:T(8,128)(2,1)S(1)}, u32[]{:S(2)}, u32[]{:S(2)}) collective-permute-start(bf16[1472,128]{1,0:T(8,128)(2,1)S(1)} %get-tuple-element.30), channel_id=1, source_target_pairs={{0,8},{4,12},{8,16},{12,20},{16,24},{20,28},{1,9},{5,13},{9,17},{1... | collective-permute-start | bytes 1130504 | tf_op jit(solution)/shard_map/ppermute | solution.py:506
  37.3 38.4 %collective-permute-start.6 = (bf16[1472,128]{1,0:T(8,128)(2,1)S(1)}, bf16[1472,128]{1,0:T(8,128)(2,1)S(1)}, u32[]{:S(2)}, u32[]{:S(2)}) collective-permute-start(bf16[1472,128]{1,0:T(8,128)(2,1)S(1)} %get-tuple-element.31), channel_id=1, source_target_pairs={{0,16},{4,20},{8,24},{12,28},{1,17},{5,21},{9,25},{13,29},{2,18},{... | collective-permute-start | bytes 1130504 | tf_op jit(solution)/shard_map/ppermute | solution.py:506
  38.6 37.1 %collective-permute-start.7 = (bf16[1472,128]{1,0:T(8,128)(2,1)S(1)}, bf16[1472,128]{1,0:T(8,128)(2,1)S(1)}, u32[]{:S(2)}, u32[]{:S(2)}) collective-permute-start(bf16[1472,128]{1,0:T(8,128)(2,1)S(1)} %get-tuple-element.32), channel_id=1, source_target_pairs={{0,24},{4,28},{1,25},{5,29},{2,26},{6,30},{3,27},{7,31}} | collective-permute-start | bytes 1130504 | tf_op jit(solution)/shard_map/ppermute | solution.py:506
  78.5 1.2 copy-start
  94.9 31.2 %collective-permute-start.8 = (bf16[256,2560]{1,0:T(8,128)(2,1)}, bf16[256,2560]{1,0:T(8,128)(2,1)S(1)}, u32[]{:S(2)}, u32[]{:S(2)}) collective-permute-start(bf16[256,2560]{1,0:T(8,128)(2,1)} %chosen_and_project.6), channel_id=1, source_target_pairs={{0,1},{1,0},{2,3},{3,2},{4,5},{5,4},{6,7},{7,6},{8,9},{9,8},{10,11... | collective-permute-start | bytes 3932168 | tf_op jit(solution)/shard_map/ppermute | solution.py:539
  110.1 35.8 %collective-permute-start.10 = (bf16[256,2560]{1,0:T(8,128)(2,1)}, bf16[256,2560]{1,0:T(8,128)(2,1)}, u32[]{:S(2)}, u32[]{:S(2)}) collective-permute-start(bf16[256,2560]{1,0:T(8,128)(2,1)} %chosen_and_project.7), channel_id=1, source_target_pairs={{0,1},{1,0},{2,3},{3,2},{4,5},{5,4},{6,7},{7,6},{8,9},{9,8},{10,11... | collective-permute-start | bytes 3932168 | tf_op jit(solution)/shard_map/ppermute | solution.py:544
  128.9 31.0 %collective-permute-start.9 = (bf16[256,2560]{1,0:T(8,128)(2,1)}, bf16[256,2560]{1,0:T(8,128)(2,1)}, u32[]{:S(2)}, u32[]{:S(2)}) collective-permute-start(bf16[256,2560]{1,0:T(8,128)(2,1)} %add_convert_fusion.1), channel_id=1, source_target_pairs={{0,2},{1,3},{2,0},{3,1},{4,6},{5,7},{6,4},{7,5},{8,10},{9,11},{10,... | collective-permute-start | bytes 3932168 | tf_op jit(solution)/shard_map/ppermute | solution.py:543
  129.5 1.2 copy-start.1
where the time goes:
time: 164 us
  Pallas kernels  98.4 us (60%)
  waiting for transfers between devices  33.2 us (20%)
  starting transfers between devices  12.9 us (8%)
  local copies, waits for them, and re-layouts  11 us (7%)
  other arithmetic  7.83 us (5%)
    pallas_call x4, Pallas kernels, chosen_and_project(): pl.pallas_call(functools.partial(chosen_kernel, heads), grid_spec=pltpu.P...  60.9 us
    pallas_call x2, Pallas kernels, near_branch(): pl.pallas_call(functools.partial(near_kernel, heads), grid=(block_count,...  29.9 us
    ppermute x3, waiting for transfers between devices, local(): lax.ppermute(sends[d], 'ctx', [(i, i + 2 * d) for i in range(n_ctx - 2 *...  19.1 us
    ppermute x1, waiting for transfers between devices, local(): arrived.append(lax.ppermute(summed, 'head', route))  14.1 us
    ppermute x3, starting transfers between devices, local(): lax.ppermute(my_picks, 'ctx', [(i, i - 2 * d) for i in range(2 * d, n_ctx)])  5.88 us
    unnamed x14, local copies, waits for them, and re-layouts  5.41 us
    ppermute x3, starting transfers between devices, local(): lax.ppermute(sends[d], 'ctx', [(i, i + 2 * d) for i in range(n_ctx - 2 *...  3.88 us
    convert_element_type x1, other arithmetic, local(): return total.astype(BF16)  3.63 us
  transfers between devices with their start and end apart: 11, of which 2 were waited for; matrix products, arithmetic and copies ran while one was open for 5% of the time, Pallas kernels for 49%

commit v1 on v0

--- a/solution.py
+++ b/solution.py
@@ -18,9 +18,10 @@
 QBLK = 256
 PAIR = 2 * QK
 BROWS = KBLK + KBLK // 2 + KBLK
-VMEM_LIMIT = 50 * 1024 * 1024
+VMEM_LIMIT = 60 * 1024 * 1024
 NEG = -1e30
 SCALE = QK ** (-0.5) * 1.4426950408889634
+LOW_TOTAL, HIGH_TOTAL = 2.0**-60, 2.0**100
 NT = (((1,), (1,)), ((), ()))
 F32 = jnp.float32
 BF16 = jnp.bfloat16
@@ -46,16 +47,24 @@
     return jnp.concatenate([values, jnp.ones_like(values)], axis=1)
 
 
-def prep_kernel(group_ref, keys_ref, values_ref, kw_ref, vw_ref, packed_ref, even_ref, odd_ref, val_ref):
-    group = group_ref[0]
-    odd = lax.rem(group, 2) == 1
-    first = pl.multiple_of(lax.div(group, 2) * PAIR, 128)
-    vfirst = pl.multiple_of(group * DV, 128)
+def prep_kernel(
+    group_ref,
+    keys_ref,
+    values_ref,
+    kw_ref,
+    vw_ref,
+    packed_ref,
+    rim_ref,
+    even_ref,
+    odd_ref,
+    val_ref,
+):
+    odd = lax.rem(group_ref[0], 2) == 1
 
     def own_columns(ref):
-        t0 = ref[:, pl.ds(first, 128)].astype(F32)
-        t1 = ref[:, pl.ds(first + 128, 128)].astype(F32)
-        t2 = ref[:, pl.ds(first + 256, 128)].astype(F32)
+        t0 = ref[:, :128].astype(F32)
+        t1 = ref[:, 128:256].astype(F32)
+        t2 = ref[:, 256:].astype(F32)
         r1, r2 = swap_halves(t1), swap_halves(t2)
         left = half_lanes(t0.shape[0])
         low = jnp.where(odd, jnp.where(left, r1, r2), t0)
@@ -63,7 +72,7 @@
         return low, high
 
     low, high = own_columns(keys_ref)
-    values = values_ref[:, pl.ds(vfirst, DV)]
+    values = values_ref[...]
     rows = low.shape[0]
     count = rows // KBLK
     high3 = high.reshape(count, KBLK, 128)
@@ -80,9 +89,10 @@
         packed_ref[at : at + KBLK] = low[token].astype(BF16)
         packed_ref[at + KBLK : at + KBLK + KBLK // 2] = packed_high[block].astype(BF16)
         packed_ref[at + KBLK + KBLK // 2 : at + BROWS] = values[token]
+    rim_rows = rim_ref.shape[0]
+    rim_ref[...] = packed_ref[count * BROWS - rim_rows : count * BROWS]
 
     wlow, whigh = own_columns(kw_ref)
-    wval = vw_ref[:, pl.ds(vfirst, DV)]
     folds = rows // CBLK
 
     def fold(x, w):
@@ -91,7 +101,7 @@
     at = count * BROWS
     packed_ref[at : at + folds] = fold(low, wlow)
     packed_ref[at + folds : at + 2 * folds] = fold(high, whigh)
-    packed_ref[at + 2 * folds :] = fold(values.astype(F32), wval)
+    packed_ref[at + 2 * folds :] = fold(values.astype(F32), vw_ref[...])
 
 
 def pack_kernel(groups, lists, per_owner, me_ref, *refs):
@@ -219,15 +229,26 @@
     return lax.broadcasted_iota(jnp.int32, (rows, cols), axis)
 
 
-def attend(q, keys, values, mask, floor=None):
-    scores = lax.dot_general(q, keys, NT, preferred_element_type=F32)
-    scores = mask(scores)
-    top = jnp.max(scores, axis=1, keepdims=True)
-    if floor is not None:
-        top = jnp.maximum(top, floor)
-    weights = jnp.exp2(scores * SCALE - top * SCALE).astype(BF16)
+def attend(q, keys, values, mask, exact):
+    scores = mask(lax.dot_general(q, keys, NT, preferred_element_type=F32)) * SCALE
+    if exact:
+        scores = scores - jnp.maximum(jnp.max(scores, axis=1, keepdims=True), -1e28)
+    weights = jnp.exp2(scores).astype(BF16)
     out = jnp.dot(weights, values, preferred_element_type=F32)
     return out[:, :DV], out[:, DV:]
+
+
+def in_range(total):
+    return jnp.where((total >= LOW_TOTAL) & (total <= HIGH_TOTAL), 1.0, 0.0)
+
+
+def with_fallback(run):
+    good = run(False)
+    worst = functools.reduce(jnp.minimum, good)
+
+    @pl.when(jnp.min(worst) < 0.5)
+    def _():
+        run(True)
 
 
 def stacked(x, times):
@@ -267,13 +288,19 @@
         new = jnp.where(stacked(col <= row, pairs), scores[:, WINDOW:], NEG)
         return jnp.concatenate([old, scores[:, QBLK:WINDOW], new], axis=1)
 
-    for side in range(2):
-        keys = (even_ref, odd_ref)[side][rows]
-        num, den = attend(stacked_queries(q_ref, side), keys, val_ref[rows], mask)
-        total = gate_columns(gate_ref, first, 2, heads, side, pairs) * (num / den)
-        for p in range(pairs):
-            at = (2 * p + side) * DV
-            out_ref[:, at : at + DV] = total[p * QBLK : (p + 1) * QBLK]
+    def run(exact):
+        good = []
+        for side in range(2):
+            keys = (even_ref, odd_ref)[side][rows]
+            num, den = attend(stacked_queries(q_ref, side), keys, val_ref[rows], mask, exact)
+            good.append(in_range(den))
+            total = gate_columns(gate_ref, first, 2, heads, side, pairs) * (num / den)
+            for p in range(pairs):
+                at = (2 * p + side) * DV
+                out_ref[:, at : at + DV] = total[p * QBLK : (p + 1) * QBLK]
+        return good
+
+    with_fallback(run)
 
 
 def near_branch(first_block, block_count, queries, gates, even, odd, val, prior):
@@ -305,7 +332,7 @@
         input_output_aliases=alias,
         compiler_params=pltpu.CompilerParams(vmem_limit_bytes=VMEM_LIMIT),
         cost_estimate=pl.CostEstimate(
-            flops=rows * (WINDOW + QBLK) * 1024,
+            flops=rows * (WINDOW + QBLK) * 64,
             bytes_accessed=rows * (2 * QK + 4 * DV),
             transcendentals=0,
         ),
@@ -313,18 +340,20 @@
     )(*operands)
 
 
-def chosen_kernel(heads, *refs):
+def chosen_kernel(heads, chunks, *refs):
     meta_ref, slots_ref, dead_ref, q_ref, gate_ref, near_ref = refs[:6]
-    pools, cfold, (weight_ref, out_ref) = refs[6:9], refs[9:12], refs[12:14]
-    keys, (attended, weight, weight_sem) = refs[14:17], refs[17:]
-    step = pl.program_id(0)
-    last = pl.num_programs(0) - 1
+    pools, cfold, weight_ref = refs[6:9], refs[9:12], refs[12]
+    outs, keys = refs[13 : 13 + chunks], refs[13 + chunks : 16 + chunks]
+    attended, weight, weight_sem = refs[16 + chunks :]
+    turn, step = pl.program_id(0), pl.program_id(1)
+    last = pl.num_programs(1) - 1
     rows = q_ref.shape[0]
     pairs = q_ref.shape[1] // PAIR
     first = step * 2 * pairs
-    list_at = meta_ref[1] * PICKS
-    first_row = meta_ref[2]
-    position = meta_ref[3]
+    chunk_start = meta_ref[1 + turn] * rows
+    list_at = lax.div(chunk_start, QBLK) * PICKS
+    first_row = lax.rem(chunk_start, QBLK)
+    position = meta_ref[0] + chunk_start
     copy = pltpu.make_async_copy(weight_ref, weight, weight_sem)
 
     @pl.when(step == 0)
@@ -342,6 +371,8 @@
                     key[at] = jnp.broadcast_to(key[:1], (KBLK, 256))
                 keys[2][at] = jnp.zeros((KBLK, 256), BF16)
 
+    @pl.when((turn == 0) & (step == 0))
+    def _():
         copy.start()
 
     def own_mask(scores):
@@ -355,49 +386,62 @@
         ends = (iota(rows, cols, 1) + 1) * CBLK - 1
         return jnp.where(stacked(ends <= position + iota(rows, cols, 0), pairs), scores, NEG)
 
-    for side in range(2):
-        q = stacked_queries(q_ref, side)
-        num, den = attend(q, keys[side][...], keys[2][...], own_mask)
-        total = gate_columns(gate_ref, first, 1, heads, side, pairs) * (num / den)
-        num, den = attend(q, cfold[side][...], cfold[2][...], comp_mask, -1e29)
-        gate = gate_columns(gate_ref, first, 0, heads, side, pairs)
-        total = total + gate * (num / jnp.maximum(den, 1.0))
-        for p in range(pairs):
-            at = (2 * p + side) * DV
-            mixed = near_ref[:, at : at + DV] + total[p * rows : (p + 1) * rows]
-            attended[step, :, at : at + DV] = mixed.astype(BF16)
-
-    @pl.when(step == last)
+    def run(exact):
+        good = []
+        empty = stacked(position + iota(rows, DV, 0) < CBLK - 1, pairs)
+        for side in range(2):
+            q = stacked_queries(q_ref, side)
+            num, den = attend(q, keys[side][...], keys[2][...], own_mask, exact)
+            good.append(in_range(den))
+            total = gate_columns(gate_ref, first, 1, heads, side, pairs) * (num / den)
+            num, den = attend(q, cfold[side][...], cfold[2][...], comp_mask, exact)
+            den = jnp.where(empty, 1.0, den)
+            good.append(in_range(den))
+            total = total + gate_columns(gate_ref, first, 0, heads, side, pairs) * (num / den)
+            for p in range(pairs):
+                at = (2 * p + side) * DV
+                mixed = near_ref[:, at : at + DV] + total[p * rows : (p + 1) * rows]
+                attended[step, :, at : at + DV] = mixed.astype(BF16)
+        return good
+
+    with_fallback(run)
+
+    @pl.when((turn == 0) & (step == last))
     def _():
         copy.wait()
-        rows_in = jnp.concatenate([attended[s] for s in range(heads // 4)], axis=1)
-        for at in range(0, out_ref.shape[1], 256):
-            out_ref[:, at : at + 256] = jnp.dot(
-                rows_in, weight[:, at : at + 256], preferred_element_type=F32
-            ).astype(out_ref.dtype)
-
-
-def chosen_and_project(chunk, rows, shard, slots, dead, queries, gates, near, pools, out_weight):
+
+    for place, out_ref in enumerate(outs):
+
+        @pl.when((turn == place) & (step == last))
+        def _():
+            rows_in = jnp.concatenate([attended[s] for s in range(heads // 4)], axis=1)
+            for at in range(0, out_ref.shape[1], 256):
+                out_ref[:, at : at + 256] = jnp.dot(
+                    rows_in, weight[:, at : at + 256], preferred_element_type=F32
+                ).astype(out_ref.dtype)
+
+
+def chosen_and_project(chunks, rows, shard, slots, dead, queries, gates, near, pools, out_weight):
     tokens, width = queries.shape
     heads = width // QK
     steps = heads // 4
     model = out_weight.shape[1]
-    start = chunk * rows
-    meta = jnp.stack([chunk, start // QBLK, lax.rem(start, QBLK), shard * tokens + start])
-    whole = lambda x: pl.BlockSpec(x.shape, lambda p, *_: (0,) * x.ndim)
+    meta = jnp.stack([shard * tokens] + chunks)
+    whole = lambda x: pl.BlockSpec(x.shape, lambda i, p, *_: (0,) * x.ndim)
+    out = jax.ShapeDtypeStruct((rows, model), BF16)
     return pl.pallas_call(
-        functools.partial(chosen_kernel, heads),
+        functools.partial(chosen_kernel, heads, len(chunks)),
         grid_spec=pltpu.PrefetchScalarGridSpec(
             num_scalar_prefetch=3,
-            grid=(steps,),
+            grid=(len(chunks), steps),
             in_specs=[
-                pl.BlockSpec((rows, 2 * PAIR), lambda p, m, *_: (m[0], p)),
-                pl.BlockSpec((rows, 128), lambda p, m, *_: (m[0], 0)),
-                pl.BlockSpec((rows, 4 * DV), lambda p, m, *_: (m[0], p)),
+                pl.BlockSpec((rows, 2 * PAIR), lambda i, p, m, *_: (m[1 + i], p)),
+                pl.BlockSpec((rows, 128), lambda i, p, m, *_: (m[1 + i], 0)),
+                pl.BlockSpec((rows, 4 * DV), lambda i, p, m, *_: (m[1 + i], p)),
             ]
             + [whole(x) for x in pools]
             + [pl.BlockSpec(memory_space=pl.ANY)],
-            out_specs=pl.BlockSpec((rows, model), lambda p, *_: (0, 0)),
+            out_specs=[whole(out)] * len(chunks),
             scratch_shapes=[pltpu.VMEM((PICKS * KBLK, 256), BF16)] * 3
             + [
                 pltpu.VMEM((steps, rows, 4 * DV), BF16),
@@ -405,11 +449,11 @@
                 pltpu.SemaphoreType.DMA,
             ],
         ),
-        out_shape=jax.ShapeDtypeStruct((rows, model), BF16),
+        out_shape=[out] * len(chunks),
         compiler_params=pltpu.CompilerParams(vmem_limit_bytes=VMEM_LIMIT),
         cost_estimate=pl.CostEstimate(
-            flops=rows * heads * (PICKS * KBLK * 1280 + 2 * DV * model),
-            bytes_accessed=out_weight.size * 2 + rows * width * 2,
+            flops=rows * heads * PICKS * KBLK * 64,
+            bytes_accessed=out_weight.size,
             transcendentals=0,
         ),
         name="chosen_and_project",
@@ -464,30 +508,38 @@
     groups = n_ctx // 2
     rim_blocks = WINDOW // KBLK
     packed_rows = per_owner * BROWS
-    params = pltpu.CompilerParams(vmem_limit_bytes=VMEM_LIMIT)
+    params = pltpu.CompilerParams(vmem_limit_bytes=24 * 1024 * 1024)
     smem = pl.BlockSpec(memory_space=pltpu.SMEM)
     vmem = pl.BlockSpec(memory_space=pltpu.VMEM)
     bf16 = lambda *shape: jax.ShapeDtypeStruct(shape, BF16)
 
+    rim_rows = rim_blocks * BROWS
+    prep_out = [bf16(packed_rows + 3 * folds, 128), bf16(rim_rows, 128)] + [bf16(tokens, 256)] * 3
+    packed, rim, even, odd, val = pl.pallas_call(
+        prep_kernel,
+        grid_spec=pltpu.PrefetchScalarGridSpec(
+            num_scalar_prefetch=1,
+            grid=(1,),
+            in_specs=[
+                pl.BlockSpec((tokens, PAIR), lambda i, g: (0, g[0] // 2)),
+                pl.BlockSpec((tokens, DV), lambda i, g: (0, g[0])),
+                pl.BlockSpec((CBLK, PAIR), lambda i, g: (0, g[0] // 2)),
+                pl.BlockSpec((CBLK, DV), lambda i, g: (0, g[0])),
+            ],
+            out_specs=[pl.BlockSpec(x.shape, lambda i, g: (0, 0)) for x in prep_out],
+        ),
+        out_shape=prep_out,
+        compiler_params=pltpu.CompilerParams(vmem_limit_bytes=VMEM_LIMIT),
+        name="prep",
+    )(group.reshape(1), key_rows, value_rows, comp_key_weight, comp_value_weight)
+    other = lax.ppermute(packed, "ctx", [(i, i ^ 1) for i in range(n_ctx)])
+    far_rim = lax.ppermute(rim, "ctx", [(i, i + 1) for i in range(1, n_ctx - 1, 2)])
+    packed, block_picks = lax.optimization_barrier((packed, block_picks))
     my_picks = lax.dynamic_index_in_dim(block_picks, group, 1, keepdims=False)
     picks = [my_picks] + [
         lax.ppermute(my_picks, "ctx", [(i, i - 2 * d) for i in range(2 * d, n_ctx)])
         for d in range(1, groups)
     ]
-    packed, even, odd, val = pl.pallas_call(
-        prep_kernel,
-        in_specs=[smem] + [vmem] * 4,
-        out_specs=[vmem] * 4,
-        out_shape=[bf16(packed_rows + 3 * folds, 128)] + [bf16(tokens, 256)] * 3,
-        compiler_params=params,
-        name="prep",
-    )(group.reshape(1), key_rows, value_rows, comp_key_weight, comp_value_weight)
-    other = lax.ppermute(packed, "ctx", [(i, i ^ 1) for i in range(n_ctx)])
-    rim_at = (per_owner - rim_blocks) * BROWS
-    far_rim = lax.ppermute(
-        packed[rim_at:packed_rows], "ctx", [(i, i + 1) for i in range(1, n_ctx - 1, 2)]
-    )
-
     gates = jax.nn.sigmoid(gate_logits).reshape(tokens, 3 * heads)
     gates = jnp.pad(gates, ((0, 0), (0, 128 - 3 * heads)))
     reach = WINDOW // QBLK
@@ -508,7 +560,7 @@
     ]
 
     ext = pl.pallas_call(
-        functools.partial(rim_kernel, rim_at),
+        functools.partial(rim_kernel, packed_rows - rim_rows),
         in_specs=[smem] + [vmem] * 5,
         out_specs=[vmem] * 3,
         out_shape=[bf16(2 * WINDOW, 256)] * 3,
@@ -527,22 +579,26 @@
         name="pool",
     )(shard.reshape(1), *received)
     rows = tokens // n_head
-    project = lambda chunk: chosen_and_project(
-        chunk, rows, shard, slots, dead, queries, gates, mixed, pools, out_weight
+    project = lambda *chunks: chosen_and_project(
+        list(chunks), rows, shard, slots, dead, queries, gates, mixed, pools, out_weight
     )
     chips = n_head // 2
     chip, core = head_at // 2, lax.rem(head_at, 2)
     across = [(i, i ^ 1) for i in range(n_head)]
-    arrived = []
+    sums = []
     for step in range(1, chips):
         target = lax.rem(chip + step, chips) * 2
-        other = lax.ppermute(project(target + 1 - core), "head", across)
-        mine = project(target + core)
+        other = lax.ppermute(project(target + 1 - core)[0], "head", across)
+        mine = project(target + core)[0]
         summed = (mine.astype(F32) + other.astype(F32)).astype(BF16)
+        summed, chip = lax.optimization_barrier((summed, chip))
+        sums.append(summed)
+    passed, kept = project(chip * 2 + 1 - core, chip * 2 + core)
+    arrived = [lax.ppermute(passed, "head", across)]
+    for step, summed in enumerate(sums, 1):
         route = [(i, (i + 2 * step) % n_head) for i in range(n_head)]
         arrived.append(lax.ppermute(summed, "head", route))
-    arrived.append(lax.ppermute(project(chip * 2 + 1 - core), "head", across))
-    total = project(head_at).astype(F32)
+    total = kept.astype(F32)
     for part in arrived:
         total = total + part.astype(F32)
     return total.astype(BF16)

time: 164 us -> 197 us (1.20)
  the two profiles are of different devices: /device:TPU:30 before, /device:TPU:5 now
where the time goes in v1:
time: 197 us; the launch traced here: 195 us
  Pallas kernels  143 us (73%)
  starting transfers between devices  26.7 us (14%)
  local copies, waits for them, and re-layouts  11.2 us (6%)
  other arithmetic  8.64 us (4%)
  waiting for transfers between devices  4.57 us (2%)
    pallas_call x3, Pallas kernels, chosen_and_project(): pl.pallas_call(functools.partial(chosen_kernel, heads, len(chunks)), grid...  88.1 us
    pallas_call x2, Pallas kernels, near_branch(): pl.pallas_call(functools.partial(near_kernel, heads), grid=(block_count,...  44.9 us
    ppermute x3, starting transfers between devices, local(): lax.ppermute(sends[d], 'ctx', [(i, i + 2 * d) for i in range(n_ctx - 2 *...  13 us
    unnamed x28, local copies, waits for them, and re-layouts  7.36 us
    ppermute x1, starting transfers between devices, local(): lax.ppermute(rim, 'ctx', [(i, i + 1) for i in range(1, n_ctx - 1, 2)])  5.27 us
  transfers between devices with their start and end apart: 11, of which 2 were waited for; matrix products, arithmetic and copies ran while one was open for 4% of the time, Pallas kernels for 59%

profile of v1, /device:TPU:5, one launch (start us, length us, event | category | flops | bytes accessed | tf_op | source)
XLA Modules:
  0.0 194.7 jit_solution(4261354155547453070)
XLA Ops:
  0.0 3.5 %prep.1 = (bf16[2656,128]{1,0:T(8,128)(2,1)}, bf16[1280,128]{1,0:T(8,128)(2,1)}, bf16[1024,256]{1,0:T(8,128)(2,1)}, bf16[1024,256]{1,0:T(8,128)(2,1)}, bf16[1024,256]{1,0:T(8,128)(2,1)}) custom-call(s32[1]{0:T(128)} %bitcast.2.group_ref, bf16[1024,768]{1,0:T(8,128)(2,1)} %keys_ref.1, bf16[1024,512]{1,0:T(8,128)(2,1)} %values_ref.1, f32[32,768]{1,0:T(8,128)} %kw_ref.1, ...), custom_call_target="tpu_custom_call" | custom-call | tf_op jit(solution)/shard_map/prep/pallas_call | solution.py:518
  4.1 1.4 fusion.5
  5.5 1.3 collective-permute-start.2
  6.8 1.3 collective-permute-start.3
  8.1 1.3 collective-permute-start.4
  9.4 5.3 %collective-permute-start.1 = (bf16[1280,128]{1,0:T(8,128)(2,1)}, bf16[1280,128]{1,0:T(8,128)(2,1)}, u32[]{:S(2)}, u32[]{:S(2)}) collective-permute-start(bf16[1280,128]{1,0:T(8,128)(2,1)} %get-tuple-element.31), channel_id=1, source_target_pairs={{4,8},{12,16},{20,24},{5,9},{13,17},{21,25},{6,10},{14,18},{22,26}... | collective-permute-start | bytes 983048 | tf_op jit(solution)/shard_map/ppermute | solution.py:536
  17.3 0.9 pad.4.gate_ref.refs_4_
  18.2 1.7 collective-permute-done.near_ref.refs_5_
  19.9 3.8 %pack.1 = (bf16[1472,128]{1,0:T(8,128)(2,1)S(1)}, bf16[1472,128]{1,0:T(8,128)(2,1)}, bf16[1472,128]{1,0:T(8,128)(2,1)}, bf16[1472,128]{1,0:T(8,128)(2,1)}) custom-call(s32[1]{0:T(128)} %bitcast.6.shard_ref.me_ref, s32[4,16]{1,0:T(4,128)S(1)} %bitcast.16, s32[4,16]{1,0:T(4,128)S(1)} %collective-permute-done.2.refs_1_, ...), custom_call_target="tpu_custom_call" | custom-call | tf_op jit(solution)/shard_map/pack/pallas_call | solution.py:549
  23.7 7.8 %collective-permute-start.5 = (bf16[1472,128]{1,0:T(8,128)(2,1)}, bf16[1472,128]{1,0:T(8,128)(2,1)S(1)}, u32[]{:S(2)}, u32[]{:S(2)}) collective-permute-start(bf16[1472,128]{1,0:T(8,128)(2,1)} %get-tuple-element.40), channel_id=1, source_target_pairs={{0,8},{4,12},{8,16},{12,20},{16,24},{20,28},{1,9},{5,13},{9,17},{1... | collective-permute-start | bytes 1130504 | tf_op jit(solution)/shard_map/ppermute | solution.py:558
  31.5 3.1 %collective-permute-start.6 = (bf16[1472,128]{1,0:T(8,128)(2,1)}, bf16[1472,128]{1,0:T(8,128)(2,1)S(1)}, u32[]{:S(2)}, u32[]{:S(2)}) collective-permute-start(bf16[1472,128]{1,0:T(8,128)(2,1)} %get-tuple-element.41), channel_id=1, source_target_pairs={{0,16},{4,20},{8,24},{12,28},{1,17},{5,21},{9,25},{13,29},{2,18},{... | collective-permute-start | bytes 1130504 | tf_op jit(solution)/shard_map/ppermute | solution.py:558
  34.7 2.0 %collective-permute-start.7 = (bf16[1472,128]{1,0:T(8,128)(2,1)}, bf16[1472,128]{1,0:T(8,128)(2,1)}, u32[]{:S(2)}, u32[]{:S(2)}) collective-permute-start(bf16[1472,128]{1,0:T(8,128)(2,1)} %get-tuple-element.42), channel_id=1, source_target_pairs={{0,24},{4,28},{1,25},{5,29},{2,26},{6,30},{3,27},{7,31}} | collective-permute-start | bytes 1130504 | tf_op jit(solution)/shard_map/ppermute | solution.py:558
  36.7 25.7 %near_branch.2.refs_0_ = f32[1024,2048]{1,0:T(8,128)} custom-call(bf16[1024,3072]{1,0:T(8,128)(2,1)} %refs_3_.5, f32[1024,128]{1,0:T(8,128)} %pad.4.gate_ref.refs_4_, bf16[1024,256]{1,0:T(8,128)(2,1)} %get-tuple-element.32.even_in.even_ref, bf16[1024,256]{1,0:T(8,128)(2,1)} %get-tuple-element.33.odd_in.odd_ref, ...), custom_call_target="tpu_custom_call" | custom-call | flops 402653184 | bytes 7340032 | tf_op jit(solution)/shard_map/near_branch/pallas_call | solution.py:326
  63.8 1.4 rim.1
  65.2 0.8 copy-done.10
  66.0 0.8 copy-done.11
  66.8 0.8 copy-done.12
  67.7 19.2 %near_branch.3.refs_5_ = f32[1024,2048]{1,0:T(8,128)} custom-call(bf16[1024,3072]{1,0:T(8,128)(2,1)} %refs_3_.5, f32[1024,128]{1,0:T(8,128)} %pad.4.gate_ref.refs_4_, bf16[1024,256]{1,0:T(8,128)(2,1)} %copy-done.10, bf16[1024,256]{1,0:T(8,128)(2,1)} %copy-done.11, bf16[1024,256]{1,0:T(8,128)(2,1)} %copy-done.12, ...), custom_call_target="tpu_custom_call", output_to_operand_aliasing={{}: (5, {})} | custom-call | flops 402653184 | bytes 7340032 | tf_op jit(solution)/shard_map/near_branch/pallas_call | solution.py:326
  86.9 1.6 pool.1
  88.5 1.0 copy-done
  89.5 1.0 copy-done.1
  90.5 1.0 copy-done.2
  92.1 0.7 copy-done.7
  93.4 23.3 %chosen_and_project.4 = bf16[256,2560]{1,0:T(8,128)(2,1)} custom-call(s32[2]{0:T(128)} %pad_add_fusion.1.refs_0_, s32[64]{0:T(128)} %add_clamp_fusion.refs_1_, s32[64]{0:T(128)} %get-tuple-element.53.refs_2_, bf16[1024,3072]{1,0:T(8,128)(2,1)} %refs_3_.5, f32[1024,128]{1,0:T(8,128)} %pad.4.gate_ref.refs_4_, f32[1024,2048]{1,0:T(8,128)} %near_branch.3.refs_5_, ...), custom_call_target="tpu_custom_call" | custom-call | flops 268435456 | bytes 5242880 | tf_op jit(solution)/shard_map/chosen_and_project/pallas_call | solution.py:432
  116.7 2.2 %collective-permute-start.8 = (bf16[256,2560]{1,0:T(8,128)(2,1)}, bf16[256,2560]{1,0:T(8,128)(2,1)S(1)}, u32[]{:S(2)}, u32[]{:S(2)}) collective-permute-start(bf16[256,2560]{1,0:T(8,128)(2,1)} %chosen_and_project.4), channel_id=1, source_target_pairs={{0,1},{1,0},{2,3},{3,2},{4,5},{5,4},{6,7},{7,6},{8,9},{9,8},{10,11... | collective-permute-start | bytes 3932168 | tf_op jit(solution)/shard_map/ppermute | solution.py:591
  119.5 23.4 %chosen_and_project.3 = bf16[256,2560]{1,0:T(8,128)(2,1)} custom-call(s32[2]{0:T(128)} %pad_add_fusion.refs_0_, s32[64]{0:T(128)} %add_clamp_fusion.refs_1_, s32[64]{0:T(128)} %get-tuple-element.53.refs_2_, bf16[1024,3072]{1,0:T(8,128)(2,1)} %refs_3_.5, f32[1024,128]{1,0:T(8,128)} %pad.4.gate_ref.refs_4_, f32[1024,2048]{1,0:T(8,128)} %near_branch.3.refs_5_, ...), custom_call_target="tpu_custom_call" | custom-call | flops 268435456 | bytes 5242880 | tf_op jit(solution)/shard_map/chosen_and_project/pallas_call | solution.py:432
  143.0 1.7 add_convert_fusion.1
  144.7 1.3 collective-permute-start.10
  146.6 41.3 %chosen_and_project.5 = (bf16[256,2560]{1,0:T(8,128)(2,1)}, bf16[256,2560]{1,0:T(8,128)(2,1)}) custom-call(s32[3]{0:T(128)} %pad_add_fusion.2.refs_0_, s32[64]{0:T(128)} %add_clamp_fusion.refs_1_, s32[64]{0:T(128)} %get-tuple-element.53.refs_2_, bf16[1024,3072]{1,0:T(8,128)(2,1)} %refs_3_.5, f32[1024,128]{1,0:T(8,128)} %pad.4.gate_ref.refs_4_, ...), custom_call_target="tpu_custom_call" | custom-call | flops 268435456 | bytes 5242880 | tf_op jit(solution)/shard_map/chosen_and_project/pallas_call | solution.py:432
  187.9 1.1 collective-permute-start.9
  189.0 2.9 %collective-permute-done.9 = bf16[256,2560]{1,0:T(8,128)(2,1)S(1)} collective-permute-done((bf16[256,2560]{1,0:T(8,128)(2,1)}, bf16[256,2560]{1,0:T(8,128)(2,1)S(1)}, u32[]{:S(2)}, u32[]{:S(2)}) %collective-permute-start.9) | collective-permute-done | bytes 1310752 | tf_op jit(solution)/shard_map/ppermute | solution.py:597
  191.8 2.9 %add_convert_fusion = bf16[256,2560]{1,0:T(8,128)(2,1)} fusion(bf16[256,2560]{1,0:T(8,128)(2,1)S(1)} %collective-permute-done.10, bf16[256,2560]{1,0:T(8,128)(2,1)S(1)} %collective-permute-done.9, bf16[256,2560]{1,0:T(8,128)(2,1)} %get-tuple-element.50), kind=kLoop, calls=%fused_computation | loop fusion | flops 3932160 | bytes 5242880 | tf_op jit(solution)/shard_map/convert_element_type | solution.py:604
  (62 shorter events, 7.1 us)
Async XLA Ops:
  0.0 16.4 %copy-start.13 = (f32[1024,3,16]{0,2,1:T(8,128)S(1)}, f32[1024,3,16]{0,2,1:T(8,128)}, u32[]{:S(2)}) copy-start(f32[1024,3,16]{0,2,1:T(8,128)} %param.14) | copy-start | bytes 589828
  3.5 16.3 %copy-start.9 = (bf16[2656,128]{1,0:T(8,128)(2,1)S(1)}, bf16[2656,128]{1,0:T(8,128)(2,1)}, u32[]{:S(2)}) copy-start(bf16[2656,128]{1,0:T(8,128)(2,1)} %get-tuple-element.38.refs_4_) | copy-start | bytes 2039812
  3.5 16.3 %collective-permute-start = (bf16[2656,128]{1,0:T(8,128)(2,1)}, bf16[2656,128]{1,0:T(8,128)(2,1)S(1)}, u32[]{:S(2)}, u32[]{:S(2)}) collective-permute-start(bf16[2656,128]{1,0:T(8,128)(2,1)} %get-tuple-element.38.refs_4_), channel_id=1, source_target_pairs={{0,4},{4,0},{8,12},{12,8},{16,20},{20,16},{24,28},{28,24},{1,5},{5... | collective-permute-start | bytes 2039816 | tf_op jit(solution)/shard_map/ppermute | solution.py:535
  5.5 12.7 %collective-permute-start.2 = (s32[4,16]{1,0:T(4,128)S(1)}, s32[4,16]{1,0:T(4,128)S(1)}, u32[]{:S(2)}, u32[]{:S(2)}) collective-permute-start(s32[4,16]{1,0:T(4,128)S(1)} %bitcast.10), channel_id=1, source_target_pairs={{8,0},{12,4},{16,8},{20,12},{24,16},{28,20},{9,1},{13,5},{17,9},{2... | collective-permute-start | bytes 776 | tf_op jit(solution)/shard_map/ppermute | solution.py:540
  6.8 11.4 %collective-permute-start.3 = (s32[4,16]{1,0:T(4,128)S(1)}, s32[4,16]{1,0:T(4,128)S(1)}, u32[]{:S(2)}, u32[]{:S(2)}) collective-permute-start(s32[4,16]{1,0:T(4,128)S(1)} %bitcast.11), channel_id=1, source_target_pairs={{16,0},{20,4},{24,8},{28,12},{17,1},{21,5},{25,9},{29,13},{18,2},{... | collective-permute-start | bytes 776 | tf_op jit(solution)/shard_map/ppermute | solution.py:540
  8.1 10.1 %collective-permute-start.4 = (s32[4,16]{1,0:T(4,128)S(1)}, s32[4,16]{1,0:T(4,128)S(1)}, u32[]{:S(2)}, u32[]{:S(2)}) collective-permute-start(s32[4,16]{1,0:T(4,128)S(1)} %bitcast.12), channel_id=1, source_target_pairs={{24,0},{28,4},{25,1},{29,5},{26,2},{30,6},{27,3},{31,7}} | collective-permute-start | bytes 776 | tf_op jit(solution)/shard_map/ppermute | solution.py:540
  9.4 54.4 %collective-permute-start.1 = (bf16[1280,128]{1,0:T(8,128)(2,1)}, bf16[1280,128]{1,0:T(8,128)(2,1)}, u32[]{:S(2)}, u32[]{:S(2)}) collective-permute-start(bf16[1280,128]{1,0:T(8,128)(2,1)} %get-tuple-element.31), channel_id=1, source_target_pairs={{4,8},{12,16},{20,24},{5,9},{13,17},{21,25},{6,10},{14,18},{22,26}... | collective-permute-start | bytes 983048 | tf_op jit(solution)/shard_map/ppermute | solution.py:536
  23.7 63.1 %collective-permute-start.5 = (bf16[1472,128]{1,0:T(8,128)(2,1)}, bf16[1472,128]{1,0:T(8,128)(2,1)S(1)}, u32[]{:S(2)}, u32[]{:S(2)}) collective-permute-start(bf16[1472,128]{1,0:T(8,128)(2,1)} %get-tuple-element.40), channel_id=1, source_target_pairs={{0,8},{4,12},{8,16},{12,20},{16,24},{20,28},{1,9},{5,13},{9,17},{1... | collective-permute-start | bytes 1130504 | tf_op jit(solution)/shard_map/ppermute | solution.py:558
  31.5 55.3 %collective-permute-start.6 = (bf16[1472,128]{1,0:T(8,128)(2,1)}, bf16[1472,128]{1,0:T(8,128)(2,1)S(1)}, u32[]{:S(2)}, u32[]{:S(2)}) collective-permute-start(bf16[1472,128]{1,0:T(8,128)(2,1)} %get-tuple-element.41), channel_id=1, source_target_pairs={{0,16},{4,20},{8,24},{12,28},{1,17},{5,21},{9,25},{13,29},{2,18},{... | collective-permute-start | bytes 1130504 | tf_op jit(solution)/shard_map/ppermute | solution.py:558
  34.7 52.2 %collective-permute-start.7 = (bf16[1472,128]{1,0:T(8,128)(2,1)}, bf16[1472,128]{1,0:T(8,128)(2,1)}, u32[]{:S(2)}, u32[]{:S(2)}) collective-permute-start(bf16[1472,128]{1,0:T(8,128)(2,1)} %get-tuple-element.42), channel_id=1, source_target_pairs={{0,24},{4,28},{1,25},{5,29},{2,26},{6,30},{3,27},{7,31}} | collective-permute-start | bytes 1130504 | tf_op jit(solution)/shard_map/ppermute | solution.py:558
  36.7 27.1 %copy-start.3 = (bf16[1024,256]{1,0:T(8,128)(2,1)S(1)}, bf16[1024,256]{1,0:T(8,128)(2,1)}, u32[]{:S(2)}) copy-start(bf16[1024,256]{1,0:T(8,128)(2,1)} %get-tuple-element.32.even_in.even_ref) | copy-start | bytes 1572868
  36.7 27.1 %copy-start.4 = (bf16[1024,256]{1,0:T(8,128)(2,1)S(1)}, bf16[1024,256]{1,0:T(8,128)(2,1)}, u32[]{:S(2)}) copy-start(bf16[1024,256]{1,0:T(8,128)(2,1)} %get-tuple-element.33.odd_in.odd_ref) | copy-start | bytes 1572868
  36.7 27.1 %copy-start.5 = (bf16[1024,256]{1,0:T(8,128)(2,1)S(1)}, bf16[1024,256]{1,0:T(8,128)(2,1)}, u32[]{:S(2)}) copy-start(bf16[1024,256]{1,0:T(8,128)(2,1)} %get-tuple-element.34.val_in.val_ref) | copy-start | bytes 1572868
  65.2 0.8 copy-start.10
  66.0 0.8 copy-start.11
  66.8 0.8 copy-start.12
  88.5 1.0 copy-start
  89.5 1.0 copy-start.1
  90.5 1.0 copy-start.2
  91.4 0.7 copy-start.6
  92.1 0.7 copy-start.7
  92.8 0.6 copy-start.8
  116.7 26.2 %collective-permute-start.8 = (bf16[256,2560]{1,0:T(8,128)(2,1)}, bf16[256,2560]{1,0:T(8,128)(2,1)S(1)}, u32[]{:S(2)}, u32[]{:S(2)}) collective-permute-start(bf16[256,2560]{1,0:T(8,128)(2,1)} %chosen_and_project.4), channel_id=1, source_target_pairs={{0,1},{1,0},{2,3},{3,2},{4,5},{5,4},{6,7},{7,6},{8,9},{9,8},{10,11... | collective-permute-start | bytes 3932168 | tf_op jit(solution)/shard_map/ppermute | solution.py:591
  144.7 44.3 %collective-permute-start.10 = (bf16[256,2560]{1,0:T(8,128)(2,1)S(1)}, bf16[256,2560]{1,0:T(8,128)(2,1)S(1)}, u32[]{:S(2)}, u32[]{:S(2)}) collective-permute-start(bf16[256,2560]{1,0:T(8,128)(2,1)S(1)} %add_convert_fusion.1), channel_id=1, source_target_pairs={{0,2},{1,3},{2,0},{3,1},{4,6},{5,7},{6,4},{7,5},{8,10},{9,11},{10,... | collective-permute-start | bytes 3932168 | tf_op jit(solution)/shard_map/ppermute | solution.py:600
  187.9 3.9 %collective-permute-start.9 = (bf16[256,2560]{1,0:T(8,128)(2,1)}, bf16[256,2560]{1,0:T(8,128)(2,1)S(1)}, u32[]{:S(2)}, u32[]{:S(2)}) collective-permute-start(bf16[256,2560]{1,0:T(8,128)(2,1)} %get-tuple-element.51), channel_id=1, source_target_pairs={{0,1},{1,0},{2,3},{3,2},{4,5},{5,4},{6,7},{7,6},{8,9},{9,8},{10,11... | collective-permute-start | bytes 3932168 | tf_op jit(solution)/shard_map/ppermute | solution.py:597

commit v2 on v1

--- a/solution.py
+++ b/solution.py
@@ -35,12 +35,15 @@
     return pltpu.roll(x, 64, 1)
 
 
-def shift_matrix():
-    return jnp.where(iota(256, 256, 1) == iota(256, 256, 0) + 64, 1.0, 0.0).astype(BF16)
-
-
-def shifted_keys(even):
-    return jnp.dot(even, shift_matrix(), preferred_element_type=F32).astype(BF16)
+def turned(keys):
+    row, col = iota(256, 256, 0), iota(256, 256, 1)
+    unit = (row == col).astype(BF16)
+    even = lax.dot_general(unit, keys, NT, preferred_element_type=F32).astype(BF16)
+    return even, lower(even)
+
+
+def lower(even):
+    return jnp.concatenate([jnp.zeros((64, even.shape[1]), BF16), even[:QK]], axis=0)
 
 
 def with_ones(values):
@@ -80,8 +83,7 @@
         high3[:, KBLK // 2 :].reshape(count * KBLK // 2, 128)
     ).reshape(count, KBLK // 2, 128)
     even = jnp.concatenate([low.astype(BF16), high.astype(BF16)], axis=1)
-    even_ref[...] = even
-    odd_ref[...] = shifted_keys(even)
+    even_ref[...], odd_ref[...] = turned(even)
     val_ref[...] = with_ones(values)
     for block in range(count):
         at = block * BROWS
@@ -104,50 +106,35 @@
     packed_ref[at + 2 * folds :] = fold(values.astype(F32), vw_ref[...])
 
 
-def pack_kernel(groups, lists, per_owner, me_ref, *refs):
-    picks, (own_ref, other_ref), outs = refs[:groups], refs[groups : groups + 2], refs[groups + 2 :]
-    me = me_ref[0]
-    parity = lax.rem(me, 2)
-    base = me - parity
+def pack_kernel(distances, lists, per_owner, limit, where_ref, picks_ref, ref, *outs):
+    owner, base = where_ref[0], where_ref[1]
     data = per_owner * BROWS
-    folded = own_ref.shape[0] - data
-    for distance in range(groups):
-        out = outs[distance]
-
-        @pl.when(base + 2 * distance < 2 * groups)
+    for distance, out in zip(distances, outs):
+
+        @pl.when(base + 2 * distance < limit)
         def _():
-            named = [jnp.int32(0), jnp.int32(0)]
-            for row in range(lists):
-                for col in range(PICKS):
-                    entry = picks[distance][row, col]
-                    for side in range(2):
-                        block = entry - (base + side) * per_owner
-                        here = (block >= 0) & (block < per_owner)
-                        bit = jnp.int32(1) << jnp.where(here, block, 0)
-                        named[side] = named[side] | jnp.where(here, bit, 0)
-            for mine, ref in ((True, own_ref), (False, other_ref)):
-                side = parity if mine else 1 - parity
-                bits = jnp.where(side == 0, named[0], named[1])
-                rank = jnp.int32(0)
-                for block in range(per_owner):
-                    bit = (bits >> block) & 1
-
-                    @pl.when((bit == 1) & (rank < lists))
-                    def _():
-                        at = pl.multiple_of(
-                            (side * lists + jnp.minimum(rank, lists - 1)) * BROWS, 16
-                        )
-                        out[pl.ds(at, BROWS)] = ref[block * BROWS : (block + 1) * BROWS]
-
-                    rank = rank + bit
-                at = pl.multiple_of(2 * lists * BROWS + side * folded, 16)
-                out[pl.ds(at, folded)] = ref[data:]
-
-
-def unpack(ref, at, count):
+            named = jnp.int32(0)
+            for entry in range(lists * PICKS):
+                block = picks_ref[distance * lists * PICKS + entry] - owner * per_owner
+                here = (block >= 0) & (block < per_owner)
+                named = named | jnp.where(here, jnp.int32(1) << jnp.where(here, block, 0), 0)
+            rank = jnp.int32(0)
+            for block in range(per_owner):
+                bit = (named >> block) & 1
+
+                @pl.when((bit == 1) & (rank < lists))
+                def _():
+                    at = pl.multiple_of(jnp.minimum(rank, lists - 1) * BROWS, BROWS)
+                    out[pl.ds(at, BROWS)] = ref[block * BROWS : (block + 1) * BROWS]
+
+                rank = rank + bit
+            out[lists * BROWS :] = ref[data:]
+
+
+def unpack(ref, at, count, step=1):
     lows, packed, values = [], [], []
     for block in range(count):
-        first = at + block * BROWS
+        first = at + block * step * BROWS
         lows.append(ref[first : first + KBLK])
         packed.append(ref[first + KBLK : first + KBLK + KBLK // 2])
         values.append(ref[first + KBLK + KBLK // 2 : first + BROWS])
@@ -166,17 +153,18 @@
     return even, jnp.concatenate(values, axis=0)
 
 
-def rim_kernel(rim_at, shard_ref, near_ref, far_ref, even_in, odd_in, val_in, even_ref, odd_ref, val_ref):
+def rim_kernel(
+    rim_at, shard_ref, near_ref, far_ref, even_in, odd_in, val_in, even_ref, odd_ref, val_ref
+):
     shard = shard_ref[0]
     rim_blocks = WINDOW // KBLK
-    even_ref[WINDOW:] = even_in[:WINDOW]
-    odd_ref[WINDOW:] = odd_in[:WINDOW]
+    even_ref[:, WINDOW:] = even_in[:, :WINDOW]
+    odd_ref[:, WINDOW:] = odd_in[:, :WINDOW]
     val_ref[WINDOW:] = val_in[:WINDOW]
 
     def fill(ref, at):
-        even, values = unpack(ref, at, rim_blocks)
-        even_ref[:WINDOW] = even
-        odd_ref[:WINDOW] = shifted_keys(even)
+        keys, values = unpack(ref, at, rim_blocks)
+        even_ref[:, :WINDOW], odd_ref[:, :WINDOW] = turned(keys)
         val_ref[:WINDOW] = with_ones(values)
 
     @pl.when(lax.rem(shard, 2) == 1)
@@ -189,40 +177,44 @@
 
     @pl.when(shard == 0)
     def _():
-        even_ref[:WINDOW] = jnp.broadcast_to(even_in[:1], (WINDOW, 256))
-        odd_ref[:WINDOW] = jnp.broadcast_to(odd_in[:1], (WINDOW, 256))
+        even = jnp.broadcast_to(even_in[:, :1].astype(F32), (256, WINDOW)).astype(BF16)
+        even_ref[:, :WINDOW], odd_ref[:, :WINDOW] = even, lower(even)
         val_ref[:WINDOW] = jnp.zeros((WINDOW, 256), BF16)
 
 
-def pool_kernel(groups, lists, shard_ref, *refs):
-    ins, (even_ref, odd_ref, val_ref, ceven_ref, codd_ref, cval_ref) = refs[:groups], refs[groups:]
+def pool_kernel(groups, lists, shard_ref, own_ref, *refs):
+    sent = 2 * groups - 1
+    ins, (key_ref, val_ref, ceven_ref, codd_ref, cval_ref, folded) = refs[:sent], refs[sent:]
     shard = shard_ref[0]
-    base = shard - lax.rem(shard, 2)
-    blocks = 2 * lists
-    rows = blocks * KBLK
-    folds = (ins[0].shape[0] - blocks * BROWS) // 6
-    ceven_ref[...] = jnp.zeros_like(ceven_ref)
-    codd_ref[...] = jnp.zeros_like(codd_ref)
+    parity = lax.rem(shard, 2)
+    base = shard - parity
+    rows = lists * KBLK
+    folds = (ins[0].shape[0] - lists * BROWS) // 3
+    folded[...] = jnp.zeros_like(folded)
     cval_ref[...] = jnp.zeros_like(cval_ref)
-    for distance in range(groups):
-        ref = ins[distance]
+
+    def fill(place, owner, ref, step, fold_at):
+        keys, values = unpack(ref, 0, lists, step)
+        at = slice(place * rows, place * rows + rows)
+        key_ref[at] = keys
+        val_ref[at] = with_ones(values)
+        low = ref[fold_at : fold_at + folds]
+        high = ref[fold_at + folds : fold_at + 2 * folds]
+        owned = pl.ds(pl.multiple_of(owner * folds, 32), folds)
+        folded[owned] = jnp.concatenate([low, high], axis=1)
+        cval_ref[owned] = with_ones(ref[fold_at + 2 * folds : fold_at + 3 * folds])
+
+    fill(0, shard, own_ref, QBLK // KBLK, own_ref.shape[0] - 3 * folds)
+    fill(1, base + 1 - parity, ins[0], 1, lists * BROWS)
+    for distance in range(1, groups):
 
         @pl.when(base >= 2 * distance)
         def _():
-            even, values = unpack(ref, 0, blocks)
-            at = slice(distance * rows, distance * rows + rows)
-            even_ref[at] = even
-            odd_ref[at] = shifted_keys(even)
-            val_ref[at] = with_ones(values)
             for side in range(2):
-                first = blocks * BROWS + side * 3 * folds
-                low = ref[first : first + folds]
-                high = ref[first + folds : first + 2 * folds]
-                folded = jnp.concatenate([low, high], axis=1)
-                place = pl.ds(pl.multiple_of((base - 2 * distance + side) * folds, 32), folds)
-                ceven_ref[place] = folded
-                codd_ref[place] = shifted_keys(folded)
-                cval_ref[place] = with_ones(ref[first + 2 * folds : first + 3 * folds])
+                owner = base - 2 * distance + (parity if side == 0 else 1 - parity)
+                fill(2 * distance + side, owner, ins[2 * distance - 1 + side], 1, lists * BROWS)
+
+    ceven_ref[...], codd_ref[...] = turned(folded[...])
 
 
 def iota(rows, cols, axis):
@@ -230,7 +222,7 @@
 
 
 def attend(q, keys, values, mask, exact):
-    scores = mask(lax.dot_general(q, keys, NT, preferred_element_type=F32)) * SCALE
+    scores = mask(jnp.dot(q, keys, preferred_element_type=F32)) * SCALE
     if exact:
         scores = scores - jnp.maximum(jnp.max(scores, axis=1, keepdims=True), -1e28)
     weights = jnp.exp2(scores).astype(BF16)
@@ -291,7 +283,7 @@
     def run(exact):
         good = []
         for side in range(2):
-            keys = (even_ref, odd_ref)[side][rows]
+            keys = (even_ref, odd_ref)[side][:, rows]
             num, den = attend(stacked_queries(q_ref, side), keys, val_ref[rows], mask, exact)
             good.append(in_range(den))
             total = gate_columns(gate_ref, first, 2, heads, side, pairs) * (num / den)
@@ -340,17 +332,20 @@
     )(*operands)
 
 
-def chosen_kernel(heads, chunks, *refs):
+def chosen_kernel(heads, span, *refs):
+    first_chunk, widths = span
+    count = sum(len(w) for w in widths)
     meta_ref, slots_ref, dead_ref, q_ref, gate_ref, near_ref = refs[:6]
-    pools, cfold, weight_ref = refs[6:9], refs[9:12], refs[12]
-    outs, keys = refs[13 : 13 + chunks], refs[13 + chunks : 16 + chunks]
-    attended, weight, weight_sem = refs[16 + chunks :]
+    (key_pool, val_pool), cfold, weight_ref = refs[6:8], refs[8:11], refs[11]
+    outs = list(refs[12 : 12 + count])
+    gathered, even, odd, val, attended, weight, weight_sem = refs[12 + count :]
+    keys = (even, odd)
     turn, step = pl.program_id(0), pl.program_id(1)
     last = pl.num_programs(1) - 1
     rows = q_ref.shape[0]
     pairs = q_ref.shape[1] // PAIR
     first = step * 2 * pairs
-    chunk_start = meta_ref[1 + turn] * rows
+    chunk_start = meta_ref[first_chunk + turn] * rows
     list_at = lax.div(chunk_start, QBLK) * PICKS
     first_row = lax.rem(chunk_start, QBLK)
     position = meta_ref[0] + chunk_start
@@ -360,16 +355,17 @@
     def _():
         for slot in range(PICKS):
             source = pl.multiple_of(slots_ref[list_at + slot] * KBLK, KBLK)
-            for pool, key in zip(pools, keys):
-                key[slot * KBLK : (slot + 1) * KBLK] = pool[pl.ds(source, KBLK)]
+            gathered[slot * KBLK : (slot + 1) * KBLK] = key_pool[pl.ds(source, KBLK)]
+            val[slot * KBLK : (slot + 1) * KBLK] = val_pool[pl.ds(source, KBLK)]
         for slot in range(1, PICKS):
 
             @pl.when(dead_ref[list_at + slot] == 1)
             def _():
                 at = slice(slot * KBLK, (slot + 1) * KBLK)
-                for key in keys[:2]:
-                    key[at] = jnp.broadcast_to(key[:1], (KBLK, 256))
-                keys[2][at] = jnp.zeros((KBLK, 256), BF16)
+                gathered[at] = jnp.broadcast_to(gathered[:1], (KBLK, 256))
+                val[at] = jnp.zeros((KBLK, 256), BF16)
+
+        even[...], odd[...] = turned(gathered[...])
 
     @pl.when((turn == 0) & (step == 0))
     def _():
@@ -391,7 +387,7 @@
         empty = stacked(position + iota(rows, DV, 0) < CBLK - 1, pairs)
         for side in range(2):
             q = stacked_queries(q_ref, side)
-            num, den = attend(q, keys[side][...], keys[2][...], own_mask, exact)
+            num, den = attend(q, keys[side][...], val[...], own_mask, exact)
             good.append(in_range(den))
             total = gate_columns(gate_ref, first, 1, heads, side, pairs) * (num / den)
             num, den = attend(q, cfold[side][...], cfold[2][...], comp_mask, exact)
@@ -410,46 +406,51 @@
     def _():
         copy.wait()
 
-    for place, out_ref in enumerate(outs):
+    for place, parts in enumerate(widths):
+        chunk_outs = [outs.pop(0) for _ in parts]
 
         @pl.when((turn == place) & (step == last))
         def _():
             rows_in = jnp.concatenate([attended[s] for s in range(heads // 4)], axis=1)
-            for at in range(0, out_ref.shape[1], 256):
-                out_ref[:, at : at + 256] = jnp.dot(
-                    rows_in, weight[:, at : at + 256], preferred_element_type=F32
-                ).astype(out_ref.dtype)
-
-
-def chosen_and_project(chunks, rows, shard, slots, dead, queries, gates, near, pools, out_weight):
+            first_col = 0
+            for out_ref in chunk_outs:
+                for at in range(0, out_ref.shape[1], 256):
+                    cols = weight[:, first_col + at : first_col + at + 256]
+                    part = jnp.dot(rows_in, cols, preferred_element_type=F32)
+                    out_ref[:, at : at + 256] = part.astype(out_ref.dtype)
+                first_col += out_ref.shape[1]
+
+
+def chosen_and_project(first_chunk, widths, rows, meta, slots, dead, queries, gates, near, pools, out_weight):
     tokens, width = queries.shape
     heads = width // QK
     steps = heads // 4
-    model = out_weight.shape[1]
-    meta = jnp.stack([shard * tokens] + chunks)
     whole = lambda x: pl.BlockSpec(x.shape, lambda i, p, *_: (0,) * x.ndim)
-    out = jax.ShapeDtypeStruct((rows, model), BF16)
+    outs = [jax.ShapeDtypeStruct((rows, width), BF16) for chunk in widths for width in chunk]
     return pl.pallas_call(
-        functools.partial(chosen_kernel, heads, len(chunks)),
+        functools.partial(chosen_kernel, heads, (first_chunk, widths)),
         grid_spec=pltpu.PrefetchScalarGridSpec(
             num_scalar_prefetch=3,
-            grid=(len(chunks), steps),
+            grid=(len(widths), steps),
             in_specs=[
-                pl.BlockSpec((rows, 2 * PAIR), lambda i, p, m, *_: (m[1 + i], p)),
-                pl.BlockSpec((rows, 128), lambda i, p, m, *_: (m[1 + i], 0)),
-                pl.BlockSpec((rows, 4 * DV), lambda i, p, m, *_: (m[1 + i], p)),
+                pl.BlockSpec((rows, 2 * PAIR), lambda i, p, m, *_: (m[first_chunk + i], p)),
+                pl.BlockSpec((rows, 128), lambda i, p, m, *_: (m[first_chunk + i], 0)),
+                pl.BlockSpec((rows, 4 * DV), lambda i, p, m, *_: (m[first_chunk + i], p)),
             ]
             + [whole(x) for x in pools]
             + [pl.BlockSpec(memory_space=pl.ANY)],
-            out_specs=[whole(out)] * len(chunks),
-            scratch_shapes=[pltpu.VMEM((PICKS * KBLK, 256), BF16)] * 3
-            + [
+            out_specs=[whole(out) for out in outs],
+            scratch_shapes=[
+                pltpu.VMEM((PICKS * KBLK, 256), BF16),
+                pltpu.VMEM((256, PICKS * KBLK), BF16),
+                pltpu.VMEM((256, PICKS * KBLK), BF16),
+                pltpu.VMEM((PICKS * KBLK, 256), BF16),
                 pltpu.VMEM((steps, rows, 4 * DV), BF16),
                 pltpu.VMEM(out_weight.shape, BF16),
                 pltpu.SemaphoreType.DMA,
             ],
         ),
-        out_shape=[out] * len(chunks),
+        out_shape=outs,
         compiler_params=pltpu.CompilerParams(vmem_limit_bytes=VMEM_LIMIT),
         cost_estimate=pl.CostEstimate(
             flops=rows * heads * PICKS * KBLK * 64,
@@ -457,7 +458,7 @@
             transcendentals=0,
         ),
         name="chosen_and_project",
-    )(meta.astype(jnp.int32), slots, dead, queries, gates, near, *pools, out_weight)
+    )(meta, slots, dead, queries, gates, near, *pools, out_weight)
 
 
 def plan_picks(my_picks, shard, per_owner, n_ctx):
@@ -481,10 +482,27 @@
     before = (block >= owner_start[..., None]) & (block < ordered[..., None])
     rank = jnp.sum(jnp.where(before, named, 0), axis=-1)
     owner = ordered // per_owner
-    slot = (shard // 2 - owner // 2) * 2 * lists + lax.rem(owner, 2) * lists
+    slot = (shard // 2 - owner // 2) * 2 * lists + lax.rem(owner + shard, 2) * lists
     slot = slot + jnp.minimum(rank, lists - 1)
     slot = jnp.clip(slot, 0, n_ctx * lists - 1)
     return slot.reshape(-1).astype(jnp.int32), dead.reshape(-1).astype(jnp.int32)
+
+
+def single_step(kernel, name, scalars, arrays, outs, scratch=()):
+    whole = lambda x: pl.BlockSpec(x.shape, lambda i, *_: (0,) * len(x.shape))
+    return pl.pallas_call(
+        kernel,
+        grid_spec=pltpu.PrefetchScalarGridSpec(
+            num_scalar_prefetch=len(scalars),
+            grid=(1,),
+            in_specs=[whole(x) for x in arrays],
+            out_specs=[whole(x) for x in outs],
+            scratch_shapes=list(scratch),
+        ),
+        out_shape=outs,
+        compiler_params=pltpu.CompilerParams(vmem_limit_bytes=VMEM_LIMIT),
+        name=name,
+    )(*scalars, *arrays)
 
 
 def local(
@@ -508,13 +526,11 @@
     groups = n_ctx // 2
     rim_blocks = WINDOW // KBLK
     packed_rows = per_owner * BROWS
-    params = pltpu.CompilerParams(vmem_limit_bytes=24 * 1024 * 1024)
-    smem = pl.BlockSpec(memory_space=pltpu.SMEM)
-    vmem = pl.BlockSpec(memory_space=pltpu.VMEM)
     bf16 = lambda *shape: jax.ShapeDtypeStruct(shape, BF16)
 
     rim_rows = rim_blocks * BROWS
-    prep_out = [bf16(packed_rows + 3 * folds, 128), bf16(rim_rows, 128)] + [bf16(tokens, 256)] * 3
+    prep_out = [bf16(packed_rows + 3 * folds, 128), bf16(rim_rows, 128)]
+    prep_out += [bf16(256, tokens)] * 2 + [bf16(tokens, 256)]
     packed, rim, even, odd, val = pl.pallas_call(
         prep_kernel,
         grid_spec=pltpu.PrefetchScalarGridSpec(
@@ -533,68 +549,91 @@
         name="prep",
     )(group.reshape(1), key_rows, value_rows, comp_key_weight, comp_value_weight)
     other = lax.ppermute(packed, "ctx", [(i, i ^ 1) for i in range(n_ctx)])
-    far_rim = lax.ppermute(rim, "ctx", [(i, i + 1) for i in range(1, n_ctx - 1, 2)])
+    slots, dead = plan_picks(
+        lax.dynamic_index_in_dim(block_picks, group, 1, keepdims=False), shard, per_owner, n_ctx
+    )
     packed, block_picks = lax.optimization_barrier((packed, block_picks))
     my_picks = lax.dynamic_index_in_dim(block_picks, group, 1, keepdims=False)
     picks = [my_picks] + [
         lax.ppermute(my_picks, "ctx", [(i, i - 2 * d) for i in range(2 * d, n_ctx)])
         for d in range(1, groups)
     ]
+    far_rim = lax.ppermute(rim, "ctx", [(i, i + 1) for i in range(1, n_ctx - 1, 2)])
+
     gates = jax.nn.sigmoid(gate_logits).reshape(tokens, 3 * heads)
     gates = jnp.pad(gates, ((0, 0), (0, 128 - 3 * heads)))
+    sent = bf16(lists * BROWS + 3 * folds, 128)
+    picks = jnp.stack(picks).reshape(-1)
+
+    def pack(owner, distances, rows):
+        return single_step(
+            functools.partial(pack_kernel, distances, lists, per_owner, n_ctx),
+            "pack",
+            [jnp.stack([owner, shard - lax.rem(shard, 2)]), picks],
+            [rows],
+            [sent] * len(distances),
+        )
+
+    def ahead(send, distance):
+        return lax.ppermute(send, "ctx", [(i, i + 2 * distance) for i in range(n_ctx - 2 * distance)])
+
+    own_sends = pack(shard, range(1, groups), packed)
+    own_sends, even = lax.optimization_barrier((own_sends, even))
+    from_same = [ahead(send, d) for d, send in enumerate(own_sends, 1)]
+
     reach = WINDOW // QBLK
     mixed = near_branch(reach, lists - reach, queries, gates, even, odd, val, None)
 
-    sent_rows = 2 * lists * BROWS + 6 * folds
-    sends = pl.pallas_call(
-        functools.partial(pack_kernel, groups, lists, per_owner),
-        in_specs=[smem] * (1 + groups) + [vmem] * 2,
-        out_specs=[vmem] * groups,
-        out_shape=[bf16(sent_rows, 128)] * groups,
-        compiler_params=params,
-        name="pack",
-    )(shard.reshape(1), *picks, packed, other)
-    received = [sends[0]] + [
-        lax.ppermute(sends[d], "ctx", [(i, i + 2 * d) for i in range(n_ctx - 2 * d)])
-        for d in range(1, groups)
-    ]
-
-    ext = pl.pallas_call(
+    other, mixed = lax.optimization_barrier((other, mixed))
+    beside, *other_sends = pack(shard + 1 - 2 * lax.rem(shard, 2), range(groups), other)
+    from_other = [ahead(send, d) for d, send in enumerate(other_sends, 1)]
+
+    ext = single_step(
         functools.partial(rim_kernel, packed_rows - rim_rows),
-        in_specs=[smem] + [vmem] * 5,
-        out_specs=[vmem] * 3,
-        out_shape=[bf16(2 * WINDOW, 256)] * 3,
-        compiler_params=params,
-        name="rim",
-    )(shard.reshape(1), other, far_rim, even, odd, val)
+        "rim",
+        [shard.reshape(1)],
+        [other, far_rim, even, odd, val],
+        [bf16(256, 2 * WINDOW)] * 2 + [bf16(2 * WINDOW, 256)],
+    )
     mixed = near_branch(0, reach, queries, gates, *ext, mixed)
 
-    slots, dead = plan_picks(my_picks, shard, per_owner, n_ctx)
-    pools = pl.pallas_call(
+    received = [beside] + [x for both in zip(from_same, from_other) for x in both]
+    pools = single_step(
         functools.partial(pool_kernel, groups, lists),
-        in_specs=[smem] + [vmem] * groups,
-        out_specs=[vmem] * 6,
-        out_shape=[bf16(n_ctx * lists * KBLK, 256)] * 3 + [bf16(n_ctx * folds, 256)] * 3,
-        compiler_params=params,
-        name="pool",
-    )(shard.reshape(1), *received)
+        "pool",
+        [shard.reshape(1)],
+        [packed] + received,
+        [bf16(n_ctx * lists * KBLK, 256)] * 2
+        + [bf16(256, n_ctx * folds)] * 2
+        + [bf16(n_ctx * folds, 256)],
+        [pltpu.VMEM((n_ctx * folds, 256), BF16)],
+    )
     rows = tokens // n_head
-    project = lambda *chunks: chosen_and_project(
-        list(chunks), rows, shard, slots, dead, queries, gates, mixed, pools, out_weight
-    )
     chips = n_head // 2
     chip, core = head_at // 2, lax.rem(head_at, 2)
+    order = []
+    for step in list(range(1, chips)) + [0]:
+        target = lax.rem(chip + step, chips) * 2
+        order += [target + 1 - core, target + core]
+    meta = jnp.stack([shard * tokens] + order).astype(jnp.int32)
     across = [(i, i ^ 1) for i in range(n_head)]
+
+    model = out_weight.shape[1]
+
+    def project(first_chunk, widths):
+        return chosen_and_project(
+            first_chunk, widths, rows, meta, slots, dead, queries, gates, mixed, pools, out_weight
+        )
+
     sums = []
-    for step in range(1, chips):
-        target = lax.rem(chip + step, chips) * 2
-        other = lax.ppermute(project(target + 1 - core)[0], "head", across)
-        mine = project(target + core)[0]
+    for step in range(chips - 1):
+        other = lax.ppermute(project(1 + 2 * step, [[model]])[0], "head", across)
+        mine = project(2 + 2 * step, [[model]])[0]
         summed = (mine.astype(F32) + other.astype(F32)).astype(BF16)
-        summed, chip = lax.optimization_barrier((summed, chip))
+        summed, meta = lax.optimization_barrier((summed, meta))
         sums.append(summed)
-    passed, kept = project(chip * 2 + 1 - core, chip * 2 + core)
-    arrived = [lax.ppermute(passed, "head", across)]
+    *passed, kept = project(n_head - 1, [[model // 2] * 2, [model]])
+    arrived = [jnp.concatenate([lax.ppermute(x, "head", across) for x in passed], axis=1)]
     for step, summed in enumerate(sums, 1):
         route = [(i, (i + 2 * step) % n_head) for i in range(n_head)]
         arrived.append(lax.ppermute(summed, "head", route))

time: 197 us -> 193 us (0.980)
  Pallas kernels: 143 us -> 151 us
  local copies, waits for them, and re-layouts: 11.2 us -> 6.24 us
  starting transfers between devices: 26.7 us -> 24.5 us
    pallas_call x6 -> x7, Pallas kernels: 94.9 us -> 103 us  [the longest x3 89.9 us: chosen_and_project(): pl.pallas_call(functools.partial(chosen_kernel, heads, (first_chunk, widt...]
    unnamed x28 -> x20, local copies, waits for them, and re-layouts: 7.36 us -> 1.81 us
    ppermute x5 -> x9, starting transfers between devices: 16.3 us -> 14.1 us  [the longest x6 11.4 us: ahead(): lax.ppermute(send, 'ctx', [(i, i + 2 * distance) for i in range(n_ctx - 2...]
  transfers between devices with their start and end apart: 11 -> 15, of which waited for: 2 -> 2; matrix products, arithmetic and copies ran while one was open for 4% -> 4% of each run, Pallas kernels for 59% -> 63%
where the time goes in v2:
time: 193 us; the launch traced here: 192 us
  Pallas kernels  151 us (78%)
  starting transfers between devices  24.5 us (13%)
  other arithmetic  7.46 us (4%)
  local copies, waits for them, and re-layouts  6.24 us (3%)
  waiting for transfers between devices  2.77 us (1%)
    pallas_call x3, Pallas kernels, chosen_and_project(): pl.pallas_call(functools.partial(chosen_kernel, heads, (first_chunk, widt...  89.9 us
    pallas_call x2, Pallas kernels, near_branch(): pl.pallas_call(functools.partial(near_kernel, heads), grid=(block_count,...  44.2 us
    pallas_call x4, Pallas kernels, single_step(): pl.pallas_call(kernel, grid_spec=pltpu.PrefetchScalarGridSpec(num_scalar_...  13.4 us
    ppermute x6, starting transfers between devices, ahead(): lax.ppermute(send, 'ctx', [(i, i + 2 * distance) for i in range(n_ctx - 2...  11.4 us
    ppermute x1, starting transfers between devices, local(): lax.ppermute(rim, 'ctx', [(i, i + 1) for i in range(1, n_ctx - 1, 2)])  5.16 us
    ppermute x3, starting transfers between devices, local(): lax.ppermute(my_picks, 'ctx', [(i, i - 2 * d) for i in range(2 * d, n_ctx)])  3.88 us
  transfers between devices with their start and end apart: 15, of which 2 were waited for; matrix products, arithmetic and copies ran while one was open for 4% of the time, Pallas kernels for 63%

profile of v2, /device:TPU:5, one launch (start us, length us, event | category | flops | bytes accessed | tf_op | source)
XLA Modules:
  0.0 192.3 jit_solution(15460642204338016203)
XLA Ops:
  0.0 3.5 %prep.1 = (bf16[2656,128]{1,0:T(8,128)(2,1)}, bf16[1280,128]{1,0:T(8,128)(2,1)}, bf16[256,1024]{1,0:T(8,128)(2,1)}, bf16[256,1024]{1,0:T(8,128)(2,1)}, bf16[1024,256]{1,0:T(8,128)(2,1)}) custom-call(s32[1]{0:T(128)} %bitcast.9.group_ref, bf16[1024,768]{1,0:T(8,128)(2,1)} %keys_ref.1, bf16[1024,512]{1,0:T(8,128)(2,1)} %values_ref.1, f32[32,768]{1,0:T(8,128)} %kw_ref.1, ...), custom_call_target="tpu_custom_call" | custom-call | tf_op jit(solution)/shard_map/prep/pallas_call | solution.py:534
  3.5 1.3 collective-permute-start.3
  4.8 1.3 collective-permute-start.2
  6.1 1.3 collective-permute-start.1
  7.5 5.2 %collective-permute-start.4 = (bf16[1280,128]{1,0:T(8,128)(2,1)}, bf16[1280,128]{1,0:T(8,128)(2,1)S(1)}, u32[]{:S(2)}, u32[]{:S(2)}) collective-permute-start(bf16[1280,128]{1,0:T(8,128)(2,1)} %get-tuple-element.49), channel_id=1, source_target_pairs={{4,8},{12,16},{20,24},{5,9},{13,17},{21,25},{6,10},{14,18},{22,26}... | collective-permute-start | bytes 983048 | tf_op jit(solution)/shard_map/ppermute | solution.py:561
  13.3 0.7 fusion.10
  16.2 0.8 pad.4.gate_ref.refs_4_
  17.0 0.7 pad_add_fusion.1
  18.3 0.7 reshape.250.picks_ref
  19.0 3.3 %pack.2 = (bf16[736,128]{1,0:T(8,128)(2,1)}, bf16[736,128]{1,0:T(8,128)(2,1)}, bf16[736,128]{1,0:T(8,128)(2,1)}) custom-call(s32[2]{0:T(128)} %get-tuple-element.77.where_ref, s32[256]{0:T(256)} %reshape.250.picks_ref, bf16[2656,128]{1,0:T(8,128)(2,1)} %get-tuple-element.40.ref.own_ref), custom_call_target="tpu_custom_call" | custom-call | tf_op jit(solution)/shard_map/pack/pallas_call | solution.py:493
  22.2 3.4 %collective-permute-start.5 = (bf16[736,128]{1,0:T(8,128)(2,1)}, bf16[736,128]{1,0:T(8,128)(2,1)S(1)}, u32[]{:S(2)}, u32[]{:S(2)}) collective-permute-start(bf16[736,128]{1,0:T(8,128)(2,1)} %get-tuple-element.55), channel_id=1, source_target_pairs={{0,8},{4,12},{8,16},{12,20},{16,24},{20,28},{1,9},{5,13},{9,17},{1... | collective-permute-start | bytes 565256 | tf_op jit(solution)/shard_map/ppermute | solution.py:578
  26.2 2.8 %collective-permute-start.7 = (bf16[736,128]{1,0:T(8,128)(2,1)}, bf16[736,128]{1,0:T(8,128)(2,1)S(1)}, u32[]{:S(2)}, u32[]{:S(2)}) collective-permute-start(bf16[736,128]{1,0:T(8,128)(2,1)} %get-tuple-element.57), channel_id=1, source_target_pairs={{0,16},{4,20},{8,24},{12,28},{1,17},{5,21},{9,25},{13,29},{2,18},{... | collective-permute-start | bytes 565256 | tf_op jit(solution)/shard_map/ppermute | solution.py:578
  29.1 1.3 collective-permute-start.9
  30.4 25.2 %near_branch.2.refs_0_ = f32[1024,2048]{1,0:T(8,128)} custom-call(bf16[1024,3072]{1,0:T(8,128)(2,1)} %refs_3_.5, f32[1024,128]{1,0:T(8,128)} %pad.4.gate_ref.refs_4_, bf16[256,1024]{1,0:T(8,128)(2,1)} %get-tuple-element.45.even_ref.even_in, bf16[256,1024]{1,0:T(8,128)(2,1)} %get-tuple-element.46.odd_ref.odd_in, ...), custom_call_target="tpu_custom_call" | custom-call | flops 402653184 | bytes 7340032 | tf_op jit(solution)/shard_map/near_branch/pallas_call | solution.py:318
  55.6 0.9 copy-done
  56.5 3.6 %pack.3 = (bf16[736,128]{1,0:T(8,128)(2,1)}, bf16[736,128]{1,0:T(8,128)(2,1)}, bf16[736,128]{1,0:T(8,128)(2,1)}, bf16[736,128]{1,0:T(8,128)(2,1)}) custom-call(s32[2]{0:T(128)} %get-tuple-element.78.where_ref, s32[256]{0:T(256)} %reshape.250.picks_ref, bf16[2656,128]{1,0:T(8,128)(2,1)} %copy-done), custom_call_target="tpu_custom_call" | custom-call | tf_op jit(solution)/shard_map/pack/pallas_call | solution.py:493
  60.1 1.3 collective-permute-start.6
  61.4 1.3 collective-permute-start.8
  62.7 1.3 collective-permute-start.10
  64.0 0.6 fusion.9.refs_1_
  64.6 3.3 %rim.1 = (bf16[256,1024]{1,0:T(8,128)(2,1)}, bf16[256,1024]{1,0:T(8,128)(2,1)}, bf16[1024,256]{1,0:T(8,128)(2,1)}) custom-call(s32[1]{0:T(128)} %bitcast.8.shard_ref, bf16[2656,128]{1,0:T(8,128)(2,1)} %copy-done, bf16[1280,128]{1,0:T(8,128)(2,1)} %copy-done.1, bf16[256,1024]{1,0:T(8,128)(2,1)} %get-tuple-element.45.even_ref.even_in, ...), custom_call_target="tpu_custom_call" | custom-call | tf_op jit(solution)/shard_map/rim/pallas_call | solution.py:493
  68.0 19.0 %near_branch.3.refs_5_ = f32[1024,2048]{1,0:T(8,128)} custom-call(bf16[1024,3072]{1,0:T(8,128)(2,1)} %refs_3_.5, f32[1024,128]{1,0:T(8,128)} %pad.4.gate_ref.refs_4_, bf16[256,1024]{1,0:T(8,128)(2,1)} %get-tuple-element.50.even_ref, bf16[256,1024]{1,0:T(8,128)(2,1)} %get-tuple-element.51.odd_ref, ...), custom_call_target="tpu_custom_call", output_to_operand_aliasing={{}: (5, {})} | custom-call | flops 402653184 | bytes 7340032 | tf_op jit(solution)/shard_map/near_branch/pallas_call | solution.py:318
  87.9 3.3 %pool.1 = (bf16[2048,256]{1,0:T(8,128)(2,1)}, bf16[2048,256]{1,0:T(8,128)(2,1)}, bf16[256,256]{1,0:T(8,128)(2,1)}, bf16[256,256]{1,0:T(8,128)(2,1)}, bf16[256,256]{1,0:T(8,128)(2,1)}) custom-call(s32[1]{0:T(128)} %bitcast.8.shard_ref, bf16[2656,128]{1,0:T(8,128)(2,1)} %get-tuple-element.40.ref.own_ref, bf16[736,128]{1,0:T(8,128)(2,1)} %get-tuple-element.54.refs_0_, ...), custom_call_target="tpu_custom_call" | custom-call | tf_op jit(solution)/shard_map/pool/pallas_call | solution.py:493
  91.2 23.3 %chosen_and_project.4 = bf16[256,2560]{1,0:T(8,128)(2,1)} custom-call(s32[5]{0:T(128)} %stack.52.refs_0_, s32[64]{0:T(128)} %fusion.9.refs_1_, s32[64]{0:T(128)} %get-tuple-element.71.refs_2_, bf16[1024,3072]{1,0:T(8,128)(2,1)} %refs_3_.5, f32[1024,128]{1,0:T(8,128)} %pad.4.gate_ref.refs_4_, f32[1024,2048]{1,0:T(8,128)} %near_branch.3.refs_5_, ...), custom_call_target="tpu_custom_call" | custom-call | flops 268435456 | bytes 5242880 | tf_op jit(solution)/shard_map/chosen_and_project/pallas_call | solution.py:430
  114.5 2.1 %collective-permute-start.11 = (bf16[256,2560]{1,0:T(8,128)(2,1)}, bf16[256,2560]{1,0:T(8,128)(2,1)S(1)}, u32[]{:S(2)}, u32[]{:S(2)}) collective-permute-start(bf16[256,2560]{1,0:T(8,128)(2,1)} %chosen_and_project.4), channel_id=1, source_target_pairs={{0,1},{1,0},{2,3},{3,2},{4,5},{5,4},{6,7},{7,6},{8,9},{9,8},{10,11... | collective-permute-start | bytes 3932168 | tf_op jit(solution)/shard_map/ppermute | solution.py:630
  116.6 23.2 %chosen_and_project.3 = bf16[256,2560]{1,0:T(8,128)(2,1)} custom-call(s32[5]{0:T(128)} %stack.52.refs_0_, s32[64]{0:T(128)} %fusion.9.refs_1_, s32[64]{0:T(128)} %get-tuple-element.71.refs_2_, bf16[1024,3072]{1,0:T(8,128)(2,1)} %refs_3_.5, f32[1024,128]{1,0:T(8,128)} %pad.4.gate_ref.refs_4_, f32[1024,2048]{1,0:T(8,128)} %near_branch.3.refs_5_, ...), custom_call_target="tpu_custom_call" | custom-call | flops 268435456 | bytes 5242880 | tf_op jit(solution)/shard_map/chosen_and_project/pallas_call | solution.py:430
  139.9 1.7 add_convert_fusion.1
  141.6 1.2 collective-permute-start.14
  142.8 43.4 %chosen_and_project.5 = (bf16[256,1280]{1,0:T(8,128)(2,1)}, bf16[256,1280]{1,0:T(8,128)(2,1)}, bf16[256,2560]{1,0:T(8,128)(2,1)}) custom-call(s32[5]{0:T(128)} %stack.52.refs_0_, s32[64]{0:T(128)} %fusion.9.refs_1_, s32[64]{0:T(128)} %get-tuple-element.71.refs_2_, bf16[1024,3072]{1,0:T(8,128)(2,1)} %refs_3_.5, f32[1024,128]{1,0:T(8,128)} %pad.4.gate_ref.refs_4_, ...), custom_call_target="tpu_custom_call" | custom-call | flops 268435456 | bytes 5242880 | tf_op jit(solution)/shard_map/chosen_and_project/pallas_call | solution.py:430
  186.8 1.8 collective-permute-done.12
  188.6 0.9 collective-permute-done.13
  189.5 2.8 %add_convert_fusion = bf16[256,2560]{1,0:T(8,128)(2,1)} fusion(bf16[256,2560]{1,0:T(8,128)(2,1)S(1)} %collective-permute-done.14, bf16[256,2560]{1,0:T(8,128)(2,1)} %get-tuple-element.67, bf16[256,1280]{1,0:T(8,128)(2,1)S(1)} %collective-permute-done.13, bf16[256,1280]{1,0:T(8,128)(2,1)S(1)} %collective-permute-done.12), kind=kLoop, calls=%fused_computation | loop fusion | flops 5898240 | bytes 5242880 | tf_op jit(solution)/shard_map/convert_element_type | solution.py:643
  (65 shorter events, 5.4 us)
Async XLA Ops:
  0.0 3.5 %copy-start.9 = (s32[4,4,16]{2,1,0:T(4,128)S(1)}, s32[4,4,16]{2,1,0:T(4,128)}, u32[]{:S(2)}) copy-start(s32[4,4,16]{2,1,0:T(4,128)} %param.13) | copy-start | bytes 3076
  0.0 15.9 %copy-start.2 = (f32[1024,3,16]{0,2,1:T(8,128)S(1)}, f32[1024,3,16]{0,2,1:T(8,128)}, u32[]{:S(2)}) copy-start(f32[1024,3,16]{0,2,1:T(8,128)} %param.14) | copy-start | bytes 589828
  3.5 14.8 %collective-permute-start.3 = (s32[4,16]{1,0:T(4,128)S(1)}, s32[4,16]{1,0:T(4,128)S(1)}, u32[]{:S(2)}, u32[]{:S(2)}) collective-permute-start(s32[4,16]{1,0:T(4,128)S(1)} %bitcast.22), channel_id=1, source_target_pairs={{24,0},{28,4},{25,1},{29,5},{26,2},{30,6},{27,3},{31,7}} | collective-permute-start | bytes 776 | tf_op jit(solution)/shard_map/ppermute | solution.py:558
  4.8 13.5 %collective-permute-start.2 = (s32[4,16]{1,0:T(4,128)S(1)}, s32[4,16]{1,0:T(4,128)S(1)}, u32[]{:S(2)}, u32[]{:S(2)}) collective-permute-start(s32[4,16]{1,0:T(4,128)S(1)} %bitcast.23), channel_id=1, source_target_pairs={{16,0},{20,4},{24,8},{28,12},{17,1},{21,5},{25,9},{29,13},{18,2},{... | collective-permute-start | bytes 776 | tf_op jit(solution)/shard_map/ppermute | solution.py:558
  6.1 12.2 %collective-permute-start.1 = (s32[4,16]{1,0:T(4,128)S(1)}, s32[4,16]{1,0:T(4,128)S(1)}, u32[]{:S(2)}, u32[]{:S(2)}) collective-permute-start(s32[4,16]{1,0:T(4,128)S(1)} %bitcast.24), channel_id=1, source_target_pairs={{8,0},{12,4},{16,8},{20,12},{24,16},{28,20},{9,1},{13,5},{17,9},{2... | collective-permute-start | bytes 776 | tf_op jit(solution)/shard_map/ppermute | solution.py:558
  7.4 48.2 %collective-permute-start = (bf16[2656,128]{1,0:T(8,128)(2,1)}, bf16[2656,128]{1,0:T(8,128)(2,1)S(1)}, u32[]{:S(2)}, u32[]{:S(2)}) collective-permute-start(bf16[2656,128]{1,0:T(8,128)(2,1)} %get-tuple-element.40.ref.own_ref), channel_id=1, source_target_pairs={{0,4},{4,0},{8,12},{12,8},{16,20},{20,16},{24,28},{28,24},{1,5},{5... | collective-permute-start | bytes 2039816 | tf_op jit(solution)/shard_map/ppermute | solution.py:551
  7.5 55.2 %collective-permute-start.4 = (bf16[1280,128]{1,0:T(8,128)(2,1)}, bf16[1280,128]{1,0:T(8,128)(2,1)S(1)}, u32[]{:S(2)}, u32[]{:S(2)}) collective-permute-start(bf16[1280,128]{1,0:T(8,128)(2,1)} %get-tuple-element.49), channel_id=1, source_target_pairs={{4,8},{12,16},{20,24},{5,9},{13,17},{21,25},{6,10},{14,18},{22,26}... | collective-permute-start | bytes 983048 | tf_op jit(solution)/shard_map/ppermute | solution.py:561
  22.2 39.2 %collective-permute-start.5 = (bf16[736,128]{1,0:T(8,128)(2,1)}, bf16[736,128]{1,0:T(8,128)(2,1)S(1)}, u32[]{:S(2)}, u32[]{:S(2)}) collective-permute-start(bf16[736,128]{1,0:T(8,128)(2,1)} %get-tuple-element.55), channel_id=1, source_target_pairs={{0,8},{4,12},{8,16},{12,20},{16,24},{20,28},{1,9},{5,13},{9,17},{1... | collective-permute-start | bytes 565256 | tf_op jit(solution)/shard_map/ppermute | solution.py:578
  26.2 60.7 %collective-permute-start.7 = (bf16[736,128]{1,0:T(8,128)(2,1)}, bf16[736,128]{1,0:T(8,128)(2,1)S(1)}, u32[]{:S(2)}, u32[]{:S(2)}) collective-permute-start(bf16[736,128]{1,0:T(8,128)(2,1)} %get-tuple-element.57), channel_id=1, source_target_pairs={{0,16},{4,20},{8,24},{12,28},{1,17},{5,21},{9,25},{13,29},{2,18},{... | collective-permute-start | bytes 565256 | tf_op jit(solution)/shard_map/ppermute | solution.py:578
  29.1 57.9 %collective-permute-start.9 = (bf16[736,128]{1,0:T(8,128)(2,1)}, bf16[736,128]{1,0:T(8,128)(2,1)S(1)}, u32[]{:S(2)}, u32[]{:S(2)}) collective-permute-start(bf16[736,128]{1,0:T(8,128)(2,1)} %get-tuple-element.59), channel_id=1, source_target_pairs={{0,24},{4,28},{1,25},{5,29},{2,26},{6,30},{3,27},{7,31}} | collective-permute-start | bytes 565256 | tf_op jit(solution)/shard_map/ppermute | solution.py:578
  55.6 0.9 copy-start
  60.1 26.9 %collective-permute-start.6 = (bf16[736,128]{1,0:T(8,128)(2,1)}, bf16[736,128]{1,0:T(8,128)(2,1)S(1)}, u32[]{:S(2)}, u32[]{:S(2)}) collective-permute-start(bf16[736,128]{1,0:T(8,128)(2,1)} %get-tuple-element.56), channel_id=1, source_target_pairs={{0,8},{4,12},{8,16},{12,20},{16,24},{20,28},{1,9},{5,13},{9,17},{1... | collective-permute-start | bytes 565256 | tf_op jit(solution)/shard_map/ppermute | solution.py:578
  61.4 25.6 %copy-start.3 = (bf16[736,128]{1,0:T(8,128)(2,1)}, bf16[736,128]{1,0:T(8,128)(2,1)S(1)}, u32[]{:S(2)}) copy-start(bf16[736,128]{1,0:T(8,128)(2,1)S(1)} %collective-permute-done.5.refs_1_) | copy-start | bytes 565252
  61.4 25.6 %collective-permute-start.8 = (bf16[736,128]{1,0:T(8,128)(2,1)}, bf16[736,128]{1,0:T(8,128)(2,1)S(1)}, u32[]{:S(2)}, u32[]{:S(2)}) collective-permute-start(bf16[736,128]{1,0:T(8,128)(2,1)} %get-tuple-element.58), channel_id=1, source_target_pairs={{0,16},{4,20},{8,24},{12,28},{1,17},{5,21},{9,25},{13,29},{2,18},{... | collective-permute-start | bytes 565256 | tf_op jit(solution)/shard_map/ppermute | solution.py:578
  62.7 1.9 %copy-start.1 = (bf16[1280,128]{1,0:T(8,128)(2,1)}, bf16[1280,128]{1,0:T(8,128)(2,1)S(1)}, u32[]{:S(2)}) copy-start(bf16[1280,128]{1,0:T(8,128)(2,1)S(1)} %collective-permute-done.4.far_ref) | copy-start | bytes 983044
  62.7 24.3 %collective-permute-start.10 = (bf16[736,128]{1,0:T(8,128)(2,1)}, bf16[736,128]{1,0:T(8,128)(2,1)S(1)}, u32[]{:S(2)}, u32[]{:S(2)}) collective-permute-start(bf16[736,128]{1,0:T(8,128)(2,1)} %get-tuple-element.60), channel_id=1, source_target_pairs={{0,24},{4,28},{1,25},{5,29},{2,26},{6,30},{3,27},{7,31}} | collective-permute-start | bytes 565256 | tf_op jit(solution)/shard_map/ppermute | solution.py:578
  87.0 0.7 copy-start.4
  87.0 0.7 copy-start.5
  87.0 0.8 copy-start.6
  87.0 0.8 copy-start.7
  87.0 0.9 copy-start.8
  114.5 25.4 %collective-permute-start.11 = (bf16[256,2560]{1,0:T(8,128)(2,1)}, bf16[256,2560]{1,0:T(8,128)(2,1)S(1)}, u32[]{:S(2)}, u32[]{:S(2)}) collective-permute-start(bf16[256,2560]{1,0:T(8,128)(2,1)} %chosen_and_project.4), channel_id=1, source_target_pairs={{0,1},{1,0},{2,3},{3,2},{4,5},{5,4},{6,7},{7,6},{8,9},{9,8},{10,11... | collective-permute-start | bytes 3932168 | tf_op jit(solution)/shard_map/ppermute | solution.py:630
  141.6 47.9 %collective-permute-start.14 = (bf16[256,2560]{1,0:T(8,128)(2,1)S(1)}, bf16[256,2560]{1,0:T(8,128)(2,1)S(1)}, u32[]{:S(2)}, u32[]{:S(2)}) collective-permute-start(bf16[256,2560]{1,0:T(8,128)(2,1)S(1)} %add_convert_fusion.1), channel_id=1, source_target_pairs={{0,2},{1,3},{2,0},{3,1},{4,6},{5,7},{6,4},{7,5},{8,10},{9,11},{10,... | collective-permute-start | bytes 3932168 | tf_op jit(solution)/shard_map/ppermute | solution.py:639
  186.2 2.4 %collective-permute-start.12 = (bf16[256,1280]{1,0:T(8,128)(2,1)}, bf16[256,1280]{1,0:T(8,128)(2,1)S(1)}, u32[]{:S(2)}, u32[]{:S(2)}) collective-permute-start(bf16[256,1280]{1,0:T(8,128)(2,1)} %get-tuple-element.68), channel_id=1, source_target_pairs={{0,1},{1,0},{2,3},{3,2},{4,5},{5,4},{6,7},{7,6},{8,9},{9,8},{10,11... | collective-permute-start | bytes 1966088 | tf_op jit(solution)/shard_map/ppermute | solution.py:636
  186.3 3.2 %collective-permute-start.13 = (bf16[256,1280]{1,0:T(8,128)(2,1)}, bf16[256,1280]{1,0:T(8,128)(2,1)S(1)}, u32[]{:S(2)}, u32[]{:S(2)}) collective-permute-start(bf16[256,1280]{1,0:T(8,128)(2,1)} %get-tuple-element.69), channel_id=1, source_target_pairs={{0,1},{1,0},{2,3},{3,2},{4,5},{5,4},{6,7},{7,6},{8,9},{9,8},{10,11... | collective-permute-start | bytes 1966088 | tf_op jit(solution)/shard_map/ppermute | solution.py:636

commit v3 on v2

--- a/solution.py
+++ b/solution.py
@@ -106,29 +106,85 @@
     packed_ref[at + 2 * folds :] = fold(values.astype(F32), vw_ref[...])
 
 
-def pack_kernel(distances, lists, per_owner, limit, where_ref, picks_ref, ref, *outs):
-    owner, base = where_ref[0], where_ref[1]
-    data = per_owner * BROWS
-    for distance, out in zip(distances, outs):
-
-        @pl.when(base + 2 * distance < limit)
-        def _():
-            named = jnp.int32(0)
-            for entry in range(lists * PICKS):
-                block = picks_ref[distance * lists * PICKS + entry] - owner * per_owner
-                here = (block >= 0) & (block < per_owner)
-                named = named | jnp.where(here, jnp.int32(1) << jnp.where(here, block, 0), 0)
-            rank = jnp.int32(0)
-            for block in range(per_owner):
-                bit = (named >> block) & 1
-
-                @pl.when((bit == 1) & (rank < lists))
-                def _():
-                    at = pl.multiple_of(jnp.minimum(rank, lists - 1) * BROWS, BROWS)
-                    out[pl.ds(at, BROWS)] = ref[block * BROWS : (block + 1) * BROWS]
-
-                rank = rank + bit
-            out[lists * BROWS :] = ref[data:]
+def plan_kernel(shape, where_ref, picks_ref, lists_ref, slots_ref, dead_ref, named, rank, seen):
+    n_ctx, lists, per_owner = shape
+    group, shard = where_ref[0], where_ref[1]
+    for owner in range(n_ctx):
+        named[owner] = 0
+    for entry in range(n_ctx * lists + 1):
+        lists_ref[entry] = 0
+
+    def mark(query_block, _):
+        for entry in range(PICKS):
+            block = picks_ref[query_block, group, entry]
+            owner = lax.div(block, per_owner)
+            named[owner] = named[owner] | (jnp.int32(1) << lax.rem(block, per_owner))
+        return 0
+
+    lax.fori_loop(0, lists, mark, 0)
+
+    def enlist(owner, _):
+        bits = named[owner]
+        count = jnp.int32(0)
+        for block in range(per_owner):
+            bit = (bits >> block) & 1
+            rank[owner * per_owner + block] = jnp.minimum(count, lists - 1)
+            taken = (bit == 1) & (count < lists)
+            lists_ref[jnp.where(taken, owner * lists + count, n_ctx * lists)] = block
+            count = count + bit
+        return 0
+
+    lax.fori_loop(0, n_ctx, enlist, 0)
+
+    def place(block):
+        owner = lax.div(block, per_owner)
+        turn = (lax.div(shard, 2) - lax.div(owner, 2)) * 2 + ((owner ^ shard) & 1)
+        return jnp.clip(turn * lists + rank[block], 0, n_ctx * lists - 1)
+
+    def one_list(query_block, _):
+        first = shard * per_owner + query_block * (QBLK // KBLK)
+        at = query_block * PICKS
+        for owner in range(n_ctx):
+            seen[owner] = 0
+        seen[shard] = jnp.int32(1) << lax.rem(first, per_owner)
+        slots_ref[at] = place(first)
+        dead_ref[at] = 0
+        at = at + 1
+        met = jnp.int32(0)
+        for entry in range(PICKS):
+            block = picks_ref[query_block, group, entry]
+            owner = lax.div(block, per_owner)
+            inside = lax.rem(block, per_owner)
+            before = (seen[owner] >> inside) & 1
+            own = jnp.where(block == first, 1, 0)
+            slots_ref[at] = place(block)
+            dead_ref[at] = before | jnp.where(block > first, 1, 0)
+            seen[owner] = seen[owner] | (jnp.int32(1) << inside)
+            at = at + 1 - (own & (1 - met))
+            met = met | own
+        return 0
+
+    lax.fori_loop(0, lists, one_list, 0)
+
+
+def pack_kernel(lists, beside, where_ref, *refs):
+    count = (len(refs) - 2) // 2
+    named, ref, outs, sems = refs[:count], refs[count], refs[count + 1 : -1], refs[-1]
+    shard = where_ref[1]
+    owner = shard + 1 - 2 * lax.rem(shard, 2) if beside else shard
+    data = ref.shape[0] - (outs[0].shape[0] - lists * BROWS)
+    copies = []
+    for blocks, out in zip(named, outs):
+        for place in range(lists):
+            at = pl.multiple_of(blocks[owner * lists + place] * BROWS, 16)
+            to = out.at[place * BROWS : (place + 1) * BROWS]
+            copies.append((ref.at[pl.ds(at, BROWS)], to))
+        copies.append((ref.at[data:], out.at[lists * BROWS :]))
+    copies = [pltpu.make_async_copy(*pair, sems.at[i]) for i, pair in enumerate(copies)]
+    for copy in copies:
+        copy.start()
+    for copy in copies:
+        copy.wait()
 
 
 def unpack(ref, at, count, step=1):
@@ -153,27 +209,20 @@
     return even, jnp.concatenate(values, axis=0)
 
 
-def rim_kernel(
-    rim_at, shard_ref, near_ref, far_ref, even_in, odd_in, val_in, even_ref, odd_ref, val_ref
-):
-    shard = shard_ref[0]
+def fill_rim(shard, near_ref, far_ref, own, ext):
     rim_blocks = WINDOW // KBLK
+    even_in, odd_in, val_in = own
+    even_ref, odd_ref, val_ref = ext
     even_ref[:, WINDOW:] = even_in[:, :WINDOW]
     odd_ref[:, WINDOW:] = odd_in[:, :WINDOW]
     val_ref[WINDOW:] = val_in[:WINDOW]
-
-    def fill(ref, at):
-        keys, values = unpack(ref, at, rim_blocks)
+    use_near = lax.rem(shard, 2) == 1
+
+    @pl.when(shard > 0)
+    def _():
+        keys, values = unpack(jnp.where(use_near, near_ref[...], far_ref[...]), 0, rim_blocks)
         even_ref[:, :WINDOW], odd_ref[:, :WINDOW] = turned(keys)
         val_ref[:WINDOW] = with_ones(values)
-
-    @pl.when(lax.rem(shard, 2) == 1)
-    def _():
-        fill(near_ref, rim_at)
-
-    @pl.when((lax.rem(shard, 2) == 0) & (shard > 0))
-    def _():
-        fill(far_ref, 0)
 
     @pl.when(shard == 0)
     def _():
@@ -231,28 +280,38 @@
 
 
 def in_range(total):
-    return jnp.where((total >= LOW_TOTAL) & (total <= HIGH_TOTAL), 1.0, 0.0)
-
-
-def with_fallback(run):
-    good = run(False)
-    worst = functools.reduce(jnp.minimum, good)
+    good = jnp.where((total >= LOW_TOTAL) & (total <= HIGH_TOTAL), 1.0, 0.0)
+    return jnp.min(good.reshape(-1, 8, DV), axis=0)
+
+
+def over_heads(run, pairs):
+    at_once = 2 if pairs % 2 == 0 else 1
+
+    def quick(turn, worst):
+        return jnp.minimum(worst, run(turn * at_once, at_once, False))
+
+    def exact(turn, _):
+        run(turn, 1, True)
+        return 0
+
+    worst = lax.fori_loop(0, pairs // at_once, quick, jnp.ones((8, DV), F32))
 
     @pl.when(jnp.min(worst) < 0.5)
     def _():
-        run(True)
+        lax.fori_loop(0, pairs, exact, 0)
 
 
 def stacked(x, times):
     return jnp.concatenate([x] * times, axis=0) if times > 1 else x
 
 
-def stacked_queries(q_ref, side):
-    pairs = q_ref.shape[1] // PAIR
-    return jnp.concatenate(
-        [q_ref[:, p * PAIR + side * 128 : p * PAIR + side * 128 + 256] for p in range(pairs)],
-        axis=0,
-    )
+def stacked_queries(q_ref, first, pairs, side):
+    at = [pl.multiple_of((first + p) * PAIR + side * 128, 128) for p in range(pairs)]
+    return jnp.concatenate([q_ref[:, pl.ds(x, 256)] for x in at], axis=0)
+
+
+def head_columns(first, pair, side):
+    return pl.ds(pl.multiple_of((first + pair) * 2 * DV + side * DV, DV), DV)
 
 
 def gate_columns(gate_ref, first, branch, heads, side, count):
@@ -268,58 +327,71 @@
     )
 
 
-def near_kernel(heads, q_ref, gate_ref, even_ref, odd_ref, val_ref, *refs):
-    out_ref = refs[-1]
+def near_kernel(heads, rim, where_ref, q_ref, gate_ref, *refs):
+    keys = refs[:3]
+    if rim:
+        out_ref, ext = refs[6], refs[7:]
+
+        @pl.when(pl.program_id(0) == 0)
+        def _():
+            fill_rim(where_ref[1], refs[3], refs[4], keys, ext)
+
+        keys = ext
+    else:
+        out_ref = refs[3]
     rows = pl.ds(pl.multiple_of(pl.program_id(0) * QBLK, QBLK), WINDOW + QBLK)
-    pairs = q_ref.shape[1] // PAIR
-    first = pl.program_id(1) * 2 * pairs
-
-    def mask(scores):
-        row, col = iota(QBLK, QBLK, 0), iota(QBLK, QBLK, 1)
-        old = jnp.where(stacked(col >= row, pairs), scores[:, :QBLK], NEG)
-        new = jnp.where(stacked(col <= row, pairs), scores[:, WINDOW:], NEG)
-        return jnp.concatenate([old, scores[:, QBLK:WINDOW], new], axis=1)
-
-    def run(exact):
+
+    def run(first, pairs, exact):
+        def mask(scores):
+            row, col = iota(QBLK, QBLK, 0), iota(QBLK, QBLK, 1)
+            old = jnp.where(stacked(col >= row, pairs), scores[:, :QBLK], NEG)
+            new = jnp.where(stacked(col <= row, pairs), scores[:, WINDOW:], NEG)
+            return jnp.concatenate([old, scores[:, QBLK:WINDOW], new], axis=1)
+
         good = []
         for side in range(2):
-            keys = (even_ref, odd_ref)[side][:, rows]
-            num, den = attend(stacked_queries(q_ref, side), keys, val_ref[rows], mask, exact)
+            q = stacked_queries(q_ref, first, pairs, side)
+            num, den = attend(q, keys[side][:, rows], keys[2][rows], mask, exact)
             good.append(in_range(den))
-            total = gate_columns(gate_ref, first, 2, heads, side, pairs) * (num / den)
+            total = gate_columns(gate_ref, 2 * first, 2, heads, side, pairs) * (num / den)
             for p in range(pairs):
-                at = (2 * p + side) * DV
-                out_ref[:, at : at + DV] = total[p * QBLK : (p + 1) * QBLK]
-        return good
-
-    with_fallback(run)
-
-
-def near_branch(first_block, block_count, queries, gates, even, odd, val, prior):
+                out_ref[:, head_columns(first, p, side)] = total[p * QBLK : (p + 1) * QBLK]
+        return jnp.minimum(*good)
+
+    over_heads(run, heads // 2)
+
+
+def near_branch(first_block, block_count, where, queries, gates, keys, rims, prior):
     tokens, width = queries.shape
     heads = width // QK
-    steps = heads // 4
-    row_block = lambda i, p: (i + first_block, p)
-    whole = lambda x: pl.BlockSpec(x.shape, lambda i, p: (0,) * x.ndim)
-    operands = [queries, gates, even, odd, val]
-    specs = [
-        pl.BlockSpec((QBLK, 2 * PAIR), row_block),
-        pl.BlockSpec((QBLK, 128), lambda i, p: (i + first_block, 0)),
-        whole(even),
-        whole(odd),
-        whole(val),
-    ]
-    alias = {}
-    if prior is not None:
+    row_block = lambda i, *_: (i + first_block, 0)
+    whole = lambda x: pl.BlockSpec(x.shape, lambda i, *_: (0,) * x.ndim)
+    operands = [queries, gates, *keys]
+    specs = [pl.BlockSpec((QBLK, width), row_block), pl.BlockSpec((QBLK, 128), row_block)]
+    specs += [whole(x) for x in keys]
+    alias, scratch = {}, []
+    if rims is not None:
+        other, far = rims
+        rim_rows = far.shape[0]
+        last_rim = tokens // KBLK * BROWS // rim_rows - 1
+        operands += [other, far, prior]
+        specs += [
+            pl.BlockSpec(far.shape, lambda i, *_: (last_rim, 0)),
+            whole(far),
+            pl.BlockSpec(memory_space=pl.ANY),
+        ]
         alias = {len(operands): 0}
-        operands.append(prior)
-        specs.append(pl.BlockSpec(memory_space=pl.ANY))
+        scratch = [pltpu.VMEM((256, 2 * WINDOW), BF16)] * 2 + [pltpu.VMEM((2 * WINDOW, 256), BF16)]
     rows = block_count * QBLK * heads
     return pl.pallas_call(
-        functools.partial(near_kernel, heads),
-        grid=(block_count, steps),
-        in_specs=specs,
-        out_specs=pl.BlockSpec((QBLK, 4 * DV), row_block),
+        functools.partial(near_kernel, heads, rims is not None),
+        grid_spec=pltpu.PrefetchScalarGridSpec(
+            num_scalar_prefetch=1,
+            grid=(block_count,),
+            in_specs=specs,
+            out_specs=pl.BlockSpec((QBLK, heads * DV), row_block),
+            scratch_shapes=scratch,
+        ),
         out_shape=jax.ShapeDtypeStruct((tokens, heads * DV), F32),
         input_output_aliases=alias,
         compiler_params=pltpu.CompilerParams(vmem_limit_bytes=VMEM_LIMIT),
@@ -329,7 +401,7 @@
             transcendentals=0,
         ),
         name="near_branch",
-    )(*operands)
+    )(where, *operands)
 
 
 def chosen_kernel(heads, span, *refs):
@@ -340,102 +412,104 @@
     outs = list(refs[12 : 12 + count])
     gathered, even, odd, val, attended, weight, weight_sem = refs[12 + count :]
     keys = (even, odd)
-    turn, step = pl.program_id(0), pl.program_id(1)
-    last = pl.num_programs(1) - 1
+    turn = pl.program_id(0)
     rows = q_ref.shape[0]
-    pairs = q_ref.shape[1] // PAIR
-    first = step * 2 * pairs
     chunk_start = meta_ref[first_chunk + turn] * rows
     list_at = lax.div(chunk_start, QBLK) * PICKS
     first_row = lax.rem(chunk_start, QBLK)
     position = meta_ref[0] + chunk_start
     copy = pltpu.make_async_copy(weight_ref, weight, weight_sem)
 
-    @pl.when(step == 0)
-    def _():
-        for slot in range(PICKS):
-            source = pl.multiple_of(slots_ref[list_at + slot] * KBLK, KBLK)
-            gathered[slot * KBLK : (slot + 1) * KBLK] = key_pool[pl.ds(source, KBLK)]
-            val[slot * KBLK : (slot + 1) * KBLK] = val_pool[pl.ds(source, KBLK)]
-        for slot in range(1, PICKS):
-
-            @pl.when(dead_ref[list_at + slot] == 1)
-            def _():
-                at = slice(slot * KBLK, (slot + 1) * KBLK)
-                gathered[at] = jnp.broadcast_to(gathered[:1], (KBLK, 256))
-                val[at] = jnp.zeros((KBLK, 256), BF16)
-
-        even[...], odd[...] = turned(gathered[...])
-
-    @pl.when((turn == 0) & (step == 0))
+    @pl.when(turn == 0)
     def _():
         copy.start()
 
-    def own_mask(scores):
-        row, col = iota(rows, 128, 0) + first_row, iota(rows, 128, 1)
-        keep = stacked((col >= KBLK) | (col <= row), pairs)
-        own = jnp.where(keep, scores[:, :128], NEG)
-        return jnp.concatenate([own, scores[:, 128:]], axis=1)
-
-    def comp_mask(scores):
-        cols = scores.shape[1]
-        ends = (iota(rows, cols, 1) + 1) * CBLK - 1
-        return jnp.where(stacked(ends <= position + iota(rows, cols, 0), pairs), scores, NEG)
-
-    def run(exact):
+    for slot in range(PICKS):
+        source = pl.multiple_of(slots_ref[list_at + slot] * KBLK, KBLK)
+        gathered[slot * KBLK : (slot + 1) * KBLK] = key_pool[pl.ds(source, KBLK)]
+        val[slot * KBLK : (slot + 1) * KBLK] = val_pool[pl.ds(source, KBLK)]
+
+    def clear(slot, _):
+        @pl.when(dead_ref[list_at + slot] == 1)
+        def _():
+            at = pl.ds(pl.multiple_of(slot * KBLK, KBLK), KBLK)
+            gathered[at] = jnp.broadcast_to(gathered[:1], (KBLK, 256))
+            val[at] = jnp.zeros((KBLK, 256), BF16)
+
+        return 0
+
+    lax.fori_loop(1, PICKS, clear, 0)
+    even[...], odd[...] = turned(gathered[...])
+
+    def run(first, pairs, exact):
+        def own_mask(scores):
+            row, col = iota(rows, 128, 0) + first_row, iota(rows, 128, 1)
+            keep = stacked((col >= KBLK) | (col <= row), pairs)
+            own = jnp.where(keep, scores[:, :128], NEG)
+            return jnp.concatenate([own, scores[:, 128:]], axis=1)
+
+        def comp_mask(scores):
+            cols = scores.shape[1]
+            ends = (iota(rows, cols, 1) + 1) * CBLK - 1
+            keep = stacked(ends <= position + iota(rows, cols, 0), pairs)
+            return jnp.where(keep, scores, NEG)
+
         good = []
         empty = stacked(position + iota(rows, DV, 0) < CBLK - 1, pairs)
         for side in range(2):
-            q = stacked_queries(q_ref, side)
+            q = stacked_queries(q_ref, first, pairs, side)
             num, den = attend(q, keys[side][...], val[...], own_mask, exact)
             good.append(in_range(den))
-            total = gate_columns(gate_ref, first, 1, heads, side, pairs) * (num / den)
+            total = gate_columns(gate_ref, 2 * first, 1, heads, side, pairs) * (num / den)
             num, den = attend(q, cfold[side][...], cfold[2][...], comp_mask, exact)
             den = jnp.where(empty, 1.0, den)
             good.append(in_range(den))
-            total = total + gate_columns(gate_ref, first, 0, heads, side, pairs) * (num / den)
+            total = total + gate_columns(gate_ref, 2 * first, 0, heads, side, pairs) * (num / den)
             for p in range(pairs):
-                at = (2 * p + side) * DV
-                mixed = near_ref[:, at : at + DV] + total[p * rows : (p + 1) * rows]
-                attended[step, :, at : at + DV] = mixed.astype(BF16)
-        return good
-
-    with_fallback(run)
-
-    @pl.when((turn == 0) & (step == last))
+                cols = head_columns(first, p, side)
+                mixed = near_ref[:, cols] + total[p * rows : (p + 1) * rows]
+                attended[:, cols] = mixed.astype(BF16)
+        return functools.reduce(jnp.minimum, good)
+
+    over_heads(run, heads // 2)
+
+    @pl.when(turn == 0)
     def _():
         copy.wait()
 
     for place, parts in enumerate(widths):
         chunk_outs = [outs.pop(0) for _ in parts]
 
-        @pl.when((turn == place) & (step == last))
+        @pl.when(turn == place)
         def _():
-            rows_in = jnp.concatenate([attended[s] for s in range(heads // 4)], axis=1)
             first_col = 0
             for out_ref in chunk_outs:
-                for at in range(0, out_ref.shape[1], 256):
-                    cols = weight[:, first_col + at : first_col + at + 256]
-                    part = jnp.dot(rows_in, cols, preferred_element_type=F32)
-                    out_ref[:, at : at + 256] = part.astype(out_ref.dtype)
+
+                def columns(tile, _, out_ref=out_ref, first_col=first_col):
+                    at = pl.multiple_of(tile * 256, 256)
+                    cols = weight[:, pl.ds(first_col + at, 256)]
+                    part = jnp.dot(attended[...], cols, preferred_element_type=F32)
+                    out_ref[:, pl.ds(at, 256)] = part.astype(out_ref.dtype)
+                    return 0
+
+                lax.fori_loop(0, out_ref.shape[1] // 256, columns, 0)
                 first_col += out_ref.shape[1]
 
 
 def chosen_and_project(first_chunk, widths, rows, meta, slots, dead, queries, gates, near, pools, out_weight):
     tokens, width = queries.shape
     heads = width // QK
-    steps = heads // 4
-    whole = lambda x: pl.BlockSpec(x.shape, lambda i, p, *_: (0,) * x.ndim)
+    whole = lambda x: pl.BlockSpec(x.shape, lambda i, *_: (0,) * x.ndim)
     outs = [jax.ShapeDtypeStruct((rows, width), BF16) for chunk in widths for width in chunk]
     return pl.pallas_call(
         functools.partial(chosen_kernel, heads, (first_chunk, widths)),
         grid_spec=pltpu.PrefetchScalarGridSpec(
             num_scalar_prefetch=3,
-            grid=(len(widths), steps),
+            grid=(len(widths),),
             in_specs=[
-                pl.BlockSpec((rows, 2 * PAIR), lambda i, p, m, *_: (m[first_chunk + i], p)),
-                pl.BlockSpec((rows, 128), lambda i, p, m, *_: (m[first_chunk + i], 0)),
-                pl.BlockSpec((rows, 4 * DV), lambda i, p, m, *_: (m[first_chunk + i], p)),
+                pl.BlockSpec((rows, width), lambda i, m, *_: (m[first_chunk + i], 0)),
+                pl.BlockSpec((rows, 128), lambda i, m, *_: (m[first_chunk + i], 0)),
+                pl.BlockSpec((rows, heads * DV), lambda i, m, *_: (m[first_chunk + i], 0)),
             ]
             + [whole(x) for x in pools]
             + [pl.BlockSpec(memory_space=pl.ANY)],
@@ -445,7 +519,7 @@
                 pltpu.VMEM((256, PICKS * KBLK), BF16),
                 pltpu.VMEM((256, PICKS * KBLK), BF16),
                 pltpu.VMEM((PICKS * KBLK, 256), BF16),
-                pltpu.VMEM((steps, rows, 4 * DV), BF16),
+                pltpu.VMEM((rows, heads * DV), BF16),
                 pltpu.VMEM(out_weight.shape, BF16),
                 pltpu.SemaphoreType.DMA,
             ],
@@ -459,33 +533,6 @@
         ),
         name="chosen_and_project",
     )(meta, slots, dead, queries, gates, near, *pools, out_weight)
-
-
-def plan_picks(my_picks, shard, per_owner, n_ctx):
-    lists = my_picks.shape[0]
-    first = shard * per_owner + jnp.arange(lists, dtype=jnp.int32) * (QBLK // KBLK)
-    place = jnp.arange(PICKS, dtype=jnp.int32)[None, :]
-    found = jnp.min(jnp.where(my_picks == first[:, None], place, PICKS), axis=1, keepdims=True)
-    ordered = jnp.where(place == found, my_picks[:, :1], my_picks)
-    ordered = jnp.where(place == 0, first[:, None], ordered)
-    repeated = jnp.any(
-        (ordered[:, :, None] == ordered[:, None, :]) & (place[0][None, :] < place[0][:, None]),
-        axis=-1,
-    )
-    dead = repeated | (ordered > first[:, None])
-    named = jnp.any(
-        my_picks.reshape(-1)[None, :] == jnp.arange(n_ctx * per_owner, dtype=jnp.int32)[:, None],
-        axis=1,
-    ).astype(jnp.int32)
-    owner_start = (ordered // per_owner) * per_owner
-    block = jnp.arange(n_ctx * per_owner, dtype=jnp.int32)
-    before = (block >= owner_start[..., None]) & (block < ordered[..., None])
-    rank = jnp.sum(jnp.where(before, named, 0), axis=-1)
-    owner = ordered // per_owner
-    slot = (shard // 2 - owner // 2) * 2 * lists + lax.rem(owner + shard, 2) * lists
-    slot = slot + jnp.minimum(rank, lists - 1)
-    slot = jnp.clip(slot, 0, n_ctx * lists - 1)
-    return slot.reshape(-1).astype(jnp.int32), dead.reshape(-1).astype(jnp.int32)
 
 
 def single_step(kernel, name, scalars, arrays, outs, scratch=()):
@@ -529,6 +576,7 @@
     bf16 = lambda *shape: jax.ShapeDtypeStruct(shape, BF16)
 
     rim_rows = rim_blocks * BROWS
+    where = jnp.stack([group, shard]).astype(jnp.int32)
     prep_out = [bf16(packed_rows + 3 * folds, 128), bf16(rim_rows, 128)]
     prep_out += [bf16(256, tokens)] * 2 + [bf16(tokens, 256)]
     packed, rim, even, odd, val = pl.pallas_call(
@@ -547,15 +595,26 @@
         out_shape=prep_out,
         compiler_params=pltpu.CompilerParams(vmem_limit_bytes=VMEM_LIMIT),
         name="prep",
-    )(group.reshape(1), key_rows, value_rows, comp_key_weight, comp_value_weight)
+    )(where, key_rows, value_rows, comp_key_weight, comp_value_weight)
     other = lax.ppermute(packed, "ctx", [(i, i ^ 1) for i in range(n_ctx)])
-    slots, dead = plan_picks(
-        lax.dynamic_index_in_dim(block_picks, group, 1, keepdims=False), shard, per_owner, n_ctx
-    )
     packed, block_picks = lax.optimization_barrier((packed, block_picks))
-    my_picks = lax.dynamic_index_in_dim(block_picks, group, 1, keepdims=False)
-    picks = [my_picks] + [
-        lax.ppermute(my_picks, "ctx", [(i, i - 2 * d) for i in range(2 * d, n_ctx)])
+    smem = pl.BlockSpec(memory_space=pltpu.SMEM)
+    plan_out = [jax.ShapeDtypeStruct((n_ctx * lists + 1,), jnp.int32)]
+    plan_out += [jax.ShapeDtypeStruct((lists * PICKS + 1,), jnp.int32)] * 2
+    named, slots, dead = pl.pallas_call(
+        functools.partial(plan_kernel, (n_ctx, lists, per_owner)),
+        in_specs=[smem] * 2,
+        out_specs=[smem] * 3,
+        out_shape=plan_out,
+        scratch_shapes=[
+            pltpu.SMEM((n_ctx,), jnp.int32),
+            pltpu.SMEM((n_ctx * per_owner,), jnp.int32),
+            pltpu.SMEM((n_ctx,), jnp.int32),
+        ],
+        name="plan",
+    )(where, block_picks)
+    named = [named] + [
+        lax.ppermute(named, "ctx", [(i, i - 2 * d) for i in range(2 * d, n_ctx)])
         for d in range(1, groups)
     ]
     far_rim = lax.ppermute(rim, "ctx", [(i, i + 1) for i in range(1, n_ctx - 1, 2)])
@@ -563,39 +622,39 @@
     gates = jax.nn.sigmoid(gate_logits).reshape(tokens, 3 * heads)
     gates = jnp.pad(gates, ((0, 0), (0, 128 - 3 * heads)))
     sent = bf16(lists * BROWS + 3 * folds, 128)
-    picks = jnp.stack(picks).reshape(-1)
-
-    def pack(owner, distances, rows):
-        return single_step(
-            functools.partial(pack_kernel, distances, lists, per_owner, n_ctx),
-            "pack",
-            [jnp.stack([owner, shard - lax.rem(shard, 2)]), picks],
-            [rows],
-            [sent] * len(distances),
-        )
+
+    def pack(beside, lists_in, rows):
+        any_space = pl.BlockSpec(memory_space=pl.ANY)
+        return pl.pallas_call(
+            functools.partial(pack_kernel, lists, beside),
+            grid_spec=pltpu.PrefetchScalarGridSpec(
+                num_scalar_prefetch=1 + len(lists_in),
+                grid=(1,),
+                in_specs=[any_space],
+                out_specs=[any_space] * len(lists_in),
+                scratch_shapes=[pltpu.SemaphoreType.DMA((len(lists_in) * (lists + 1),))],
+            ),
+            out_shape=[sent] * len(lists_in),
+            compiler_params=pltpu.CompilerParams(vmem_limit_bytes=VMEM_LIMIT),
+            name="pack",
+        )(where, *lists_in, rows)
 
     def ahead(send, distance):
         return lax.ppermute(send, "ctx", [(i, i + 2 * distance) for i in range(n_ctx - 2 * distance)])
 
-    own_sends = pack(shard, range(1, groups), packed)
+    own_sends = pack(False, named[1:], packed)
     own_sends, even = lax.optimization_barrier((own_sends, even))
     from_same = [ahead(send, d) for d, send in enumerate(own_sends, 1)]
 
     reach = WINDOW // QBLK
-    mixed = near_branch(reach, lists - reach, queries, gates, even, odd, val, None)
+    near = functools.partial(near_branch, where=where, queries=queries, gates=gates)
+    mixed = near(reach, lists - reach, keys=(even, odd, val), rims=None, prior=None)
 
     other, mixed = lax.optimization_barrier((other, mixed))
-    beside, *other_sends = pack(shard + 1 - 2 * lax.rem(shard, 2), range(groups), other)
+    beside, *other_sends = pack(True, named, other)
     from_other = [ahead(send, d) for d, send in enumerate(other_sends, 1)]
 
-    ext = single_step(
-        functools.partial(rim_kernel, packed_rows - rim_rows),
-        "rim",
-        [shard.reshape(1)],
-        [other, far_rim, even, odd, val],
-        [bf16(256, 2 * WINDOW)] * 2 + [bf16(2 * WINDOW, 256)],
-    )
-    mixed = near_branch(0, reach, queries, gates, *ext, mixed)
+    mixed = near(0, reach, keys=(even, odd, val), rims=(other, far_rim), prior=mixed)
 
     received = [beside] + [x for both in zip(from_same, from_other) for x in both]
     pools = single_step(

time: 193 us -> 253 us (1.31)
  Pallas kernels: 151 us -> 211 us
  waiting for transfers between devices: 2.77 us -> 6.09 us
    pallas_call x2 -> x5, Pallas kernels: 44.2 us -> 97.2 us  [the longest x2 50.1 us: near_branch(): pl.pallas_call(functools.partial(near_kernel, heads, rims is not None), g...]
    pallas_call x3, Pallas kernels: 89.9 us -> 106 us  [chosen_and_project(): pl.pallas_call(functools.partial(chosen_kernel, heads, (first_chunk, widt...]
    pallas_call x4 -> x1, Pallas kernels: 13.4 us -> 3.24 us  [single_step(): pl.pallas_call(kernel, grid_spec=pltpu.PrefetchScalarGridSpec(num_scalar_...]
    ppermute x3, waiting for transfers between devices: 0.01 us -> 3.33 us  [local(): lax.ppermute(named, 'ctx', [(i, i - 2 * d) for i in range(2 * d, n_ctx)])]
  transfers between devices with their start and end apart: 15 -> 15, of which waited for: 2 -> 5; matrix products, arithmetic and copies ran while one was open for 4% -> 1% of each run, Pallas kernels for 63% -> 70%
where the time goes in v3:
time: 253 us; the launch traced here: 252 us
  Pallas kernels  211 us (83%)
  starting transfers between devices  25.1 us (10%)
  waiting for transfers between devices  6.09 us (2%)
  other arithmetic  5.18 us (2%)
  local copies, waits for them, and re-layouts  4.12 us (2%)
    pallas_call x3, Pallas kernels, chosen_and_project(): pl.pallas_call(functools.partial(chosen_kernel, heads, (first_chunk, widt...  106 us
    pallas_call x2, Pallas kernels, near_branch(): pl.pallas_call(functools.partial(near_kernel, heads, rims is not None), g...  50.1 us
    pallas_call x2, Pallas kernels, pack(): pl.pallas_call(functools.partial(pack_kernel, lists, beside), grid_spec=p...  43.9 us
    ppermute x6, starting transfers between devices, ahead(): lax.ppermute(send, 'ctx', [(i, i + 2 * distance) for i in range(n_ctx - 2...  12.1 us
  transfers between devices with their start and end apart: 15, of which 5 were waited for; matrix products, arithmetic and copies ran while one was open for 1% of the time, Pallas kernels for 70%

profile of v3, /device:TPU:5, one launch (start us, length us, event | category | flops | bytes accessed | tf_op | source)
XLA Modules:
  0.0 252.0 jit_solution(460645834012814067)
XLA Ops:
  0.0 0.6 pad_add_fusion.group_ref.where_ref
  0.7 4.3 %prep.1 = (bf16[2656,128]{1,0:T(8,128)(2,1)}, bf16[1280,128]{1,0:T(8,128)(2,1)}, bf16[256,1024]{1,0:T(8,128)(2,1)}, bf16[256,1024]{1,0:T(8,128)(2,1)}, bf16[1024,256]{1,0:T(8,128)(2,1)}) custom-call(s32[2]{0:T(128)} %pad_add_fusion.group_ref.where_ref, bf16[1024,768]{1,0:T(8,128)(2,1)} %keys_ref.1, bf16[1024,512]{1,0:T(8,128)(2,1)} %values_ref.1, ...), custom_call_target="tpu_custom_call" | custom-call | tf_op jit(solution)/shard_map/prep/pallas_call | solution.py:582
  4.9 4.4 %collective-permute-start.4 = (bf16[1280,128]{1,0:T(8,128)(2,1)}, bf16[1280,128]{1,0:T(8,128)(2,1)S(1)}, u32[]{:S(2)}, u32[]{:S(2)}) collective-permute-start(bf16[1280,128]{1,0:T(8,128)(2,1)} %get-tuple-element.52), channel_id=1, source_target_pairs={{4,8},{12,16},{20,24},{5,9},{13,17},{21,25},{6,10},{14,18},{22,26}... | collective-permute-start | bytes 983048 | tf_op jit(solution)/shard_map/ppermute | solution.py:620
  9.3 3.2 %plan.1 = (s32[33]{0:T(128)}, s32[65]{0:T(128)}, s32[65]{0:T(128)}) custom-call(s32[2]{0:T(128)} %pad_add_fusion.group_ref.where_ref, s32[4,4,16]{2,1,0:T(4,128)} %picks_ref), custom_call_target="tpu_custom_call" | custom-call | tf_op jit(solution)/shard_map/plan/pallas_call | solution.py:604
  12.5 1.3 collective-permute-start.2
  13.8 1.3 collective-permute-start.1
  15.1 1.3 collective-permute-start
  16.4 2.2 collective-permute-done.2.refs_2_.refs_3_
  19.1 0.7 collective-permute-done.refs_0_.refs_1_
  20.3 19.1 %pack.2 = (bf16[736,128]{1,0:T(8,128)(2,1)}, bf16[736,128]{1,0:T(8,128)(2,1)}, bf16[736,128]{1,0:T(8,128)(2,1)}) custom-call(s32[2]{0:T(128)} %pad_add_fusion.group_ref.where_ref, s32[33]{0:T(128)} %copy-done.11, s32[33]{0:T(128)} %copy-done.10, s32[33]{0:T(128)} %copy-done.9, bf16[2656,128]{1,0:T(8,128)(2,1)} %get-tuple-element.43.refs_3_.own_ref), custom_call_target="tpu_custom_call" | custom-call | tf_op jit(solution)/shard_map/pack/pallas_call | solution.py:628
  39.4 3.9 %collective-permute-start.5 = (bf16[736,128]{1,0:T(8,128)(2,1)}, bf16[736,128]{1,0:T(8,128)(2,1)S(1)}, u32[]{:S(2)}, u32[]{:S(2)}) collective-permute-start(bf16[736,128]{1,0:T(8,128)(2,1)} %get-tuple-element.55), channel_id=1, source_target_pairs={{0,8},{4,12},{8,16},{12,20},{16,24},{20,28},{1,9},{5,13},{9,17},{1... | collective-permute-start | bytes 565256 | tf_op jit(solution)/shard_map/ppermute | solution.py:643
  43.6 0.9 pad.4.gate_ref.refs_4_
  44.4 3.1 %collective-permute-start.7 = (bf16[736,128]{1,0:T(8,128)(2,1)S(1)}, bf16[736,128]{1,0:T(8,128)(2,1)S(1)}, u32[]{:S(2)}, u32[]{:S(2)}) collective-permute-start(bf16[736,128]{1,0:T(8,128)(2,1)S(1)} %copy-done.13), channel_id=1, source_target_pairs={{0,16},{4,20},{8,24},{12,28},{1,17},{5,21},{9,25},{13,29},{2,18},{... | collective-permute-start | bytes 565256 | tf_op jit(solution)/shard_map/ppermute | solution.py:643
  47.5 1.3 collective-permute-start.9
  48.8 28.6 %near_branch.2.refs_5_ = f32[1024,2048]{1,0:T(8,128)} custom-call(s32[2]{0:T(128)} %pad_add_fusion.group_ref.where_ref, bf16[1024,3072]{1,0:T(8,128)(2,1)} %refs_3_.5, f32[1024,128]{1,0:T(8,128)} %pad.4.gate_ref.refs_4_, bf16[256,1024]{1,0:T(8,128)(2,1)} %get-tuple-element.48.refs_0_, bf16[256,1024]{1,0:T(8,128)(2,1)} %get-tuple-element.49.refs_1_, ...), custom_call_target="tpu_custom_call" | custom-call | flops 402653184 | bytes 7340032 | tf_op jit(solution)/shard_map/near_branch/pallas_call | solution.py:386
  77.4 0.9 copy-done
  78.3 24.8 %pack.3 = (bf16[736,128]{1,0:T(8,128)(2,1)}, bf16[736,128]{1,0:T(8,128)(2,1)}, bf16[736,128]{1,0:T(8,128)(2,1)}, bf16[736,128]{1,0:T(8,128)(2,1)}) custom-call(s32[2]{0:T(128)} %pad_add_fusion.group_ref.where_ref, s32[33]{0:T(128)} %get-tuple-element.42.refs_0_, s32[33]{0:T(128)} %copy-done.11, s32[33]{0:T(128)} %copy-done.10, s32[33]{0:T(128)} %copy-done.9, ...), custom_call_target="tpu_custom_call" | custom-call | tf_op jit(solution)/shard_map/pack/pallas_call | solution.py:628
  103.1 1.3 collective-permute-start.6
  104.5 1.3 collective-permute-start.8
  105.8 1.3 collective-permute-start.10
  107.1 0.7 stack.32.refs_0_
  107.8 21.5 %near_branch.3.refs_5_ = f32[1024,2048]{1,0:T(8,128)} custom-call(s32[2]{0:T(128)} %pad_add_fusion.group_ref.where_ref, bf16[1024,3072]{1,0:T(8,128)(2,1)} %refs_3_.5, f32[1024,128]{1,0:T(8,128)} %pad.4.gate_ref.refs_4_, bf16[256,1024]{1,0:T(8,128)(2,1)} %get-tuple-element.48.refs_0_, ...), custom_call_target="tpu_custom_call", output_to_operand_aliasing={{}: (8, {})} | custom-call | flops 402653184 | bytes 7340032 | tf_op jit(solution)/shard_map/near_branch/pallas_call | solution.py:386
  130.3 3.2 %pool.1 = (bf16[2048,256]{1,0:T(8,128)(2,1)}, bf16[2048,256]{1,0:T(8,128)(2,1)}, bf16[256,256]{1,0:T(8,128)(2,1)}, bf16[256,256]{1,0:T(8,128)(2,1)}, bf16[256,256]{1,0:T(8,128)(2,1)}) custom-call(s32[1]{0:T(128)} %bitcast.6.shard_ref, bf16[2656,128]{1,0:T(8,128)(2,1)} %get-tuple-element.43.refs_3_.own_ref, bf16[736,128]{1,0:T(8,128)(2,1)} %get-tuple-element.54.refs_0_, ...), custom_call_target="tpu_custom_call" | custom-call | tf_op jit(solution)/shard_map/pool/pallas_call | solution.py:540
  133.6 27.7 %chosen_and_project.4 = bf16[256,2560]{1,0:T(8,128)(2,1)} custom-call(s32[5]{0:T(128)} %stack.32.refs_0_, s32[65]{0:T(128)} %get-tuple-element.40.refs_1_, s32[65]{0:T(128)} %get-tuple-element.41.refs_2_, bf16[1024,3072]{1,0:T(8,128)(2,1)} %refs_3_.5, f32[1024,128]{1,0:T(8,128)} %pad.4.gate_ref.refs_4_, f32[1024,2048]{1,0:T(8,128)} %near_branch.3.refs_5_, ...), custom_call_target="tpu_custom_call" | custom-call | flops 268435456 | bytes 5242880 | tf_op jit(solution)/shard_map/chosen_and_project/pallas_call | solution.py:504
  161.3 2.9 %collective-permute-start.11 = (bf16[256,2560]{1,0:T(8,128)(2,1)}, bf16[256,2560]{1,0:T(8,128)(2,1)S(1)}, u32[]{:S(2)}, u32[]{:S(2)}) collective-permute-start(bf16[256,2560]{1,0:T(8,128)(2,1)} %chosen_and_project.4), channel_id=1, source_target_pairs={{0,1},{1,0},{2,3},{3,2},{4,5},{5,4},{6,7},{7,6},{8,9},{9,8},{10,11... | collective-permute-start | bytes 3932168 | tf_op jit(solution)/shard_map/ppermute | solution.py:689
  164.2 27.6 %chosen_and_project.3 = bf16[256,2560]{1,0:T(8,128)(2,1)} custom-call(s32[5]{0:T(128)} %stack.32.refs_0_, s32[65]{0:T(128)} %get-tuple-element.40.refs_1_, s32[65]{0:T(128)} %get-tuple-element.41.refs_2_, bf16[1024,3072]{1,0:T(8,128)(2,1)} %refs_3_.5, f32[1024,128]{1,0:T(8,128)} %pad.4.gate_ref.refs_4_, f32[1024,2048]{1,0:T(8,128)} %near_branch.3.refs_5_, ...), custom_call_target="tpu_custom_call" | custom-call | flops 268435456 | bytes 5242880 | tf_op jit(solution)/shard_map/chosen_and_project/pallas_call | solution.py:504
  191.8 1.6 add_convert_fusion.1
  193.4 1.3 collective-permute-start.14
  194.7 51.1 %chosen_and_project.5 = (bf16[256,1280]{1,0:T(8,128)(2,1)}, bf16[256,1280]{1,0:T(8,128)(2,1)}, bf16[256,2560]{1,0:T(8,128)(2,1)}) custom-call(s32[5]{0:T(128)} %stack.32.refs_0_, s32[65]{0:T(128)} %get-tuple-element.40.refs_1_, s32[65]{0:T(128)} %get-tuple-element.41.refs_2_, bf16[1024,3072]{1,0:T(8,128)(2,1)} %refs_3_.5, f32[1024,128]{1,0:T(8,128)} %pad.4.gate_ref.refs_4_, ...), custom_call_target="tpu_custom_call" | custom-call | flops 268435456 | bytes 5242880 | tf_op jit(solution)/shard_map/chosen_and_project/pallas_call | solution.py:504
  246.4 1.8 collective-permute-done.12
  248.2 0.9 collective-permute-done.13
  249.1 2.8 %add_convert_fusion = bf16[256,2560]{1,0:T(8,128)(2,1)} fusion(bf16[256,2560]{1,0:T(8,128)(2,1)S(1)} %collective-permute-done.14, bf16[256,2560]{1,0:T(8,128)(2,1)} %get-tuple-element.67, bf16[256,1280]{1,0:T(8,128)(2,1)S(1)} %collective-permute-done.13, bf16[256,1280]{1,0:T(8,128)(2,1)S(1)} %collective-permute-done.12), kind=kLoop, calls=%fused_computation | loop fusion | flops 5898240 | bytes 5242880 | tf_op jit(solution)/shard_map/convert_element_type | solution.py:702
  (43 shorter events, 2.8 us)
Async XLA Ops:
  0.6 42.6 %copy-start.2 = (f32[1024,3,16]{0,2,1:T(8,128)S(1)}, f32[1024,3,16]{0,2,1:T(8,128)}, u32[]{:S(2)}) copy-start(f32[1024,3,16]{0,2,1:T(8,128)} %param.14) | copy-start | bytes 589828
  4.9 72.5 %collective-permute-start.3 = (bf16[2656,128]{1,0:T(8,128)(2,1)}, bf16[2656,128]{1,0:T(8,128)(2,1)S(1)}, u32[]{:S(2)}, u32[]{:S(2)}) collective-permute-start(bf16[2656,128]{1,0:T(8,128)(2,1)} %get-tuple-element.43.refs_3_.own_ref), channel_id=1, source_target_pairs={{0,4},{4,0},{8,12},{12,8},{16,20},{20,16},{24,28},{28,24},{1,5},{5... | collective-permute-start | bytes 2039816 | tf_op jit(solution)/shard_map/ppermute | solution.py:599
  4.9 100.9 %collective-permute-start.4 = (bf16[1280,128]{1,0:T(8,128)(2,1)}, bf16[1280,128]{1,0:T(8,128)(2,1)S(1)}, u32[]{:S(2)}, u32[]{:S(2)}) collective-permute-start(bf16[1280,128]{1,0:T(8,128)(2,1)} %get-tuple-element.52), channel_id=1, source_target_pairs={{4,8},{12,16},{20,24},{5,9},{13,17},{21,25},{6,10},{14,18},{22,26}... | collective-permute-start | bytes 983048 | tf_op jit(solution)/shard_map/ppermute | solution.py:620
  12.5 6.1 %collective-permute-start.2 = (s32[33]{0:T(128)}, s32[33]{0:T(128)S(1)}, u32[]{:S(2)}, u32[]{:S(2)}) collective-permute-start(s32[33]{0:T(128)} %get-tuple-element.42.refs_0_), channel_id=1, source_target_pairs={{24,0},{28,4},{25,1},{29,5},{26,2},{30,6},{27,3},{31,7}} | collective-permute-start | bytes 404 | tf_op jit(solution)/shard_map/ppermute | solution.py:617
  13.8 5.2 %collective-permute-start.1 = (s32[33]{0:T(128)}, s32[33]{0:T(128)S(1)}, u32[]{:S(2)}, u32[]{:S(2)}) collective-permute-start(s32[33]{0:T(128)} %get-tuple-element.42.refs_0_), channel_id=1, source_target_pairs={{16,0},{20,4},{24,8},{28,12},{17,1},{21,5},{25,9},{29,13},{18,2},{... | collective-permute-start | bytes 404 | tf_op jit(solution)/shard_map/ppermute | solution.py:617
  15.1 4.6 %collective-permute-start = (s32[33]{0:T(128)}, s32[33]{0:T(128)S(1)}, u32[]{:S(2)}, u32[]{:S(2)}) collective-permute-start(s32[33]{0:T(128)} %get-tuple-element.42.refs_0_), channel_id=1, source_target_pairs={{8,0},{12,4},{16,8},{20,12},{24,16},{28,20},{9,1},{13,5},{17,9},{2... | collective-permute-start | bytes 404 | tf_op jit(solution)/shard_map/ppermute | solution.py:617
  18.7 1.1 copy-start.9
  19.1 0.7 copy-start.10
  19.8 0.6 copy-start.11
  39.4 5.0 %copy-start.13 = (bf16[736,128]{1,0:T(8,128)(2,1)S(1)}, bf16[736,128]{1,0:T(8,128)(2,1)}, u32[]{:S(2)}) copy-start(bf16[736,128]{1,0:T(8,128)(2,1)} %get-tuple-element.57) | copy-start | bytes 565252
  39.4 8.1 %copy-start.12 = (bf16[736,128]{1,0:T(8,128)(2,1)S(1)}, bf16[736,128]{1,0:T(8,128)(2,1)}, u32[]{:S(2)}) copy-start(bf16[736,128]{1,0:T(8,128)(2,1)} %get-tuple-element.59) | copy-start | bytes 565252
  39.4 65.0 %collective-permute-start.5 = (bf16[736,128]{1,0:T(8,128)(2,1)}, bf16[736,128]{1,0:T(8,128)(2,1)S(1)}, u32[]{:S(2)}, u32[]{:S(2)}) collective-permute-start(bf16[736,128]{1,0:T(8,128)(2,1)} %get-tuple-element.55), channel_id=1, source_target_pairs={{0,8},{4,12},{8,16},{12,20},{16,24},{20,28},{1,9},{5,13},{9,17},{1... | collective-permute-start | bytes 565256 | tf_op jit(solution)/shard_map/ppermute | solution.py:643
  44.4 84.9 %collective-permute-start.7 = (bf16[736,128]{1,0:T(8,128)(2,1)S(1)}, bf16[736,128]{1,0:T(8,128)(2,1)S(1)}, u32[]{:S(2)}, u32[]{:S(2)}) collective-permute-start(bf16[736,128]{1,0:T(8,128)(2,1)S(1)} %copy-done.13), channel_id=1, source_target_pairs={{0,16},{4,20},{8,24},{12,28},{1,17},{5,21},{9,25},{13,29},{2,18},{... | collective-permute-start | bytes 565256 | tf_op jit(solution)/shard_map/ppermute | solution.py:643
  47.5 81.8 %collective-permute-start.9 = (bf16[736,128]{1,0:T(8,128)(2,1)S(1)}, bf16[736,128]{1,0:T(8,128)(2,1)S(1)}, u32[]{:S(2)}, u32[]{:S(2)}) collective-permute-start(bf16[736,128]{1,0:T(8,128)(2,1)S(1)} %copy-done.12), channel_id=1, source_target_pairs={{0,24},{4,28},{1,25},{5,29},{2,26},{6,30},{3,27},{7,31}} | collective-permute-start | bytes 565256 | tf_op jit(solution)/shard_map/ppermute | solution.py:643
  77.4 0.9 copy-start
  103.1 26.2 %collective-permute-start.6 = (bf16[736,128]{1,0:T(8,128)(2,1)}, bf16[736,128]{1,0:T(8,128)(2,1)S(1)}, u32[]{:S(2)}, u32[]{:S(2)}) collective-permute-start(bf16[736,128]{1,0:T(8,128)(2,1)} %get-tuple-element.56), channel_id=1, source_target_pairs={{0,8},{4,12},{8,16},{12,20},{16,24},{20,28},{1,9},{5,13},{9,17},{1... | collective-permute-start | bytes 565256 | tf_op jit(solution)/shard_map/ppermute | solution.py:643
  104.5 24.9 %copy-start.3 = (bf16[736,128]{1,0:T(8,128)(2,1)}, bf16[736,128]{1,0:T(8,128)(2,1)S(1)}, u32[]{:S(2)}) copy-start(bf16[736,128]{1,0:T(8,128)(2,1)S(1)} %collective-permute-done.5.refs_1_) | copy-start | bytes 565252
  104.5 24.9 %collective-permute-start.8 = (bf16[736,128]{1,0:T(8,128)(2,1)}, bf16[736,128]{1,0:T(8,128)(2,1)S(1)}, u32[]{:S(2)}, u32[]{:S(2)}) collective-permute-start(bf16[736,128]{1,0:T(8,128)(2,1)} %get-tuple-element.58), channel_id=1, source_target_pairs={{0,16},{4,20},{8,24},{12,28},{1,17},{5,21},{9,25},{13,29},{2,18},{... | collective-permute-start | bytes 565256 | tf_op jit(solution)/shard_map/ppermute | solution.py:643
  105.8 2.0 copy-start.1
  105.8 23.6 %collective-permute-start.10 = (bf16[736,128]{1,0:T(8,128)(2,1)}, bf16[736,128]{1,0:T(8,128)(2,1)S(1)}, u32[]{:S(2)}, u32[]{:S(2)}) collective-permute-start(bf16[736,128]{1,0:T(8,128)(2,1)} %get-tuple-element.60), channel_id=1, source_target_pairs={{0,24},{4,28},{1,25},{5,29},{2,26},{6,30},{3,27},{7,31}} | collective-permute-start | bytes 565256 | tf_op jit(solution)/shard_map/ppermute | solution.py:643
  129.3 0.7 copy-start.4
  129.4 0.8 copy-start.5
  129.4 0.8 copy-start.6
  129.4 0.9 copy-start.7
  129.4 0.9 copy-start.8
  161.3 30.4 %collective-permute-start.11 = (bf16[256,2560]{1,0:T(8,128)(2,1)}, bf16[256,2560]{1,0:T(8,128)(2,1)S(1)}, u32[]{:S(2)}, u32[]{:S(2)}) collective-permute-start(bf16[256,2560]{1,0:T(8,128)(2,1)} %chosen_and_project.4), channel_id=1, source_target_pairs={{0,1},{1,0},{2,3},{3,2},{4,5},{5,4},{6,7},{7,6},{8,9},{9,8},{10,11... | collective-permute-start | bytes 3932168 | tf_op jit(solution)/shard_map/ppermute | solution.py:689
  193.4 55.7 %collective-permute-start.14 = (bf16[256,2560]{1,0:T(8,128)(2,1)S(1)}, bf16[256,2560]{1,0:T(8,128)(2,1)S(1)}, u32[]{:S(2)}, u32[]{:S(2)}) collective-permute-start(bf16[256,2560]{1,0:T(8,128)(2,1)S(1)} %add_convert_fusion.1), channel_id=1, source_target_pairs={{0,2},{1,3},{2,0},{3,1},{4,6},{5,7},{6,4},{7,5},{8,10},{9,11},{10,... | collective-permute-start | bytes 3932168 | tf_op jit(solution)/shard_map/ppermute | solution.py:698
  245.8 2.4 collective-permute-start.12
  246.2 3.0 %collective-permute-start.13 = (bf16[256,1280]{1,0:T(8,128)(2,1)}, bf16[256,1280]{1,0:T(8,128)(2,1)S(1)}, u32[]{:S(2)}, u32[]{:S(2)}) collective-permute-start(bf16[256,1280]{1,0:T(8,128)(2,1)} %get-tuple-element.69), channel_id=1, source_target_pairs={{0,1},{1,0},{2,3},{3,2},{4,5},{5,4},{6,7},{7,6},{8,9},{9,8},{10,11... | collective-permute-start | bytes 1966088 | tf_op jit(solution)/shard_map/ppermute | solution.py:695

commit v4 on v3

--- a/solution.py
+++ b/solution.py
@@ -21,7 +21,7 @@
 VMEM_LIMIT = 60 * 1024 * 1024
 NEG = -1e30
 SCALE = QK ** (-0.5) * 1.4426950408889634
-LOW_TOTAL, HIGH_TOTAL = 2.0**-60, 2.0**100
+TOP = 3.0
 NT = (((1,), (1,)), ((), ()))
 F32 = jnp.float32
 BF16 = jnp.bfloat16
@@ -168,23 +168,16 @@
 
 
 def pack_kernel(lists, beside, where_ref, *refs):
-    count = (len(refs) - 2) // 2
-    named, ref, outs, sems = refs[:count], refs[count], refs[count + 1 : -1], refs[-1]
+    count = len(refs) // 2
+    named, ref, outs = refs[:count], refs[count], refs[count + 1 :]
     shard = where_ref[1]
     owner = shard + 1 - 2 * lax.rem(shard, 2) if beside else shard
     data = ref.shape[0] - (outs[0].shape[0] - lists * BROWS)
-    copies = []
     for blocks, out in zip(named, outs):
         for place in range(lists):
             at = pl.multiple_of(blocks[owner * lists + place] * BROWS, 16)
-            to = out.at[place * BROWS : (place + 1) * BROWS]
-            copies.append((ref.at[pl.ds(at, BROWS)], to))
-        copies.append((ref.at[data:], out.at[lists * BROWS :]))
-    copies = [pltpu.make_async_copy(*pair, sems.at[i]) for i, pair in enumerate(copies)]
-    for copy in copies:
-        copy.start()
-    for copy in copies:
-        copy.wait()
+            out[place * BROWS : (place + 1) * BROWS] = ref[pl.ds(at, BROWS)]
+        out[lists * BROWS :] = ref[data:]
 
 
 def unpack(ref, at, count, step=1):
@@ -270,48 +263,24 @@
     return lax.broadcasted_iota(jnp.int32, (rows, cols), axis)
 
 
-def attend(q, keys, values, mask, exact):
-    scores = mask(jnp.dot(q, keys, preferred_element_type=F32)) * SCALE
-    if exact:
-        scores = scores - jnp.maximum(jnp.max(scores, axis=1, keepdims=True), -1e28)
-    weights = jnp.exp2(scores).astype(BF16)
+def attend(q, keys, values, mask):
+    scores = mask(jnp.dot(q, keys, preferred_element_type=F32))
+    top = jnp.maximum(jnp.max(scores, axis=1, keepdims=True), -1e28) * SCALE - TOP
+    weights = jnp.exp2((scores * SCALE - top).astype(BF16))
     out = jnp.dot(weights, values, preferred_element_type=F32)
     return out[:, :DV], out[:, DV:]
 
 
-def in_range(total):
-    good = jnp.where((total >= LOW_TOTAL) & (total <= HIGH_TOTAL), 1.0, 0.0)
-    return jnp.min(good.reshape(-1, 8, DV), axis=0)
-
-
-def over_heads(run, pairs):
-    at_once = 2 if pairs % 2 == 0 else 1
-
-    def quick(turn, worst):
-        return jnp.minimum(worst, run(turn * at_once, at_once, False))
-
-    def exact(turn, _):
-        run(turn, 1, True)
-        return 0
-
-    worst = lax.fori_loop(0, pairs // at_once, quick, jnp.ones((8, DV), F32))
-
-    @pl.when(jnp.min(worst) < 0.5)
-    def _():
-        lax.fori_loop(0, pairs, exact, 0)
-
-
 def stacked(x, times):
     return jnp.concatenate([x] * times, axis=0) if times > 1 else x
 
 
-def stacked_queries(q_ref, first, pairs, side):
-    at = [pl.multiple_of((first + p) * PAIR + side * 128, 128) for p in range(pairs)]
-    return jnp.concatenate([q_ref[:, pl.ds(x, 256)] for x in at], axis=0)
-
-
-def head_columns(first, pair, side):
-    return pl.ds(pl.multiple_of((first + pair) * 2 * DV + side * DV, DV), DV)
+def stacked_queries(q_ref, side):
+    pairs = q_ref.shape[1] // PAIR
+    return jnp.concatenate(
+        [q_ref[:, p * PAIR + side * 128 : p * PAIR + side * 128 + 256] for p in range(pairs)],
+        axis=0,
+    )
 
 
 def gate_columns(gate_ref, first, branch, heads, side, count):
@@ -332,7 +301,7 @@
     if rim:
         out_ref, ext = refs[6], refs[7:]
 
-        @pl.when(pl.program_id(0) == 0)
+        @pl.when((pl.program_id(0) == 0) & (pl.program_id(1) == 0))
         def _():
             fill_rim(where_ref[1], refs[3], refs[4], keys, ext)
 
@@ -341,33 +310,33 @@
         out_ref = refs[3]
     rows = pl.ds(pl.multiple_of(pl.program_id(0) * QBLK, QBLK), WINDOW + QBLK)
 
-    def run(first, pairs, exact):
-        def mask(scores):
-            row, col = iota(QBLK, QBLK, 0), iota(QBLK, QBLK, 1)
-            old = jnp.where(stacked(col >= row, pairs), scores[:, :QBLK], NEG)
-            new = jnp.where(stacked(col <= row, pairs), scores[:, WINDOW:], NEG)
-            return jnp.concatenate([old, scores[:, QBLK:WINDOW], new], axis=1)
-
-        good = []
-        for side in range(2):
-            q = stacked_queries(q_ref, first, pairs, side)
-            num, den = attend(q, keys[side][:, rows], keys[2][rows], mask, exact)
-            good.append(in_range(den))
-            total = gate_columns(gate_ref, 2 * first, 2, heads, side, pairs) * (num / den)
-            for p in range(pairs):
-                out_ref[:, head_columns(first, p, side)] = total[p * QBLK : (p + 1) * QBLK]
-        return jnp.minimum(*good)
-
-    over_heads(run, heads // 2)
+    pairs = q_ref.shape[1] // PAIR
+    first = pl.program_id(1) * 2 * pairs
+
+    def mask(scores):
+        row, col = iota(QBLK, QBLK, 0), iota(QBLK, QBLK, 1)
+        old = jnp.where(stacked(col >= row, pairs), scores[:, :QBLK], NEG)
+        new = jnp.where(stacked(col <= row, pairs), scores[:, WINDOW:], NEG)
+        return jnp.concatenate([old, scores[:, QBLK:WINDOW], new], axis=1)
+
+    for side in range(2):
+        num, den = attend(stacked_queries(q_ref, side), keys[side][:, rows], keys[2][rows], mask)
+        total = gate_columns(gate_ref, first, 2, heads, side, pairs) * (num / den)
+        for p in range(pairs):
+            at = (2 * p + side) * DV
+            out_ref[:, at : at + DV] = total[p * QBLK : (p + 1) * QBLK]
 
 
 def near_branch(first_block, block_count, where, queries, gates, keys, rims, prior):
     tokens, width = queries.shape
     heads = width // QK
-    row_block = lambda i, *_: (i + first_block, 0)
-    whole = lambda x: pl.BlockSpec(x.shape, lambda i, *_: (0,) * x.ndim)
+    row_block = lambda i, p, *_: (i + first_block, p)
+    whole = lambda x: pl.BlockSpec(x.shape, lambda i, p, *_: (0,) * x.ndim)
     operands = [queries, gates, *keys]
-    specs = [pl.BlockSpec((QBLK, width), row_block), pl.BlockSpec((QBLK, 128), row_block)]
+    specs = [
+        pl.BlockSpec((QBLK, 2 * PAIR), row_block),
+        pl.BlockSpec((QBLK, 128), lambda i, p, *_: (i + first_block, 0)),
+    ]
     specs += [whole(x) for x in keys]
     alias, scratch = {}, []
     if rims is not None:
@@ -376,7 +345,7 @@
         last_rim = tokens // KBLK * BROWS // rim_rows - 1
         operands += [other, far, prior]
         specs += [
-            pl.BlockSpec(far.shape, lambda i, *_: (last_rim, 0)),
+            pl.BlockSpec(far.shape, lambda i, p, *_: (last_rim, 0)),
             whole(far),
             pl.BlockSpec(memory_space=pl.ANY),
         ]
@@ -387,9 +356,9 @@
         functools.partial(near_kernel, heads, rims is not None),
         grid_spec=pltpu.PrefetchScalarGridSpec(
             num_scalar_prefetch=1,
-            grid=(block_count,),
+            grid=(block_count, heads // 4),
             in_specs=specs,
-            out_specs=pl.BlockSpec((QBLK, heads * DV), row_block),
+            out_specs=pl.BlockSpec((QBLK, 4 * DV), row_block),
             scratch_shapes=scratch,
         ),
         out_shape=jax.ShapeDtypeStruct((tokens, heads * DV), F32),
@@ -412,104 +381,95 @@
     outs = list(refs[12 : 12 + count])
     gathered, even, odd, val, attended, weight, weight_sem = refs[12 + count :]
     keys = (even, odd)
-    turn = pl.program_id(0)
+    turn, step = pl.program_id(0), pl.program_id(1)
+    last = pl.num_programs(1) - 1
     rows = q_ref.shape[0]
+    pairs = q_ref.shape[1] // PAIR
+    first = step * 2 * pairs
     chunk_start = meta_ref[first_chunk + turn] * rows
     list_at = lax.div(chunk_start, QBLK) * PICKS
     first_row = lax.rem(chunk_start, QBLK)
     position = meta_ref[0] + chunk_start
     copy = pltpu.make_async_copy(weight_ref, weight, weight_sem)
 
-    @pl.when(turn == 0)
+    @pl.when(step == 0)
+    def _():
+        for slot in range(PICKS):
+            source = pl.multiple_of(slots_ref[list_at + slot] * KBLK, KBLK)
+            gathered[slot * KBLK : (slot + 1) * KBLK] = key_pool[pl.ds(source, KBLK)]
+            val[slot * KBLK : (slot + 1) * KBLK] = val_pool[pl.ds(source, KBLK)]
+        for slot in range(1, PICKS):
+
+            @pl.when(dead_ref[list_at + slot] == 1)
+            def _():
+                at = slice(slot * KBLK, (slot + 1) * KBLK)
+                gathered[at] = jnp.broadcast_to(gathered[:1], (KBLK, 256))
+                val[at] = jnp.zeros((KBLK, 256), BF16)
+
+        even[...], odd[...] = turned(gathered[...])
+
+    @pl.when((turn == 0) & (step == 0))
     def _():
         copy.start()
 
-    for slot in range(PICKS):
-        source = pl.multiple_of(slots_ref[list_at + slot] * KBLK, KBLK)
-        gathered[slot * KBLK : (slot + 1) * KBLK] = key_pool[pl.ds(source, KBLK)]
-        val[slot * KBLK : (slot + 1) * KBLK] = val_pool[pl.ds(source, KBLK)]
-
-    def clear(slot, _):
-        @pl.when(dead_ref[list_at + slot] == 1)
-        def _():
-            at = pl.ds(pl.multiple_of(slot * KBLK, KBLK), KBLK)
-            gathered[at] = jnp.broadcast_to(gathered[:1], (KBLK, 256))
-            val[at] = jnp.zeros((KBLK, 256), BF16)
-
-        return 0
-
-    lax.fori_loop(1, PICKS, clear, 0)
-    even[...], odd[...] = turned(gathered[...])
-
-    def run(first, pairs, exact):
-        def own_mask(scores):
-            row, col = iota(rows, 128, 0) + first_row, iota(rows, 128, 1)
-            keep = stacked((col >= KBLK) | (col <= row), pairs)
-            own = jnp.where(keep, scores[:, :128], NEG)
-            return jnp.concatenate([own, scores[:, 128:]], axis=1)
-
-        def comp_mask(scores):
-            cols = scores.shape[1]
-            ends = (iota(rows, cols, 1) + 1) * CBLK - 1
-            keep = stacked(ends <= position + iota(rows, cols, 0), pairs)
-            return jnp.where(keep, scores, NEG)
-
-        good = []
-        empty = stacked(position + iota(rows, DV, 0) < CBLK - 1, pairs)
-        for side in range(2):
-            q = stacked_queries(q_ref, first, pairs, side)
-            num, den = attend(q, keys[side][...], val[...], own_mask, exact)
-            good.append(in_range(den))
-            total = gate_columns(gate_ref, 2 * first, 1, heads, side, pairs) * (num / den)
-            num, den = attend(q, cfold[side][...], cfold[2][...], comp_mask, exact)
-            den = jnp.where(empty, 1.0, den)
-            good.append(in_range(den))
-            total = total + gate_columns(gate_ref, 2 * first, 0, heads, side, pairs) * (num / den)
-            for p in range(pairs):
-                cols = head_columns(first, p, side)
-                mixed = near_ref[:, cols] + total[p * rows : (p + 1) * rows]
-                attended[:, cols] = mixed.astype(BF16)
-        return functools.reduce(jnp.minimum, good)
-
-    over_heads(run, heads // 2)
-
-    @pl.when(turn == 0)
+    def own_mask(scores):
+        row, col = iota(rows, 128, 0) + first_row, iota(rows, 128, 1)
+        keep = stacked((col >= KBLK) | (col <= row), pairs)
+        own = jnp.where(keep, scores[:, :128], NEG)
+        return jnp.concatenate([own, scores[:, 128:]], axis=1)
+
+    def comp_mask(scores):
+        cols = scores.shape[1]
+        ends = (iota(rows, cols, 1) + 1) * CBLK - 1
+        return jnp.where(stacked(ends <= position + iota(rows, cols, 0), pairs), scores, NEG)
+
+    empty = stacked(position + iota(rows, DV, 0) < CBLK - 1, pairs)
+    for side in range(2):
+        q = stacked_queries(q_ref, side)
+        num, den = attend(q, keys[side][...], val[...], own_mask)
+        total = gate_columns(gate_ref, first, 1, heads, side, pairs) * (num / den)
+        num, den = attend(q, cfold[side][...], cfold[2][...], comp_mask)
+        den = jnp.where(empty, 1.0, den)
+        total = total + gate_columns(gate_ref, first, 0, heads, side, pairs) * (num / den)
+        for p in range(pairs):
+            at = (2 * p + side) * DV
+            mixed = near_ref[:, at : at + DV] + total[p * rows : (p + 1) * rows]
+            attended[step, :, at : at + DV] = mixed.astype(BF16)
+
+    @pl.when((turn == 0) & (step == last))
     def _():
         copy.wait()
 
     for place, parts in enumerate(widths):
         chunk_outs = [outs.pop(0) for _ in parts]
 
-        @pl.when(turn == place)
+        @pl.when((turn == place) & (step == last))
         def _():
+            rows_in = jnp.concatenate([attended[s] for s in range(heads // 4)], axis=1)
             first_col = 0
             for out_ref in chunk_outs:
-
-                def columns(tile, _, out_ref=out_ref, first_col=first_col):
-                    at = pl.multiple_of(tile * 256, 256)
-                    cols = weight[:, pl.ds(first_col + at, 256)]
-                    part = jnp.dot(attended[...], cols, preferred_element_type=F32)
-                    out_ref[:, pl.ds(at, 256)] = part.astype(out_ref.dtype)
-                    return 0
-
-                lax.fori_loop(0, out_ref.shape[1] // 256, columns, 0)
+                for at in range(0, out_ref.shape[1], 256):
+                    cols = weight[:, first_col + at : first_col + at + 256]
+                    part = jnp.dot(rows_in, cols, preferred_element_type=F32)
+                    out_ref[:, at : at + 256] = part.astype(out_ref.dtype)
                 first_col += out_ref.shape[1]
 
 
 def chosen_and_project(first_chunk, widths, rows, meta, slots, dead, queries, gates, near, pools, out_weight):
     tokens, width = queries.shape
     heads = width // QK
-    whole = lambda x: pl.BlockSpec(x.shape, lambda i, *_: (0,) * x.ndim)
+    steps = heads // 4
+    whole = lambda x: pl.BlockSpec(x.shape, lambda i, p, *_: (0,) * x.ndim)
     outs = [jax.ShapeDtypeStruct((rows, width), BF16) for chunk in widths for width in chunk]
     return pl.pallas_call(
         functools.partial(chosen_kernel, heads, (first_chunk, widths)),
         grid_spec=pltpu.PrefetchScalarGridSpec(
             num_scalar_prefetch=3,
-            grid=(len(widths),),
+            grid=(len(widths), steps),
             in_specs=[
-                pl.BlockSpec((rows, width), lambda i, m, *_: (m[first_chunk + i], 0)),
-                pl.BlockSpec((rows, 128), lambda i, m, *_: (m[first_chunk + i], 0)),
-                pl.BlockSpec((rows, heads * DV), lambda i, m, *_: (m[first_chunk + i], 0)),
+                pl.BlockSpec((rows, 2 * PAIR), lambda i, p, m, *_: (m[first_chunk + i], p)),
+                pl.BlockSpec((rows, 128), lambda i, p, m, *_: (m[first_chunk + i], 0)),
+                pl.BlockSpec((rows, 4 * DV), lambda i, p, m, *_: (m[first_chunk + i], p)),
             ]
             + [whole(x) for x in pools]
             + [pl.BlockSpec(memory_space=pl.ANY)],
@@ -519,7 +479,7 @@
                 pltpu.VMEM((256, PICKS * KBLK), BF16),
                 pltpu.VMEM((256, PICKS * KBLK), BF16),
                 pltpu.VMEM((PICKS * KBLK, 256), BF16),
-                pltpu.VMEM((rows, heads * DV), BF16),
+                pltpu.VMEM((steps, rows, 4 * DV), BF16),
                 pltpu.VMEM(out_weight.shape, BF16),
                 pltpu.SemaphoreType.DMA,
             ],
@@ -624,20 +584,13 @@
     sent = bf16(lists * BROWS + 3 * folds, 128)
 
     def pack(beside, lists_in, rows):
-        any_space = pl.BlockSpec(memory_space=pl.ANY)
-        return pl.pallas_call(
+        return single_step(
             functools.partial(pack_kernel, lists, beside),
-            grid_spec=pltpu.PrefetchScalarGridSpec(
-                num_scalar_prefetch=1 + len(lists_in),
-                grid=(1,),
-                in_specs=[any_space],
-                out_specs=[any_space] * len(lists_in),
-                scratch_shapes=[pltpu.SemaphoreType.DMA((len(lists_in) * (lists + 1),))],
-            ),
-            out_shape=[sent] * len(lists_in),
-            compiler_params=pltpu.CompilerParams(vmem_limit_bytes=VMEM_LIMIT),
-            name="pack",
-        )(where, *lists_in, rows)
+            "pack",
+            [where, *lists_in],
+            [rows],
+            [sent] * len(lists_in),
+        )
 
     def ahead(send, distance):
         return lax.ppermute(send, "ctx", [(i, i + 2 * distance) for i in range(n_ctx - 2 * distance)])

time: 253 us -> 159 us (0.63)
  Pallas kernels: 211 us -> 117 us
    pallas_call x2 -> x0, Pallas kernels: 43.9 us -> none  [pack(): pl.pallas_call(functools.partial(pack_kernel, lists, beside), grid_spec=p...]
    pallas_call x3, Pallas kernels: 106 us -> 67.4 us  [chosen_and_project(): pl.pallas_call(functools.partial(chosen_kernel, heads, (first_chunk, widt...]
    pallas_call x2, Pallas kernels: 50.1 us -> 33.7 us  [near_branch(): pl.pallas_call(functools.partial(near_kernel, heads, rims is not None), g...]
    pallas_call x1 -> x3, Pallas kernels: 3.24 us -> 8.79 us  [single_step(): pl.pallas_call(kernel, grid_spec=pltpu.PrefetchScalarGridSpec(num_scalar_...]
  transfers between devices with their start and end apart: 15 -> 15, of which waited for: 5 -> 5; matrix products, arithmetic and copies ran while one was open for 1% -> 1% of each run, Pallas kernels for 70% -> 58%
where the time goes in v4:
time: 159 us; the launch traced here: 158 us
  Pallas kernels  117 us (74%)
  starting transfers between devices  25.1 us (16%)
  waiting for transfers between devices  6.09 us (4%)
  other arithmetic  5.18 us (3%)
  local copies, waits for them, and re-layouts  4.12 us (3%)
    pallas_call x3, Pallas kernels, chosen_and_project(): pl.pallas_call(functools.partial(chosen_kernel, heads, (first_chunk, widt...  67.4 us
    pallas_call x2, Pallas kernels, near_branch(): pl.pallas_call(functools.partial(near_kernel, heads, rims is not None), g...  33.7 us
    ppermute x6, starting transfers between devices, ahead(): lax.ppermute(send, 'ctx', [(i, i + 2 * distance) for i in range(n_ctx - 2...  12.1 us
    pallas_call x3, Pallas kernels, single_step(): pl.pallas_call(kernel, grid_spec=pltpu.PrefetchScalarGridSpec(num_scalar_...  8.79 us
    ppermute x1, starting transfers between devices, local(): lax.ppermute(rim, 'ctx', [(i, i + 1) for i in range(1, n_ctx - 1, 2)])  4.39 us
    pallas_call x1, Pallas kernels, local(): pl.pallas_call(prep_kernel, grid_spec=pltpu.PrefetchScalarGridSpec(num_sc...  4.25 us
    ppermute x3, starting transfers between devices, local(): lax.ppermute(named, 'ctx', [(i, i - 2 * d) for i in range(2 * d, n_ctx)])  3.88 us
    ppermute x3, waiting for transfers between devices, local(): lax.ppermute(named, 'ctx', [(i, i - 2 * d) for i in range(2 * d, n_ctx)])  3.33 us
  transfers between devices with their start and end apart: 15, of which 5 were waited for; matrix products, arithmetic and copies ran while one was open for 1% of the time, Pallas kernels for 58%

profile of v4, /device:TPU:5, one launch (start us, length us, event | category | flops | bytes accessed | tf_op | source)
XLA Modules:
  0.0 158.2 jit_solution(5742031571931647607)
XLA Ops:
  0.0 0.6 pad_add_fusion.group_ref.where_ref
  0.7 4.3 %prep.1 = (bf16[2656,128]{1,0:T(8,128)(2,1)}, bf16[1280,128]{1,0:T(8,128)(2,1)}, bf16[256,1024]{1,0:T(8,128)(2,1)}, bf16[256,1024]{1,0:T(8,128)(2,1)}, bf16[1024,256]{1,0:T(8,128)(2,1)}) custom-call(s32[2]{0:T(128)} %pad_add_fusion.group_ref.where_ref, bf16[1024,768]{1,0:T(8,128)(2,1)} %keys_ref.1, bf16[1024,512]{1,0:T(8,128)(2,1)} %values_ref.1, ...), custom_call_target="tpu_custom_call" | custom-call | tf_op jit(solution)/shard_map/prep/pallas_call | solution.py:542
  4.9 4.4 %collective-permute-start.4 = (bf16[1280,128]{1,0:T(8,128)(2,1)}, bf16[1280,128]{1,0:T(8,128)(2,1)S(1)}, u32[]{:S(2)}, u32[]{:S(2)}) collective-permute-start(bf16[1280,128]{1,0:T(8,128)(2,1)} %get-tuple-element.52), channel_id=1, source_target_pairs={{4,8},{12,16},{20,24},{5,9},{13,17},{21,25},{6,10},{14,18},{22,26}... | collective-permute-start | bytes 983048 | tf_op jit(solution)/shard_map/ppermute | solution.py:580
  9.3 3.2 %plan.1 = (s32[33]{0:T(128)}, s32[65]{0:T(128)}, s32[65]{0:T(128)}) custom-call(s32[2]{0:T(128)} %pad_add_fusion.group_ref.where_ref, s32[4,4,16]{2,1,0:T(4,128)} %picks_ref), custom_call_target="tpu_custom_call" | custom-call | tf_op jit(solution)/shard_map/plan/pallas_call | solution.py:564
  12.5 1.3 collective-permute-start.2
  13.8 1.3 collective-permute-start.1
  15.1 1.3 collective-permute-start
  16.4 2.2 %collective-permute-done.2.refs_2_.refs_3_ = s32[33]{0:T(128)S(1)} collective-permute-done((s32[33]{0:T(128)}, s32[33]{0:T(128)S(1)}, u32[]{:S(2)}, u32[]{:S(2)}) %collective-permute-start.2) | collective-permute-done | bytes 164 | tf_op jit(solution)/shard_map/ppermute | solution.py:577
  19.1 0.7 collective-permute-done.refs_0_.refs_1_
  20.3 2.6 %pack.2 = (bf16[736,128]{1,0:T(8,128)(2,1)}, bf16[736,128]{1,0:T(8,128)(2,1)}, bf16[736,128]{1,0:T(8,128)(2,1)}) custom-call(s32[2]{0:T(128)} %pad_add_fusion.group_ref.where_ref, s32[33]{0:T(128)} %copy-done.11, s32[33]{0:T(128)} %copy-done.10, s32[33]{0:T(128)} %copy-done.9, bf16[2656,128]{1,0:T(8,128)(2,1)} %get-tuple-element.43.refs_3_.own_ref), custom_call_target="tpu_custom_call" | custom-call | tf_op jit(solution)/shard_map/pack/pallas_call | solution.py:500
  23.0 3.8 %collective-permute-start.5 = (bf16[736,128]{1,0:T(8,128)(2,1)}, bf16[736,128]{1,0:T(8,128)(2,1)S(1)}, u32[]{:S(2)}, u32[]{:S(2)}) collective-permute-start(bf16[736,128]{1,0:T(8,128)(2,1)} %get-tuple-element.55), channel_id=1, source_target_pairs={{0,8},{4,12},{8,16},{12,20},{16,24},{20,28},{1,9},{5,13},{9,17},{1... | collective-permute-start | bytes 565256 | tf_op jit(solution)/shard_map/ppermute | solution.py:596
  27.1 0.9 pad.4.gate_ref.refs_4_
  28.0 3.1 %collective-permute-start.7 = (bf16[736,128]{1,0:T(8,128)(2,1)S(1)}, bf16[736,128]{1,0:T(8,128)(2,1)S(1)}, u32[]{:S(2)}, u32[]{:S(2)}) collective-permute-start(bf16[736,128]{1,0:T(8,128)(2,1)S(1)} %copy-done.13), channel_id=1, source_target_pairs={{0,16},{4,20},{8,24},{12,28},{1,17},{5,21},{9,25},{13,29},{2,18},{... | collective-permute-start | bytes 565256 | tf_op jit(solution)/shard_map/ppermute | solution.py:596
  31.1 1.3 collective-permute-start.9
  32.4 16.5 %near_branch.2.refs_5_ = f32[1024,2048]{1,0:T(8,128)} custom-call(s32[2]{0:T(128)} %pad_add_fusion.group_ref.where_ref, bf16[1024,3072]{1,0:T(8,128)(2,1)} %refs_3_.5, f32[1024,128]{1,0:T(8,128)} %pad.4.gate_ref.refs_4_, bf16[256,1024]{1,0:T(8,128)(2,1)} %get-tuple-element.48.refs_0_, bf16[256,1024]{1,0:T(8,128)(2,1)} %get-tuple-element.49.refs_1_, ...), custom_call_target="tpu_custom_call" | custom-call | flops 402653184 | bytes 7340032 | tf_op jit(solution)/shard_map/near_branch/pallas_call | solution.py:355
  48.9 0.9 copy-done
  49.8 2.7 %pack.3 = (bf16[736,128]{1,0:T(8,128)(2,1)}, bf16[736,128]{1,0:T(8,128)(2,1)}, bf16[736,128]{1,0:T(8,128)(2,1)}, bf16[736,128]{1,0:T(8,128)(2,1)}) custom-call(s32[2]{0:T(128)} %pad_add_fusion.group_ref.where_ref, s32[33]{0:T(128)} %get-tuple-element.42.refs_0_, s32[33]{0:T(128)} %copy-done.11, s32[33]{0:T(128)} %copy-done.10, s32[33]{0:T(128)} %copy-done.9, ...), custom_call_target="tpu_custom_call" | custom-call | tf_op jit(solution)/shard_map/pack/pallas_call | solution.py:500
  52.5 1.3 collective-permute-start.6
  53.8 1.3 collective-permute-start.8
  55.1 1.3 collective-permute-start.10
  56.5 0.7 stack.32.refs_0_
  57.2 17.2 %near_branch.3.refs_5_ = f32[1024,2048]{1,0:T(8,128)} custom-call(s32[2]{0:T(128)} %pad_add_fusion.group_ref.where_ref, bf16[1024,3072]{1,0:T(8,128)(2,1)} %refs_3_.5, f32[1024,128]{1,0:T(8,128)} %pad.4.gate_ref.refs_4_, bf16[256,1024]{1,0:T(8,128)(2,1)} %get-tuple-element.48.refs_0_, ...), custom_call_target="tpu_custom_call", output_to_operand_aliasing={{}: (8, {})} | custom-call | flops 402653184 | bytes 7340032 | tf_op jit(solution)/shard_map/near_branch/pallas_call | solution.py:355
  75.4 3.4 %pool.1 = (bf16[2048,256]{1,0:T(8,128)(2,1)}, bf16[2048,256]{1,0:T(8,128)(2,1)}, bf16[256,256]{1,0:T(8,128)(2,1)}, bf16[256,256]{1,0:T(8,128)(2,1)}, bf16[256,256]{1,0:T(8,128)(2,1)}) custom-call(s32[1]{0:T(128)} %bitcast.6.shard_ref, bf16[2656,128]{1,0:T(8,128)(2,1)} %get-tuple-element.43.refs_3_.own_ref, bf16[736,128]{1,0:T(8,128)(2,1)} %get-tuple-element.54.refs_0_, ...), custom_call_target="tpu_custom_call" | custom-call | tf_op jit(solution)/shard_map/pool/pallas_call | solution.py:500
  78.8 17.9 %chosen_and_project.4 = bf16[256,2560]{1,0:T(8,128)(2,1)} custom-call(s32[5]{0:T(128)} %stack.32.refs_0_, s32[65]{0:T(128)} %get-tuple-element.40.refs_1_, s32[65]{0:T(128)} %get-tuple-element.41.refs_2_, bf16[1024,3072]{1,0:T(8,128)(2,1)} %refs_3_.5, f32[1024,128]{1,0:T(8,128)} %pad.4.gate_ref.refs_4_, f32[1024,2048]{1,0:T(8,128)} %near_branch.3.refs_5_, ...), custom_call_target="tpu_custom_call" | custom-call | flops 268435456 | bytes 5242880 | tf_op jit(solution)/shard_map/chosen_and_project/pallas_call | solution.py:464
  96.7 2.9 %collective-permute-start.11 = (bf16[256,2560]{1,0:T(8,128)(2,1)}, bf16[256,2560]{1,0:T(8,128)(2,1)S(1)}, u32[]{:S(2)}, u32[]{:S(2)}) collective-permute-start(bf16[256,2560]{1,0:T(8,128)(2,1)} %chosen_and_project.4), channel_id=1, source_target_pairs={{0,1},{1,0},{2,3},{3,2},{4,5},{5,4},{6,7},{7,6},{8,9},{9,8},{10,11... | collective-permute-start | bytes 3932168 | tf_op jit(solution)/shard_map/ppermute | solution.py:642
  99.5 17.9 %chosen_and_project.3 = bf16[256,2560]{1,0:T(8,128)(2,1)} custom-call(s32[5]{0:T(128)} %stack.32.refs_0_, s32[65]{0:T(128)} %get-tuple-element.40.refs_1_, s32[65]{0:T(128)} %get-tuple-element.41.refs_2_, bf16[1024,3072]{1,0:T(8,128)(2,1)} %refs_3_.5, f32[1024,128]{1,0:T(8,128)} %pad.4.gate_ref.refs_4_, f32[1024,2048]{1,0:T(8,128)} %near_branch.3.refs_5_, ...), custom_call_target="tpu_custom_call" | custom-call | flops 268435456 | bytes 5242880 | tf_op jit(solution)/shard_map/chosen_and_project/pallas_call | solution.py:464
  117.5 1.6 %add_convert_fusion.1 = bf16[256,2560]{1,0:T(8,128)(2,1)S(1)} fusion(bf16[256,2560]{1,0:T(8,128)(2,1)S(1)} %collective-permute-done.11, bf16[256,2560]{1,0:T(8,128)(2,1)} %chosen_and_project.3), kind=kLoop, calls=%fused_computation.1 | loop fusion | flops 2621440 | bytes 3932160 | tf_op jit(solution)/shard_map/convert_element_type | solution.py:644
  119.1 1.3 collective-permute-start.14
  120.4 31.7 %chosen_and_project.5 = (bf16[256,1280]{1,0:T(8,128)(2,1)}, bf16[256,1280]{1,0:T(8,128)(2,1)}, bf16[256,2560]{1,0:T(8,128)(2,1)}) custom-call(s32[5]{0:T(128)} %stack.32.refs_0_, s32[65]{0:T(128)} %get-tuple-element.40.refs_1_, s32[65]{0:T(128)} %get-tuple-element.41.refs_2_, bf16[1024,3072]{1,0:T(8,128)(2,1)} %refs_3_.5, f32[1024,128]{1,0:T(8,128)} %pad.4.gate_ref.refs_4_, ...), custom_call_target="tpu_custom_call" | custom-call | flops 268435456 | bytes 5242880 | tf_op jit(solution)/shard_map/chosen_and_project/pallas_call | solution.py:464
  152.6 1.8 %collective-permute-done.12 = bf16[256,1280]{1,0:T(8,128)(2,1)S(1)} collective-permute-done((bf16[256,1280]{1,0:T(8,128)(2,1)}, bf16[256,1280]{1,0:T(8,128)(2,1)S(1)}, u32[]{:S(2)}, u32[]{:S(2)}) %collective-permute-start.12) | collective-permute-done | bytes 655392 | tf_op jit(solution)/shard_map/ppermute | solution.py:648
  154.4 0.9 collective-permute-done.13
  155.4 2.8 %add_convert_fusion = bf16[256,2560]{1,0:T(8,128)(2,1)} fusion(bf16[256,2560]{1,0:T(8,128)(2,1)S(1)} %collective-permute-done.14, bf16[256,2560]{1,0:T(8,128)(2,1)} %get-tuple-element.67, bf16[256,1280]{1,0:T(8,128)(2,1)S(1)} %collective-permute-done.13, bf16[256,1280]{1,0:T(8,128)(2,1)S(1)} %collective-permute-done.12), kind=kLoop, calls=%fused_computation | loop fusion | flops 5898240 | bytes 5242880 | tf_op jit(solution)/shard_map/convert_element_type | solution.py:655
  (43 shorter events, 2.8 us)
Async XLA Ops:
  0.6 26.2 %copy-start.2 = (f32[1024,3,16]{0,2,1:T(8,128)S(1)}, f32[1024,3,16]{0,2,1:T(8,128)}, u32[]{:S(2)}) copy-start(f32[1024,3,16]{0,2,1:T(8,128)} %param.14) | copy-start | bytes 589828
  4.9 44.0 %collective-permute-start.3 = (bf16[2656,128]{1,0:T(8,128)(2,1)}, bf16[2656,128]{1,0:T(8,128)(2,1)S(1)}, u32[]{:S(2)}, u32[]{:S(2)}) collective-permute-start(bf16[2656,128]{1,0:T(8,128)(2,1)} %get-tuple-element.43.refs_3_.own_ref), channel_id=1, source_target_pairs={{0,4},{4,0},{8,12},{12,8},{16,20},{20,16},{24,28},{28,24},{1,5},{5... | collective-permute-start | bytes 2039816 | tf_op jit(solution)/shard_map/ppermute | solution.py:559
  4.9 50.2 %collective-permute-start.4 = (bf16[1280,128]{1,0:T(8,128)(2,1)}, bf16[1280,128]{1,0:T(8,128)(2,1)S(1)}, u32[]{:S(2)}, u32[]{:S(2)}) collective-permute-start(bf16[1280,128]{1,0:T(8,128)(2,1)} %get-tuple-element.52), channel_id=1, source_target_pairs={{4,8},{12,16},{20,24},{5,9},{13,17},{21,25},{6,10},{14,18},{22,26}... | collective-permute-start | bytes 983048 | tf_op jit(solution)/shard_map/ppermute | solution.py:580
  12.5 6.1 %collective-permute-start.2 = (s32[33]{0:T(128)}, s32[33]{0:T(128)S(1)}, u32[]{:S(2)}, u32[]{:S(2)}) collective-permute-start(s32[33]{0:T(128)} %get-tuple-element.42.refs_0_), channel_id=1, source_target_pairs={{24,0},{28,4},{25,1},{29,5},{26,2},{30,6},{27,3},{31,7}} | collective-permute-start | bytes 404 | tf_op jit(solution)/shard_map/ppermute | solution.py:577
  13.8 5.2 %collective-permute-start.1 = (s32[33]{0:T(128)}, s32[33]{0:T(128)S(1)}, u32[]{:S(2)}, u32[]{:S(2)}) collective-permute-start(s32[33]{0:T(128)} %get-tuple-element.42.refs_0_), channel_id=1, source_target_pairs={{16,0},{20,4},{24,8},{28,12},{17,1},{21,5},{25,9},{29,13},{18,2},{... | collective-permute-start | bytes 404 | tf_op jit(solution)/shard_map/ppermute | solution.py:577
  15.1 4.6 %collective-permute-start = (s32[33]{0:T(128)}, s32[33]{0:T(128)S(1)}, u32[]{:S(2)}, u32[]{:S(2)}) collective-permute-start(s32[33]{0:T(128)} %get-tuple-element.42.refs_0_), channel_id=1, source_target_pairs={{8,0},{12,4},{16,8},{20,12},{24,16},{28,20},{9,1},{13,5},{17,9},{2... | collective-permute-start | bytes 404 | tf_op jit(solution)/shard_map/ppermute | solution.py:577
  18.7 1.1 copy-start.9
  19.1 0.7 copy-start.10
  19.8 0.6 copy-start.11
  23.0 5.0 %copy-start.13 = (bf16[736,128]{1,0:T(8,128)(2,1)S(1)}, bf16[736,128]{1,0:T(8,128)(2,1)}, u32[]{:S(2)}) copy-start(bf16[736,128]{1,0:T(8,128)(2,1)} %get-tuple-element.57) | copy-start | bytes 565252
  23.0 8.1 %copy-start.12 = (bf16[736,128]{1,0:T(8,128)(2,1)S(1)}, bf16[736,128]{1,0:T(8,128)(2,1)}, u32[]{:S(2)}) copy-start(bf16[736,128]{1,0:T(8,128)(2,1)} %get-tuple-element.59) | copy-start | bytes 565252
  23.0 30.8 %collective-permute-start.5 = (bf16[736,128]{1,0:T(8,128)(2,1)}, bf16[736,128]{1,0:T(8,128)(2,1)S(1)}, u32[]{:S(2)}, u32[]{:S(2)}) collective-permute-start(bf16[736,128]{1,0:T(8,128)(2,1)} %get-tuple-element.55), channel_id=1, source_target_pairs={{0,8},{4,12},{8,16},{12,20},{16,24},{20,28},{1,9},{5,13},{9,17},{1... | collective-permute-start | bytes 565256 | tf_op jit(solution)/shard_map/ppermute | solution.py:596
  28.0 46.4 %collective-permute-start.7 = (bf16[736,128]{1,0:T(8,128)(2,1)S(1)}, bf16[736,128]{1,0:T(8,128)(2,1)S(1)}, u32[]{:S(2)}, u32[]{:S(2)}) collective-permute-start(bf16[736,128]{1,0:T(8,128)(2,1)S(1)} %copy-done.13), channel_id=1, source_target_pairs={{0,16},{4,20},{8,24},{12,28},{1,17},{5,21},{9,25},{13,29},{2,18},{... | collective-permute-start | bytes 565256 | tf_op jit(solution)/shard_map/ppermute | solution.py:596
  31.1 43.3 %collective-permute-start.9 = (bf16[736,128]{1,0:T(8,128)(2,1)S(1)}, bf16[736,128]{1,0:T(8,128)(2,1)S(1)}, u32[]{:S(2)}, u32[]{:S(2)}) collective-permute-start(bf16[736,128]{1,0:T(8,128)(2,1)S(1)} %copy-done.12), channel_id=1, source_target_pairs={{0,24},{4,28},{1,25},{5,29},{2,26},{6,30},{3,27},{7,31}} | collective-permute-start | bytes 565256 | tf_op jit(solution)/shard_map/ppermute | solution.py:596
  48.9 0.9 copy-start
  52.5 21.9 %collective-permute-start.6 = (bf16[736,128]{1,0:T(8,128)(2,1)}, bf16[736,128]{1,0:T(8,128)(2,1)S(1)}, u32[]{:S(2)}, u32[]{:S(2)}) collective-permute-start(bf16[736,128]{1,0:T(8,128)(2,1)} %get-tuple-element.56), channel_id=1, source_target_pairs={{0,8},{4,12},{8,16},{12,20},{16,24},{20,28},{1,9},{5,13},{9,17},{1... | collective-permute-start | bytes 565256 | tf_op jit(solution)/shard_map/ppermute | solution.py:596
  53.8 20.6 %copy-start.3 = (bf16[736,128]{1,0:T(8,128)(2,1)}, bf16[736,128]{1,0:T(8,128)(2,1)S(1)}, u32[]{:S(2)}) copy-start(bf16[736,128]{1,0:T(8,128)(2,1)S(1)} %collective-permute-done.5.refs_1_) | copy-start | bytes 565252
  53.8 20.6 %collective-permute-start.8 = (bf16[736,128]{1,0:T(8,128)(2,1)}, bf16[736,128]{1,0:T(8,128)(2,1)S(1)}, u32[]{:S(2)}, u32[]{:S(2)}) collective-permute-start(bf16[736,128]{1,0:T(8,128)(2,1)} %get-tuple-element.58), channel_id=1, source_target_pairs={{0,16},{4,20},{8,24},{12,28},{1,17},{5,21},{9,25},{13,29},{2,18},{... | collective-permute-start | bytes 565256 | tf_op jit(solution)/shard_map/ppermute | solution.py:596
  55.1 2.0 %copy-start.1 = (bf16[1280,128]{1,0:T(8,128)(2,1)}, bf16[1280,128]{1,0:T(8,128)(2,1)S(1)}, u32[]{:S(2)}) copy-start(bf16[1280,128]{1,0:T(8,128)(2,1)S(1)} %collective-permute-done.4.refs_4_) | copy-start | bytes 983044
  55.1 19.3 %collective-permute-start.10 = (bf16[736,128]{1,0:T(8,128)(2,1)}, bf16[736,128]{1,0:T(8,128)(2,1)S(1)}, u32[]{:S(2)}, u32[]{:S(2)}) collective-permute-start(bf16[736,128]{1,0:T(8,128)(2,1)} %get-tuple-element.60), channel_id=1, source_target_pairs={{0,24},{4,28},{1,25},{5,29},{2,26},{6,30},{3,27},{7,31}} | collective-permute-start | bytes 565256 | tf_op jit(solution)/shard_map/ppermute | solution.py:596
  74.4 0.7 copy-start.4
  74.4 0.8 copy-start.5
  74.4 0.8 copy-start.6
  74.5 0.9 copy-start.7
  74.5 0.9 copy-start.8
  96.7 20.8 %collective-permute-start.11 = (bf16[256,2560]{1,0:T(8,128)(2,1)}, bf16[256,2560]{1,0:T(8,128)(2,1)S(1)}, u32[]{:S(2)}, u32[]{:S(2)}) collective-permute-start(bf16[256,2560]{1,0:T(8,128)(2,1)} %chosen_and_project.4), channel_id=1, source_target_pairs={{0,1},{1,0},{2,3},{3,2},{4,5},{5,4},{6,7},{7,6},{8,9},{9,8},{10,11... | collective-permute-start | bytes 3932168 | tf_op jit(solution)/shard_map/ppermute | solution.py:642
  119.1 36.3 %collective-permute-start.14 = (bf16[256,2560]{1,0:T(8,128)(2,1)S(1)}, bf16[256,2560]{1,0:T(8,128)(2,1)S(1)}, u32[]{:S(2)}, u32[]{:S(2)}) collective-permute-start(bf16[256,2560]{1,0:T(8,128)(2,1)S(1)} %add_convert_fusion.1), channel_id=1, source_target_pairs={{0,2},{1,3},{2,0},{3,1},{4,6},{5,7},{6,4},{7,5},{8,10},{9,11},{10,... | collective-permute-start | bytes 3932168 | tf_op jit(solution)/shard_map/ppermute | solution.py:651
  152.1 2.4 %collective-permute-start.12 = (bf16[256,1280]{1,0:T(8,128)(2,1)}, bf16[256,1280]{1,0:T(8,128)(2,1)S(1)}, u32[]{:S(2)}, u32[]{:S(2)}) collective-permute-start(bf16[256,1280]{1,0:T(8,128)(2,1)} %get-tuple-element.68), channel_id=1, source_target_pairs={{0,1},{1,0},{2,3},{3,2},{4,5},{5,4},{6,7},{7,6},{8,9},{9,8},{10,11... | collective-permute-start | bytes 1966088 | tf_op jit(solution)/shard_map/ppermute | solution.py:648
  152.4 2.9 %collective-permute-start.13 = (bf16[256,1280]{1,0:T(8,128)(2,1)}, bf16[256,1280]{1,0:T(8,128)(2,1)S(1)}, u32[]{:S(2)}, u32[]{:S(2)}) collective-permute-start(bf16[256,1280]{1,0:T(8,128)(2,1)} %get-tuple-element.69), channel_id=1, source_target_pairs={{0,1},{1,0},{2,3},{3,2},{4,5},{5,4},{6,7},{7,6},{8,9},{9,8},{10,11... | collective-permute-start | bytes 1966088 | tf_op jit(solution)/shard_map/ppermute | solution.py:648

commit v5 on v4

--- a/solution.py
+++ b/solution.py
@@ -21,7 +21,8 @@
 VMEM_LIMIT = 60 * 1024 * 1024
 NEG = -1e30
 SCALE = QK ** (-0.5) * 1.4426950408889634
-TOP = 3.0
+LOW_TOTAL, HIGH_TOTAL = 2.0**-60, 2.0**100
+TILE = 256
 NT = (((1,), (1,)), ((), ()))
 F32 = jnp.float32
 BF16 = jnp.bfloat16
@@ -263,37 +264,84 @@
     return lax.broadcasted_iota(jnp.int32, (rows, cols), axis)
 
 
-def attend(q, keys, values, mask):
-    scores = mask(jnp.dot(q, keys, preferred_element_type=F32))
-    top = jnp.maximum(jnp.max(scores, axis=1, keepdims=True), -1e28) * SCALE - TOP
-    weights = jnp.exp2((scores * SCALE - top).astype(BF16))
-    out = jnp.dot(weights, values, preferred_element_type=F32)
-    return out[:, :DV], out[:, DV:]
-
-
-def stacked(x, times):
-    return jnp.concatenate([x] * times, axis=0) if times > 1 else x
-
-
-def stacked_queries(q_ref, side):
-    pairs = q_ref.shape[1] // PAIR
-    return jnp.concatenate(
-        [q_ref[:, p * PAIR + side * 128 : p * PAIR + side * 128 + 256] for p in range(pairs)],
-        axis=0,
-    )
-
-
-def gate_columns(gate_ref, first, branch, heads, side, count):
+def scores_of(q, keys, mask):
+    scores = jnp.dot(q, keys, preferred_element_type=F32)
+    return scores if mask is None else mask(scores)
+
+
+def in_range(total):
+    good = jnp.where((total >= LOW_TOTAL) & (total <= HIGH_TOTAL), 1.0, 0.0)
+    return jnp.min(good.reshape(-1, 8, DV), axis=0)
+
+
+def over_heads(count, load, branches, finish):
+    def sums(weights, values):
+        out = jnp.dot(weights, values(), preferred_element_type=F32)
+        return out[:, :DV], out[:, DV:]
+
+    worst, held = [], None
+    for head in range(count + 1):
+        side = head % 2
+        q = load(head // 2, side) if head < count else None
+        fresh, parts = [], []
+        for at, (tiles, values) in enumerate(branches):
+            weights, ahead = [], []
+            for place, (keys, mask) in enumerate(tiles):
+                if q is not None:
+                    ahead.append(scores_of(q, keys(side), mask))
+                if held is not None:
+                    weights.append(jnp.exp2(held[at][place] * SCALE).astype(BF16))
+            fresh.append(ahead)
+            if held is not None:
+                parts.append((weights, values))
+        if held is not None:
+            parts = [sums(jnp.concatenate(w, axis=1), values) for w, values in parts]
+            worst += [in_range(x) for x in finish((head - 1) // 2, (head - 1) % 2, parts)]
+        held = fresh if q is not None else None
+
+    @pl.when(jnp.min(functools.reduce(jnp.minimum, worst)) < 0.5)
+    def _():
+        def exact(pair, _):
+            for side in range(2):
+                q = load(pair, side)
+                parts = []
+                for tiles, values in branches:
+                    scores = [scores_of(q, keys(side), mask) for keys, mask in tiles]
+                    scores = jnp.concatenate(scores, axis=1)
+                    top = jnp.max(scores, axis=1, keepdims=True)
+                    shifted = (scores - jnp.maximum(top, -1e28)) * SCALE
+                    parts.append(sums(jnp.exp2(shifted).astype(BF16), values))
+                finish(pair, side, parts)
+            return 0
+
+        lax.fori_loop(0, count // 2, exact, 0)
+
+
+def query_loader(q_ref):
+    def load(pair, side):
+        at = pair * PAIR + side * 128
+        return q_ref[:, pl.ds(at if isinstance(at, int) else pl.multiple_of(at, 128), 256)]
+
+    return load
+
+
+def head_columns(pair, side):
+    at = pair * 2 * DV + side * DV
+    return pl.ds(at if isinstance(at, int) else pl.multiple_of(at, DV), DV)
+
+
+def gate_loader(gate_ref, first, heads):
     turned = pltpu.roll(gate_ref[...], lax.rem(128 - first, 128), 1)
-    at = branch * heads + side
-    rows = turned.shape[0]
-    return jnp.concatenate(
-        [
-            jnp.broadcast_to(turned[:, at + 2 * p : at + 2 * p + 1], (rows, DV))
-            for p in range(count)
-        ],
-        axis=0,
-    )
+
+    def load(pair, side, branch):
+        at = branch * heads + side
+        if isinstance(pair, int):
+            column = turned[:, at + 2 * pair : at + 2 * pair + 1]
+        else:
+            column = pltpu.roll(turned, lax.rem(128 - 2 * pair, 128), 1)[:, at : at + 1]
+        return jnp.broadcast_to(column, (turned.shape[0], DV))
+
+    return load
 
 
 def near_kernel(heads, rim, where_ref, q_ref, gate_ref, *refs):
@@ -308,33 +356,37 @@
         keys = ext
     else:
         out_ref = refs[3]
-    rows = pl.ds(pl.multiple_of(pl.program_id(0) * QBLK, QBLK), WINDOW + QBLK)
-
-    pairs = q_ref.shape[1] // PAIR
-    first = pl.program_id(1) * 2 * pairs
-
-    def mask(scores):
-        row, col = iota(QBLK, QBLK, 0), iota(QBLK, QBLK, 1)
-        old = jnp.where(stacked(col >= row, pairs), scores[:, :QBLK], NEG)
-        new = jnp.where(stacked(col <= row, pairs), scores[:, WINDOW:], NEG)
-        return jnp.concatenate([old, scores[:, QBLK:WINDOW], new], axis=1)
-
-    for side in range(2):
-        num, den = attend(stacked_queries(q_ref, side), keys[side][:, rows], keys[2][rows], mask)
-        total = gate_columns(gate_ref, first, 2, heads, side, pairs) * (num / den)
-        for p in range(pairs):
-            at = (2 * p + side) * DV
-            out_ref[:, at : at + DV] = total[p * QBLK : (p + 1) * QBLK]
+    count = q_ref.shape[1] // QK
+    gate = gate_loader(gate_ref, pl.program_id(1) * count, heads)
+    base = pl.multiple_of(pl.program_id(0) * QBLK, QBLK)
+    row, col = iota(QBLK, QBLK, 0), iota(QBLK, QBLK, 1)
+
+    def tile(place, mask):
+        return (lambda side: keys[side][:, pl.ds(base + place * QBLK, QBLK)]), mask
+
+    def finish(pair, side, parts):
+        ((num, den),) = parts
+        out_ref[:, head_columns(pair, side)] = gate(pair, side, 2) * (num / den)
+        return [den]
+
+    tiles = [
+        tile(0, lambda scores: jnp.where(col >= row, scores, NEG)),
+        tile(1, None),
+        tile(2, lambda scores: jnp.where(col <= row, scores, NEG)),
+    ]
+    values = lambda: keys[2][pl.ds(base, WINDOW + QBLK)]
+    over_heads(count, query_loader(q_ref), [(tiles, values)], finish)
 
 
 def near_branch(first_block, block_count, where, queries, gates, keys, rims, prior):
     tokens, width = queries.shape
     heads = width // QK
+    at_once = 8 if heads % 8 == 0 else 2
     row_block = lambda i, p, *_: (i + first_block, p)
     whole = lambda x: pl.BlockSpec(x.shape, lambda i, p, *_: (0,) * x.ndim)
     operands = [queries, gates, *keys]
     specs = [
-        pl.BlockSpec((QBLK, 2 * PAIR), row_block),
+        pl.BlockSpec((QBLK, at_once * QK), row_block),
         pl.BlockSpec((QBLK, 128), lambda i, p, *_: (i + first_block, 0)),
     ]
     specs += [whole(x) for x in keys]
@@ -356,9 +408,9 @@
         functools.partial(near_kernel, heads, rims is not None),
         grid_spec=pltpu.PrefetchScalarGridSpec(
             num_scalar_prefetch=1,
-            grid=(block_count, heads // 4),
+            grid=(block_count, heads // at_once),
             in_specs=specs,
-            out_specs=pl.BlockSpec((QBLK, 4 * DV), row_block),
+            out_specs=pl.BlockSpec((QBLK, at_once * DV), row_block),
             scratch_shapes=scratch,
         ),
         out_shape=jax.ShapeDtypeStruct((tokens, heads * DV), F32),
@@ -375,17 +427,16 @@
 
 def chosen_kernel(heads, span, *refs):
     first_chunk, widths = span
-    count = sum(len(w) for w in widths)
+    out_count = sum(len(w) for w in widths)
     meta_ref, slots_ref, dead_ref, q_ref, gate_ref, near_ref = refs[:6]
     (key_pool, val_pool), cfold, weight_ref = refs[6:8], refs[8:11], refs[11]
-    outs = list(refs[12 : 12 + count])
-    gathered, even, odd, val, attended, weight, weight_sem = refs[12 + count :]
+    outs = list(refs[12 : 12 + out_count])
+    gathered, even, odd, val, attended, weight, weight_sem = refs[12 + out_count :]
     keys = (even, odd)
     turn, step = pl.program_id(0), pl.program_id(1)
     last = pl.num_programs(1) - 1
     rows = q_ref.shape[0]
-    pairs = q_ref.shape[1] // PAIR
-    first = step * 2 * pairs
+    count = q_ref.shape[1] // QK
     chunk_start = meta_ref[first_chunk + turn] * rows
     list_at = lax.div(chunk_start, QBLK) * PICKS
     first_row = lax.rem(chunk_start, QBLK)
@@ -412,29 +463,37 @@
     def _():
         copy.start()
 
+    gate = gate_loader(gate_ref, step * count, heads)
+    row = iota(rows, TILE, 0)
+    col = iota(rows, TILE, 1)
+    own_keep = (col >= KBLK) | (col <= row + first_row)
+
     def own_mask(scores):
-        row, col = iota(rows, 128, 0) + first_row, iota(rows, 128, 1)
-        keep = stacked((col >= KBLK) | (col <= row), pairs)
-        own = jnp.where(keep, scores[:, :128], NEG)
+        own = jnp.where(own_keep[:, :128], scores[:, :128], NEG)
         return jnp.concatenate([own, scores[:, 128:]], axis=1)
 
-    def comp_mask(scores):
-        cols = scores.shape[1]
-        ends = (iota(rows, cols, 1) + 1) * CBLK - 1
-        return jnp.where(stacked(ends <= position + iota(rows, cols, 0), pairs), scores, NEG)
-
-    empty = stacked(position + iota(rows, DV, 0) < CBLK - 1, pairs)
-    for side in range(2):
-        q = stacked_queries(q_ref, side)
-        num, den = attend(q, keys[side][...], val[...], own_mask)
-        total = gate_columns(gate_ref, first, 1, heads, side, pairs) * (num / den)
-        num, den = attend(q, cfold[side][...], cfold[2][...], comp_mask)
-        den = jnp.where(empty, 1.0, den)
-        total = total + gate_columns(gate_ref, first, 0, heads, side, pairs) * (num / den)
-        for p in range(pairs):
-            at = (2 * p + side) * DV
-            mixed = near_ref[:, at : at + DV] + total[p * rows : (p + 1) * rows]
-            attended[step, :, at : at + DV] = mixed.astype(BF16)
+    def comp_mask(place):
+        ends = (col + place * TILE + 1) * CBLK - 1
+        return lambda scores: jnp.where(ends <= row + position, scores, NEG)
+
+    def tile(refs, place, mask):
+        return (lambda side: refs[side][:, place * TILE : (place + 1) * TILE]), mask
+
+    chosen = [tile(keys, p, own_mask if p == 0 else None) for p in range(PICKS * KBLK // TILE)]
+    folded = [tile(cfold, p, comp_mask(p)) for p in range(cfold[2].shape[0] // TILE)]
+    empty = row[:, :DV] + position < CBLK - 1
+
+    def finish(pair, side, parts):
+        (num, den), (folded_num, folded_den) = parts
+        folded_den = jnp.where(empty, 1.0, folded_den)
+        cols = head_columns(pair, side)
+        mixed = near_ref[:, cols] + gate(pair, side, 1) * (num / den)
+        mixed = mixed + gate(pair, side, 0) * (folded_num / folded_den)
+        attended[step, :, cols] = mixed.astype(BF16)
+        return [den, folded_den]
+
+    branches = [(chosen, lambda: val[...]), (folded, lambda: cfold[2][...])]
+    over_heads(count, query_loader(q_ref), branches, finish)
 
     @pl.when((turn == 0) & (step == last))
     def _():
@@ -445,7 +504,7 @@
 
         @pl.when((turn == place) & (step == last))
         def _():
-            rows_in = jnp.concatenate([attended[s] for s in range(heads // 4)], axis=1)
+            rows_in = jnp.concatenate([attended[s] for s in range(attended.shape[0])], axis=1)
             first_col = 0
             for out_ref in chunk_outs:
                 for at in range(0, out_ref.shape[1], 256):
@@ -458,7 +517,8 @@
 def chosen_and_project(first_chunk, widths, rows, meta, slots, dead, queries, gates, near, pools, out_weight):
     tokens, width = queries.shape
     heads = width // QK
-    steps = heads // 4
+    at_once = 8 if heads % 8 == 0 else 2
+    steps = heads // at_once
     whole = lambda x: pl.BlockSpec(x.shape, lambda i, p, *_: (0,) * x.ndim)
     outs = [jax.ShapeDtypeStruct((rows, width), BF16) for chunk in widths for width in chunk]
     return pl.pallas_call(
@@ -467,9 +527,9 @@
             num_scalar_prefetch=3,
             grid=(len(widths), steps),
             in_specs=[
-                pl.BlockSpec((rows, 2 * PAIR), lambda i, p, m, *_: (m[first_chunk + i], p)),
+                pl.BlockSpec((rows, at_once * QK), lambda i, p, m, *_: (m[first_chunk + i], p)),
                 pl.BlockSpec((rows, 128), lambda i, p, m, *_: (m[first_chunk + i], 0)),
-                pl.BlockSpec((rows, 4 * DV), lambda i, p, m, *_: (m[first_chunk + i], p)),
+                pl.BlockSpec((rows, at_once * DV), lambda i, p, m, *_: (m[first_chunk + i], p)),
             ]
             + [whole(x) for x in pools]
             + [pl.BlockSpec(memory_space=pl.ANY)],
@@ -479,7 +539,7 @@
                 pltpu.VMEM((256, PICKS * KBLK), BF16),
                 pltpu.VMEM((256, PICKS * KBLK), BF16),
                 pltpu.VMEM((PICKS * KBLK, 256), BF16),
-                pltpu.VMEM((steps, rows, 4 * DV), BF16),
+                pltpu.VMEM((steps, rows, at_once * DV), BF16),
                 pltpu.VMEM(out_weight.shape, BF16),
                 pltpu.SemaphoreType.DMA,
             ],

time: 159 us -> 201 us (1.26)
  Pallas kernels: 117 us -> 160 us
    pallas_call x3, Pallas kernels: 67.4 us -> 96.8 us  [chosen_and_project(): pl.pallas_call(functools.partial(chosen_kernel, heads, (first_chunk, widt...]
    pallas_call x2, Pallas kernels: 33.7 us -> 47 us  [near_branch(): pl.pallas_call(functools.partial(near_kernel, heads, rims is not None), g...]
  transfers between devices with their start and end apart: 15 -> 15, of which waited for: 5 -> 5; matrix products, arithmetic and copies ran while one was open for 1% -> 1% of each run, Pallas kernels for 58% -> 63%
where the time goes in v5:
time: 201 us
  Pallas kernels  160 us (80%)
  starting transfers between devices  25.1 us (12%)
  waiting for transfers between devices  6.09 us (3%)
  other arithmetic  5.18 us (3%)
  local copies, waits for them, and re-layouts  4.12 us (2%)
    pallas_call x3, Pallas kernels, chosen_and_project(): pl.pallas_call(functools.partial(chosen_kernel, heads, (first_chunk, widt...  96.8 us
    pallas_call x2, Pallas kernels, near_branch(): pl.pallas_call(functools.partial(near_kernel, heads, rims is not None), g...  47 us
    ppermute x6, starting transfers between devices, ahead(): lax.ppermute(send, 'ctx', [(i, i + 2 * distance) for i in range(n_ctx - 2...  12.1 us
    pallas_call x3, Pallas kernels, single_step(): pl.pallas_call(kernel, grid_spec=pltpu.PrefetchScalarGridSpec(num_scalar_...  8.79 us
    ppermute x1, starting transfers between devices, local(): lax.ppermute(rim, 'ctx', [(i, i + 1) for i in range(1, n_ctx - 1, 2)])  4.39 us
    pallas_call x1, Pallas kernels, local(): pl.pallas_call(prep_kernel, grid_spec=pltpu.PrefetchScalarGridSpec(num_sc...  4.25 us
  transfers between devices with their start and end apart: 15, of which 5 were waited for; matrix products, arithmetic and copies ran while one was open for 1% of the time, Pallas kernels for 63%

profile of v5, /device:TPU:5, one launch (start us, length us, event | category | flops | bytes accessed | tf_op | source)
XLA Modules:
  0.0 200.8 jit_solution(15297039013684969220)
XLA Ops:
  0.0 0.6 pad_add_fusion.group_ref.where_ref
  0.7 4.3 %prep.1 = (bf16[2656,128]{1,0:T(8,128)(2,1)}, bf16[1280,128]{1,0:T(8,128)(2,1)}, bf16[256,1024]{1,0:T(8,128)(2,1)}, bf16[256,1024]{1,0:T(8,128)(2,1)}, bf16[1024,256]{1,0:T(8,128)(2,1)}) custom-call(s32[2]{0:T(128)} %pad_add_fusion.group_ref.where_ref, bf16[1024,768]{1,0:T(8,128)(2,1)} %keys_ref.1, bf16[1024,512]{1,0:T(8,128)(2,1)} %values_ref.1, ...), custom_call_target="tpu_custom_call" | custom-call | tf_op jit(solution)/shard_map/prep/pallas_call | solution.py:602
  4.9 4.4 %collective-permute-start.4 = (bf16[1280,128]{1,0:T(8,128)(2,1)}, bf16[1280,128]{1,0:T(8,128)(2,1)S(1)}, u32[]{:S(2)}, u32[]{:S(2)}) collective-permute-start(bf16[1280,128]{1,0:T(8,128)(2,1)} %get-tuple-element.52), channel_id=1, source_target_pairs={{4,8},{12,16},{20,24},{5,9},{13,17},{21,25},{6,10},{14,18},{22,26}... | collective-permute-start | bytes 983048 | tf_op jit(solution)/shard_map/ppermute | solution.py:640
  9.3 3.2 %plan.1 = (s32[33]{0:T(128)}, s32[65]{0:T(128)}, s32[65]{0:T(128)}) custom-call(s32[2]{0:T(128)} %pad_add_fusion.group_ref.where_ref, s32[4,4,16]{2,1,0:T(4,128)} %picks_ref), custom_call_target="tpu_custom_call" | custom-call | tf_op jit(solution)/shard_map/plan/pallas_call | solution.py:624
  12.5 1.3 collective-permute-start.2
  13.8 1.3 collective-permute-start.1
  15.1 1.3 collective-permute-start
  16.4 2.2 %collective-permute-done.2.refs_2_.refs_3_ = s32[33]{0:T(128)S(1)} collective-permute-done((s32[33]{0:T(128)}, s32[33]{0:T(128)S(1)}, u32[]{:S(2)}, u32[]{:S(2)}) %collective-permute-start.2) | collective-permute-done | bytes 164 | tf_op jit(solution)/shard_map/ppermute | solution.py:637
  19.1 0.7 collective-permute-done.refs_0_.refs_1_
  20.3 2.6 %pack.2 = (bf16[736,128]{1,0:T(8,128)(2,1)}, bf16[736,128]{1,0:T(8,128)(2,1)}, bf16[736,128]{1,0:T(8,128)(2,1)}) custom-call(s32[2]{0:T(128)} %pad_add_fusion.group_ref.where_ref, s32[33]{0:T(128)} %copy-done.11, s32[33]{0:T(128)} %copy-done.10, s32[33]{0:T(128)} %copy-done.9, bf16[2656,128]{1,0:T(8,128)(2,1)} %get-tuple-element.43.refs_3_.own_ref), custom_call_target="tpu_custom_call" | custom-call | tf_op jit(solution)/shard_map/pack/pallas_call | solution.py:560
  23.0 3.8 %collective-permute-start.5 = (bf16[736,128]{1,0:T(8,128)(2,1)}, bf16[736,128]{1,0:T(8,128)(2,1)S(1)}, u32[]{:S(2)}, u32[]{:S(2)}) collective-permute-start(bf16[736,128]{1,0:T(8,128)(2,1)} %get-tuple-element.55), channel_id=1, source_target_pairs={{0,8},{4,12},{8,16},{12,20},{16,24},{20,28},{1,9},{5,13},{9,17},{1... | collective-permute-start | bytes 565256 | tf_op jit(solution)/shard_map/ppermute | solution.py:656
  27.1 0.9 pad.4.gate_ref.refs_4_
  28.0 3.1 %collective-permute-start.7 = (bf16[736,128]{1,0:T(8,128)(2,1)S(1)}, bf16[736,128]{1,0:T(8,128)(2,1)S(1)}, u32[]{:S(2)}, u32[]{:S(2)}) collective-permute-start(bf16[736,128]{1,0:T(8,128)(2,1)S(1)} %copy-done.13), channel_id=1, source_target_pairs={{0,16},{4,20},{8,24},{12,28},{1,17},{5,21},{9,25},{13,29},{2,18},{... | collective-permute-start | bytes 565256 | tf_op jit(solution)/shard_map/ppermute | solution.py:656
  31.1 1.3 collective-permute-start.9
  32.4 26.8 %near_branch.2.refs_5_ = f32[1024,2048]{1,0:T(8,128)} custom-call(s32[2]{0:T(128)} %pad_add_fusion.group_ref.where_ref, bf16[1024,3072]{1,0:T(8,128)(2,1)} %refs_3_.5, f32[1024,128]{1,0:T(8,128)} %pad.4.gate_ref.refs_4_, bf16[256,1024]{1,0:T(8,128)(2,1)} %get-tuple-element.48.refs_0_, bf16[256,1024]{1,0:T(8,128)(2,1)} %get-tuple-element.49.refs_1_, ...), custom_call_target="tpu_custom_call" | custom-call | flops 402653184 | bytes 7340032 | tf_op jit(solution)/shard_map/near_branch/pallas_call | solution.py:407
  59.2 0.9 copy-done
  60.1 2.7 %pack.3 = (bf16[736,128]{1,0:T(8,128)(2,1)}, bf16[736,128]{1,0:T(8,128)(2,1)}, bf16[736,128]{1,0:T(8,128)(2,1)}, bf16[736,128]{1,0:T(8,128)(2,1)}) custom-call(s32[2]{0:T(128)} %pad_add_fusion.group_ref.where_ref, s32[33]{0:T(128)} %get-tuple-element.42.refs_0_, s32[33]{0:T(128)} %copy-done.11, s32[33]{0:T(128)} %copy-done.10, s32[33]{0:T(128)} %copy-done.9, ...), custom_call_target="tpu_custom_call" | custom-call | tf_op jit(solution)/shard_map/pack/pallas_call | solution.py:560
  62.8 1.3 collective-permute-start.6
  64.1 1.3 collective-permute-start.8
  65.4 1.3 collective-permute-start.10
  66.8 0.7 stack.32.refs_0_
  67.5 20.2 %near_branch.3.refs_5_ = f32[1024,2048]{1,0:T(8,128)} custom-call(s32[2]{0:T(128)} %pad_add_fusion.group_ref.where_ref, bf16[1024,3072]{1,0:T(8,128)(2,1)} %refs_3_.5, f32[1024,128]{1,0:T(8,128)} %pad.4.gate_ref.refs_4_, bf16[256,1024]{1,0:T(8,128)(2,1)} %get-tuple-element.48.refs_0_, ...), custom_call_target="tpu_custom_call", output_to_operand_aliasing={{}: (8, {})} | custom-call | flops 402653184 | bytes 7340032 | tf_op jit(solution)/shard_map/near_branch/pallas_call | solution.py:407
  88.6 3.4 %pool.1 = (bf16[2048,256]{1,0:T(8,128)(2,1)}, bf16[2048,256]{1,0:T(8,128)(2,1)}, bf16[256,256]{1,0:T(8,128)(2,1)}, bf16[256,256]{1,0:T(8,128)(2,1)}, bf16[256,256]{1,0:T(8,128)(2,1)}) custom-call(s32[1]{0:T(128)} %bitcast.6.shard_ref, bf16[2656,128]{1,0:T(8,128)(2,1)} %get-tuple-element.43.refs_3_.own_ref, bf16[736,128]{1,0:T(8,128)(2,1)} %get-tuple-element.54.refs_0_, ...), custom_call_target="tpu_custom_call" | custom-call | tf_op jit(solution)/shard_map/pool/pallas_call | solution.py:560
  92.1 24.9 %chosen_and_project.4 = bf16[256,2560]{1,0:T(8,128)(2,1)} custom-call(s32[5]{0:T(128)} %stack.32.refs_0_, s32[65]{0:T(128)} %get-tuple-element.40.refs_1_, s32[65]{0:T(128)} %get-tuple-element.41.refs_2_, bf16[1024,3072]{1,0:T(8,128)(2,1)} %refs_3_.5, f32[1024,128]{1,0:T(8,128)} %pad.4.gate_ref.refs_4_, f32[1024,2048]{1,0:T(8,128)} %near_branch.3.refs_5_, ...), custom_call_target="tpu_custom_call" | custom-call | flops 268435456 | bytes 5242880 | tf_op jit(solution)/shard_map/chosen_and_project/pallas_call | solution.py:524
  117.0 2.9 %collective-permute-start.11 = (bf16[256,2560]{1,0:T(8,128)(2,1)}, bf16[256,2560]{1,0:T(8,128)(2,1)S(1)}, u32[]{:S(2)}, u32[]{:S(2)}) collective-permute-start(bf16[256,2560]{1,0:T(8,128)(2,1)} %chosen_and_project.4), channel_id=1, source_target_pairs={{0,1},{1,0},{2,3},{3,2},{4,5},{5,4},{6,7},{7,6},{8,9},{9,8},{10,11... | collective-permute-start | bytes 3932168 | tf_op jit(solution)/shard_map/ppermute | solution.py:702
  119.8 25.1 %chosen_and_project.3 = bf16[256,2560]{1,0:T(8,128)(2,1)} custom-call(s32[5]{0:T(128)} %stack.32.refs_0_, s32[65]{0:T(128)} %get-tuple-element.40.refs_1_, s32[65]{0:T(128)} %get-tuple-element.41.refs_2_, bf16[1024,3072]{1,0:T(8,128)(2,1)} %refs_3_.5, f32[1024,128]{1,0:T(8,128)} %pad.4.gate_ref.refs_4_, f32[1024,2048]{1,0:T(8,128)} %near_branch.3.refs_5_, ...), custom_call_target="tpu_custom_call" | custom-call | flops 268435456 | bytes 5242880 | tf_op jit(solution)/shard_map/chosen_and_project/pallas_call | solution.py:524
  145.0 1.6 add_convert_fusion.1
  146.6 1.3 collective-permute-start.14
  147.9 46.7 %chosen_and_project.5 = (bf16[256,1280]{1,0:T(8,128)(2,1)}, bf16[256,1280]{1,0:T(8,128)(2,1)}, bf16[256,2560]{1,0:T(8,128)(2,1)}) custom-call(s32[5]{0:T(128)} %stack.32.refs_0_, s32[65]{0:T(128)} %get-tuple-element.40.refs_1_, s32[65]{0:T(128)} %get-tuple-element.41.refs_2_, bf16[1024,3072]{1,0:T(8,128)(2,1)} %refs_3_.5, f32[1024,128]{1,0:T(8,128)} %pad.4.gate_ref.refs_4_, ...), custom_call_target="tpu_custom_call" | custom-call | flops 268435456 | bytes 5242880 | tf_op jit(solution)/shard_map/chosen_and_project/pallas_call | solution.py:524
  195.2 1.8 collective-permute-done.12
  197.0 0.9 collective-permute-done.13
  198.0 2.8 %add_convert_fusion = bf16[256,2560]{1,0:T(8,128)(2,1)} fusion(bf16[256,2560]{1,0:T(8,128)(2,1)S(1)} %collective-permute-done.14, bf16[256,2560]{1,0:T(8,128)(2,1)} %get-tuple-element.67, bf16[256,1280]{1,0:T(8,128)(2,1)S(1)} %collective-permute-done.13, bf16[256,1280]{1,0:T(8,128)(2,1)S(1)} %collective-permute-done.12), kind=kLoop, calls=%fused_computation | loop fusion | flops 5898240 | bytes 5242880 | tf_op jit(solution)/shard_map/convert_element_type | solution.py:715
  (43 shorter events, 2.8 us)
Async XLA Ops:
  0.6 26.2 %copy-start.2 = (f32[1024,3,16]{0,2,1:T(8,128)S(1)}, f32[1024,3,16]{0,2,1:T(8,128)}, u32[]{:S(2)}) copy-start(f32[1024,3,16]{0,2,1:T(8,128)} %param.14) | copy-start | bytes 589828
  4.9 54.2 %collective-permute-start.3 = (bf16[2656,128]{1,0:T(8,128)(2,1)}, bf16[2656,128]{1,0:T(8,128)(2,1)S(1)}, u32[]{:S(2)}, u32[]{:S(2)}) collective-permute-start(bf16[2656,128]{1,0:T(8,128)(2,1)} %get-tuple-element.43.refs_3_.own_ref), channel_id=1, source_target_pairs={{0,4},{4,0},{8,12},{12,8},{16,20},{20,16},{24,28},{28,24},{1,5},{5... | collective-permute-start | bytes 2039816 | tf_op jit(solution)/shard_map/ppermute | solution.py:619
  4.9 60.5 %collective-permute-start.4 = (bf16[1280,128]{1,0:T(8,128)(2,1)}, bf16[1280,128]{1,0:T(8,128)(2,1)S(1)}, u32[]{:S(2)}, u32[]{:S(2)}) collective-permute-start(bf16[1280,128]{1,0:T(8,128)(2,1)} %get-tuple-element.52), channel_id=1, source_target_pairs={{4,8},{12,16},{20,24},{5,9},{13,17},{21,25},{6,10},{14,18},{22,26}... | collective-permute-start | bytes 983048 | tf_op jit(solution)/shard_map/ppermute | solution.py:640
  12.5 6.1 %collective-permute-start.2 = (s32[33]{0:T(128)}, s32[33]{0:T(128)S(1)}, u32[]{:S(2)}, u32[]{:S(2)}) collective-permute-start(s32[33]{0:T(128)} %get-tuple-element.42.refs_0_), channel_id=1, source_target_pairs={{24,0},{28,4},{25,1},{29,5},{26,2},{30,6},{27,3},{31,7}} | collective-permute-start | bytes 404 | tf_op jit(solution)/shard_map/ppermute | solution.py:637
  13.8 5.2 %collective-permute-start.1 = (s32[33]{0:T(128)}, s32[33]{0:T(128)S(1)}, u32[]{:S(2)}, u32[]{:S(2)}) collective-permute-start(s32[33]{0:T(128)} %get-tuple-element.42.refs_0_), channel_id=1, source_target_pairs={{16,0},{20,4},{24,8},{28,12},{17,1},{21,5},{25,9},{29,13},{18,2},{... | collective-permute-start | bytes 404 | tf_op jit(solution)/shard_map/ppermute | solution.py:637
  15.1 4.6 %collective-permute-start = (s32[33]{0:T(128)}, s32[33]{0:T(128)S(1)}, u32[]{:S(2)}, u32[]{:S(2)}) collective-permute-start(s32[33]{0:T(128)} %get-tuple-element.42.refs_0_), channel_id=1, source_target_pairs={{8,0},{12,4},{16,8},{20,12},{24,16},{28,20},{9,1},{13,5},{17,9},{2... | collective-permute-start | bytes 404 | tf_op jit(solution)/shard_map/ppermute | solution.py:637
  18.7 1.1 copy-start.9
  19.1 0.7 copy-start.10
  19.8 0.6 copy-start.11
  23.0 5.0 %copy-start.13 = (bf16[736,128]{1,0:T(8,128)(2,1)S(1)}, bf16[736,128]{1,0:T(8,128)(2,1)}, u32[]{:S(2)}) copy-start(bf16[736,128]{1,0:T(8,128)(2,1)} %get-tuple-element.57) | copy-start | bytes 565252
  23.0 8.1 %copy-start.12 = (bf16[736,128]{1,0:T(8,128)(2,1)S(1)}, bf16[736,128]{1,0:T(8,128)(2,1)}, u32[]{:S(2)}) copy-start(bf16[736,128]{1,0:T(8,128)(2,1)} %get-tuple-element.59) | copy-start | bytes 565252
  23.0 41.1 %collective-permute-start.5 = (bf16[736,128]{1,0:T(8,128)(2,1)}, bf16[736,128]{1,0:T(8,128)(2,1)S(1)}, u32[]{:S(2)}, u32[]{:S(2)}) collective-permute-start(bf16[736,128]{1,0:T(8,128)(2,1)} %get-tuple-element.55), channel_id=1, source_target_pairs={{0,8},{4,12},{8,16},{12,20},{16,24},{20,28},{1,9},{5,13},{9,17},{1... | collective-permute-start | bytes 565256 | tf_op jit(solution)/shard_map/ppermute | solution.py:656
  28.0 59.7 %collective-permute-start.7 = (bf16[736,128]{1,0:T(8,128)(2,1)S(1)}, bf16[736,128]{1,0:T(8,128)(2,1)S(1)}, u32[]{:S(2)}, u32[]{:S(2)}) collective-permute-start(bf16[736,128]{1,0:T(8,128)(2,1)S(1)} %copy-done.13), channel_id=1, source_target_pairs={{0,16},{4,20},{8,24},{12,28},{1,17},{5,21},{9,25},{13,29},{2,18},{... | collective-permute-start | bytes 565256 | tf_op jit(solution)/shard_map/ppermute | solution.py:656
  31.1 56.6 %collective-permute-start.9 = (bf16[736,128]{1,0:T(8,128)(2,1)S(1)}, bf16[736,128]{1,0:T(8,128)(2,1)S(1)}, u32[]{:S(2)}, u32[]{:S(2)}) collective-permute-start(bf16[736,128]{1,0:T(8,128)(2,1)S(1)} %copy-done.12), channel_id=1, source_target_pairs={{0,24},{4,28},{1,25},{5,29},{2,26},{6,30},{3,27},{7,31}} | collective-permute-start | bytes 565256 | tf_op jit(solution)/shard_map/ppermute | solution.py:656
  59.2 0.9 copy-start
  62.8 24.9 %collective-permute-start.6 = (bf16[736,128]{1,0:T(8,128)(2,1)}, bf16[736,128]{1,0:T(8,128)(2,1)S(1)}, u32[]{:S(2)}, u32[]{:S(2)}) collective-permute-start(bf16[736,128]{1,0:T(8,128)(2,1)} %get-tuple-element.56), channel_id=1, source_target_pairs={{0,8},{4,12},{8,16},{12,20},{16,24},{20,28},{1,9},{5,13},{9,17},{1... | collective-permute-start | bytes 565256 | tf_op jit(solution)/shard_map/ppermute | solution.py:656
  64.1 23.5 %copy-start.3 = (bf16[736,128]{1,0:T(8,128)(2,1)}, bf16[736,128]{1,0:T(8,128)(2,1)S(1)}, u32[]{:S(2)}) copy-start(bf16[736,128]{1,0:T(8,128)(2,1)S(1)} %collective-permute-done.5.refs_1_) | copy-start | bytes 565252
  64.1 23.6 %collective-permute-start.8 = (bf16[736,128]{1,0:T(8,128)(2,1)}, bf16[736,128]{1,0:T(8,128)(2,1)S(1)}, u32[]{:S(2)}, u32[]{:S(2)}) collective-permute-start(bf16[736,128]{1,0:T(8,128)(2,1)} %get-tuple-element.58), channel_id=1, source_target_pairs={{0,16},{4,20},{8,24},{12,28},{1,17},{5,21},{9,25},{13,29},{2,18},{... | collective-permute-start | bytes 565256 | tf_op jit(solution)/shard_map/ppermute | solution.py:656
  65.4 2.0 %copy-start.1 = (bf16[1280,128]{1,0:T(8,128)(2,1)}, bf16[1280,128]{1,0:T(8,128)(2,1)S(1)}, u32[]{:S(2)}) copy-start(bf16[1280,128]{1,0:T(8,128)(2,1)S(1)} %collective-permute-done.4.refs_4_) | copy-start | bytes 983044
  65.4 22.3 %collective-permute-start.10 = (bf16[736,128]{1,0:T(8,128)(2,1)}, bf16[736,128]{1,0:T(8,128)(2,1)S(1)}, u32[]{:S(2)}, u32[]{:S(2)}) collective-permute-start(bf16[736,128]{1,0:T(8,128)(2,1)} %get-tuple-element.60), channel_id=1, source_target_pairs={{0,24},{4,28},{1,25},{5,29},{2,26},{6,30},{3,27},{7,31}} | collective-permute-start | bytes 565256 | tf_op jit(solution)/shard_map/ppermute | solution.py:656
  87.7 0.7 copy-start.4
  87.7 0.8 copy-start.5
  87.7 0.8 copy-start.6
  87.7 0.9 copy-start.7
  87.7 0.9 copy-start.8
  117.0 28.0 %collective-permute-start.11 = (bf16[256,2560]{1,0:T(8,128)(2,1)}, bf16[256,2560]{1,0:T(8,128)(2,1)S(1)}, u32[]{:S(2)}, u32[]{:S(2)}) collective-permute-start(bf16[256,2560]{1,0:T(8,128)(2,1)} %chosen_and_project.4), channel_id=1, source_target_pairs={{0,1},{1,0},{2,3},{3,2},{4,5},{5,4},{6,7},{7,6},{8,9},{9,8},{10,11... | collective-permute-start | bytes 3932168 | tf_op jit(solution)/shard_map/ppermute | solution.py:702
  146.6 51.3 %collective-permute-start.14 = (bf16[256,2560]{1,0:T(8,128)(2,1)S(1)}, bf16[256,2560]{1,0:T(8,128)(2,1)S(1)}, u32[]{:S(2)}, u32[]{:S(2)}) collective-permute-start(bf16[256,2560]{1,0:T(8,128)(2,1)S(1)} %add_convert_fusion.1), channel_id=1, source_target_pairs={{0,2},{1,3},{2,0},{3,1},{4,6},{5,7},{6,4},{7,5},{8,10},{9,11},{10,... | collective-permute-start | bytes 3932168 | tf_op jit(solution)/shard_map/ppermute | solution.py:711
  194.6 2.4 %collective-permute-start.12 = (bf16[256,1280]{1,0:T(8,128)(2,1)}, bf16[256,1280]{1,0:T(8,128)(2,1)S(1)}, u32[]{:S(2)}, u32[]{:S(2)}) collective-permute-start(bf16[256,1280]{1,0:T(8,128)(2,1)} %get-tuple-element.68), channel_id=1, source_target_pairs={{0,1},{1,0},{2,3},{3,2},{4,5},{5,4},{6,7},{7,6},{8,9},{9,8},{10,11... | collective-permute-start | bytes 1966088 | tf_op jit(solution)/shard_map/ppermute | solution.py:708
  195.0 2.9 %collective-permute-start.13 = (bf16[256,1280]{1,0:T(8,128)(2,1)}, bf16[256,1280]{1,0:T(8,128)(2,1)S(1)}, u32[]{:S(2)}, u32[]{:S(2)}) collective-permute-start(bf16[256,1280]{1,0:T(8,128)(2,1)} %get-tuple-element.69), channel_id=1, source_target_pairs={{0,1},{1,0},{2,3},{3,2},{4,5},{5,4},{6,7},{7,6},{8,9},{9,8},{10,11... | collective-permute-start | bytes 1966088 | tf_op jit(solution)/shard_map/ppermute | solution.py:708

commit v6 on v5

--- a/solution.py
+++ b/solution.py
@@ -225,10 +225,10 @@
         val_ref[:WINDOW] = jnp.zeros((WINDOW, 256), BF16)
 
 
-def pool_kernel(groups, lists, shard_ref, own_ref, *refs):
+def pool_kernel(groups, lists, where_ref, own_ref, *refs):
     sent = 2 * groups - 1
     ins, (key_ref, val_ref, ceven_ref, codd_ref, cval_ref, folded) = refs[:sent], refs[sent:]
-    shard = shard_ref[0]
+    shard = where_ref[1]
     parity = lax.rem(shard, 2)
     base = shard - parity
     rows = lists * KBLK
@@ -240,7 +240,7 @@
         keys, values = unpack(ref, 0, lists, step)
         at = slice(place * rows, place * rows + rows)
         key_ref[at] = keys
-        val_ref[at] = with_ones(values)
+        val_ref[at] = values
         low = ref[fold_at : fold_at + folds]
         high = ref[fold_at + folds : fold_at + 2 * folds]
         owned = pl.ds(pl.multiple_of(owner * folds, 32), folds)
@@ -274,36 +274,36 @@
     return jnp.min(good.reshape(-1, 8, DV), axis=0)
 
 
-def over_heads(count, load, branches, finish):
+def over_heads(pairs, load, branches, finish):
     def sums(weights, values):
         out = jnp.dot(weights, values(), preferred_element_type=F32)
         return out[:, :DV], out[:, DV:]
 
+    at_once = 2 if pairs % 2 == 0 else 1
+    units = [(pair, side) for pair in range(0, pairs, at_once) for side in range(2)]
     worst, held = [], None
-    for head in range(count + 1):
-        side = head % 2
-        q = load(head // 2, side) if head < count else None
+    for now, unit in zip([None] + units, units + [None]):
+        q = None if unit is None else load(*unit, at_once)
         fresh, parts = [], []
         for at, (tiles, values) in enumerate(branches):
             weights, ahead = [], []
             for place, (keys, mask) in enumerate(tiles):
                 if q is not None:
-                    ahead.append(scores_of(q, keys(side), mask))
+                    ahead.append(scores_of(q, keys(unit[1]), mask))
                 if held is not None:
                     weights.append(jnp.exp2(held[at][place] * SCALE).astype(BF16))
             fresh.append(ahead)
-            if held is not None:
-                parts.append((weights, values))
+            parts.append((weights, values))
         if held is not None:
             parts = [sums(jnp.concatenate(w, axis=1), values) for w, values in parts]
-            worst += [in_range(x) for x in finish((head - 1) // 2, (head - 1) % 2, parts)]
-        held = fresh if q is not None else None
+            worst += [in_range(x) for x in finish(*now, at_once, parts)]
+        held = fresh
 
     @pl.when(jnp.min(functools.reduce(jnp.minimum, worst)) < 0.5)
     def _():
         def exact(pair, _):
             for side in range(2):
-                q = load(pair, side)
+                q = load(pair, side, 1)
                 parts = []
                 for tiles, values in branches:
                     scores = [scores_of(q, keys(side), mask) for keys, mask in tiles]
@@ -311,37 +311,49 @@
                     top = jnp.max(scores, axis=1, keepdims=True)
                     shifted = (scores - jnp.maximum(top, -1e28)) * SCALE
                     parts.append(sums(jnp.exp2(shifted).astype(BF16), values))
-                finish(pair, side, parts)
+                finish(pair, side, 1, parts)
             return 0
 
-        lax.fori_loop(0, count // 2, exact, 0)
+        lax.fori_loop(0, pairs, exact, 0)
+
+
+def aligned(at):
+    return at if isinstance(at, int) else pl.multiple_of(at, 128)
 
 
 def query_loader(q_ref):
-    def load(pair, side):
-        at = pair * PAIR + side * 128
-        return q_ref[:, pl.ds(at if isinstance(at, int) else pl.multiple_of(at, 128), 256)]
+    def load(pair, side, n):
+        at = [aligned((pair + p) * PAIR + side * 128) for p in range(n)]
+        return jnp.concatenate([q_ref[:, pl.ds(x, 256)] for x in at], axis=0)
 
     return load
 
 
 def head_columns(pair, side):
-    at = pair * 2 * DV + side * DV
-    return pl.ds(at if isinstance(at, int) else pl.multiple_of(at, DV), DV)
+    return pl.ds(aligned(pair * 2 * DV + side * DV), DV)
 
 
 def gate_loader(gate_ref, first, heads):
     turned = pltpu.roll(gate_ref[...], lax.rem(128 - first, 128), 1)
 
-    def load(pair, side, branch):
-        at = branch * heads + side
+    def load(pair, side, n, branch):
         if isinstance(pair, int):
-            column = turned[:, at + 2 * pair : at + 2 * pair + 1]
+            local, at = turned, branch * heads + side + 2 * pair
         else:
-            column = pltpu.roll(turned, lax.rem(128 - 2 * pair, 128), 1)[:, at : at + 1]
-        return jnp.broadcast_to(column, (turned.shape[0], DV))
+            local, at = pltpu.roll(turned, lax.rem(128 - 2 * pair, 128), 1), branch * heads + side
+        columns = [local[:, at + 2 * p : at + 2 * p + 1] for p in range(n)]
+        shape = (turned.shape[0], DV)
+        return jnp.concatenate([jnp.broadcast_to(x, shape) for x in columns], axis=0)
 
     return load
+
+
+def stacked(x, times):
+    return jnp.concatenate([x] * times, axis=0) if times > 1 else x
+
+
+def repeated(keep, rows):
+    return stacked(keep, rows // keep.shape[0])
 
 
 def near_kernel(heads, rim, where_ref, q_ref, gate_ref, *refs):
@@ -364,18 +376,20 @@
     def tile(place, mask):
         return (lambda side: keys[side][:, pl.ds(base + place * QBLK, QBLK)]), mask
 
-    def finish(pair, side, parts):
+    def finish(pair, side, n, parts):
         ((num, den),) = parts
-        out_ref[:, head_columns(pair, side)] = gate(pair, side, 2) * (num / den)
+        total = gate(pair, side, n, 2) * (num / den)
+        for p in range(n):
+            out_ref[:, head_columns(pair + p, side)] = total[p * QBLK : (p + 1) * QBLK]
         return [den]
 
     tiles = [
-        tile(0, lambda scores: jnp.where(col >= row, scores, NEG)),
+        tile(0, lambda x: jnp.where(repeated(col >= row, x.shape[0]), x, NEG)),
         tile(1, None),
-        tile(2, lambda scores: jnp.where(col <= row, scores, NEG)),
+        tile(2, lambda x: jnp.where(repeated(col <= row, x.shape[0]), x, NEG)),
     ]
     values = lambda: keys[2][pl.ds(base, WINDOW + QBLK)]
-    over_heads(count, query_loader(q_ref), [(tiles, values)], finish)
+    over_heads(count // 2, query_loader(q_ref), [(tiles, values)], finish)
 
 
 def near_branch(first_block, block_count, where, queries, gates, keys, rims, prior):
@@ -437,10 +451,10 @@
     last = pl.num_programs(1) - 1
     rows = q_ref.shape[0]
     count = q_ref.shape[1] // QK
-    chunk_start = meta_ref[first_chunk + turn] * rows
+    chunk_start = meta_ref[2 + first_chunk + turn] * rows
     list_at = lax.div(chunk_start, QBLK) * PICKS
     first_row = lax.rem(chunk_start, QBLK)
-    position = meta_ref[0] + chunk_start
+    position = meta_ref[2] + chunk_start
     copy = pltpu.make_async_copy(weight_ref, weight, weight_sem)
 
     @pl.when(step == 0)
@@ -448,7 +462,7 @@
         for slot in range(PICKS):
             source = pl.multiple_of(slots_ref[list_at + slot] * KBLK, KBLK)
             gathered[slot * KBLK : (slot + 1) * KBLK] = key_pool[pl.ds(source, KBLK)]
-            val[slot * KBLK : (slot + 1) * KBLK] = val_pool[pl.ds(source, KBLK)]
+            val[slot * KBLK : (slot + 1) * KBLK] = with_ones(val_pool[pl.ds(source, KBLK)])
         for slot in range(1, PICKS):
 
             @pl.when(dead_ref[list_at + slot] == 1)
@@ -469,12 +483,12 @@
     own_keep = (col >= KBLK) | (col <= row + first_row)
 
     def own_mask(scores):
-        own = jnp.where(own_keep[:, :128], scores[:, :128], NEG)
+        own = jnp.where(repeated(own_keep[:, :128], scores.shape[0]), scores[:, :128], NEG)
         return jnp.concatenate([own, scores[:, 128:]], axis=1)
 
     def comp_mask(place):
         ends = (col + place * TILE + 1) * CBLK - 1
-        return lambda scores: jnp.where(ends <= row + position, scores, NEG)
+        return lambda x: jnp.where(repeated(ends <= row + position, x.shape[0]), x, NEG)
 
     def tile(refs, place, mask):
         return (lambda side: refs[side][:, place * TILE : (place + 1) * TILE]), mask
@@ -483,17 +497,19 @@
     folded = [tile(cfold, p, comp_mask(p)) for p in range(cfold[2].shape[0] // TILE)]
     empty = row[:, :DV] + position < CBLK - 1
 
-    def finish(pair, side, parts):
+    def finish(pair, side, n, parts):
         (num, den), (folded_num, folded_den) = parts
-        folded_den = jnp.where(empty, 1.0, folded_den)
-        cols = head_columns(pair, side)
-        mixed = near_ref[:, cols] + gate(pair, side, 1) * (num / den)
-        mixed = mixed + gate(pair, side, 0) * (folded_num / folded_den)
-        attended[step, :, cols] = mixed.astype(BF16)
+        folded_den = jnp.where(stacked(empty, n), 1.0, folded_den)
+        total = gate(pair, side, n, 1) * (num / den)
+        total = total + gate(pair, side, n, 0) * (folded_num / folded_den)
+        for p in range(n):
+            cols = head_columns(pair + p, side)
+            mixed = near_ref[:, cols] + total[p * rows : (p + 1) * rows]
+            attended[step, :, cols] = mixed.astype(BF16)
         return [den, folded_den]
 
     branches = [(chosen, lambda: val[...]), (folded, lambda: cfold[2][...])]
-    over_heads(count, query_loader(q_ref), branches, finish)
+    over_heads(count // 2, query_loader(q_ref), branches, finish)
 
     @pl.when((turn == 0) & (step == last))
     def _():
@@ -527,9 +543,9 @@
             num_scalar_prefetch=3,
             grid=(len(widths), steps),
             in_specs=[
-                pl.BlockSpec((rows, at_once * QK), lambda i, p, m, *_: (m[first_chunk + i], p)),
-                pl.BlockSpec((rows, 128), lambda i, p, m, *_: (m[first_chunk + i], 0)),
-                pl.BlockSpec((rows, at_once * DV), lambda i, p, m, *_: (m[first_chunk + i], p)),
+                pl.BlockSpec((rows, at_once * QK), lambda i, p, m, *_: (m[2 + first_chunk + i], p)),
+                pl.BlockSpec((rows, 128), lambda i, p, m, *_: (m[2 + first_chunk + i], 0)),
+                pl.BlockSpec((rows, at_once * DV), lambda i, p, m, *_: (m[2 + first_chunk + i], p)),
             ]
             + [whole(x) for x in pools]
             + [pl.BlockSpec(memory_space=pl.ANY)],
@@ -595,8 +611,14 @@
     packed_rows = per_owner * BROWS
     bf16 = lambda *shape: jax.ShapeDtypeStruct(shape, BF16)
 
+    chips = n_head // 2
+    chip, core = head_at // 2, lax.rem(head_at, 2)
+    order = []
+    for step in list(range(1, chips)) + [0]:
+        target = lax.rem(chip + step, chips) * 2
+        order += [target + 1 - core, target + core]
+    where = jnp.stack([group, shard, shard * tokens] + order).astype(jnp.int32)
     rim_rows = rim_blocks * BROWS
-    where = jnp.stack([group, shard]).astype(jnp.int32)
     prep_out = [bf16(packed_rows + 3 * folds, 128), bf16(rim_rows, 128)]
     prep_out += [bf16(256, tokens)] * 2 + [bf16(tokens, 256)]
     packed, rim, even, odd, val = pl.pallas_call(
@@ -673,28 +695,21 @@
     pools = single_step(
         functools.partial(pool_kernel, groups, lists),
         "pool",
-        [shard.reshape(1)],
+        [where],
         [packed] + received,
-        [bf16(n_ctx * lists * KBLK, 256)] * 2
+        [bf16(n_ctx * lists * KBLK, 256), bf16(n_ctx * lists * KBLK, DV)]
         + [bf16(256, n_ctx * folds)] * 2
         + [bf16(n_ctx * folds, 256)],
         [pltpu.VMEM((n_ctx * folds, 256), BF16)],
     )
     rows = tokens // n_head
-    chips = n_head // 2
-    chip, core = head_at // 2, lax.rem(head_at, 2)
-    order = []
-    for step in list(range(1, chips)) + [0]:
-        target = lax.rem(chip + step, chips) * 2
-        order += [target + 1 - core, target + core]
-    meta = jnp.stack([shard * tokens] + order).astype(jnp.int32)
     across = [(i, i ^ 1) for i in range(n_head)]
 
     model = out_weight.shape[1]
 
     def project(first_chunk, widths):
         return chosen_and_project(
-            first_chunk, widths, rows, meta, slots, dead, queries, gates, mixed, pools, out_weight
+            first_chunk, widths, rows, where, slots, dead, queries, gates, mixed, pools, out_weight
         )
 
     sums = []
@@ -702,7 +717,7 @@
         other = lax.ppermute(project(1 + 2 * step, [[model]])[0], "head", across)
         mine = project(2 + 2 * step, [[model]])[0]
         summed = (mine.astype(F32) + other.astype(F32)).astype(BF16)
-        summed, meta = lax.optimization_barrier((summed, meta))
+        summed, where = lax.optimization_barrier((summed, where))
         sums.append(summed)
     *passed, kept = project(n_head - 1, [[model // 2] * 2, [model]])
     arrived = [jnp.concatenate([lax.ppermute(x, "head", across) for x in passed], axis=1)]

time: 201 us -> 200 us (level)
  no operation moved by 1% of the time
where the time goes in v6:
time: 200 us; the launch traced here: 199 us
  Pallas kernels  159 us (80%)
  starting transfers between devices  25.1 us (13%)
  waiting for transfers between devices  6.09 us (3%)
  other arithmetic  4.53 us (2%)
  local copies, waits for them, and re-layouts  4.07 us (2%)
    pallas_call x3, Pallas kernels, chosen_and_project(): pl.pallas_call(functools.partial(chosen_kernel, heads, (first_chunk, widt...  96.1 us
    pallas_call x2, Pallas kernels, near_branch(): pl.pallas_call(functools.partial(near_kernel, heads, rims is not None), g...  46.1 us
    ppermute x6, starting transfers between devices, ahead(): lax.ppermute(send, 'ctx', [(i, i + 2 * distance) for i in range(n_ctx - 2...  12.1 us
    pallas_call x3, Pallas kernels, single_step(): pl.pallas_call(kernel, grid_spec=pltpu.PrefetchScalarGridSpec(num_scalar_...  9.28 us
    ppermute x1, starting transfers between devices, local(): lax.ppermute(rim, 'ctx', [(i, i + 1) for i in range(1, n_ctx - 1, 2)])  4.39 us
    pallas_call x1, Pallas kernels, local(): pl.pallas_call(prep_kernel, grid_spec=pltpu.PrefetchScalarGridSpec(num_sc...  4.25 us
  transfers between devices with their start and end apart: 15, of which 5 were waited for; matrix products, arithmetic and copies ran while one was open for 1% of the time, Pallas kernels for 63%

profile of v6, /device:TPU:5, one launch (start us, length us, event | category | flops | bytes accessed | tf_op | source)
XLA Modules:
  0.0 199.0 jit_solution(9232696644783634705)
XLA Ops:
  0.0 0.7 stack.31.group_ref.where_ref.refs_0_
  0.7 4.3 %prep.1 = (bf16[2656,128]{1,0:T(8,128)(2,1)}, bf16[1280,128]{1,0:T(8,128)(2,1)}, bf16[256,1024]{1,0:T(8,128)(2,1)}, bf16[256,1024]{1,0:T(8,128)(2,1)}, bf16[1024,256]{1,0:T(8,128)(2,1)}) custom-call(s32[7]{0:T(128)} %stack.31.group_ref.where_ref.refs_0_, bf16[1024,768]{1,0:T(8,128)(2,1)} %keys_ref.1, bf16[1024,512]{1,0:T(8,128)(2,1)} %values_ref.1, ...), custom_call_target="tpu_custom_call" | custom-call | tf_op jit(solution)/shard_map/prep/pallas_call | solution.py:624
  4.9 4.4 %collective-permute-start.4 = (bf16[1280,128]{1,0:T(8,128)(2,1)}, bf16[1280,128]{1,0:T(8,128)(2,1)S(1)}, u32[]{:S(2)}, u32[]{:S(2)}) collective-permute-start(bf16[1280,128]{1,0:T(8,128)(2,1)} %get-tuple-element.52), channel_id=1, source_target_pairs={{4,8},{12,16},{20,24},{5,9},{13,17},{21,25},{6,10},{14,18},{22,26}... | collective-permute-start | bytes 983048 | tf_op jit(solution)/shard_map/ppermute | solution.py:662
  9.3 3.2 %plan.1 = (s32[33]{0:T(128)}, s32[65]{0:T(128)}, s32[65]{0:T(128)}) custom-call(s32[7]{0:T(128)} %stack.31.group_ref.where_ref.refs_0_, s32[4,4,16]{2,1,0:T(4,128)} %picks_ref), custom_call_target="tpu_custom_call" | custom-call | tf_op jit(solution)/shard_map/plan/pallas_call | solution.py:646
  12.5 1.3 collective-permute-start.2
  13.8 1.3 collective-permute-start.1
  15.1 1.3 collective-permute-start
  16.4 2.2 %collective-permute-done.2.refs_2_.refs_3_ = s32[33]{0:T(128)S(1)} collective-permute-done((s32[33]{0:T(128)}, s32[33]{0:T(128)S(1)}, u32[]{:S(2)}, u32[]{:S(2)}) %collective-permute-start.2) | collective-permute-done | bytes 164 | tf_op jit(solution)/shard_map/ppermute | solution.py:659
  19.1 0.7 collective-permute-done.refs_0_.refs_1_
  20.3 2.7 %pack.2 = (bf16[736,128]{1,0:T(8,128)(2,1)}, bf16[736,128]{1,0:T(8,128)(2,1)}, bf16[736,128]{1,0:T(8,128)(2,1)}) custom-call(s32[7]{0:T(128)} %stack.31.group_ref.where_ref.refs_0_, s32[33]{0:T(128)} %copy-done.11, s32[33]{0:T(128)} %copy-done.10, s32[33]{0:T(128)} %copy-done.9, bf16[2656,128]{1,0:T(8,128)(2,1)} %get-tuple-element.43.refs_3_.own_ref), custom_call_target="tpu_custom_call" | custom-call | tf_op jit(solution)/shard_map/pack/pallas_call | solution.py:576
  23.0 3.8 %collective-permute-start.5 = (bf16[736,128]{1,0:T(8,128)(2,1)}, bf16[736,128]{1,0:T(8,128)(2,1)S(1)}, u32[]{:S(2)}, u32[]{:S(2)}) collective-permute-start(bf16[736,128]{1,0:T(8,128)(2,1)} %get-tuple-element.55), channel_id=1, source_target_pairs={{0,8},{4,12},{8,16},{12,20},{16,24},{20,28},{1,9},{5,13},{9,17},{1... | collective-permute-start | bytes 565256 | tf_op jit(solution)/shard_map/ppermute | solution.py:678
  27.1 0.8 pad.4.gate_ref.refs_4_
  28.0 3.1 %collective-permute-start.7 = (bf16[736,128]{1,0:T(8,128)(2,1)S(1)}, bf16[736,128]{1,0:T(8,128)(2,1)S(1)}, u32[]{:S(2)}, u32[]{:S(2)}) collective-permute-start(bf16[736,128]{1,0:T(8,128)(2,1)S(1)} %copy-done.13), channel_id=1, source_target_pairs={{0,16},{4,20},{8,24},{12,28},{1,17},{5,21},{9,25},{13,29},{2,18},{... | collective-permute-start | bytes 565256 | tf_op jit(solution)/shard_map/ppermute | solution.py:678
  31.1 1.3 collective-permute-start.9
  32.4 26.4 %near_branch.2.refs_5_ = f32[1024,2048]{1,0:T(8,128)} custom-call(s32[7]{0:T(128)} %stack.31.group_ref.where_ref.refs_0_, bf16[1024,3072]{1,0:T(8,128)(2,1)} %refs_3_.5, f32[1024,128]{1,0:T(8,128)} %pad.4.gate_ref.refs_4_, bf16[256,1024]{1,0:T(8,128)(2,1)} %get-tuple-element.48.refs_0_, bf16[256,1024]{1,0:T(8,128)(2,1)} %get-tuple-element.49.refs_1_, ...), custom_call_target="tpu_custom_call" | custom-call | flops 402653184 | bytes 7340032 | tf_op jit(solution)/shard_map/near_branch/pallas_call | solution.py:421
  58.8 0.9 copy-done
  59.7 2.7 %pack.3 = (bf16[736,128]{1,0:T(8,128)(2,1)}, bf16[736,128]{1,0:T(8,128)(2,1)}, bf16[736,128]{1,0:T(8,128)(2,1)}, bf16[736,128]{1,0:T(8,128)(2,1)}) custom-call(s32[7]{0:T(128)} %stack.31.group_ref.where_ref.refs_0_, s32[33]{0:T(128)} %get-tuple-element.42.refs_0_, s32[33]{0:T(128)} %copy-done.11, s32[33]{0:T(128)} %copy-done.10, s32[33]{0:T(128)} %copy-done.9, ...), custom_call_target="tpu_custom_call" | custom-call | tf_op jit(solution)/shard_map/pack/pallas_call | solution.py:576
  62.4 1.3 collective-permute-start.6
  63.8 1.3 collective-permute-start.8
  65.1 1.3 collective-permute-start.10
  66.4 19.6 %near_branch.3.refs_5_ = f32[1024,2048]{1,0:T(8,128)} custom-call(s32[7]{0:T(128)} %stack.31.group_ref.where_ref.refs_0_, bf16[1024,3072]{1,0:T(8,128)(2,1)} %refs_3_.5, f32[1024,128]{1,0:T(8,128)} %pad.4.gate_ref.refs_4_, bf16[256,1024]{1,0:T(8,128)(2,1)} %get-tuple-element.48.refs_0_, ...), custom_call_target="tpu_custom_call", output_to_operand_aliasing={{}: (8, {})} | custom-call | flops 402653184 | bytes 7340032 | tf_op jit(solution)/shard_map/near_branch/pallas_call | solution.py:421
  86.1 0.6 copy-done.4
  87.0 3.9 %pool.1 = (bf16[2048,256]{1,0:T(8,128)(2,1)}, bf16[2048,128]{1,0:T(8,128)(2,1)}, bf16[256,256]{1,0:T(8,128)(2,1)}, bf16[256,256]{1,0:T(8,128)(2,1)}, bf16[256,256]{1,0:T(8,128)(2,1)}) custom-call(s32[7]{0:T(128)} %stack.31.group_ref.where_ref.refs_0_, bf16[2656,128]{1,0:T(8,128)(2,1)} %get-tuple-element.43.refs_3_.own_ref, ...), custom_call_target="tpu_custom_call" | custom-call | tf_op jit(solution)/shard_map/pool/pallas_call | solution.py:576
  90.9 24.7 %chosen_and_project.4 = bf16[256,2560]{1,0:T(8,128)(2,1)} custom-call(s32[7]{0:T(128)} %stack.31.group_ref.where_ref.refs_0_, s32[65]{0:T(128)} %get-tuple-element.40.refs_1_, s32[65]{0:T(128)} %get-tuple-element.41.refs_2_, bf16[1024,3072]{1,0:T(8,128)(2,1)} %refs_3_.5, f32[1024,128]{1,0:T(8,128)} %pad.4.gate_ref.refs_4_, f32[1024,2048]{1,0:T(8,128)} %near_branch.3.refs_5_, ...), custom_call_target="tpu_custom_call" | custom-call | flops 268435456 | bytes 5242880 | tf_op jit(solution)/shard_map/chosen_and_project/pallas_call | solution.py:540
  115.6 2.9 %collective-permute-start.11 = (bf16[256,2560]{1,0:T(8,128)(2,1)}, bf16[256,2560]{1,0:T(8,128)(2,1)S(1)}, u32[]{:S(2)}, u32[]{:S(2)}) collective-permute-start(bf16[256,2560]{1,0:T(8,128)(2,1)} %chosen_and_project.4), channel_id=1, source_target_pairs={{0,1},{1,0},{2,3},{3,2},{4,5},{5,4},{6,7},{7,6},{8,9},{9,8},{10,11... | collective-permute-start | bytes 3932168 | tf_op jit(solution)/shard_map/ppermute | solution.py:717
  118.5 25.0 %chosen_and_project.3 = bf16[256,2560]{1,0:T(8,128)(2,1)} custom-call(s32[7]{0:T(128)} %stack.31.group_ref.where_ref.refs_0_, s32[65]{0:T(128)} %get-tuple-element.40.refs_1_, s32[65]{0:T(128)} %get-tuple-element.41.refs_2_, bf16[1024,3072]{1,0:T(8,128)(2,1)} %refs_3_.5, f32[1024,128]{1,0:T(8,128)} %pad.4.gate_ref.refs_4_, f32[1024,2048]{1,0:T(8,128)} %near_branch.3.refs_5_, ...), custom_call_target="tpu_custom_call" | custom-call | flops 268435456 | bytes 5242880 | tf_op jit(solution)/shard_map/chosen_and_project/pallas_call | solution.py:540
  143.5 1.6 add_convert_fusion.1
  145.1 1.3 collective-permute-start.14
  146.4 46.5 %chosen_and_project.5 = (bf16[256,1280]{1,0:T(8,128)(2,1)}, bf16[256,1280]{1,0:T(8,128)(2,1)}, bf16[256,2560]{1,0:T(8,128)(2,1)}) custom-call(s32[7]{0:T(128)} %stack.31.group_ref.where_ref.refs_0_, s32[65]{0:T(128)} %get-tuple-element.40.refs_1_, s32[65]{0:T(128)} %get-tuple-element.41.refs_2_, bf16[1024,3072]{1,0:T(8,128)(2,1)} %refs_3_.5, ...), custom_call_target="tpu_custom_call" | custom-call | flops 268435456 | bytes 5242880 | tf_op jit(solution)/shard_map/chosen_and_project/pallas_call | solution.py:540
  193.4 1.8 collective-permute-done.12
  195.2 0.9 collective-permute-done.13
  196.2 2.8 %add_convert_fusion = bf16[256,2560]{1,0:T(8,128)(2,1)} fusion(bf16[256,2560]{1,0:T(8,128)(2,1)S(1)} %collective-permute-done.14, bf16[256,2560]{1,0:T(8,128)(2,1)} %get-tuple-element.67, bf16[256,1280]{1,0:T(8,128)(2,1)S(1)} %collective-permute-done.13, bf16[256,1280]{1,0:T(8,128)(2,1)S(1)} %collective-permute-done.12), kind=kLoop, calls=%fused_computation | loop fusion | flops 5898240 | bytes 5242880 | tf_op jit(solution)/shard_map/convert_element_type | solution.py:730
  (42 shorter events, 2.2 us)
Async XLA Ops:
  0.7 26.2 %copy-start.2 = (f32[1024,3,16]{0,2,1:T(8,128)S(1)}, f32[1024,3,16]{0,2,1:T(8,128)}, u32[]{:S(2)}) copy-start(f32[1024,3,16]{0,2,1:T(8,128)} %param.14) | copy-start | bytes 589828
  4.9 53.9 %collective-permute-start.3 = (bf16[2656,128]{1,0:T(8,128)(2,1)}, bf16[2656,128]{1,0:T(8,128)(2,1)S(1)}, u32[]{:S(2)}, u32[]{:S(2)}) collective-permute-start(bf16[2656,128]{1,0:T(8,128)(2,1)} %get-tuple-element.43.refs_3_.own_ref), channel_id=1, source_target_pairs={{0,4},{4,0},{8,12},{12,8},{16,20},{20,16},{24,28},{28,24},{1,5},{5... | collective-permute-start | bytes 2039816 | tf_op jit(solution)/shard_map/ppermute | solution.py:641
  4.9 60.2 %collective-permute-start.4 = (bf16[1280,128]{1,0:T(8,128)(2,1)}, bf16[1280,128]{1,0:T(8,128)(2,1)S(1)}, u32[]{:S(2)}, u32[]{:S(2)}) collective-permute-start(bf16[1280,128]{1,0:T(8,128)(2,1)} %get-tuple-element.52), channel_id=1, source_target_pairs={{4,8},{12,16},{20,24},{5,9},{13,17},{21,25},{6,10},{14,18},{22,26}... | collective-permute-start | bytes 983048 | tf_op jit(solution)/shard_map/ppermute | solution.py:662
  12.5 6.1 %collective-permute-start.2 = (s32[33]{0:T(128)}, s32[33]{0:T(128)S(1)}, u32[]{:S(2)}, u32[]{:S(2)}) collective-permute-start(s32[33]{0:T(128)} %get-tuple-element.42.refs_0_), channel_id=1, source_target_pairs={{24,0},{28,4},{25,1},{29,5},{26,2},{30,6},{27,3},{31,7}} | collective-permute-start | bytes 404 | tf_op jit(solution)/shard_map/ppermute | solution.py:659
  13.8 5.2 %collective-permute-start.1 = (s32[33]{0:T(128)}, s32[33]{0:T(128)S(1)}, u32[]{:S(2)}, u32[]{:S(2)}) collective-permute-start(s32[33]{0:T(128)} %get-tuple-element.42.refs_0_), channel_id=1, source_target_pairs={{16,0},{20,4},{24,8},{28,12},{17,1},{21,5},{25,9},{29,13},{18,2},{... | collective-permute-start | bytes 404 | tf_op jit(solution)/shard_map/ppermute | solution.py:659
  15.1 4.6 %collective-permute-start = (s32[33]{0:T(128)}, s32[33]{0:T(128)S(1)}, u32[]{:S(2)}, u32[]{:S(2)}) collective-permute-start(s32[33]{0:T(128)} %get-tuple-element.42.refs_0_), channel_id=1, source_target_pairs={{8,0},{12,4},{16,8},{20,12},{24,16},{28,20},{9,1},{13,5},{17,9},{2... | collective-permute-start | bytes 404 | tf_op jit(solution)/shard_map/ppermute | solution.py:659
  18.7 1.1 copy-start.9
  19.1 0.7 copy-start.10
  19.8 0.5 copy-start.11
  23.0 5.0 %copy-start.13 = (bf16[736,128]{1,0:T(8,128)(2,1)S(1)}, bf16[736,128]{1,0:T(8,128)(2,1)}, u32[]{:S(2)}) copy-start(bf16[736,128]{1,0:T(8,128)(2,1)} %get-tuple-element.57) | copy-start | bytes 565252
  23.0 8.1 %copy-start.12 = (bf16[736,128]{1,0:T(8,128)(2,1)S(1)}, bf16[736,128]{1,0:T(8,128)(2,1)}, u32[]{:S(2)}) copy-start(bf16[736,128]{1,0:T(8,128)(2,1)} %get-tuple-element.59) | copy-start | bytes 565252
  23.0 40.8 %collective-permute-start.5 = (bf16[736,128]{1,0:T(8,128)(2,1)}, bf16[736,128]{1,0:T(8,128)(2,1)S(1)}, u32[]{:S(2)}, u32[]{:S(2)}) collective-permute-start(bf16[736,128]{1,0:T(8,128)(2,1)} %get-tuple-element.55), channel_id=1, source_target_pairs={{0,8},{4,12},{8,16},{12,20},{16,24},{20,28},{1,9},{5,13},{9,17},{1... | collective-permute-start | bytes 565256 | tf_op jit(solution)/shard_map/ppermute | solution.py:678
  28.0 58.1 %collective-permute-start.7 = (bf16[736,128]{1,0:T(8,128)(2,1)S(1)}, bf16[736,128]{1,0:T(8,128)(2,1)S(1)}, u32[]{:S(2)}, u32[]{:S(2)}) collective-permute-start(bf16[736,128]{1,0:T(8,128)(2,1)S(1)} %copy-done.13), channel_id=1, source_target_pairs={{0,16},{4,20},{8,24},{12,28},{1,17},{5,21},{9,25},{13,29},{2,18},{... | collective-permute-start | bytes 565256 | tf_op jit(solution)/shard_map/ppermute | solution.py:678
  31.1 55.0 %collective-permute-start.9 = (bf16[736,128]{1,0:T(8,128)(2,1)S(1)}, bf16[736,128]{1,0:T(8,128)(2,1)S(1)}, u32[]{:S(2)}, u32[]{:S(2)}) collective-permute-start(bf16[736,128]{1,0:T(8,128)(2,1)S(1)} %copy-done.12), channel_id=1, source_target_pairs={{0,24},{4,28},{1,25},{5,29},{2,26},{6,30},{3,27},{7,31}} | collective-permute-start | bytes 565256 | tf_op jit(solution)/shard_map/ppermute | solution.py:678
  58.8 0.9 copy-start
  62.4 23.6 %collective-permute-start.6 = (bf16[736,128]{1,0:T(8,128)(2,1)}, bf16[736,128]{1,0:T(8,128)(2,1)S(1)}, u32[]{:S(2)}, u32[]{:S(2)}) collective-permute-start(bf16[736,128]{1,0:T(8,128)(2,1)} %get-tuple-element.56), channel_id=1, source_target_pairs={{0,8},{4,12},{8,16},{12,20},{16,24},{20,28},{1,9},{5,13},{9,17},{1... | collective-permute-start | bytes 565256 | tf_op jit(solution)/shard_map/ppermute | solution.py:678
  63.8 22.3 %copy-start.3 = (bf16[736,128]{1,0:T(8,128)(2,1)}, bf16[736,128]{1,0:T(8,128)(2,1)S(1)}, u32[]{:S(2)}) copy-start(bf16[736,128]{1,0:T(8,128)(2,1)S(1)} %collective-permute-done.5.refs_1_) | copy-start | bytes 565252
  63.8 22.3 %collective-permute-start.8 = (bf16[736,128]{1,0:T(8,128)(2,1)}, bf16[736,128]{1,0:T(8,128)(2,1)S(1)}, u32[]{:S(2)}, u32[]{:S(2)}) collective-permute-start(bf16[736,128]{1,0:T(8,128)(2,1)} %get-tuple-element.58), channel_id=1, source_target_pairs={{0,16},{4,20},{8,24},{12,28},{1,17},{5,21},{9,25},{13,29},{2,18},{... | collective-permute-start | bytes 565256 | tf_op jit(solution)/shard_map/ppermute | solution.py:678
  65.1 1.3 copy-start.1
  65.1 21.0 %collective-permute-start.10 = (bf16[736,128]{1,0:T(8,128)(2,1)}, bf16[736,128]{1,0:T(8,128)(2,1)S(1)}, u32[]{:S(2)}, u32[]{:S(2)}) collective-permute-start(bf16[736,128]{1,0:T(8,128)(2,1)} %get-tuple-element.60), channel_id=1, source_target_pairs={{0,24},{4,28},{1,25},{5,29},{2,26},{6,30},{3,27},{7,31}} | collective-permute-start | bytes 565256 | tf_op jit(solution)/shard_map/ppermute | solution.py:678
  86.0 0.7 copy-start.4
  86.1 0.8 copy-start.5
  86.1 0.8 copy-start.6
  86.1 0.9 copy-start.7
  86.1 0.9 copy-start.8
  115.6 27.8 %collective-permute-start.11 = (bf16[256,2560]{1,0:T(8,128)(2,1)}, bf16[256,2560]{1,0:T(8,128)(2,1)S(1)}, u32[]{:S(2)}, u32[]{:S(2)}) collective-permute-start(bf16[256,2560]{1,0:T(8,128)(2,1)} %chosen_and_project.4), channel_id=1, source_target_pairs={{0,1},{1,0},{2,3},{3,2},{4,5},{5,4},{6,7},{7,6},{8,9},{9,8},{10,11... | collective-permute-start | bytes 3932168 | tf_op jit(solution)/shard_map/ppermute | solution.py:717
  145.1 51.1 %collective-permute-start.14 = (bf16[256,2560]{1,0:T(8,128)(2,1)S(1)}, bf16[256,2560]{1,0:T(8,128)(2,1)S(1)}, u32[]{:S(2)}, u32[]{:S(2)}) collective-permute-start(bf16[256,2560]{1,0:T(8,128)(2,1)S(1)} %add_convert_fusion.1), channel_id=1, source_target_pairs={{0,2},{1,3},{2,0},{3,1},{4,6},{5,7},{6,4},{7,5},{8,10},{9,11},{10,... | collective-permute-start | bytes 3932168 | tf_op jit(solution)/shard_map/ppermute | solution.py:726
  192.9 2.4 %collective-permute-start.12 = (bf16[256,1280]{1,0:T(8,128)(2,1)}, bf16[256,1280]{1,0:T(8,128)(2,1)S(1)}, u32[]{:S(2)}, u32[]{:S(2)}) collective-permute-start(bf16[256,1280]{1,0:T(8,128)(2,1)} %get-tuple-element.68), channel_id=1, source_target_pairs={{0,1},{1,0},{2,3},{3,2},{4,5},{5,4},{6,7},{7,6},{8,9},{9,8},{10,11... | collective-permute-start | bytes 1966088 | tf_op jit(solution)/shard_map/ppermute | solution.py:723
  193.2 2.9 %collective-permute-start.13 = (bf16[256,1280]{1,0:T(8,128)(2,1)}, bf16[256,1280]{1,0:T(8,128)(2,1)S(1)}, u32[]{:S(2)}, u32[]{:S(2)}) collective-permute-start(bf16[256,1280]{1,0:T(8,128)(2,1)} %get-tuple-element.69), channel_id=1, source_target_pairs={{0,1},{1,0},{2,3},{3,2},{4,5},{5,4},{6,7},{7,6},{8,9},{9,8},{10,11... | collective-permute-start | bytes 1966088 | tf_op jit(solution)/shard_map/ppermute | solution.py:723

commit v7 on v6

--- a/solution.py
+++ b/solution.py
@@ -18,7 +18,7 @@
 QBLK = 256
 PAIR = 2 * QK
 BROWS = KBLK + KBLK // 2 + KBLK
-VMEM_LIMIT = 60 * 1024 * 1024
+VMEM_LIMIT = 58 * 1024 * 1024
 NEG = -1e30
 SCALE = QK ** (-0.5) * 1.4426950408889634
 LOW_TOTAL, HIGH_TOTAL = 2.0**-60, 2.0**100
@@ -51,19 +51,78 @@
     return jnp.concatenate([values, jnp.ones_like(values)], axis=1)
 
 
+def plan(group, shard, per_owner, picks_ref, lists_ref, slots_ref, dead_ref):
+    lists = picks_ref.shape[0]
+    total = lists_ref.shape[1] // lists * per_owner
+    width = slots_ref.shape[1]
+    picks = jnp.zeros((lists, PICKS), jnp.int32)
+    for each in range(picks_ref.shape[1]):
+        picks = jnp.where(group == each, picks_ref[:, each, :], picks)
+    block = iota(lists, total, 1)
+    hits = [block == picks[:, entry : entry + 1] for entry in range(PICKS)]
+    named = functools.reduce(jnp.logical_or, hits).astype(F32)
+    named = jnp.broadcast_to(jnp.max(named, axis=0, keepdims=True), (8, total))
+    row, col = iota(total, total, 0), iota(total, total, 1)
+    before = (lax.div(row, per_owner) == lax.div(col, per_owner)) & (row < col)
+    rank = jnp.dot(named, before.astype(F32), preferred_element_type=F32)
+    rank = jnp.minimum(rank, float(lists - 1))
+    inside = lax.rem(iota(8, total, 1), per_owner).astype(F32)
+    found = jnp.zeros((8, lists_ref.shape[1]), F32)
+    row, col = iota(total, lists_ref.shape[1], 0), iota(total, lists_ref.shape[1], 1)
+    for place in range(lists):
+        to = (col == lax.div(row, per_owner) * lists + place).astype(F32)
+        value = jnp.where(rank == float(place), named * inside, 0.0)
+        found = found + jnp.dot(value, to, preferred_element_type=F32)
+    lists_ref[...] = found[:1].astype(jnp.int32)
+
+    owner = lax.div(block, per_owner)
+    turn = (lax.div(shard, 2) - lax.div(owner, 2)) * 2 + ((owner ^ shard) & 1)
+    slot = jnp.clip(turn * lists + rank[:lists].astype(jnp.int32), 0, lists_ref.shape[1] - 1)
+    slot = slot.astype(F32)
+    first = shard * per_owner + iota(lists, 1, 0) * (QBLK // KBLK)
+    own = block == first
+
+    def pick_out(hit, values):
+        return jnp.sum(jnp.where(hit, values, 0.0), axis=1, keepdims=True)
+
+    lane = iota(lists, width, 1)
+    slots = jnp.where(lane == 0, pick_out(own, slot), 0.0)
+    dead = jnp.zeros((lists, width), F32)
+    seen = own.astype(F32)
+    at = jnp.ones((lists, 1), jnp.int32)
+    met = jnp.zeros((lists, 1), jnp.int32)
+    for entry, hit in enumerate(hits):
+        pick = picks[:, entry : entry + 1]
+        is_own = (pick == first).astype(jnp.int32)
+        gone = jnp.maximum(pick_out(hit, seen), (pick > first).astype(F32))
+        slots = jnp.where(lane == at, pick_out(hit, slot), slots)
+        dead = jnp.where(lane == at, gone, dead)
+        seen = jnp.maximum(seen, hit.astype(F32))
+        at = at + 1 - is_own * (1 - met)
+        met = jnp.maximum(met, is_own)
+    slots_ref[...] = slots.astype(jnp.int32)
+    dead_ref[...] = dead.astype(jnp.int32)
+
+
 def prep_kernel(
-    group_ref,
+    where_ref,
+    picks_ref,
     keys_ref,
     values_ref,
     kw_ref,
     vw_ref,
     packed_ref,
     rim_ref,
+    lists_ref,
+    slots_ref,
+    dead_ref,
     even_ref,
     odd_ref,
     val_ref,
 ):
-    odd = lax.rem(group_ref[0], 2) == 1
+    group, shard = where_ref[0], where_ref[1]
+    plan(group, shard, keys_ref.shape[0] // KBLK, picks_ref, lists_ref, slots_ref, dead_ref)
+    odd = lax.rem(group, 2) == 1
 
     def own_columns(ref):
         t0 = ref[:, :128].astype(F32)
@@ -107,78 +166,23 @@
     packed_ref[at + 2 * folds :] = fold(values.astype(F32), vw_ref[...])
 
 
-def plan_kernel(shape, where_ref, picks_ref, lists_ref, slots_ref, dead_ref, named, rank, seen):
-    n_ctx, lists, per_owner = shape
-    group, shard = where_ref[0], where_ref[1]
-    for owner in range(n_ctx):
-        named[owner] = 0
-    for entry in range(n_ctx * lists + 1):
-        lists_ref[entry] = 0
-
-    def mark(query_block, _):
-        for entry in range(PICKS):
-            block = picks_ref[query_block, group, entry]
-            owner = lax.div(block, per_owner)
-            named[owner] = named[owner] | (jnp.int32(1) << lax.rem(block, per_owner))
-        return 0
-
-    lax.fori_loop(0, lists, mark, 0)
-
-    def enlist(owner, _):
-        bits = named[owner]
-        count = jnp.int32(0)
-        for block in range(per_owner):
-            bit = (bits >> block) & 1
-            rank[owner * per_owner + block] = jnp.minimum(count, lists - 1)
-            taken = (bit == 1) & (count < lists)
-            lists_ref[jnp.where(taken, owner * lists + count, n_ctx * lists)] = block
-            count = count + bit
-        return 0
-
-    lax.fori_loop(0, n_ctx, enlist, 0)
-
-    def place(block):
-        owner = lax.div(block, per_owner)
-        turn = (lax.div(shard, 2) - lax.div(owner, 2)) * 2 + ((owner ^ shard) & 1)
-        return jnp.clip(turn * lists + rank[block], 0, n_ctx * lists - 1)
-
-    def one_list(query_block, _):
-        first = shard * per_owner + query_block * (QBLK // KBLK)
-        at = query_block * PICKS
-        for owner in range(n_ctx):
-            seen[owner] = 0
-        seen[shard] = jnp.int32(1) << lax.rem(first, per_owner)
-        slots_ref[at] = place(first)
-        dead_ref[at] = 0
-        at = at + 1
-        met = jnp.int32(0)
-        for entry in range(PICKS):
-            block = picks_ref[query_block, group, entry]
-            owner = lax.div(block, per_owner)
-            inside = lax.rem(block, per_owner)
-            before = (seen[owner] >> inside) & 1
-            own = jnp.where(block == first, 1, 0)
-            slots_ref[at] = place(block)
-            dead_ref[at] = before | jnp.where(block > first, 1, 0)
-            seen[owner] = seen[owner] | (jnp.int32(1) << inside)
-            at = at + 1 - (own & (1 - met))
-            met = met | own
-        return 0
-
-    lax.fori_loop(0, lists, one_list, 0)
-
-
 def pack_kernel(lists, beside, where_ref, *refs):
-    count = len(refs) // 2
-    named, ref, outs = refs[:count], refs[count], refs[count + 1 :]
+    count = (len(refs) - 2) // 2
+    named, ref, outs, sems = refs[:count], refs[count], refs[count + 1 : -1], refs[-1]
     shard = where_ref[1]
     owner = shard + 1 - 2 * lax.rem(shard, 2) if beside else shard
     data = ref.shape[0] - (outs[0].shape[0] - lists * BROWS)
+    copies = []
     for blocks, out in zip(named, outs):
         for place in range(lists):
-            at = pl.multiple_of(blocks[owner * lists + place] * BROWS, 16)
-            out[place * BROWS : (place + 1) * BROWS] = ref[pl.ds(at, BROWS)]
-        out[lists * BROWS :] = ref[data:]
+            at = pl.multiple_of(blocks[0, owner * lists + place] * BROWS, 16)
+            copies.append((ref.at[pl.ds(at, BROWS)], out.at[place * BROWS : (place + 1) * BROWS]))
+        copies.append((ref.at[data:], out.at[lists * BROWS :]))
+    copies = [pltpu.make_async_copy(*pair, sems.at[i]) for i, pair in enumerate(copies)]
+    for copy in copies:
+        copy.start()
+    for copy in copies:
+        copy.wait()
 
 
 def unpack(ref, at, count, step=1):
@@ -380,7 +384,8 @@
         ((num, den),) = parts
         total = gate(pair, side, n, 2) * (num / den)
         for p in range(n):
-            out_ref[:, head_columns(pair + p, side)] = total[p * QBLK : (p + 1) * QBLK]
+            part = total[p * QBLK : (p + 1) * QBLK]
+            out_ref[:, head_columns(pair + p, side)] = part.astype(BF16)
         return [den]
 
     tiles = [
@@ -403,7 +408,7 @@
         pl.BlockSpec((QBLK, at_once * QK), row_block),
         pl.BlockSpec((QBLK, 128), lambda i, p, *_: (i + first_block, 0)),
     ]
-    specs += [whole(x) for x in keys]
+    specs += [VMEM_SPEC] * len(keys)
     alias, scratch = {}, []
     if rims is not None:
         other, far = rims
@@ -427,7 +432,7 @@
             out_specs=pl.BlockSpec((QBLK, at_once * DV), row_block),
             scratch_shapes=scratch,
         ),
-        out_shape=jax.ShapeDtypeStruct((tokens, heads * DV), F32),
+        out_shape=jax.ShapeDtypeStruct((tokens, heads * DV), BF16),
         input_output_aliases=alias,
         compiler_params=pltpu.CompilerParams(vmem_limit_bytes=VMEM_LIMIT),
         cost_estimate=pl.CostEstimate(
@@ -452,7 +457,7 @@
     rows = q_ref.shape[0]
     count = q_ref.shape[1] // QK
     chunk_start = meta_ref[2 + first_chunk + turn] * rows
-    list_at = lax.div(chunk_start, QBLK) * PICKS
+    list_at = lax.div(chunk_start, QBLK)
     first_row = lax.rem(chunk_start, QBLK)
     position = meta_ref[2] + chunk_start
     copy = pltpu.make_async_copy(weight_ref, weight, weight_sem)
@@ -460,12 +465,12 @@
     @pl.when(step == 0)
     def _():
         for slot in range(PICKS):
-            source = pl.multiple_of(slots_ref[list_at + slot] * KBLK, KBLK)
+            source = pl.multiple_of(slots_ref[list_at, slot] * KBLK, KBLK)
             gathered[slot * KBLK : (slot + 1) * KBLK] = key_pool[pl.ds(source, KBLK)]
             val[slot * KBLK : (slot + 1) * KBLK] = with_ones(val_pool[pl.ds(source, KBLK)])
         for slot in range(1, PICKS):
 
-            @pl.when(dead_ref[list_at + slot] == 1)
+            @pl.when(dead_ref[list_at, slot] == 1)
             def _():
                 at = slice(slot * KBLK, (slot + 1) * KBLK)
                 gathered[at] = jnp.broadcast_to(gathered[:1], (KBLK, 256))
@@ -504,7 +509,7 @@
         total = total + gate(pair, side, n, 0) * (folded_num / folded_den)
         for p in range(n):
             cols = head_columns(pair + p, side)
-            mixed = near_ref[:, cols] + total[p * rows : (p + 1) * rows]
+            mixed = near_ref[:, cols].astype(F32) + total[p * rows : (p + 1) * rows]
             attended[step, :, cols] = mixed.astype(BF16)
         return [den, folded_den]
 
@@ -547,7 +552,7 @@
                 pl.BlockSpec((rows, 128), lambda i, p, m, *_: (m[2 + first_chunk + i], 0)),
                 pl.BlockSpec((rows, at_once * DV), lambda i, p, m, *_: (m[2 + first_chunk + i], p)),
             ]
-            + [whole(x) for x in pools]
+            + [VMEM_SPEC] * len(pools)
             + [pl.BlockSpec(memory_space=pl.ANY)],
             out_specs=[whole(out) for out in outs],
             scratch_shapes=[
@@ -571,15 +576,18 @@
     )(meta, slots, dead, queries, gates, near, *pools, out_weight)
 
 
-def single_step(kernel, name, scalars, arrays, outs, scratch=()):
+VMEM_SPEC = pl.BlockSpec(memory_space=pltpu.VMEM)
+
+
+def single_step(kernel, name, scalars, arrays, outs, scratch=(), in_spec=None, out_spec=None):
     whole = lambda x: pl.BlockSpec(x.shape, lambda i, *_: (0,) * len(x.shape))
     return pl.pallas_call(
         kernel,
         grid_spec=pltpu.PrefetchScalarGridSpec(
             num_scalar_prefetch=len(scalars),
             grid=(1,),
-            in_specs=[whole(x) for x in arrays],
-            out_specs=[whole(x) for x in outs],
+            in_specs=[in_spec or whole(x) for x in arrays],
+            out_specs=[out_spec or whole(x) for x in outs],
             scratch_shapes=list(scratch),
         ),
         out_shape=outs,
@@ -619,42 +627,30 @@
         order += [target + 1 - core, target + core]
     where = jnp.stack([group, shard, shard * tokens] + order).astype(jnp.int32)
     rim_rows = rim_blocks * BROWS
+    int32 = lambda *shape: jax.ShapeDtypeStruct(shape, jnp.int32)
     prep_out = [bf16(packed_rows + 3 * folds, 128), bf16(rim_rows, 128)]
+    prep_out += [int32(1, n_ctx * lists), int32(lists, 2 * PICKS), int32(lists, 2 * PICKS)]
     prep_out += [bf16(256, tokens)] * 2 + [bf16(tokens, 256)]
-    packed, rim, even, odd, val = pl.pallas_call(
+    packed, rim, named, slots, dead, even, odd, val = pl.pallas_call(
         prep_kernel,
         grid_spec=pltpu.PrefetchScalarGridSpec(
             num_scalar_prefetch=1,
             grid=(1,),
             in_specs=[
+                pl.BlockSpec(block_picks.shape, lambda i, g: (0, 0, 0)),
                 pl.BlockSpec((tokens, PAIR), lambda i, g: (0, g[0] // 2)),
                 pl.BlockSpec((tokens, DV), lambda i, g: (0, g[0])),
                 pl.BlockSpec((CBLK, PAIR), lambda i, g: (0, g[0] // 2)),
                 pl.BlockSpec((CBLK, DV), lambda i, g: (0, g[0])),
             ],
-            out_specs=[pl.BlockSpec(x.shape, lambda i, g: (0, 0)) for x in prep_out],
+            out_specs=[pl.BlockSpec(x.shape, lambda i, g: (0, 0)) for x in prep_out[:5]]
+            + [VMEM_SPEC] * 3,
         ),
         out_shape=prep_out,
         compiler_params=pltpu.CompilerParams(vmem_limit_bytes=VMEM_LIMIT),
         name="prep",
-    )(where, key_rows, value_rows, comp_key_weight, comp_value_weight)
+    )(where, block_picks, key_rows, value_rows, comp_key_weight, comp_value_weight)
     other = lax.ppermute(packed, "ctx", [(i, i ^ 1) for i in range(n_ctx)])
-    packed, block_picks = lax.optimization_barrier((packed, block_picks))
-    smem = pl.BlockSpec(memory_space=pltpu.SMEM)
-    plan_out = [jax.ShapeDtypeStruct((n_ctx * lists + 1,), jnp.int32)]
-    plan_out += [jax.ShapeDtypeStruct((lists * PICKS + 1,), jnp.int32)] * 2
-    named, slots, dead = pl.pallas_call(
-        functools.partial(plan_kernel, (n_ctx, lists, per_owner)),
-        in_specs=[smem] * 2,
-        out_specs=[smem] * 3,
-        out_shape=plan_out,
-        scratch_shapes=[
-            pltpu.SMEM((n_ctx,), jnp.int32),
-            pltpu.SMEM((n_ctx * per_owner,), jnp.int32),
-            pltpu.SMEM((n_ctx,), jnp.int32),
-        ],
-        name="plan",
-    )(where, block_picks)
     named = [named] + [
         lax.ppermute(named, "ctx", [(i, i - 2 * d) for i in range(2 * d, n_ctx)])
         for d in range(1, groups)
@@ -672,6 +668,8 @@
             [where, *lists_in],
             [rows],
             [sent] * len(lists_in),
+            [pltpu.SemaphoreType.DMA((len(lists_in) * (lists + 1),))],
+            pl.BlockSpec(memory_space=pl.ANY),
         )
 
     def ahead(send, distance):
@@ -701,6 +699,7 @@
         + [bf16(256, n_ctx * folds)] * 2
         + [bf16(n_ctx * folds, 256)],
         [pltpu.VMEM((n_ctx * folds, 256), BF16)],
+        out_spec=VMEM_SPEC,
     )
     rows = tokens // n_head
     across = [(i, i ^ 1) for i in range(n_head)]

time: 200 us -> 198 us (0.990)
  Pallas kernels: 159 us -> 156 us
    pallas_call x1 -> x0, Pallas kernels: 3.23 us -> none  [local(): pl.pallas_call(functools.partial(plan_kernel, (n_ctx, lists, per_owner)),...]
  transfers between devices with their start and end apart: 15 -> 15, of which waited for: 5 -> 5; matrix products, arithmetic and copies ran while one was open for 1% -> 1% of each run, Pallas kernels for 63% -> 62%
where the time goes in v7:
time: 198 us; the launch traced here: 197 us
  Pallas kernels  156 us (79%)
  starting transfers between devices  25.9 us (13%)
  waiting for transfers between devices  6.09 us (3%)
  other arithmetic  4.53 us (2%)
  local copies, waits for them, and re-layouts  3.95 us (2%)
    pallas_call x3, Pallas kernels, chosen_and_project(): pl.pallas_call(functools.partial(chosen_kernel, heads, (first_chunk, widt...  96.1 us
    pallas_call x2, Pallas kernels, near_branch(): pl.pallas_call(functools.partial(near_kernel, heads, rims is not None), g...  45.8 us
    ppermute x6, starting transfers between devices, ahead(): lax.ppermute(send, 'ctx', [(i, i + 2 * distance) for i in range(n_ctx - 2...  12.8 us
    pallas_call x3, Pallas kernels, single_step(): pl.pallas_call(kernel, grid_spec=pltpu.PrefetchScalarGridSpec(num_scalar_...  9.63 us
    pallas_call x1, Pallas kernels, local(): pl.pallas_call(prep_kernel, grid_spec=pltpu.PrefetchScalarGridSpec(num_sc...  4.62 us
    ppermute x1, starting transfers between devices, local(): lax.ppermute(rim, 'ctx', [(i, i + 1) for i in range(1, n_ctx - 1, 2)])  4.39 us
  transfers between devices with their start and end apart: 15, of which 5 were waited for; matrix products, arithmetic and copies ran while one was open for 1% of the time, Pallas kernels for 62%

profile of v7, /device:TPU:5, one launch (start us, length us, event | category | flops | bytes accessed | tf_op | source)
XLA Modules:
  0.0 197.0 jit_solution(17340747327203748818)
XLA Ops:
  0.0 0.6 stack.31.where_ref.refs_0_
  0.6 4.6 %prep.1 = (bf16[2656,128]{1,0:T(8,128)(2,1)}, bf16[1280,128]{1,0:T(8,128)(2,1)}, s32[1,32]{1,0:T(1,128)}, s32[4,32]{1,0:T(4,128)}, s32[4,32]{1,0:T(4,128)}, /*in...) custom-call(s32[7]{0:T(128)} %stack.31.where_ref.refs_0_, s32[4,4,16]{2,1,0:T(4,128)} %picks_ref.1, ...), custom_call_target="tpu_custom_call" | custom-call | tf_op jit(solution)/shard_map/prep/pallas_call | solution.py:634
  5.3 4.4 %collective-permute-start.4 = (bf16[1280,128]{1,0:T(8,128)(2,1)}, bf16[1280,128]{1,0:T(8,128)(2,1)S(1)}, u32[]{:S(2)}, u32[]{:S(2)}) collective-permute-start(bf16[1280,128]{1,0:T(8,128)(2,1)} %get-tuple-element.48), channel_id=1, source_target_pairs={{4,8},{12,16},{20,24},{5,9},{13,17},{21,25},{6,10},{14,18},{22,26}... | collective-permute-start | bytes 983048 | tf_op jit(solution)/shard_map/ppermute | solution.py:658
  9.6 1.3 collective-permute-start.2
  10.9 1.3 collective-permute-start.1
  12.2 1.3 collective-permute-start
  13.5 2.2 %collective-permute-done.2.refs_2_.refs_3_ = s32[1,32]{1,0:T(1,128)S(1)} collective-permute-done((s32[1,32]{1,0:T(1,128)}, s32[1,32]{1,0:T(1,128)S(1)}, u32[]{:S(2)}, u32[]{:S(2)}) %collective-permute-start.2) | collective-permute-done | bytes 160 | tf_op jit(solution)/shard_map/ppermute | solution.py:655
  16.2 0.7 collective-permute-done.refs_0_.refs_1_
  16.9 0.5 copy-done.11
  17.4 2.8 %pack.2 = (bf16[736,128]{1,0:T(8,128)(2,1)}, bf16[736,128]{1,0:T(8,128)(2,1)}, bf16[736,128]{1,0:T(8,128)(2,1)}) custom-call(s32[7]{0:T(128)} %stack.31.where_ref.refs_0_, s32[1,32]{1,0:T(1,128)} %copy-done.11, s32[1,32]{1,0:T(1,128)} %copy-done.10, s32[1,32]{1,0:T(1,128)} %copy-done.9, bf16[2656,128]{1,0:T(8,128)(2,1)} %get-tuple-element.39.refs_3_.own_ref), custom_call_target="tpu_custom_call" | custom-call | tf_op jit(solution)/shard_map/pack/pallas_call | solution.py:584
  20.2 3.9 %collective-permute-start.5 = (bf16[736,128]{1,0:T(8,128)(2,1)}, bf16[736,128]{1,0:T(8,128)(2,1)S(1)}, u32[]{:S(2)}, u32[]{:S(2)}) collective-permute-start(bf16[736,128]{1,0:T(8,128)(2,1)} %get-tuple-element.51), channel_id=1, source_target_pairs={{0,8},{4,12},{8,16},{12,20},{16,24},{20,28},{1,9},{5,13},{9,17},{1... | collective-permute-start | bytes 565256 | tf_op jit(solution)/shard_map/ppermute | solution.py:676
  24.4 0.8 pad.4.gate_ref.refs_4_
  25.3 3.4 %collective-permute-start.7 = (bf16[736,128]{1,0:T(8,128)(2,1)S(1)}, bf16[736,128]{1,0:T(8,128)(2,1)S(1)}, u32[]{:S(2)}, u32[]{:S(2)}) collective-permute-start(bf16[736,128]{1,0:T(8,128)(2,1)S(1)} %copy-done.13), channel_id=1, source_target_pairs={{0,16},{4,20},{8,24},{12,28},{1,17},{5,21},{9,25},{13,29},{2,18},{... | collective-permute-start | bytes 565256 | tf_op jit(solution)/shard_map/ppermute | solution.py:676
  28.6 1.3 collective-permute-start.9
  30.0 26.3 %near_branch.2.refs_5_ = bf16[1024,2048]{1,0:T(8,128)(2,1)} custom-call(s32[7]{0:T(128)} %stack.31.where_ref.refs_0_, bf16[1024,3072]{1,0:T(8,128)(2,1)} %refs_3_.5, f32[1024,128]{1,0:T(8,128)} %pad.4.gate_ref.refs_4_, bf16[256,1024]{1,0:T(8,128)(2,1)} %get-tuple-element.44.refs_0_, bf16[256,1024]{1,0:T(8,128)(2,1)} %get-tuple-element.45.refs_1_, ...), custom_call_target="tpu_custom_call" | custom-call | flops 402653184 | bytes 7340032 | tf_op jit(solution)/shard_map/near_branch/pallas_call | solution.py:426
  56.2 0.8 copy-done
  57.1 2.9 %pack.3 = (bf16[736,128]{1,0:T(8,128)(2,1)}, bf16[736,128]{1,0:T(8,128)(2,1)}, bf16[736,128]{1,0:T(8,128)(2,1)}, bf16[736,128]{1,0:T(8,128)(2,1)}) custom-call(s32[7]{0:T(128)} %stack.31.where_ref.refs_0_, s32[1,32]{1,0:T(1,128)} %get-tuple-element.38.refs_0_, s32[1,32]{1,0:T(1,128)} %copy-done.11, s32[1,32]{1,0:T(1,128)} %copy-done.10, s32[1,32]{1,0:T(1,128)} %copy-done.9, ...), custom_call_target="tpu_custom_call" | custom-call | tf_op jit(solution)/shard_map/pack/pallas_call | solution.py:584
  60.0 1.3 collective-permute-start.6
  61.4 1.6 collective-permute-start.8
  63.0 1.3 collective-permute-start.10
  64.3 19.5 %near_branch.3.refs_5_ = bf16[1024,2048]{1,0:T(8,128)(2,1)} custom-call(s32[7]{0:T(128)} %stack.31.where_ref.refs_0_, bf16[1024,3072]{1,0:T(8,128)(2,1)} %refs_3_.5, f32[1024,128]{1,0:T(8,128)} %pad.4.gate_ref.refs_4_, bf16[256,1024]{1,0:T(8,128)(2,1)} %get-tuple-element.44.refs_0_, ...), custom_call_target="tpu_custom_call", output_to_operand_aliasing={{}: (8, {})} | custom-call | flops 402653184 | bytes 7340032 | tf_op jit(solution)/shard_map/near_branch/pallas_call | solution.py:426
  83.9 0.6 copy-done.4
  84.8 3.9 %pool.1 = (bf16[2048,256]{1,0:T(8,128)(2,1)}, bf16[2048,128]{1,0:T(8,128)(2,1)}, bf16[256,256]{1,0:T(8,128)(2,1)}, bf16[256,256]{1,0:T(8,128)(2,1)}, bf16[256,256]{1,0:T(8,128)(2,1)}) custom-call(s32[7]{0:T(128)} %stack.31.where_ref.refs_0_, bf16[2656,128]{1,0:T(8,128)(2,1)} %get-tuple-element.39.refs_3_.own_ref, ...), custom_call_target="tpu_custom_call" | custom-call | tf_op jit(solution)/shard_map/pool/pallas_call | solution.py:584
  88.7 24.7 %chosen_and_project.4 = bf16[256,2560]{1,0:T(8,128)(2,1)} custom-call(s32[7]{0:T(128)} %stack.31.where_ref.refs_0_, s32[4,32]{1,0:T(4,128)} %get-tuple-element.36.refs_1_, s32[4,32]{1,0:T(4,128)} %get-tuple-element.37.refs_2_, bf16[1024,3072]{1,0:T(8,128)(2,1)} %refs_3_.5, f32[1024,128]{1,0:T(8,128)} %pad.4.gate_ref.refs_4_, ...), custom_call_target="tpu_custom_call" | custom-call | flops 268435456 | bytes 5242880 | tf_op jit(solution)/shard_map/chosen_and_project/pallas_call | solution.py:545
  113.4 3.0 %collective-permute-start.11 = (bf16[256,2560]{1,0:T(8,128)(2,1)}, bf16[256,2560]{1,0:T(8,128)(2,1)S(1)}, u32[]{:S(2)}, u32[]{:S(2)}) collective-permute-start(bf16[256,2560]{1,0:T(8,128)(2,1)} %chosen_and_project.4), channel_id=1, source_target_pairs={{0,1},{1,0},{2,3},{3,2},{4,5},{5,4},{6,7},{7,6},{8,9},{9,8},{10,11... | collective-permute-start | bytes 3932168 | tf_op jit(solution)/shard_map/ppermute | solution.py:716
  116.5 24.9 %chosen_and_project.3 = bf16[256,2560]{1,0:T(8,128)(2,1)} custom-call(s32[7]{0:T(128)} %stack.31.where_ref.refs_0_, s32[4,32]{1,0:T(4,128)} %get-tuple-element.36.refs_1_, s32[4,32]{1,0:T(4,128)} %get-tuple-element.37.refs_2_, bf16[1024,3072]{1,0:T(8,128)(2,1)} %refs_3_.5, f32[1024,128]{1,0:T(8,128)} %pad.4.gate_ref.refs_4_, ...), custom_call_target="tpu_custom_call" | custom-call | flops 268435456 | bytes 5242880 | tf_op jit(solution)/shard_map/chosen_and_project/pallas_call | solution.py:545
  141.4 1.6 add_convert_fusion.1
  143.0 1.3 collective-permute-start.14
  144.3 46.5 %chosen_and_project.5 = (bf16[256,1280]{1,0:T(8,128)(2,1)}, bf16[256,1280]{1,0:T(8,128)(2,1)}, bf16[256,2560]{1,0:T(8,128)(2,1)}) custom-call(s32[7]{0:T(128)} %stack.31.where_ref.refs_0_, s32[4,32]{1,0:T(4,128)} %get-tuple-element.36.refs_1_, s32[4,32]{1,0:T(4,128)} %get-tuple-element.37.refs_2_, bf16[1024,3072]{1,0:T(8,128)(2,1)} %refs_3_.5, ...), custom_call_target="tpu_custom_call" | custom-call | flops 268435456 | bytes 5242880 | tf_op jit(solution)/shard_map/chosen_and_project/pallas_call | solution.py:545
  191.4 1.8 collective-permute-done.12
  193.2 0.9 collective-permute-done.13
  194.2 2.8 %add_convert_fusion = bf16[256,2560]{1,0:T(8,128)(2,1)} fusion(bf16[256,2560]{1,0:T(8,128)(2,1)S(1)} %collective-permute-done.14, bf16[256,2560]{1,0:T(8,128)(2,1)} %get-tuple-element.63, bf16[256,1280]{1,0:T(8,128)(2,1)S(1)} %collective-permute-done.13, bf16[256,1280]{1,0:T(8,128)(2,1)S(1)} %collective-permute-done.12), kind=kLoop, calls=%fused_computation | loop fusion | flops 5898240 | bytes 5242880 | tf_op jit(solution)/shard_map/convert_element_type | solution.py:729
  (41 shorter events, 1.6 us)
Async XLA Ops:
  0.6 23.5 %copy-start.2 = (f32[1024,3,16]{0,2,1:T(8,128)S(1)}, f32[1024,3,16]{0,2,1:T(8,128)}, u32[]{:S(2)}) copy-start(f32[1024,3,16]{0,2,1:T(8,128)} %param.14) | copy-start | bytes 589828
  5.2 51.0 %collective-permute-start.3 = (bf16[2656,128]{1,0:T(8,128)(2,1)}, bf16[2656,128]{1,0:T(8,128)(2,1)S(1)}, u32[]{:S(2)}, u32[]{:S(2)}) collective-permute-start(bf16[2656,128]{1,0:T(8,128)(2,1)} %get-tuple-element.39.refs_3_.own_ref), channel_id=1, source_target_pairs={{0,4},{4,0},{8,12},{12,8},{16,20},{20,16},{24,28},{28,24},{1,5},{5... | collective-permute-start | bytes 2039816 | tf_op jit(solution)/shard_map/ppermute | solution.py:653
  5.3 57.7 %collective-permute-start.4 = (bf16[1280,128]{1,0:T(8,128)(2,1)}, bf16[1280,128]{1,0:T(8,128)(2,1)S(1)}, u32[]{:S(2)}, u32[]{:S(2)}) collective-permute-start(bf16[1280,128]{1,0:T(8,128)(2,1)} %get-tuple-element.48), channel_id=1, source_target_pairs={{4,8},{12,16},{20,24},{5,9},{13,17},{21,25},{6,10},{14,18},{22,26}... | collective-permute-start | bytes 983048 | tf_op jit(solution)/shard_map/ppermute | solution.py:658
  9.6 6.1 %collective-permute-start.2 = (s32[1,32]{1,0:T(1,128)}, s32[1,32]{1,0:T(1,128)S(1)}, u32[]{:S(2)}, u32[]{:S(2)}) collective-permute-start(s32[1,32]{1,0:T(1,128)} %get-tuple-element.38.refs_0_), channel_id=1, source_target_pairs={{24,0},{28,4},{25,1},{29,5},{26,2},{30,6},{27,3},{31,7}} | collective-permute-start | bytes 392 | tf_op jit(solution)/shard_map/ppermute | solution.py:655
  10.9 5.2 %collective-permute-start.1 = (s32[1,32]{1,0:T(1,128)}, s32[1,32]{1,0:T(1,128)S(1)}, u32[]{:S(2)}, u32[]{:S(2)}) collective-permute-start(s32[1,32]{1,0:T(1,128)} %get-tuple-element.38.refs_0_), channel_id=1, source_target_pairs={{16,0},{20,4},{24,8},{28,12},{17,1},{21,5},{25,9},{29,13},{18,2},{... | collective-permute-start | bytes 392 | tf_op jit(solution)/shard_map/ppermute | solution.py:655
  12.2 4.6 %collective-permute-start = (s32[1,32]{1,0:T(1,128)}, s32[1,32]{1,0:T(1,128)S(1)}, u32[]{:S(2)}, u32[]{:S(2)}) collective-permute-start(s32[1,32]{1,0:T(1,128)} %get-tuple-element.38.refs_0_), channel_id=1, source_target_pairs={{8,0},{12,4},{16,8},{20,12},{24,16},{28,20},{9,1},{13,5},{17,9},{2... | collective-permute-start | bytes 392 | tf_op jit(solution)/shard_map/ppermute | solution.py:655
  15.8 1.1 copy-start.9
  16.2 0.7 copy-start.10
  16.9 0.5 copy-start.11
  20.2 5.1 %copy-start.13 = (bf16[736,128]{1,0:T(8,128)(2,1)S(1)}, bf16[736,128]{1,0:T(8,128)(2,1)}, u32[]{:S(2)}) copy-start(bf16[736,128]{1,0:T(8,128)(2,1)} %get-tuple-element.53) | copy-start | bytes 565252
  20.2 8.4 %copy-start.12 = (bf16[736,128]{1,0:T(8,128)(2,1)S(1)}, bf16[736,128]{1,0:T(8,128)(2,1)}, u32[]{:S(2)}) copy-start(bf16[736,128]{1,0:T(8,128)(2,1)} %get-tuple-element.55) | copy-start | bytes 565252
  20.2 41.1 %collective-permute-start.5 = (bf16[736,128]{1,0:T(8,128)(2,1)}, bf16[736,128]{1,0:T(8,128)(2,1)S(1)}, u32[]{:S(2)}, u32[]{:S(2)}) collective-permute-start(bf16[736,128]{1,0:T(8,128)(2,1)} %get-tuple-element.51), channel_id=1, source_target_pairs={{0,8},{4,12},{8,16},{12,20},{16,24},{20,28},{1,9},{5,13},{9,17},{1... | collective-permute-start | bytes 565256 | tf_op jit(solution)/shard_map/ppermute | solution.py:676
  25.3 58.6 %collective-permute-start.7 = (bf16[736,128]{1,0:T(8,128)(2,1)S(1)}, bf16[736,128]{1,0:T(8,128)(2,1)S(1)}, u32[]{:S(2)}, u32[]{:S(2)}) collective-permute-start(bf16[736,128]{1,0:T(8,128)(2,1)S(1)} %copy-done.13), channel_id=1, source_target_pairs={{0,16},{4,20},{8,24},{12,28},{1,17},{5,21},{9,25},{13,29},{2,18},{... | collective-permute-start | bytes 565256 | tf_op jit(solution)/shard_map/ppermute | solution.py:676
  28.6 55.2 %collective-permute-start.9 = (bf16[736,128]{1,0:T(8,128)(2,1)S(1)}, bf16[736,128]{1,0:T(8,128)(2,1)S(1)}, u32[]{:S(2)}, u32[]{:S(2)}) collective-permute-start(bf16[736,128]{1,0:T(8,128)(2,1)S(1)} %copy-done.12), channel_id=1, source_target_pairs={{0,24},{4,28},{1,25},{5,29},{2,26},{6,30},{3,27},{7,31}} | collective-permute-start | bytes 565256 | tf_op jit(solution)/shard_map/ppermute | solution.py:676
  56.2 0.8 copy-start
  60.0 23.8 %collective-permute-start.6 = (bf16[736,128]{1,0:T(8,128)(2,1)}, bf16[736,128]{1,0:T(8,128)(2,1)S(1)}, u32[]{:S(2)}, u32[]{:S(2)}) collective-permute-start(bf16[736,128]{1,0:T(8,128)(2,1)} %get-tuple-element.52), channel_id=1, source_target_pairs={{0,8},{4,12},{8,16},{12,20},{16,24},{20,28},{1,9},{5,13},{9,17},{1... | collective-permute-start | bytes 565256 | tf_op jit(solution)/shard_map/ppermute | solution.py:676
  61.4 22.5 %copy-start.3 = (bf16[736,128]{1,0:T(8,128)(2,1)}, bf16[736,128]{1,0:T(8,128)(2,1)S(1)}, u32[]{:S(2)}) copy-start(bf16[736,128]{1,0:T(8,128)(2,1)S(1)} %collective-permute-done.5.refs_1_) | copy-start | bytes 565252
  61.4 22.5 %collective-permute-start.8 = (bf16[736,128]{1,0:T(8,128)(2,1)}, bf16[736,128]{1,0:T(8,128)(2,1)S(1)}, u32[]{:S(2)}, u32[]{:S(2)}) collective-permute-start(bf16[736,128]{1,0:T(8,128)(2,1)} %get-tuple-element.54), channel_id=1, source_target_pairs={{0,16},{4,20},{8,24},{12,28},{1,17},{5,21},{9,25},{13,29},{2,18},{... | collective-permute-start | bytes 565256 | tf_op jit(solution)/shard_map/ppermute | solution.py:676
  63.0 1.3 copy-start.1
  63.0 20.9 %collective-permute-start.10 = (bf16[736,128]{1,0:T(8,128)(2,1)}, bf16[736,128]{1,0:T(8,128)(2,1)S(1)}, u32[]{:S(2)}, u32[]{:S(2)}) collective-permute-start(bf16[736,128]{1,0:T(8,128)(2,1)} %get-tuple-element.56), channel_id=1, source_target_pairs={{0,24},{4,28},{1,25},{5,29},{2,26},{6,30},{3,27},{7,31}} | collective-permute-start | bytes 565256 | tf_op jit(solution)/shard_map/ppermute | solution.py:676
  83.8 0.7 copy-start.4
  83.9 0.7 copy-start.5
  83.9 0.8 copy-start.6
  83.9 0.8 copy-start.7
  83.9 0.9 copy-start.8
  113.4 28.0 %collective-permute-start.11 = (bf16[256,2560]{1,0:T(8,128)(2,1)}, bf16[256,2560]{1,0:T(8,128)(2,1)S(1)}, u32[]{:S(2)}, u32[]{:S(2)}) collective-permute-start(bf16[256,2560]{1,0:T(8,128)(2,1)} %chosen_and_project.4), channel_id=1, source_target_pairs={{0,1},{1,0},{2,3},{3,2},{4,5},{5,4},{6,7},{7,6},{8,9},{9,8},{10,11... | collective-permute-start | bytes 3932168 | tf_op jit(solution)/shard_map/ppermute | solution.py:716
  143.0 51.1 %collective-permute-start.14 = (bf16[256,2560]{1,0:T(8,128)(2,1)S(1)}, bf16[256,2560]{1,0:T(8,128)(2,1)S(1)}, u32[]{:S(2)}, u32[]{:S(2)}) collective-permute-start(bf16[256,2560]{1,0:T(8,128)(2,1)S(1)} %add_convert_fusion.1), channel_id=1, source_target_pairs={{0,2},{1,3},{2,0},{3,1},{4,6},{5,7},{6,4},{7,5},{8,10},{9,11},{10,... | collective-permute-start | bytes 3932168 | tf_op jit(solution)/shard_map/ppermute | solution.py:725
  190.9 2.4 %collective-permute-start.12 = (bf16[256,1280]{1,0:T(8,128)(2,1)}, bf16[256,1280]{1,0:T(8,128)(2,1)S(1)}, u32[]{:S(2)}, u32[]{:S(2)}) collective-permute-start(bf16[256,1280]{1,0:T(8,128)(2,1)} %get-tuple-element.64), channel_id=1, source_target_pairs={{0,1},{1,0},{2,3},{3,2},{4,5},{5,4},{6,7},{7,6},{8,9},{9,8},{10,11... | collective-permute-start | bytes 1966088 | tf_op jit(solution)/shard_map/ppermute | solution.py:722
  191.2 3.0 %collective-permute-start.13 = (bf16[256,1280]{1,0:T(8,128)(2,1)}, bf16[256,1280]{1,0:T(8,128)(2,1)S(1)}, u32[]{:S(2)}, u32[]{:S(2)}) collective-permute-start(bf16[256,1280]{1,0:T(8,128)(2,1)} %get-tuple-element.65), channel_id=1, source_target_pairs={{0,1},{1,0},{2,3},{3,2},{4,5},{5,4},{6,7},{7,6},{8,9},{9,8},{10,11... | collective-permute-start | bytes 1966088 | tf_op jit(solution)/shard_map/ppermute | solution.py:722

commit v8 on v7

--- a/solution.py
+++ b/solution.py
@@ -18,7 +18,7 @@
 QBLK = 256
 PAIR = 2 * QK
 BROWS = KBLK + KBLK // 2 + KBLK
-VMEM_LIMIT = 58 * 1024 * 1024
+VMEM_LIMIT = 50 * 1024 * 1024
 NEG = -1e30
 SCALE = QK ** (-0.5) * 1.4426950408889634
 LOW_TOTAL, HIGH_TOTAL = 2.0**-60, 2.0**100
@@ -106,11 +106,11 @@
 
 def prep_kernel(
     where_ref,
-    picks_ref,
-    keys_ref,
-    values_ref,
-    kw_ref,
-    vw_ref,
+    picks_in,
+    keys_in,
+    values_in,
+    kw_in,
+    vw_in,
     packed_ref,
     rim_ref,
     lists_ref,
@@ -119,9 +119,34 @@
     even_ref,
     odd_ref,
     val_ref,
+    picks_ref,
+    keys_ref,
+    values_ref,
+    kw_ref,
+    vw_ref,
+    sems,
 ):
     group, shard = where_ref[0], where_ref[1]
+    pair = pl.ds(pl.multiple_of(lax.div(group, 2) * PAIR, 128), PAIR)
+    single = pl.ds(pl.multiple_of(group * DV, 128), DV)
+    copies = [
+        pltpu.make_async_copy(source, target, sems.at[i])
+        for i, (source, target) in enumerate(
+            [
+                (picks_in, picks_ref),
+                (keys_in.at[:, pair], keys_ref),
+                (values_in.at[:, single], values_ref),
+                (kw_in.at[:, pair], kw_ref),
+                (vw_in.at[:, single], vw_ref),
+            ]
+        )
+    ]
+    for copy in copies:
+        copy.start()
+    copies[0].wait()
     plan(group, shard, keys_ref.shape[0] // KBLK, picks_ref, lists_ref, slots_ref, dead_ref)
+    for copy in copies[1:]:
+        copy.wait()
     odd = lax.rem(group, 2) == 1
 
     def own_columns(ref):
@@ -167,22 +192,16 @@
 
 
 def pack_kernel(lists, beside, where_ref, *refs):
-    count = (len(refs) - 2) // 2
-    named, ref, outs, sems = refs[:count], refs[count], refs[count + 1 : -1], refs[-1]
+    count = len(refs) // 2
+    named, ref, outs = refs[:count], refs[count], refs[count + 1 :]
     shard = where_ref[1]
     owner = shard + 1 - 2 * lax.rem(shard, 2) if beside else shard
     data = ref.shape[0] - (outs[0].shape[0] - lists * BROWS)
-    copies = []
     for blocks, out in zip(named, outs):
         for place in range(lists):
             at = pl.multiple_of(blocks[0, owner * lists + place] * BROWS, 16)
-            copies.append((ref.at[pl.ds(at, BROWS)], out.at[place * BROWS : (place + 1) * BROWS]))
-        copies.append((ref.at[data:], out.at[lists * BROWS :]))
-    copies = [pltpu.make_async_copy(*pair, sems.at[i]) for i, pair in enumerate(copies)]
-    for copy in copies:
-        copy.start()
-    for copy in copies:
-        copy.wait()
+            out[place * BROWS : (place + 1) * BROWS] = ref[pl.ds(at, BROWS)]
+        out[lists * BROWS :] = ref[data:]
 
 
 def unpack(ref, at, count, step=1):
@@ -215,10 +234,12 @@
     odd_ref[:, WINDOW:] = odd_in[:, :WINDOW]
     val_ref[WINDOW:] = val_in[:WINDOW]
     use_near = lax.rem(shard, 2) == 1
+    rim_end = near_ref.shape[0] // BROWS * BROWS
+    near_rim = near_ref[rim_end - far_ref.shape[0] : rim_end]
 
     @pl.when(shard > 0)
     def _():
-        keys, values = unpack(jnp.where(use_near, near_ref[...], far_ref[...]), 0, rim_blocks)
+        keys, values = unpack(jnp.where(use_near, near_rim, far_ref[...]), 0, rim_blocks)
         even_ref[:, :WINDOW], odd_ref[:, :WINDOW] = turned(keys)
         val_ref[:WINDOW] = with_ones(values)
 
@@ -402,7 +423,6 @@
     heads = width // QK
     at_once = 8 if heads % 8 == 0 else 2
     row_block = lambda i, p, *_: (i + first_block, p)
-    whole = lambda x: pl.BlockSpec(x.shape, lambda i, p, *_: (0,) * x.ndim)
     operands = [queries, gates, *keys]
     specs = [
         pl.BlockSpec((QBLK, at_once * QK), row_block),
@@ -412,14 +432,8 @@
     alias, scratch = {}, []
     if rims is not None:
         other, far = rims
-        rim_rows = far.shape[0]
-        last_rim = tokens // KBLK * BROWS // rim_rows - 1
         operands += [other, far, prior]
-        specs += [
-            pl.BlockSpec(far.shape, lambda i, p, *_: (last_rim, 0)),
-            whole(far),
-            pl.BlockSpec(memory_space=pl.ANY),
-        ]
+        specs += [VMEM_SPEC, VMEM_SPEC, pl.BlockSpec(memory_space=pl.ANY)]
         alias = {len(operands): 0}
         scratch = [pltpu.VMEM((256, 2 * WINDOW), BF16)] * 2 + [pltpu.VMEM((2 * WINDOW, 256), BF16)]
     rows = block_count * QBLK * heads
@@ -636,18 +650,21 @@
         grid_spec=pltpu.PrefetchScalarGridSpec(
             num_scalar_prefetch=1,
             grid=(1,),
-            in_specs=[
-                pl.BlockSpec(block_picks.shape, lambda i, g: (0, 0, 0)),
-                pl.BlockSpec((tokens, PAIR), lambda i, g: (0, g[0] // 2)),
-                pl.BlockSpec((tokens, DV), lambda i, g: (0, g[0])),
-                pl.BlockSpec((CBLK, PAIR), lambda i, g: (0, g[0] // 2)),
-                pl.BlockSpec((CBLK, DV), lambda i, g: (0, g[0])),
+            in_specs=[pl.BlockSpec(memory_space=pltpu.HBM)] * 5,
+            out_specs=[VMEM_SPEC] * 2
+            + [pl.BlockSpec(x.shape, lambda i, g: (0, 0)) for x in prep_out[2:5]]
+            + [VMEM_SPEC] * 3,
+            scratch_shapes=[
+                pltpu.VMEM(block_picks.shape, jnp.int32),
+                pltpu.VMEM((tokens, PAIR), BF16),
+                pltpu.VMEM((tokens, DV), BF16),
+                pltpu.VMEM((CBLK, PAIR), F32),
+                pltpu.VMEM((CBLK, DV), F32),
+                pltpu.SemaphoreType.DMA((5,)),
             ],
-            out_specs=[pl.BlockSpec(x.shape, lambda i, g: (0, 0)) for x in prep_out[:5]]
-            + [VMEM_SPEC] * 3,
         ),
         out_shape=prep_out,
-        compiler_params=pltpu.CompilerParams(vmem_limit_bytes=VMEM_LIMIT),
+        compiler_params=pltpu.CompilerParams(vmem_limit_bytes=51 * 1024 * 1024),
         name="prep",
     )(where, block_picks, key_rows, value_rows, comp_key_weight, comp_value_weight)
     other = lax.ppermute(packed, "ctx", [(i, i ^ 1) for i in range(n_ctx)])
@@ -668,25 +685,23 @@
             [where, *lists_in],
             [rows],
             [sent] * len(lists_in),
-            [pltpu.SemaphoreType.DMA((len(lists_in) * (lists + 1),))],
-            pl.BlockSpec(memory_space=pl.ANY),
+            in_spec=VMEM_SPEC,
+            out_spec=VMEM_SPEC,
         )
 
     def ahead(send, distance):
         return lax.ppermute(send, "ctx", [(i, i + 2 * distance) for i in range(n_ctx - 2 * distance)])
 
     own_sends = pack(False, named[1:], packed)
-    own_sends, even = lax.optimization_barrier((own_sends, even))
     from_same = [ahead(send, d) for d, send in enumerate(own_sends, 1)]
+    other, own_sends = lax.optimization_barrier((other, own_sends))
+    beside, *other_sends = pack(True, named, other)
+    other_sends, even = lax.optimization_barrier((other_sends, even))
+    from_other = [ahead(send, d) for d, send in enumerate(other_sends, 1)]
 
     reach = WINDOW // QBLK
     near = functools.partial(near_branch, where=where, queries=queries, gates=gates)
     mixed = near(reach, lists - reach, keys=(even, odd, val), rims=None, prior=None)
-
-    other, mixed = lax.optimization_barrier((other, mixed))
-    beside, *other_sends = pack(True, named, other)
-    from_other = [ahead(send, d) for d, send in enumerate(other_sends, 1)]
-
     mixed = near(0, reach, keys=(even, odd, val), rims=(other, far_rim), prior=mixed)
 
     received = [beside] + [x for both in zip(from_same, from_other) for x in both]
@@ -699,6 +714,7 @@
         + [bf16(256, n_ctx * folds)] * 2
         + [bf16(n_ctx * folds, 256)],
         [pltpu.VMEM((n_ctx * folds, 256), BF16)],
+        in_spec=VMEM_SPEC,
         out_spec=VMEM_SPEC,
     )
     rows = tokens // n_head

time: 198 us -> 197 us (level)
  Pallas kernels: 156 us -> 144 us
  starting transfers between devices: 25.9 us -> 36.1 us
  local copies, waits for them, and re-layouts: 3.95 us -> 6.2 us
    ppermute x6, starting transfers between devices: 12.8 us -> 18.3 us  [ahead(): lax.ppermute(send, 'ctx', [(i, i + 2 * distance) for i in range(n_ctx - 2...]
    pallas_call x3, Pallas kernels: 96.1 us -> 91.4 us  [chosen_and_project(): pl.pallas_call(functools.partial(chosen_kernel, heads, (first_chunk, widt...]
    ppermute x1, starting transfers between devices: 3.05 us -> 7.61 us  [local(): other = lax.ppermute(project(1 + 2 * step, [[model]])[0], 'head', across)]
    pallas_call x3, Pallas kernels: 9.63 us -> 5.18 us  [single_step(): pl.pallas_call(kernel, grid_spec=pltpu.PrefetchScalarGridSpec(num_scalar_...]
    pallas_call x1, Pallas kernels: 4.62 us -> 2.61 us  [local(): pl.pallas_call(prep_kernel, grid_spec=pltpu.PrefetchScalarGridSpec(num_sc...]
  transfers between devices with their start and end apart: 15 -> 15, of which waited for: 5 -> 5; matrix products, arithmetic and copies ran while one was open for 1% -> 2% of each run, Pallas kernels for 62% -> 59%
where the time goes in v8:
time: 197 us; the launch traced here: 196 us
  Pallas kernels  144 us (73%)
  starting transfers between devices  36.1 us (18%)
  local copies, waits for them, and re-layouts  6.2 us (3%)
  waiting for transfers between devices  5.83 us (3%)
  other arithmetic  3.89 us (2%)
    pallas_call x3, Pallas kernels, chosen_and_project(): pl.pallas_call(functools.partial(chosen_kernel, heads, (first_chunk, widt...  91.4 us
    pallas_call x2, Pallas kernels, near_branch(): pl.pallas_call(functools.partial(near_kernel, heads, rims is not None), g...  44.6 us
    ppermute x6, starting transfers between devices, ahead(): lax.ppermute(send, 'ctx', [(i, i + 2 * distance) for i in range(n_ctx - 2...  18.3 us
    ppermute x1, starting transfers between devices, local(): other = lax.ppermute(project(1 + 2 * step, [[model]])[0], 'head', across)  7.61 us
    pallas_call x3, Pallas kernels, single_step(): pl.pallas_call(kernel, grid_spec=pltpu.PrefetchScalarGridSpec(num_scalar_...  5.18 us
    ppermute x1, starting transfers between devices, local(): lax.ppermute(rim, 'ctx', [(i, i + 1) for i in range(1, n_ctx - 1, 2)])  4.38 us
  transfers between devices with their start and end apart: 15, of which 5 were waited for; matrix products, arithmetic and copies ran while one was open for 2% of the time, Pallas kernels for 59%

profile of v8, /device:TPU:5, one launch (start us, length us, event | category | flops | bytes accessed | tf_op | source)
XLA Modules:
  0.0 195.9 jit_solution(10169468411162744673)
XLA Ops:
  0.1 0.9 copy-done.2
  1.0 0.8 copy-done.3
  1.8 0.7 copy-done.4
  2.5 2.6 %prep.1 = (bf16[2656,128]{1,0:T(8,128)(2,1)S(1)}, bf16[1280,128]{1,0:T(8,128)(2,1)S(1)}, s32[1,32]{1,0:T(1,128)S(1)}, s32[4,32]{1,0:T(4,128)S(1)}, s32[4,32]{1,0...) custom-call(s32[7]{0:T(128)S(1)} %stack.31.where_ref.refs_0_, ...), custom_call_target="tpu_custom_call" | custom-call | tf_op jit(solution)/shard_map/prep/pallas_call | solution.py:648
  5.2 4.4 %collective-permute-start.4 = (bf16[1280,128]{1,0:T(8,128)(2,1)S(1)}, bf16[1280,128]{1,0:T(8,128)(2,1)S(1)}, u32[]{:S(2)}, u32[]{:S(2)}) collective-permute-start(bf16[1280,128]{1,0:T(8,128)(2,1)S(1)} %get-tuple-element.50), channel_id=1, source_target_pairs={{4,8},{12,16},{20,24},{5,9},{13,17},{21,25},{6,10},{14,18},{22,26}... | collective-permute-start | bytes 983048 | tf_op jit(solution)/shard_map/ppermute | solution.py:675
  9.6 1.3 collective-permute-start.2
  10.9 1.3 collective-permute-start.1
  12.2 1.3 collective-permute-start
  13.5 2.2 %collective-permute-done.2.refs_2_.refs_3_ = s32[1,32]{1,0:T(1,128)S(1)} collective-permute-done((s32[1,32]{1,0:T(1,128)S(1)}, s32[1,32]{1,0:T(1,128)S(1)}, u32[]{:S(2)}, u32[]{:S(2)}) %collective-permute-start.2) | collective-permute-done | bytes 160 | tf_op jit(solution)/shard_map/ppermute | solution.py:672
  16.1 0.7 collective-permute-done.refs_0_.refs_1_
  16.8 1.3 pack.2
  18.1 3.7 %collective-permute-start.5 = (bf16[736,128]{1,0:T(8,128)(2,1)S(1)}, bf16[736,128]{1,0:T(8,128)(2,1)S(1)}, u32[]{:S(2)}, u32[]{:S(2)}) collective-permute-start(bf16[736,128]{1,0:T(8,128)(2,1)S(1)} %get-tuple-element.39), channel_id=1, source_target_pairs={{0,8},{4,12},{8,16},{12,20},{16,24},{20,28},{1,9},{5,13},{9,17},{1... | collective-permute-start | bytes 565256 | tf_op jit(solution)/shard_map/ppermute | solution.py:693
  21.8 3.8 %collective-permute-start.7 = (bf16[736,128]{1,0:T(8,128)(2,1)}, bf16[736,128]{1,0:T(8,128)(2,1)}, u32[]{:S(2)}, u32[]{:S(2)}) collective-permute-start(bf16[736,128]{1,0:T(8,128)(2,1)} %get-tuple-element.40), channel_id=1, source_target_pairs={{0,16},{4,20},{8,24},{12,28},{1,17},{5,21},{9,25},{13,29},{2,18},{... | collective-permute-start | bytes 565256 | tf_op jit(solution)/shard_map/ppermute | solution.py:693
  25.6 2.0 %collective-permute-start.9 = (bf16[736,128]{1,0:T(8,128)(2,1)}, bf16[736,128]{1,0:T(8,128)(2,1)}, u32[]{:S(2)}, u32[]{:S(2)}) collective-permute-start(bf16[736,128]{1,0:T(8,128)(2,1)} %get-tuple-element.41), channel_id=1, source_target_pairs={{0,24},{4,28},{1,25},{5,29},{2,26},{6,30},{3,27},{7,31}} | collective-permute-start | bytes 565256 | tf_op jit(solution)/shard_map/ppermute | solution.py:693
  27.6 1.4 pack.3
  29.7 2.7 %collective-permute-start.6 = (bf16[736,128]{1,0:T(8,128)(2,1)}, bf16[736,128]{1,0:T(8,128)(2,1)}, u32[]{:S(2)}, u32[]{:S(2)}) collective-permute-start(bf16[736,128]{1,0:T(8,128)(2,1)} %get-tuple-element.52), channel_id=1, source_target_pairs={{0,8},{4,12},{8,16},{12,20},{16,24},{20,28},{1,9},{5,13},{9,17},{1... | collective-permute-start | bytes 565256 | tf_op jit(solution)/shard_map/ppermute | solution.py:693
  32.4 4.2 %collective-permute-start.8 = (bf16[736,128]{1,0:T(8,128)(2,1)}, bf16[736,128]{1,0:T(8,128)(2,1)}, u32[]{:S(2)}, u32[]{:S(2)}) collective-permute-start(bf16[736,128]{1,0:T(8,128)(2,1)} %get-tuple-element.53), channel_id=1, source_target_pairs={{0,16},{4,20},{8,24},{12,28},{1,17},{5,21},{9,25},{13,29},{2,18},{... | collective-permute-start | bytes 565256 | tf_op jit(solution)/shard_map/ppermute | solution.py:693
  36.6 2.0 %collective-permute-start.10 = (bf16[736,128]{1,0:T(8,128)(2,1)}, bf16[736,128]{1,0:T(8,128)(2,1)}, u32[]{:S(2)}, u32[]{:S(2)}) collective-permute-start(bf16[736,128]{1,0:T(8,128)(2,1)} %get-tuple-element.54), channel_id=1, source_target_pairs={{0,24},{4,28},{1,25},{5,29},{2,26},{6,30},{3,27},{7,31}} | collective-permute-start | bytes 565256 | tf_op jit(solution)/shard_map/ppermute | solution.py:693
  38.6 0.7 add_divide_fusion
  39.3 1.9 copy.11
  41.2 1.1 pad.4.gate_ref.refs_4_
  42.3 25.9 %near_branch.2.refs_5_ = bf16[1024,2048]{1,0:T(8,128)(2,1)} custom-call(s32[7]{0:T(128)S(1)} %stack.31.where_ref.refs_0_, bf16[1024,3072]{1,0:T(8,128)(2,1)} %refs_3_.5, f32[1024,128]{1,0:T(8,128)S(1)} %pad.4.gate_ref.refs_4_, bf16[256,1024]{1,0:T(8,128)(2,1)S(1)} %get-tuple-element.47.refs_0_, bf16[256,1024]{1,0:T(8,128)(2,1)S(1)} %get-tuple-element.48.refs_1_, ...), custom_call_target="tpu_custom_call" | custom-call | flops 402653184 | bytes 7340032 | tf_op jit(solution)/shard_map/near_branch/pallas_call | solution.py:440
  68.2 18.7 %near_branch.3.refs_5_ = bf16[1024,2048]{1,0:T(8,128)(2,1)} custom-call(s32[7]{0:T(128)S(1)} %stack.31.where_ref.refs_0_, bf16[1024,3072]{1,0:T(8,128)(2,1)} %refs_3_.5, f32[1024,128]{1,0:T(8,128)S(1)} %pad.4.gate_ref.refs_4_, bf16[256,1024]{1,0:T(8,128)(2,1)S(1)} %get-tuple-element.47.refs_0_, ...), custom_call_target="tpu_custom_call", output_to_operand_aliasing={{}: (8, {})} | custom-call | flops 402653184 | bytes 7340032 | tf_op jit(solution)/shard_map/near_branch/pallas_call | solution.py:440
  86.9 2.4 %pool.1 = (bf16[2048,256]{1,0:T(8,128)(2,1)S(1)}, bf16[2048,128]{1,0:T(8,128)(2,1)S(1)}, bf16[256,256]{1,0:T(8,128)(2,1)S(1)}, bf16[256,256]{1,0:T(8,128)(2,1)S(1)}, bf16[256,256]{1,0:T(8,128)(2,1)S(1)}) custom-call(s32[7]{0:T(128)S(1)} %stack.31.where_ref.refs_0_, bf16[2656,128]{1,0:T(8,128)(2,1)S(1)} %get-tuple-element.38.refs_3_.own_ref, ...), custom_call_target="tpu_custom_call" | custom-call | tf_op jit(solution)/shard_map/pool/pallas_call | solution.py:598
  89.3 22.9 %chosen_and_project.4 = bf16[256,2560]{1,0:T(8,128)(2,1)S(1)} custom-call(s32[7]{0:T(128)S(1)} %stack.31.where_ref.refs_0_, s32[4,32]{1,0:T(4,128)S(1)} %get-tuple-element.35.refs_1_, s32[4,32]{1,0:T(4,128)S(1)} %get-tuple-element.36.refs_2_, bf16[1024,3072]{1,0:T(8,128)(2,1)} %refs_3_.5, f32[1024,128]{1,0:T(8,128)S(1)} %pad.4.gate_ref.refs_4_, ...), custom_call_target="tpu_custom_call" | custom-call | flops 268435456 | bytes 5242880 | tf_op jit(solution)/shard_map/chosen_and_project/pallas_call | solution.py:559
  112.3 7.6 %collective-permute-start.11 = (bf16[256,2560]{1,0:T(8,128)(2,1)S(1)}, bf16[256,2560]{1,0:T(8,128)(2,1)S(1)}, u32[]{:S(2)}, u32[]{:S(2)}) collective-permute-start(bf16[256,2560]{1,0:T(8,128)(2,1)S(1)} %chosen_and_project.4), channel_id=1, source_target_pairs={{0,1},{1,0},{2,3},{3,2},{4,5},{5,4},{6,7},{7,6},{8,9},{9,8},{10,11... | collective-permute-start | bytes 3932168 | tf_op jit(solution)/shard_map/ppermute | solution.py:732
  119.9 23.1 %chosen_and_project.3 = bf16[256,2560]{1,0:T(8,128)(2,1)S(1)} custom-call(s32[7]{0:T(128)S(1)} %stack.31.where_ref.refs_0_, s32[4,32]{1,0:T(4,128)S(1)} %get-tuple-element.35.refs_1_, s32[4,32]{1,0:T(4,128)S(1)} %get-tuple-element.36.refs_2_, bf16[1024,3072]{1,0:T(8,128)(2,1)} %refs_3_.5, f32[1024,128]{1,0:T(8,128)S(1)} %pad.4.gate_ref.refs_4_, ...), custom_call_target="tpu_custom_call" | custom-call | flops 268435456 | bytes 5242880 | tf_op jit(solution)/shard_map/chosen_and_project/pallas_call | solution.py:559
  143.4 1.3 collective-permute-start.14
  144.7 45.3 %chosen_and_project.5 = (bf16[256,1280]{1,0:T(8,128)(2,1)S(1)}, bf16[256,1280]{1,0:T(8,128)(2,1)S(1)}, bf16[256,2560]{1,0:T(8,128)(2,1)}) custom-call(s32[7]{0:T(128)S(1)} %stack.31.where_ref.refs_0_, s32[4,32]{1,0:T(4,128)S(1)} %get-tuple-element.35.refs_1_, s32[4,32]{1,0:T(4,128)S(1)} %get-tuple-element.36.refs_2_, bf16[1024,3072]{1,0:T(8,128)(2,1)} %refs_3_.5, ...), custom_call_target="tpu_custom_call" | custom-call | flops 268435456 | bytes 5242880 | tf_op jit(solution)/shard_map/chosen_and_project/pallas_call | solution.py:559
  190.6 1.6 collective-permute-done.12
  192.2 0.9 collective-permute-done.13
  193.1 2.8 %add_convert_fusion = bf16[256,2560]{1,0:T(8,128)(2,1)} fusion(bf16[256,2560]{1,0:T(8,128)(2,1)S(1)} %collective-permute-done.14, bf16[256,2560]{1,0:T(8,128)(2,1)} %get-tuple-element.61, bf16[256,1280]{1,0:T(8,128)(2,1)S(1)} %collective-permute-done.13, bf16[256,1280]{1,0:T(8,128)(2,1)S(1)} %collective-permute-done.12), kind=kLoop, calls=%fused_computation | loop fusion | flops 5898240 | bytes 5242880 | tf_op jit(solution)/shard_map/convert_element_type | solution.py:745
  (25 shorter events, 2.2 us)
Async XLA Ops:
  0.1 0.9 copy-start.2
  1.0 0.8 copy-start.3
  1.8 0.7 copy-start.4
  2.5 36.1 %copy-start.5 = (f32[1024,3,16]{0,2,1:T(8,128)S(1)}, f32[1024,3,16]{0,2,1:T(8,128)}, u32[]{:S(2)}) copy-start(f32[1024,3,16]{0,2,1:T(8,128)} %param.14) | copy-start | bytes 589828
  5.1 22.4 %collective-permute-start.3 = (bf16[2656,128]{1,0:T(8,128)(2,1)S(1)}, bf16[2656,128]{1,0:T(8,128)(2,1)S(1)}, u32[]{:S(2)}, u32[]{:S(2)}) collective-permute-start(bf16[2656,128]{1,0:T(8,128)(2,1)S(1)} %get-tuple-element.38.refs_3_.own_ref), channel_id=1, source_target_pairs={{0,4},{4,0},{8,12},{12,8},{16,20},{20,16},{24,28},{28,24},{1,5},{5... | collective-permute-start | bytes 2039816 | tf_op jit(solution)/shard_map/ppermute | solution.py:670
  5.2 31.4 %collective-permute-start.4 = (bf16[1280,128]{1,0:T(8,128)(2,1)S(1)}, bf16[1280,128]{1,0:T(8,128)(2,1)S(1)}, u32[]{:S(2)}, u32[]{:S(2)}) collective-permute-start(bf16[1280,128]{1,0:T(8,128)(2,1)S(1)} %get-tuple-element.50), channel_id=1, source_target_pairs={{4,8},{12,16},{20,24},{5,9},{13,17},{21,25},{6,10},{14,18},{22,26}... | collective-permute-start | bytes 983048 | tf_op jit(solution)/shard_map/ppermute | solution.py:675
  9.6 6.1 %collective-permute-start.2 = (s32[1,32]{1,0:T(1,128)S(1)}, s32[1,32]{1,0:T(1,128)S(1)}, u32[]{:S(2)}, u32[]{:S(2)}) collective-permute-start(s32[1,32]{1,0:T(1,128)S(1)} %get-tuple-element.37.refs_0_), channel_id=1, source_target_pairs={{24,0},{28,4},{25,1},{29,5},{26,2},{30,6},{27,3},{31,7}} | collective-permute-start | bytes 392 | tf_op jit(solution)/shard_map/ppermute | solution.py:672
  10.9 5.2 %collective-permute-start.1 = (s32[1,32]{1,0:T(1,128)S(1)}, s32[1,32]{1,0:T(1,128)S(1)}, u32[]{:S(2)}, u32[]{:S(2)}) collective-permute-start(s32[1,32]{1,0:T(1,128)S(1)} %get-tuple-element.37.refs_0_), channel_id=1, source_target_pairs={{16,0},{20,4},{24,8},{28,12},{17,1},{21,5},{25,9},{29,13},{18,2},{... | collective-permute-start | bytes 392 | tf_op jit(solution)/shard_map/ppermute | solution.py:672
  12.2 4.6 %collective-permute-start = (s32[1,32]{1,0:T(1,128)S(1)}, s32[1,32]{1,0:T(1,128)S(1)}, u32[]{:S(2)}, u32[]{:S(2)}) collective-permute-start(s32[1,32]{1,0:T(1,128)S(1)} %get-tuple-element.37.refs_0_), channel_id=1, source_target_pairs={{8,0},{12,4},{16,8},{20,12},{24,16},{28,20},{9,1},{13,5},{17,9},{2... | collective-permute-start | bytes 392 | tf_op jit(solution)/shard_map/ppermute | solution.py:672
  18.1 14.3 %collective-permute-start.5 = (bf16[736,128]{1,0:T(8,128)(2,1)S(1)}, bf16[736,128]{1,0:T(8,128)(2,1)S(1)}, u32[]{:S(2)}, u32[]{:S(2)}) collective-permute-start(bf16[736,128]{1,0:T(8,128)(2,1)S(1)} %get-tuple-element.39), channel_id=1, source_target_pairs={{0,8},{4,12},{8,16},{12,20},{16,24},{20,28},{1,9},{5,13},{9,17},{1... | collective-permute-start | bytes 565256 | tf_op jit(solution)/shard_map/ppermute | solution.py:693
  21.8 65.0 %collective-permute-start.7 = (bf16[736,128]{1,0:T(8,128)(2,1)}, bf16[736,128]{1,0:T(8,128)(2,1)}, u32[]{:S(2)}, u32[]{:S(2)}) collective-permute-start(bf16[736,128]{1,0:T(8,128)(2,1)} %get-tuple-element.40), channel_id=1, source_target_pairs={{0,16},{4,20},{8,24},{12,28},{1,17},{5,21},{9,25},{13,29},{2,18},{... | collective-permute-start | bytes 565256 | tf_op jit(solution)/shard_map/ppermute | solution.py:693
  25.6 61.3 %collective-permute-start.9 = (bf16[736,128]{1,0:T(8,128)(2,1)}, bf16[736,128]{1,0:T(8,128)(2,1)}, u32[]{:S(2)}, u32[]{:S(2)}) collective-permute-start(bf16[736,128]{1,0:T(8,128)(2,1)} %get-tuple-element.41), channel_id=1, source_target_pairs={{0,24},{4,28},{1,25},{5,29},{2,26},{6,30},{3,27},{7,31}} | collective-permute-start | bytes 565256 | tf_op jit(solution)/shard_map/ppermute | solution.py:693
  29.0 0.7 copy-start
  29.7 57.2 %collective-permute-start.6 = (bf16[736,128]{1,0:T(8,128)(2,1)}, bf16[736,128]{1,0:T(8,128)(2,1)}, u32[]{:S(2)}, u32[]{:S(2)}) collective-permute-start(bf16[736,128]{1,0:T(8,128)(2,1)} %get-tuple-element.52), channel_id=1, source_target_pairs={{0,8},{4,12},{8,16},{12,20},{16,24},{20,28},{1,9},{5,13},{9,17},{1... | collective-permute-start | bytes 565256 | tf_op jit(solution)/shard_map/ppermute | solution.py:693
  32.4 54.5 %collective-permute-start.8 = (bf16[736,128]{1,0:T(8,128)(2,1)}, bf16[736,128]{1,0:T(8,128)(2,1)}, u32[]{:S(2)}, u32[]{:S(2)}) collective-permute-start(bf16[736,128]{1,0:T(8,128)(2,1)} %get-tuple-element.53), channel_id=1, source_target_pairs={{0,16},{4,20},{8,24},{12,28},{1,17},{5,21},{9,25},{13,29},{2,18},{... | collective-permute-start | bytes 565256 | tf_op jit(solution)/shard_map/ppermute | solution.py:693
  36.6 50.3 %collective-permute-start.10 = (bf16[736,128]{1,0:T(8,128)(2,1)}, bf16[736,128]{1,0:T(8,128)(2,1)}, u32[]{:S(2)}, u32[]{:S(2)}) collective-permute-start(bf16[736,128]{1,0:T(8,128)(2,1)} %get-tuple-element.54), channel_id=1, source_target_pairs={{0,24},{4,28},{1,25},{5,29},{2,26},{6,30},{3,27},{7,31}} | collective-permute-start | bytes 565256 | tf_op jit(solution)/shard_map/ppermute | solution.py:693
  68.2 18.7 %copy-start.1 = (bf16[736,128]{1,0:T(8,128)(2,1)S(1)}, bf16[736,128]{1,0:T(8,128)(2,1)}, u32[]{:S(2)}) copy-start(bf16[736,128]{1,0:T(8,128)(2,1)} %copy-done) | copy-start | bytes 565252
  112.3 30.8 %collective-permute-start.11 = (bf16[256,2560]{1,0:T(8,128)(2,1)S(1)}, bf16[256,2560]{1,0:T(8,128)(2,1)S(1)}, u32[]{:S(2)}, u32[]{:S(2)}) collective-permute-start(bf16[256,2560]{1,0:T(8,128)(2,1)S(1)} %chosen_and_project.4), channel_id=1, source_target_pairs={{0,1},{1,0},{2,3},{3,2},{4,5},{5,4},{6,7},{7,6},{8,9},{9,8},{10,11... | collective-permute-start | bytes 3932168 | tf_op jit(solution)/shard_map/ppermute | solution.py:732
  143.4 49.7 %collective-permute-start.14 = (bf16[256,2560]{1,0:T(8,128)(2,1)S(1)}, bf16[256,2560]{1,0:T(8,128)(2,1)S(1)}, u32[]{:S(2)}, u32[]{:S(2)}) collective-permute-start(bf16[256,2560]{1,0:T(8,128)(2,1)S(1)} %add_convert_fusion.1), channel_id=1, source_target_pairs={{0,2},{1,3},{2,0},{3,1},{4,6},{5,7},{6,4},{7,5},{8,10},{9,11},{10,... | collective-permute-start | bytes 3932168 | tf_op jit(solution)/shard_map/ppermute | solution.py:741
  190.0 2.2 %collective-permute-start.12 = (bf16[256,1280]{1,0:T(8,128)(2,1)S(1)}, bf16[256,1280]{1,0:T(8,128)(2,1)S(1)}, u32[]{:S(2)}, u32[]{:S(2)}) collective-permute-start(bf16[256,1280]{1,0:T(8,128)(2,1)S(1)} %get-tuple-element.62), channel_id=1, source_target_pairs={{0,1},{1,0},{2,3},{3,2},{4,5},{5,4},{6,7},{7,6},{8,9},{9,8},{10,11... | collective-permute-start | bytes 1966088 | tf_op jit(solution)/shard_map/ppermute | solution.py:738
  190.4 2.7 %collective-permute-start.13 = (bf16[256,1280]{1,0:T(8,128)(2,1)S(1)}, bf16[256,1280]{1,0:T(8,128)(2,1)S(1)}, u32[]{:S(2)}, u32[]{:S(2)}) collective-permute-start(bf16[256,1280]{1,0:T(8,128)(2,1)S(1)} %get-tuple-element.63), channel_id=1, source_target_pairs={{0,1},{1,0},{2,3},{3,2},{4,5},{5,4},{6,7},{7,6},{8,9},{9,8},{10,11... | collective-permute-start | bytes 1966088 | tf_op jit(solution)/shard_map/ppermute | solution.py:738

commit v9 on v8

--- a/solution.py
+++ b/solution.py
@@ -109,8 +109,7 @@
     picks_in,
     keys_in,
     values_in,
-    kw_in,
-    vw_in,
+    fold_in,
     packed_ref,
     rim_ref,
     lists_ref,
@@ -129,6 +128,7 @@
     group, shard = where_ref[0], where_ref[1]
     pair = pl.ds(pl.multiple_of(lax.div(group, 2) * PAIR, 128), PAIR)
     single = pl.ds(pl.multiple_of(group * DV, 128), DV)
+    folded_value = pl.ds(pl.multiple_of(GROUPS * QK + group * DV, 128), DV)
     copies = [
         pltpu.make_async_copy(source, target, sems.at[i])
         for i, (source, target) in enumerate(
@@ -136,8 +136,8 @@
                 (picks_in, picks_ref),
                 (keys_in.at[:, pair], keys_ref),
                 (values_in.at[:, single], values_ref),
-                (kw_in.at[:, pair], kw_ref),
-                (vw_in.at[:, single], vw_ref),
+                (fold_in.at[:, pair], kw_ref),
+                (fold_in.at[:, folded_value], vw_ref),
             ]
         )
     ]
@@ -641,6 +641,7 @@
         order += [target + 1 - core, target + core]
     where = jnp.stack([group, shard, shard * tokens] + order).astype(jnp.int32)
     rim_rows = rim_blocks * BROWS
+    fold_weights = jnp.concatenate([comp_key_weight, comp_value_weight], axis=1)
     int32 = lambda *shape: jax.ShapeDtypeStruct(shape, jnp.int32)
     prep_out = [bf16(packed_rows + 3 * folds, 128), bf16(rim_rows, 128)]
     prep_out += [int32(1, n_ctx * lists), int32(lists, 2 * PICKS), int32(lists, 2 * PICKS)]
@@ -650,7 +651,7 @@
         grid_spec=pltpu.PrefetchScalarGridSpec(
             num_scalar_prefetch=1,
             grid=(1,),
-            in_specs=[pl.BlockSpec(memory_space=pltpu.HBM)] * 5,
+            in_specs=[pl.BlockSpec(memory_space=pl.ANY)] * 4,
             out_specs=[VMEM_SPEC] * 2
             + [pl.BlockSpec(x.shape, lambda i, g: (0, 0)) for x in prep_out[2:5]]
             + [VMEM_SPEC] * 3,
@@ -666,7 +667,7 @@
         out_shape=prep_out,
         compiler_params=pltpu.CompilerParams(vmem_limit_bytes=51 * 1024 * 1024),
         name="prep",
-    )(where, block_picks, key_rows, value_rows, comp_key_weight, comp_value_weight)
+    )(where, block_picks, key_rows, value_rows, fold_weights)
     other = lax.ppermute(packed, "ctx", [(i, i ^ 1) for i in range(n_ctx)])
     named = [named] + [
         lax.ppermute(named, "ctx", [(i, i - 2 * d) for i in range(2 * d, n_ctx)])
@@ -692,16 +693,18 @@
     def ahead(send, distance):
         return lax.ppermute(send, "ctx", [(i, i + 2 * distance) for i in range(n_ctx - 2 * distance)])
 
+    named, gates = lax.optimization_barrier((named, gates))
     own_sends = pack(False, named[1:], packed)
+    own_sends, even = lax.optimization_barrier((own_sends, even))
     from_same = [ahead(send, d) for d, send in enumerate(own_sends, 1)]
-    other, own_sends = lax.optimization_barrier((other, own_sends))
-    beside, *other_sends = pack(True, named, other)
-    other_sends, even = lax.optimization_barrier((other_sends, even))
-    from_other = [ahead(send, d) for d, send in enumerate(other_sends, 1)]
 
     reach = WINDOW // QBLK
     near = functools.partial(near_branch, where=where, queries=queries, gates=gates)
     mixed = near(reach, lists - reach, keys=(even, odd, val), rims=None, prior=None)
+
+    other, mixed = lax.optimization_barrier((other, mixed))
+    beside, *other_sends = pack(True, named, other)
+    from_other = [ahead(send, d) for d, send in enumerate(other_sends, 1)]
     mixed = near(0, reach, keys=(even, odd, val), rims=(other, far_rim), prior=mixed)
 
     received = [beside] + [x for both in zip(from_same, from_other) for x in both]

time: 197 us -> 178 us (0.904)
  starting transfers between devices: 36.1 us -> 25.1 us
  local copies, waits for them, and re-layouts: 6.2 us -> 2.87 us
  waiting for transfers between devices: 5.83 us -> 2.56 us
  Pallas kernels: 144 us -> 142 us
    ppermute x6, starting transfers between devices: 18.3 us -> 12 us  [ahead(): lax.ppermute(send, 'ctx', [(i, i + 2 * distance) for i in range(n_ctx - 2...]
    ppermute x1, starting transfers between devices: 7.61 us -> 2.15 us  [local(): other = lax.ppermute(project(1 + 2 * step, [[model]])[0], 'head', across)]
    ppermute x3, waiting for transfers between devices: 3.28 us -> 0.01 us  [local(): lax.ppermute(named, 'ctx', [(i, i - 2 * d) for i in range(2 * d, n_ctx)])]
    pallas_call x3, Pallas kernels: 5.18 us -> 2.38 us  [single_step(): pl.pallas_call(kernel, grid_spec=pltpu.PrefetchScalarGridSpec(num_scalar_...]
    unnamed x12 -> x2, local copies, waits for them, and re-layouts: 3.11 us -> 0.7 us
  transfers between devices with their start and end apart: 15 -> 15, of which waited for: 5 -> 2; matrix products, arithmetic and copies ran while one was open for 2% -> 2% of each run, Pallas kernels for 59% -> 64%
where the time goes in v9:
time: 178 us
  Pallas kernels  142 us (80%)
  starting transfers between devices  25.1 us (14%)
  other arithmetic  5.1 us (3%)
  local copies, waits for them, and re-layouts  2.87 us (2%)
  waiting for transfers between devices  2.56 us (1%)
    pallas_call x3, Pallas kernels, chosen_and_project(): pl.pallas_call(functools.partial(chosen_kernel, heads, (first_chunk, widt...  91.8 us
    pallas_call x2, Pallas kernels, near_branch(): pl.pallas_call(functools.partial(near_kernel, heads, rims is not None), g...  44.5 us
    ppermute x6, starting transfers between devices, ahead(): lax.ppermute(send, 'ctx', [(i, i + 2 * distance) for i in range(n_ctx - 2...  12 us
    ppermute x1, starting transfers between devices, local(): lax.ppermute(rim, 'ctx', [(i, i + 1) for i in range(1, n_ctx - 1, 2)])  5.16 us
    ppermute x3, starting transfers between devices, local(): lax.ppermute(named, 'ctx', [(i, i - 2 * d) for i in range(2 * d, n_ctx)])  3.88 us
  transfers between devices with their start and end apart: 15, of which 2 were waited for; matrix products, arithmetic and copies ran while one was open for 2% of the time, Pallas kernels for 64%

profile of v9, /device:TPU:5, one launch (start us, length us, event | category | flops | bytes accessed | tf_op | source)
XLA Modules:
  0.0 177.8 jit_solution(14200904315848939063)
XLA Ops:
  0.0 0.9 pad_maximum_fusion.fold_in
  1.0 0.7 copy-done
  1.7 3.2 %prep.1 = (bf16[2656,128]{1,0:T(8,128)(2,1)S(1)}, bf16[1280,128]{1,0:T(8,128)(2,1)}, s32[1,32]{1,0:T(1,128)S(1)}, s32[4,32]{1,0:T(4,128)S(1)}, s32[4,32]{1,0:T(4...) custom-call(s32[7]{0:T(128)S(1)} %stack.31.where_ref.refs_0_, ...), custom_call_target="tpu_custom_call" | custom-call | tf_op jit(solution)/shard_map/prep/pallas_call | solution.py:649
  5.0 1.3 collective-permute-start.2
  6.3 1.3 collective-permute-start.1
  7.6 1.3 collective-permute-start
  8.9 5.2 %collective-permute-start.4 = (bf16[1280,128]{1,0:T(8,128)(2,1)}, bf16[1280,128]{1,0:T(8,128)(2,1)S(1)}, u32[]{:S(2)}, u32[]{:S(2)}) collective-permute-start(bf16[1280,128]{1,0:T(8,128)(2,1)} %get-tuple-element.57), channel_id=1, source_target_pairs={{4,8},{12,16},{20,24},{5,9},{13,17},{21,25},{6,10},{14,18},{22,26}... | collective-permute-start | bytes 983048 | tf_op jit(solution)/shard_map/ppermute | solution.py:676
  14.1 1.0 add_divide_fusion
  15.1 1.0 copy.11
  16.1 1.1 pad.4.gate_ref.refs_4_
  17.2 0.6 pack.2
  17.8 3.7 %collective-permute-start.5 = (bf16[736,128]{1,0:T(8,128)(2,1)S(1)}, bf16[736,128]{1,0:T(8,128)(2,1)S(1)}, u32[]{:S(2)}, u32[]{:S(2)}) collective-permute-start(bf16[736,128]{1,0:T(8,128)(2,1)S(1)} %get-tuple-element.61), channel_id=1, source_target_pairs={{0,8},{4,12},{8,16},{12,20},{16,24},{20,28},{1,9},{5,13},{9,17},{1... | collective-permute-start | bytes 565256 | tf_op jit(solution)/shard_map/ppermute | solution.py:694
  21.5 3.1 %collective-permute-start.7 = (bf16[736,128]{1,0:T(8,128)(2,1)S(1)}, bf16[736,128]{1,0:T(8,128)(2,1)S(1)}, u32[]{:S(2)}, u32[]{:S(2)}) collective-permute-start(bf16[736,128]{1,0:T(8,128)(2,1)S(1)} %get-tuple-element.63), channel_id=1, source_target_pairs={{0,16},{4,20},{8,24},{12,28},{1,17},{5,21},{9,25},{13,29},{2,18},{... | collective-permute-start | bytes 565256 | tf_op jit(solution)/shard_map/ppermute | solution.py:694
  24.6 1.3 collective-permute-start.9
  25.9 25.9 %near_branch.2.refs_5_ = bf16[1024,2048]{1,0:T(8,128)(2,1)} custom-call(s32[7]{0:T(128)S(1)} %stack.31.where_ref.refs_0_, bf16[1024,3072]{1,0:T(8,128)(2,1)} %refs_3_.5, f32[1024,128]{1,0:T(8,128)S(1)} %pad.4.gate_ref.refs_4_, bf16[256,1024]{1,0:T(8,128)(2,1)S(1)} %get-tuple-element.53.refs_0_, bf16[256,1024]{1,0:T(8,128)(2,1)S(1)} %get-tuple-element.54.refs_1_, ...), custom_call_target="tpu_custom_call" | custom-call | flops 402653184 | bytes 7340032 | tf_op jit(solution)/shard_map/near_branch/pallas_call | solution.py:440
  51.8 0.6 pack.3
  52.5 1.3 collective-permute-start.6
  53.8 1.3 collective-permute-start.8
  55.1 1.3 collective-permute-start.10
  56.4 18.6 %near_branch.3.refs_5_ = bf16[1024,2048]{1,0:T(8,128)(2,1)} custom-call(s32[7]{0:T(128)S(1)} %stack.31.where_ref.refs_0_, bf16[1024,3072]{1,0:T(8,128)(2,1)} %refs_3_.5, f32[1024,128]{1,0:T(8,128)S(1)} %pad.4.gate_ref.refs_4_, bf16[256,1024]{1,0:T(8,128)(2,1)S(1)} %get-tuple-element.53.refs_0_, ...), custom_call_target="tpu_custom_call", output_to_operand_aliasing={{}: (8, {})} | custom-call | flops 402653184 | bytes 7340032 | tf_op jit(solution)/shard_map/near_branch/pallas_call | solution.py:440
  75.1 1.2 pool.1
  76.2 23.0 %chosen_and_project.4 = bf16[256,2560]{1,0:T(8,128)(2,1)S(1)} custom-call(s32[7]{0:T(128)S(1)} %stack.31.where_ref.refs_0_, s32[4,32]{1,0:T(4,128)S(1)} %get-tuple-element.41.refs_1_, s32[4,32]{1,0:T(4,128)S(1)} %get-tuple-element.42.refs_2_, bf16[1024,3072]{1,0:T(8,128)(2,1)} %refs_3_.5, f32[1024,128]{1,0:T(8,128)S(1)} %pad.4.gate_ref.refs_4_, ...), custom_call_target="tpu_custom_call" | custom-call | flops 268435456 | bytes 5242880 | tf_op jit(solution)/shard_map/chosen_and_project/pallas_call | solution.py:559
  99.3 2.2 %collective-permute-start.11 = (bf16[256,2560]{1,0:T(8,128)(2,1)S(1)}, bf16[256,2560]{1,0:T(8,128)(2,1)S(1)}, u32[]{:S(2)}, u32[]{:S(2)}) collective-permute-start(bf16[256,2560]{1,0:T(8,128)(2,1)S(1)} %chosen_and_project.4), channel_id=1, source_target_pairs={{0,1},{1,0},{2,3},{3,2},{4,5},{5,4},{6,7},{7,6},{8,9},{9,8},{10,11... | collective-permute-start | bytes 3932168 | tf_op jit(solution)/shard_map/ppermute | solution.py:735
  101.4 23.2 %chosen_and_project.3 = bf16[256,2560]{1,0:T(8,128)(2,1)S(1)} custom-call(s32[7]{0:T(128)S(1)} %stack.31.where_ref.refs_0_, s32[4,32]{1,0:T(4,128)S(1)} %get-tuple-element.41.refs_1_, s32[4,32]{1,0:T(4,128)S(1)} %get-tuple-element.42.refs_2_, bf16[1024,3072]{1,0:T(8,128)(2,1)} %refs_3_.5, f32[1024,128]{1,0:T(8,128)S(1)} %pad.4.gate_ref.refs_4_, ...), custom_call_target="tpu_custom_call" | custom-call | flops 268435456 | bytes 5242880 | tf_op jit(solution)/shard_map/chosen_and_project/pallas_call | solution.py:559
  124.7 0.3 add_convert_fusion.1
  125.0 1.3 collective-permute-start.14
  126.3 45.5 %chosen_and_project.5 = (bf16[256,1280]{1,0:T(8,128)(2,1)S(1)}, bf16[256,1280]{1,0:T(8,128)(2,1)S(1)}, bf16[256,2560]{1,0:T(8,128)(2,1)}) custom-call(s32[7]{0:T(128)S(1)} %stack.31.where_ref.refs_0_, s32[4,32]{1,0:T(4,128)S(1)} %get-tuple-element.41.refs_1_, s32[4,32]{1,0:T(4,128)S(1)} %get-tuple-element.42.refs_2_, bf16[1024,3072]{1,0:T(8,128)(2,1)} %refs_3_.5, ...), custom_call_target="tpu_custom_call" | custom-call | flops 268435456 | bytes 5242880 | tf_op jit(solution)/shard_map/chosen_and_project/pallas_call | solution.py:559
  171.8 0.4 collective-permute-start.12
  172.2 0.2 collective-permute-start.13
  172.4 1.6 collective-permute-done.12
  174.0 0.9 collective-permute-done.13
  174.9 2.8 %add_convert_fusion = bf16[256,2560]{1,0:T(8,128)(2,1)} fusion(bf16[256,2560]{1,0:T(8,128)(2,1)S(1)} %collective-permute-done.14, bf16[256,2560]{1,0:T(8,128)(2,1)} %get-tuple-element.73, bf16[256,1280]{1,0:T(8,128)(2,1)S(1)} %collective-permute-done.13, bf16[256,1280]{1,0:T(8,128)(2,1)S(1)} %collective-permute-done.12), kind=kLoop, calls=%fused_computation | loop fusion | flops 5898240 | bytes 5242880 | tf_op jit(solution)/shard_map/convert_element_type | solution.py:748
  (16 shorter events, 0.2 us)
Async XLA Ops:
  1.0 0.7 copy-start
  4.9 46.9 %collective-permute-start.3 = (bf16[2656,128]{1,0:T(8,128)(2,1)S(1)}, bf16[2656,128]{1,0:T(8,128)(2,1)S(1)}, u32[]{:S(2)}, u32[]{:S(2)}) collective-permute-start(bf16[2656,128]{1,0:T(8,128)(2,1)S(1)} %get-tuple-element.48.refs_3_.own_ref), channel_id=1, source_target_pairs={{0,4},{4,0},{8,12},{12,8},{16,20},{20,16},{24,28},{28,24},{1,5},{5... | collective-permute-start | bytes 2039816 | tf_op jit(solution)/shard_map/ppermute | solution.py:671
  5.0 12.1 %collective-permute-start.2 = (s32[1,32]{1,0:T(1,128)S(1)}, s32[1,32]{1,0:T(1,128)S(1)}, u32[]{:S(2)}, u32[]{:S(2)}) collective-permute-start(s32[1,32]{1,0:T(1,128)S(1)} %get-tuple-element.59.refs_0_), channel_id=1, source_target_pairs={{24,0},{28,4},{25,1},{29,5},{26,2},{30,6},{27,3},{31,7}} | collective-permute-start | bytes 392 | tf_op jit(solution)/shard_map/ppermute | solution.py:673
  6.3 10.9 %collective-permute-start.1 = (s32[1,32]{1,0:T(1,128)S(1)}, s32[1,32]{1,0:T(1,128)S(1)}, u32[]{:S(2)}, u32[]{:S(2)}) collective-permute-start(s32[1,32]{1,0:T(1,128)S(1)} %get-tuple-element.59.refs_0_), channel_id=1, source_target_pairs={{16,0},{20,4},{24,8},{28,12},{17,1},{21,5},{25,9},{29,13},{18,2},{... | collective-permute-start | bytes 392 | tf_op jit(solution)/shard_map/ppermute | solution.py:673
  7.6 9.6 %collective-permute-start = (s32[1,32]{1,0:T(1,128)S(1)}, s32[1,32]{1,0:T(1,128)S(1)}, u32[]{:S(2)}, u32[]{:S(2)}) collective-permute-start(s32[1,32]{1,0:T(1,128)S(1)} %get-tuple-element.59.refs_0_), channel_id=1, source_target_pairs={{8,0},{12,4},{16,8},{20,12},{24,16},{28,20},{9,1},{13,5},{17,9},{2... | collective-permute-start | bytes 392 | tf_op jit(solution)/shard_map/ppermute | solution.py:673
  8.9 46.2 %collective-permute-start.4 = (bf16[1280,128]{1,0:T(8,128)(2,1)}, bf16[1280,128]{1,0:T(8,128)(2,1)S(1)}, u32[]{:S(2)}, u32[]{:S(2)}) collective-permute-start(bf16[1280,128]{1,0:T(8,128)(2,1)} %get-tuple-element.57), channel_id=1, source_target_pairs={{4,8},{12,16},{20,24},{5,9},{13,17},{21,25},{6,10},{14,18},{22,26}... | collective-permute-start | bytes 983048 | tf_op jit(solution)/shard_map/ppermute | solution.py:676
  17.8 36.0 %collective-permute-start.5 = (bf16[736,128]{1,0:T(8,128)(2,1)S(1)}, bf16[736,128]{1,0:T(8,128)(2,1)S(1)}, u32[]{:S(2)}, u32[]{:S(2)}) collective-permute-start(bf16[736,128]{1,0:T(8,128)(2,1)S(1)} %get-tuple-element.61), channel_id=1, source_target_pairs={{0,8},{4,12},{8,16},{12,20},{16,24},{20,28},{1,9},{5,13},{9,17},{1... | collective-permute-start | bytes 565256 | tf_op jit(solution)/shard_map/ppermute | solution.py:694
  21.5 53.5 %collective-permute-start.7 = (bf16[736,128]{1,0:T(8,128)(2,1)S(1)}, bf16[736,128]{1,0:T(8,128)(2,1)S(1)}, u32[]{:S(2)}, u32[]{:S(2)}) collective-permute-start(bf16[736,128]{1,0:T(8,128)(2,1)S(1)} %get-tuple-element.63), channel_id=1, source_target_pairs={{0,16},{4,20},{8,24},{12,28},{1,17},{5,21},{9,25},{13,29},{2,18},{... | collective-permute-start | bytes 565256 | tf_op jit(solution)/shard_map/ppermute | solution.py:694
  24.6 50.4 %collective-permute-start.9 = (bf16[736,128]{1,0:T(8,128)(2,1)S(1)}, bf16[736,128]{1,0:T(8,128)(2,1)S(1)}, u32[]{:S(2)}, u32[]{:S(2)}) collective-permute-start(bf16[736,128]{1,0:T(8,128)(2,1)S(1)} %get-tuple-element.65), channel_id=1, source_target_pairs={{0,24},{4,28},{1,25},{5,29},{2,26},{6,30},{3,27},{7,31}} | collective-permute-start | bytes 565256 | tf_op jit(solution)/shard_map/ppermute | solution.py:694
  52.5 22.6 %collective-permute-start.6 = (bf16[736,128]{1,0:T(8,128)(2,1)S(1)}, bf16[736,128]{1,0:T(8,128)(2,1)S(1)}, u32[]{:S(2)}, u32[]{:S(2)}) collective-permute-start(bf16[736,128]{1,0:T(8,128)(2,1)S(1)} %get-tuple-element.62), channel_id=1, source_target_pairs={{0,8},{4,12},{8,16},{12,20},{16,24},{20,28},{1,9},{5,13},{9,17},{1... | collective-permute-start | bytes 565256 | tf_op jit(solution)/shard_map/ppermute | solution.py:694
  53.8 21.3 %collective-permute-start.8 = (bf16[736,128]{1,0:T(8,128)(2,1)S(1)}, bf16[736,128]{1,0:T(8,128)(2,1)S(1)}, u32[]{:S(2)}, u32[]{:S(2)}) collective-permute-start(bf16[736,128]{1,0:T(8,128)(2,1)S(1)} %get-tuple-element.64), channel_id=1, source_target_pairs={{0,16},{4,20},{8,24},{12,28},{1,17},{5,21},{9,25},{13,29},{2,18},{... | collective-permute-start | bytes 565256 | tf_op jit(solution)/shard_map/ppermute | solution.py:694
  55.1 20.0 %collective-permute-start.10 = (bf16[736,128]{1,0:T(8,128)(2,1)S(1)}, bf16[736,128]{1,0:T(8,128)(2,1)S(1)}, u32[]{:S(2)}, u32[]{:S(2)}) collective-permute-start(bf16[736,128]{1,0:T(8,128)(2,1)S(1)} %get-tuple-element.66), channel_id=1, source_target_pairs={{0,24},{4,28},{1,25},{5,29},{2,26},{6,30},{3,27},{7,31}} | collective-permute-start | bytes 565256 | tf_op jit(solution)/shard_map/ppermute | solution.py:694
  99.3 25.4 %collective-permute-start.11 = (bf16[256,2560]{1,0:T(8,128)(2,1)S(1)}, bf16[256,2560]{1,0:T(8,128)(2,1)S(1)}, u32[]{:S(2)}, u32[]{:S(2)}) collective-permute-start(bf16[256,2560]{1,0:T(8,128)(2,1)S(1)} %chosen_and_project.4), channel_id=1, source_target_pairs={{0,1},{1,0},{2,3},{3,2},{4,5},{5,4},{6,7},{7,6},{8,9},{9,8},{10,11... | collective-permute-start | bytes 3932168 | tf_op jit(solution)/shard_map/ppermute | solution.py:735
  125.0 49.9 %collective-permute-start.14 = (bf16[256,2560]{1,0:T(8,128)(2,1)S(1)}, bf16[256,2560]{1,0:T(8,128)(2,1)S(1)}, u32[]{:S(2)}, u32[]{:S(2)}) collective-permute-start(bf16[256,2560]{1,0:T(8,128)(2,1)S(1)} %add_convert_fusion.1), channel_id=1, source_target_pairs={{0,2},{1,3},{2,0},{3,1},{4,6},{5,7},{6,4},{7,5},{8,10},{9,11},{10,... | collective-permute-start | bytes 3932168 | tf_op jit(solution)/shard_map/ppermute | solution.py:744
  171.8 2.2 %collective-permute-start.12 = (bf16[256,1280]{1,0:T(8,128)(2,1)S(1)}, bf16[256,1280]{1,0:T(8,128)(2,1)S(1)}, u32[]{:S(2)}, u32[]{:S(2)}) collective-permute-start(bf16[256,1280]{1,0:T(8,128)(2,1)S(1)} %get-tuple-element.74), channel_id=1, source_target_pairs={{0,1},{1,0},{2,3},{3,2},{4,5},{5,4},{6,7},{7,6},{8,9},{9,8},{10,11... | collective-permute-start | bytes 1966088 | tf_op jit(solution)/shard_map/ppermute | solution.py:741
  172.2 2.7 %collective-permute-start.13 = (bf16[256,1280]{1,0:T(8,128)(2,1)S(1)}, bf16[256,1280]{1,0:T(8,128)(2,1)S(1)}, u32[]{:S(2)}, u32[]{:S(2)}) collective-permute-start(bf16[256,1280]{1,0:T(8,128)(2,1)S(1)} %get-tuple-element.75), channel_id=1, source_target_pairs={{0,1},{1,0},{2,3},{3,2},{4,5},{5,4},{6,7},{7,6},{8,9},{9,8},{10,11... | collective-permute-start | bytes 1966088 | tf_op jit(solution)/shard_map/ppermute | solution.py:741

commit v10 on v9

--- a/solution.py
+++ b/solution.py
@@ -381,21 +381,21 @@
     return stacked(keep, rows // keep.shape[0])
 
 
-def near_kernel(heads, rim, where_ref, q_ref, gate_ref, *refs):
+def near_kernel(heads, first_block, rim, where_ref, q_ref, gate_ref, *refs):
     keys = refs[:3]
     if rim:
-        out_ref, ext = refs[6], refs[7:]
+        out_ref, ext = refs[-4], refs[-3:]
 
         @pl.when((pl.program_id(0) == 0) & (pl.program_id(1) == 0))
         def _():
             fill_rim(where_ref[1], refs[3], refs[4], keys, ext)
 
-        keys = ext
+        keys, reach = ext, 0
     else:
-        out_ref = refs[3]
+        out_ref, reach = refs[-1], WINDOW
     count = q_ref.shape[1] // QK
     gate = gate_loader(gate_ref, pl.program_id(1) * count, heads)
-    base = pl.multiple_of(pl.program_id(0) * QBLK, QBLK)
+    base = pl.multiple_of((first_block + pl.program_id(0)) * QBLK - reach, QBLK)
     row, col = iota(QBLK, QBLK, 0), iota(QBLK, QBLK, 1)
 
     def tile(place, mask):
@@ -432,13 +432,16 @@
     alias, scratch = {}, []
     if rims is not None:
         other, far = rims
-        operands += [other, far, prior]
-        specs += [VMEM_SPEC, VMEM_SPEC, pl.BlockSpec(memory_space=pl.ANY)]
+        operands += [other, far]
+        specs += [VMEM_SPEC, VMEM_SPEC]
+        scratch = [pltpu.VMEM((256, 2 * WINDOW), BF16)] * 2 + [pltpu.VMEM((2 * WINDOW, 256), BF16)]
+    if prior is not None:
+        operands.append(prior)
+        specs.append(pl.BlockSpec(memory_space=pl.ANY))
         alias = {len(operands): 0}
-        scratch = [pltpu.VMEM((256, 2 * WINDOW), BF16)] * 2 + [pltpu.VMEM((2 * WINDOW, 256), BF16)]
     rows = block_count * QBLK * heads
     return pl.pallas_call(
-        functools.partial(near_kernel, heads, rims is not None),
+        functools.partial(near_kernel, heads, first_block, rims is not None),
         grid_spec=pltpu.PrefetchScalarGridSpec(
             num_scalar_prefetch=1,
             grid=(block_count, heads // at_once),
@@ -568,7 +571,7 @@
             ]
             + [VMEM_SPEC] * len(pools)
             + [pl.BlockSpec(memory_space=pl.ANY)],
-            out_specs=[whole(out) for out in outs],
+            out_specs=[VMEM_SPEC] * len(outs),
             scratch_shapes=[
                 pltpu.VMEM((PICKS * KBLK, 256), BF16),
                 pltpu.VMEM((256, PICKS * KBLK), BF16),
@@ -608,6 +611,19 @@
         compiler_params=pltpu.CompilerParams(vmem_limit_bytes=VMEM_LIMIT),
         name=name,
     )(*scalars, *arrays)
+
+
+def last_sum(halves, rows, kept_ref, *refs):
+    halves, others, out_ref = refs[:halves], refs[halves:-1], refs[-1]
+    at = pl.ds(pl.multiple_of(pl.program_id(0) * rows, rows), rows)
+    first = 0
+    for half in halves:
+        cols = slice(first, first + half.shape[1])
+        total = kept_ref[:, cols].astype(F32) + half[at].astype(F32)
+        for other in others:
+            total = total + other[at, cols].astype(F32)
+        out_ref[:, cols] = total.astype(BF16)
+        first += half.shape[1]
 
 
 def local(
@@ -700,12 +716,16 @@
 
     reach = WINDOW // QBLK
     near = functools.partial(near_branch, where=where, queries=queries, gates=gates)
-    mixed = near(reach, lists - reach, keys=(even, odd, val), rims=None, prior=None)
+    near = functools.partial(near, keys=(even, odd, val))
+    mixed = near(lists - 1, 1, rims=None, prior=None)
 
     other, mixed = lax.optimization_barrier((other, mixed))
     beside, *other_sends = pack(True, named, other)
+    other_sends, mixed = lax.optimization_barrier((other_sends, mixed))
     from_other = [ahead(send, d) for d, send in enumerate(other_sends, 1)]
-    mixed = near(0, reach, keys=(even, odd, val), rims=(other, far_rim), prior=mixed)
+    if lists - reach > 1:
+        mixed = near(reach, lists - reach - 1, rims=None, prior=mixed)
+    mixed = near(0, reach, rims=(other, far_rim), prior=mixed)
 
     received = [beside] + [x for both in zip(from_same, from_other) for x in both]
     pools = single_step(
@@ -738,14 +758,22 @@
         summed, where = lax.optimization_barrier((summed, where))
         sums.append(summed)
     *passed, kept = project(n_head - 1, [[model // 2] * 2, [model]])
-    arrived = [jnp.concatenate([lax.ppermute(x, "head", across) for x in passed], axis=1)]
+    near_parts = [lax.ppermute(x, "head", across) for x in passed]
+    arrived = []
     for step, summed in enumerate(sums, 1):
         route = [(i, (i + 2 * step) % n_head) for i in range(n_head)]
         arrived.append(lax.ppermute(summed, "head", route))
-    total = kept.astype(F32)
-    for part in arrived:
-        total = total + part.astype(F32)
-    return total.astype(BF16)
+    steps = 4 if rows % 64 == 0 else 1
+    row_block = pl.BlockSpec((rows // steps, model), lambda i: (i, 0))
+    return pl.pallas_call(
+        functools.partial(last_sum, len(near_parts), rows // steps),
+        grid=(steps,),
+        in_specs=[row_block] + [VMEM_SPEC] * (len(near_parts) + len(arrived)),
+        out_specs=row_block,
+        out_shape=bf16(rows, model),
+        compiler_params=pltpu.CompilerParams(vmem_limit_bytes=VMEM_LIMIT),
+        name="last_sum",
+    )(kept, *near_parts, *arrived)
 
 
 def solution(mesh):

time: 178 us -> 180 us (1.011)
  Pallas kernels: 142 us -> 146 us
  other arithmetic: 5.1 us -> 1.32 us
    pallas_call x2 -> x4, Pallas kernels: 44.5 us -> 48.8 us  [the longest x3 46.9 us: near_branch(): pl.pallas_call(functools.partial(near_kernel, heads, first_block, rims is...]
    convert_element_type x1 -> x0, other arithmetic: 2.85 us -> none  [local(): return total.astype(BF16)]
  transfers between devices with their start and end apart: 15 -> 15, of which waited for: 2 -> 2; matrix products, arithmetic and copies ran while one was open for 2% -> 1% of each run, Pallas kernels for 64% -> 65%
where the time goes in v10:
time: 180 us; the launch traced here: 179 us
  Pallas kernels  146 us (81%)
  starting transfers between devices  25.1 us (14%)
  local copies, waits for them, and re-layouts  4.19 us (2%)
  waiting for transfers between devices  2.56 us (1%)
    pallas_call x3, Pallas kernels, chosen_and_project(): pl.pallas_call(functools.partial(chosen_kernel, heads, (first_chunk, widt...  91.2 us
    pallas_call x3, Pallas kernels, near_branch(): pl.pallas_call(functools.partial(near_kernel, heads, first_block, rims is...  46.9 us
    ppermute x6, starting transfers between devices, ahead(): lax.ppermute(send, 'ctx', [(i, i + 2 * distance) for i in range(n_ctx - 2...  12.6 us
    ppermute x1, starting transfers between devices, local(): lax.ppermute(rim, 'ctx', [(i, i + 1) for i in range(1, n_ctx - 1, 2)])  4.53 us
    ppermute x3, starting transfers between devices, local(): lax.ppermute(named, 'ctx', [(i, i - 2 * d) for i in range(2 * d, n_ctx)])  3.88 us
  transfers between devices with their start and end apart: 15, of which 2 were waited for; matrix products, arithmetic and copies ran while one was open for 1% of the time, Pallas kernels for 65%

profile of v10, /device:TPU:5, one launch (start us, length us, event | category | flops | bytes accessed | tf_op | source)
XLA Modules:
  0.0 178.9 jit_solution(3876540993102637009)
XLA Ops:
  0.0 0.9 pad_maximum_fusion.fold_in
  1.0 0.7 copy-done.1
  1.7 3.2 %prep.1 = (bf16[2656,128]{1,0:T(8,128)(2,1)S(1)}, bf16[1280,128]{1,0:T(8,128)(2,1)}, s32[1,32]{1,0:T(1,128)S(1)}, s32[4,32]{1,0:T(4,128)S(1)}, s32[4,32]{1,0:T(4...) custom-call(s32[7]{0:T(128)S(1)} %stack.31.where_ref.refs_0_, ...), custom_call_target="tpu_custom_call" | custom-call | tf_op jit(solution)/shard_map/prep/pallas_call | solution.py:665
  5.0 1.3 collective-permute-start
  6.3 1.3 collective-permute-start.1
  7.6 1.3 collective-permute-start.2
  8.9 4.5 %collective-permute-start.4 = (bf16[1280,128]{1,0:T(8,128)(2,1)}, bf16[1280,128]{1,0:T(8,128)(2,1)S(1)}, u32[]{:S(2)}, u32[]{:S(2)}) collective-permute-start(bf16[1280,128]{1,0:T(8,128)(2,1)} %get-tuple-element.61), channel_id=1, source_target_pairs={{4,8},{12,16},{20,24},{5,9},{13,17},{21,25},{6,10},{14,18},{22,26}... | collective-permute-start | bytes 983048 | tf_op jit(solution)/shard_map/ppermute | solution.py:692
  13.5 1.0 copy.12
  14.5 1.1 pad.4.gate_ref.refs_4_
  15.6 0.6 pack.2
  16.3 3.2 %collective-permute-start.5 = (bf16[736,128]{1,0:T(8,128)(2,1)S(1)}, bf16[736,128]{1,0:T(8,128)(2,1)S(1)}, u32[]{:S(2)}, u32[]{:S(2)}) collective-permute-start(bf16[736,128]{1,0:T(8,128)(2,1)S(1)} %get-tuple-element.69), channel_id=1, source_target_pairs={{0,8},{4,12},{8,16},{12,20},{16,24},{20,28},{1,9},{5,13},{9,17},{1... | collective-permute-start | bytes 565256 | tf_op jit(solution)/shard_map/ppermute | solution.py:710
  19.5 4.2 %collective-permute-start.7 = (bf16[736,128]{1,0:T(8,128)(2,1)S(1)}, bf16[736,128]{1,0:T(8,128)(2,1)S(1)}, u32[]{:S(2)}, u32[]{:S(2)}) collective-permute-start(bf16[736,128]{1,0:T(8,128)(2,1)S(1)} %get-tuple-element.71), channel_id=1, source_target_pairs={{0,16},{4,20},{8,24},{12,28},{1,17},{5,21},{9,25},{13,29},{2,18},{... | collective-permute-start | bytes 565256 | tf_op jit(solution)/shard_map/ppermute | solution.py:710
  23.7 1.3 collective-permute-start.9
  25.0 14.2 %near_branch.3.refs_3_ = bf16[1024,2048]{1,0:T(8,128)(2,1)} custom-call(s32[7]{0:T(128)S(1)} %stack.31.where_ref.refs_0_, bf16[1024,3072]{1,0:T(8,128)(2,1)} %refs_3_.5, f32[1024,128]{1,0:T(8,128)S(1)} %pad.4.gate_ref.refs_4_, bf16[256,1024]{1,0:T(8,128)(2,1)S(1)} %get-tuple-element.57.refs_0_, bf16[256,1024]{1,0:T(8,128)(2,1)S(1)} %get-tuple-element.58.refs_1_, ...), custom_call_target="tpu_custom_call" | custom-call | flops 201326592 | bytes 3670016 | tf_op jit(solution)/shard_map/near_branch/pallas_call | solution.py:443
  39.2 0.6 pack.3
  39.8 1.3 collective-permute-start.10
  41.1 1.3 collective-permute-start.6
  42.5 1.3 collective-permute-start.8
  43.8 14.1 %near_branch.4.refs_5_ = bf16[1024,2048]{1,0:T(8,128)(2,1)} custom-call(s32[7]{0:T(128)S(1)} %stack.31.where_ref.refs_0_, bf16[1024,3072]{1,0:T(8,128)(2,1)} %refs_3_.5, f32[1024,128]{1,0:T(8,128)S(1)} %pad.4.gate_ref.refs_4_, bf16[256,1024]{1,0:T(8,128)(2,1)S(1)} %get-tuple-element.57.refs_0_, ...), custom_call_target="tpu_custom_call", output_to_operand_aliasing={{}: (6, {})} | custom-call | flops 201326592 | bytes 3670016 | tf_op jit(solution)/shard_map/near_branch/pallas_call | solution.py:443
  57.9 18.6 %near_branch.5.refs_5_ = bf16[1024,2048]{1,0:T(8,128)(2,1)} custom-call(s32[7]{0:T(128)S(1)} %stack.31.where_ref.refs_0_, bf16[1024,3072]{1,0:T(8,128)(2,1)} %refs_3_.5, f32[1024,128]{1,0:T(8,128)S(1)} %pad.4.gate_ref.refs_4_, bf16[256,1024]{1,0:T(8,128)(2,1)S(1)} %get-tuple-element.57.refs_0_, ...), custom_call_target="tpu_custom_call", output_to_operand_aliasing={{}: (8, {})} | custom-call | flops 402653184 | bytes 7340032 | tf_op jit(solution)/shard_map/near_branch/pallas_call | solution.py:443
  76.6 1.2 pool.1
  77.7 22.9 %chosen_and_project.4 = bf16[256,2560]{1,0:T(8,128)(2,1)S(1)} custom-call(s32[7]{0:T(128)S(1)} %stack.31.where_ref.refs_0_, s32[4,32]{1,0:T(4,128)S(1)} %get-tuple-element.45.refs_1_, s32[4,32]{1,0:T(4,128)S(1)} %get-tuple-element.46.refs_2_, bf16[1024,3072]{1,0:T(8,128)(2,1)} %refs_3_.5, f32[1024,128]{1,0:T(8,128)S(1)} %pad.4.gate_ref.refs_4_, ...), custom_call_target="tpu_custom_call" | custom-call | flops 268435456 | bytes 5242880 | tf_op jit(solution)/shard_map/chosen_and_project/pallas_call | solution.py:562
  100.6 2.1 %collective-permute-start.11 = (bf16[256,2560]{1,0:T(8,128)(2,1)S(1)}, bf16[256,2560]{1,0:T(8,128)(2,1)S(1)}, u32[]{:S(2)}, u32[]{:S(2)}) collective-permute-start(bf16[256,2560]{1,0:T(8,128)(2,1)S(1)} %chosen_and_project.4), channel_id=1, source_target_pairs={{0,1},{1,0},{2,3},{3,2},{4,5},{5,4},{6,7},{7,6},{8,9},{9,8},{10,11... | collective-permute-start | bytes 3932168 | tf_op jit(solution)/shard_map/ppermute | solution.py:755
  102.8 23.1 %chosen_and_project.3 = bf16[256,2560]{1,0:T(8,128)(2,1)S(1)} custom-call(s32[7]{0:T(128)S(1)} %stack.31.where_ref.refs_0_, s32[4,32]{1,0:T(4,128)S(1)} %get-tuple-element.45.refs_1_, s32[4,32]{1,0:T(4,128)S(1)} %get-tuple-element.46.refs_2_, bf16[1024,3072]{1,0:T(8,128)(2,1)} %refs_3_.5, f32[1024,128]{1,0:T(8,128)S(1)} %pad.4.gate_ref.refs_4_, ...), custom_call_target="tpu_custom_call" | custom-call | flops 268435456 | bytes 5242880 | tf_op jit(solution)/shard_map/chosen_and_project/pallas_call | solution.py:562
  125.9 0.3 add_convert_fusion
  126.2 1.3 collective-permute-start.14
  127.5 45.2 %chosen_and_project.5 = (bf16[256,1280]{1,0:T(8,128)(2,1)S(1)}, bf16[256,1280]{1,0:T(8,128)(2,1)S(1)}, bf16[256,2560]{1,0:T(8,128)(2,1)}) custom-call(s32[7]{0:T(128)S(1)} %stack.31.where_ref.refs_0_, s32[4,32]{1,0:T(4,128)S(1)} %get-tuple-element.45.refs_1_, s32[4,32]{1,0:T(4,128)S(1)} %get-tuple-element.46.refs_2_, bf16[1024,3072]{1,0:T(8,128)(2,1)} %refs_3_.5, ...), custom_call_target="tpu_custom_call" | custom-call | flops 268435456 | bytes 5242880 | tf_op jit(solution)/shard_map/chosen_and_project/pallas_call | solution.py:562
  172.7 0.4 collective-permute-start.12
  173.3 1.6 collective-permute-done.12.refs_0_
  174.9 0.9 collective-permute-done.13.refs_1_
  175.8 1.3 copy-done
  177.1 1.8 %last_sum.1 = bf16[256,2560]{1,0:T(8,128)(2,1)} custom-call(bf16[256,2560]{1,0:T(8,128)(2,1)S(1)} %copy-done, bf16[256,1280]{1,0:T(8,128)(2,1)S(1)} %collective-permute-done.12.refs_0_, bf16[256,1280]{1,0:T(8,128)(2,1)S(1)} %collective-permute-done.13.refs_1_, bf16[256,2560]{1,0:T(8,128)(2,1)S(1)} %collective-permute-done.14.refs_2_), custom_call_target="tpu_custom_call" | custom-call | tf_op jit(solution)/shard_map/last_sum/pallas_call | solution.py:768
  (21 shorter events, 0.5 us)
Async XLA Ops:
  1.0 0.7 copy-start.1
  1.7 11.7 %copy-start.2 = (f32[1024,3,16]{0,2,1:T(8,128)S(1)}, f32[1024,3,16]{0,2,1:T(8,128)}, u32[]{:S(2)}) copy-start(f32[1024,3,16]{0,2,1:T(8,128)} %param.14) | copy-start | bytes 589828
  4.9 34.3 %collective-permute-start.3 = (bf16[2656,128]{1,0:T(8,128)(2,1)S(1)}, bf16[2656,128]{1,0:T(8,128)(2,1)S(1)}, u32[]{:S(2)}, u32[]{:S(2)}) collective-permute-start(bf16[2656,128]{1,0:T(8,128)(2,1)S(1)} %get-tuple-element.52.refs_3_.own_ref), channel_id=1, source_target_pairs={{0,4},{4,0},{8,12},{12,8},{16,20},{20,16},{24,28},{28,24},{1,5},{5... | collective-permute-start | bytes 2039816 | tf_op jit(solution)/shard_map/ppermute | solution.py:687
  5.0 10.6 %collective-permute-start = (s32[1,32]{1,0:T(1,128)S(1)}, s32[1,32]{1,0:T(1,128)S(1)}, u32[]{:S(2)}, u32[]{:S(2)}) collective-permute-start(s32[1,32]{1,0:T(1,128)S(1)} %get-tuple-element.62.refs_0_), channel_id=1, source_target_pairs={{8,0},{12,4},{16,8},{20,12},{24,16},{28,20},{9,1},{13,5},{17,9},{2... | collective-permute-start | bytes 392 | tf_op jit(solution)/shard_map/ppermute | solution.py:689
  6.3 9.3 %collective-permute-start.1 = (s32[1,32]{1,0:T(1,128)S(1)}, s32[1,32]{1,0:T(1,128)S(1)}, u32[]{:S(2)}, u32[]{:S(2)}) collective-permute-start(s32[1,32]{1,0:T(1,128)S(1)} %get-tuple-element.62.refs_0_), channel_id=1, source_target_pairs={{16,0},{20,4},{24,8},{28,12},{17,1},{21,5},{25,9},{29,13},{18,2},{... | collective-permute-start | bytes 392 | tf_op jit(solution)/shard_map/ppermute | solution.py:689
  7.6 8.0 %collective-permute-start.2 = (s32[1,32]{1,0:T(1,128)S(1)}, s32[1,32]{1,0:T(1,128)S(1)}, u32[]{:S(2)}, u32[]{:S(2)}) collective-permute-start(s32[1,32]{1,0:T(1,128)S(1)} %get-tuple-element.62.refs_0_), channel_id=1, source_target_pairs={{24,0},{28,4},{25,1},{29,5},{26,2},{30,6},{27,3},{31,7}} | collective-permute-start | bytes 392 | tf_op jit(solution)/shard_map/ppermute | solution.py:689
  8.9 33.5 %collective-permute-start.4 = (bf16[1280,128]{1,0:T(8,128)(2,1)}, bf16[1280,128]{1,0:T(8,128)(2,1)S(1)}, u32[]{:S(2)}, u32[]{:S(2)}) collective-permute-start(bf16[1280,128]{1,0:T(8,128)(2,1)} %get-tuple-element.61), channel_id=1, source_target_pairs={{4,8},{12,16},{20,24},{5,9},{13,17},{21,25},{6,10},{14,18},{22,26}... | collective-permute-start | bytes 983048 | tf_op jit(solution)/shard_map/ppermute | solution.py:692
  16.3 24.9 %collective-permute-start.5 = (bf16[736,128]{1,0:T(8,128)(2,1)S(1)}, bf16[736,128]{1,0:T(8,128)(2,1)S(1)}, u32[]{:S(2)}, u32[]{:S(2)}) collective-permute-start(bf16[736,128]{1,0:T(8,128)(2,1)S(1)} %get-tuple-element.69), channel_id=1, source_target_pairs={{0,8},{4,12},{8,16},{12,20},{16,24},{20,28},{1,9},{5,13},{9,17},{1... | collective-permute-start | bytes 565256 | tf_op jit(solution)/shard_map/ppermute | solution.py:710
  19.5 57.1 %collective-permute-start.7 = (bf16[736,128]{1,0:T(8,128)(2,1)S(1)}, bf16[736,128]{1,0:T(8,128)(2,1)S(1)}, u32[]{:S(2)}, u32[]{:S(2)}) collective-permute-start(bf16[736,128]{1,0:T(8,128)(2,1)S(1)} %get-tuple-element.71), channel_id=1, source_target_pairs={{0,16},{4,20},{8,24},{12,28},{1,17},{5,21},{9,25},{13,29},{2,18},{... | collective-permute-start | bytes 565256 | tf_op jit(solution)/shard_map/ppermute | solution.py:710
  23.7 52.8 %collective-permute-start.9 = (bf16[736,128]{1,0:T(8,128)(2,1)S(1)}, bf16[736,128]{1,0:T(8,128)(2,1)S(1)}, u32[]{:S(2)}, u32[]{:S(2)}) collective-permute-start(bf16[736,128]{1,0:T(8,128)(2,1)S(1)} %get-tuple-element.73), channel_id=1, source_target_pairs={{0,24},{4,28},{1,25},{5,29},{2,26},{6,30},{3,27},{7,31}} | collective-permute-start | bytes 565256 | tf_op jit(solution)/shard_map/ppermute | solution.py:710
  39.8 36.7 %collective-permute-start.10 = (bf16[736,128]{1,0:T(8,128)(2,1)S(1)}, bf16[736,128]{1,0:T(8,128)(2,1)S(1)}, u32[]{:S(2)}, u32[]{:S(2)}) collective-permute-start(bf16[736,128]{1,0:T(8,128)(2,1)S(1)} %get-tuple-element.74), channel_id=1, source_target_pairs={{0,24},{4,28},{1,25},{5,29},{2,26},{6,30},{3,27},{7,31}} | collective-permute-start | bytes 565256 | tf_op jit(solution)/shard_map/ppermute | solution.py:710
  41.1 35.4 %collective-permute-start.6 = (bf16[736,128]{1,0:T(8,128)(2,1)S(1)}, bf16[736,128]{1,0:T(8,128)(2,1)S(1)}, u32[]{:S(2)}, u32[]{:S(2)}) collective-permute-start(bf16[736,128]{1,0:T(8,128)(2,1)S(1)} %get-tuple-element.70), channel_id=1, source_target_pairs={{0,8},{4,12},{8,16},{12,20},{16,24},{20,28},{1,9},{5,13},{9,17},{1... | collective-permute-start | bytes 565256 | tf_op jit(solution)/shard_map/ppermute | solution.py:710
  42.5 34.1 %collective-permute-start.8 = (bf16[736,128]{1,0:T(8,128)(2,1)S(1)}, bf16[736,128]{1,0:T(8,128)(2,1)S(1)}, u32[]{:S(2)}, u32[]{:S(2)}) collective-permute-start(bf16[736,128]{1,0:T(8,128)(2,1)S(1)} %get-tuple-element.72), channel_id=1, source_target_pairs={{0,16},{4,20},{8,24},{12,28},{1,17},{5,21},{9,25},{13,29},{2,18},{... | collective-permute-start | bytes 565256 | tf_op jit(solution)/shard_map/ppermute | solution.py:710
  100.6 25.2 %collective-permute-start.11 = (bf16[256,2560]{1,0:T(8,128)(2,1)S(1)}, bf16[256,2560]{1,0:T(8,128)(2,1)S(1)}, u32[]{:S(2)}, u32[]{:S(2)}) collective-permute-start(bf16[256,2560]{1,0:T(8,128)(2,1)S(1)} %chosen_and_project.4), channel_id=1, source_target_pairs={{0,1},{1,0},{2,3},{3,2},{4,5},{5,4},{6,7},{7,6},{8,9},{9,8},{10,11... | collective-permute-start | bytes 3932168 | tf_op jit(solution)/shard_map/ppermute | solution.py:755
  126.2 49.6 %collective-permute-start.14 = (bf16[256,2560]{1,0:T(8,128)(2,1)S(1)}, bf16[256,2560]{1,0:T(8,128)(2,1)S(1)}, u32[]{:S(2)}, u32[]{:S(2)}) collective-permute-start(bf16[256,2560]{1,0:T(8,128)(2,1)S(1)} %add_convert_fusion), channel_id=1, source_target_pairs={{0,2},{1,3},{2,0},{3,1},{4,6},{5,7},{6,4},{7,5},{8,10},{9,11},{10,... | collective-permute-start | bytes 3932168 | tf_op jit(solution)/shard_map/ppermute | solution.py:765
  172.7 2.2 %collective-permute-start.12 = (bf16[256,1280]{1,0:T(8,128)(2,1)S(1)}, bf16[256,1280]{1,0:T(8,128)(2,1)S(1)}, u32[]{:S(2)}, u32[]{:S(2)}) collective-permute-start(bf16[256,1280]{1,0:T(8,128)(2,1)S(1)} %get-tuple-element.82), channel_id=1, source_target_pairs={{0,1},{1,0},{2,3},{3,2},{4,5},{5,4},{6,7},{7,6},{8,9},{9,8},{10,11... | collective-permute-start | bytes 1966088 | tf_op jit(solution)/shard_map/ppermute | solution.py:761
  173.1 2.7 %collective-permute-start.13 = (bf16[256,1280]{1,0:T(8,128)(2,1)S(1)}, bf16[256,1280]{1,0:T(8,128)(2,1)S(1)}, u32[]{:S(2)}, u32[]{:S(2)}) collective-permute-start(bf16[256,1280]{1,0:T(8,128)(2,1)S(1)} %get-tuple-element.83), channel_id=1, source_target_pairs={{0,1},{1,0},{2,3},{3,2},{4,5},{5,4},{6,7},{7,6},{8,9},{9,8},{10,11... | collective-permute-start | bytes 1966088 | tf_op jit(solution)/shard_map/ppermute | solution.py:761
  175.8 1.3 copy-start
